TPU v7x, 32 devices: a whole 2x2x4 slice. The times are simulated.
32 devices in a mesh: grp: 2 (over y), aux: 4 (over x, core), pair: 4 (over z).
Axes of the slice: x: 2, y: 2, z: 4, core: 2. Of those that a mesh axis runs over, the one named last changes fastest.
Arguments:
- three_centre: bfloat16 [8, 4, 8, 3, 1, 128, 640], P(('grp', 'aux'), 'pair'), parts along dimension 0, may hold values from -0.23925781 to 0.23925781
- locality: int32 [8, 4, 8, 3, 1], P(('grp', 'aux'), 'pair'), parts along dimension 0, may hold values 0 or 1
- live_blocks: int32 [8, 4], P(('grp', 'aux'), 'pair'), parts along dimension 0, may hold values from 2 to 8
- occ_energy: float32 [16], P('grp'), parts along dimension 0, may hold values from -1.2 to -0.4
- virt_energy: float32 [20480], P('grp'), parts along dimension 0, may hold values from 0.2 to 3
- frequencies: float32 [4], P('grp'), parts along dimension 0, may hold values from 0.3 to 3
Outputs:
- polarizability: float32 [2, 8, 8, 128, 384], P(None, None, ('grp', 'aux'), 'pair'), parts along dimension 2
There are 2 independent parts, one for each index of `grp`. A program takes and returns all parts, laid end to end along the dimension named above; each array names one. Nothing has to cross between parts.
All inputs are finite; a program needn't handle non-finite values. No bound on the sum of `locality` on one device may be relied on, other than what follows from the above.
Results may differ from a plain program's by a relative error of at most 0.00095.
Values may be sent and summed in bfloat16 or wider, within the bound.
No kernel may reach another device: no remote copies, remote signals or barrier semaphores. Data moves between devices by JAX's collectives and lax.ppermute only.
A program may use at most 64 MiB of HBM per device.

v0:
```python
import jax
import jax.numpy as jnp
from jax import lax
from jax.sharding import PartitionSpec as P


def weigh(tiles, present, gaps, frequencies):
    omega = frequencies.reshape((-1,) + (1,) * gaps.ndim)
    factor = 2.0 * gaps[None] / (gaps[None] * gaps[None] + omega * omega)
    root = jnp.sqrt(factor)
    scaled = tiles.astype(jnp.float32)[None] * root[..., None, :]
    return (scaled * present[None, ..., None, None]).astype(jnp.bfloat16)


def pair_gaps(centre, members, blocks_dev, pair_col, columns, occ_energy, virt_energy, pair_rows):
    virt_blocks = virt_energy.shape[0] // pair_rows
    region = centre // blocks_dev
    number = centre % blocks_dev + blocks_dev * members
    global_block = (region * columns + pair_col) * (blocks_dev * members.shape[-1]) + number
    table = virt_energy.reshape(virt_blocks, pair_rows)
    gaps = (
        jnp.take(table, global_block % virt_blocks, axis=0)
        - jnp.take(occ_energy, global_block // virt_blocks)[..., None]
    )
    return (gaps, region, number)


def route_out(partial_value, aux_pos, blocks_dev, n_aux, repeats, n_blocks):
    span = partial_value.shape[1]
    target = jnp.arange(n_aux, dtype=jnp.int32)[:, None]
    turn = jnp.arange(repeats, dtype=jnp.int32)[None, :]
    offset = (target - aux_pos * blocks_dev) % n_aux + turn * n_aux
    good = (offset < span) & (aux_pos * blocks_dev + offset < n_blocks)
    picked = jnp.take(partial_value, jnp.minimum(offset, span - 1), axis=1)
    good_shape = good.reshape((1,) + good.shape + (1,) * (partial_value.ndim - 2))
    return jnp.where(good_shape, picked, 0.0)


def route_in(received, aux_pos, blocks_dev, n_aux, repeats, n_blocks, span):
    source = jnp.arange(n_aux, dtype=jnp.int32)[:, None]
    turn = jnp.arange(repeats, dtype=jnp.int32)[None, :]
    offset = (aux_pos - source * blocks_dev) % n_aux + turn * n_aux
    block_ids = source * blocks_dev + offset
    good = (offset < span) & (block_ids < n_blocks)
    slots = jnp.arange(blocks_dev, dtype=jnp.int32)
    onehot = (good[..., None] & (block_ids[..., None] // n_aux == slots)).astype(jnp.float32)
    return jnp.einsum("fqtdxy,qtm->fmxdy", received, onehot, precision=lax.Precision.HIGHEST)


def on_device(three_centre, locality, live_blocks, occ_energy, virt_energy, frequencies):
    n_aux = lax.axis_size("aux")
    n_pair = lax.axis_size("pair")
    aux_pos = lax.axis_index("aux")
    pair_col = lax.axis_index("pair")
    tiles = three_centre[0, 0]
    local_mask = locality[0, 0]
    blocks_dev, band, per_centre, aux_rows, pair_rows = tiles.shape
    n_blocks = blocks_dev * n_aux
    freq_count = frequencies.shape[0]
    rows_dev = aux_rows // n_pair
    members = jnp.arange(per_centre, dtype=jnp.int32)
    repeats = (blocks_dev + band - 2) // n_aux + 1
    span = blocks_dev + band - 1
    target = jnp.arange(n_aux, dtype=jnp.int32)[:, None, None, None]
    turn = jnp.arange(repeats, dtype=jnp.int32)[None, :, None, None]
    slot_grid = jnp.arange(band, dtype=jnp.int32)[None, None, :, None]
    member_grid = members[None, None, None, :]
    offset = (aux_pos - target * blocks_dev) % n_aux + turn * n_aux
    block_ids = target * blocks_dev + offset
    fits = (
        (offset < span)
        & (offset >= slot_grid)
        & (offset - slot_grid < blocks_dev)
        & (block_ids < n_blocks)
    )
    source_block = jnp.minimum(block_ids // n_aux, blocks_dev - 1)
    flat = (source_block * band + slot_grid) * per_centre + member_grid
    send_tiles = jnp.take(tiles.reshape(-1, aux_rows, pair_rows), flat, axis=0)
    send_mask = jnp.where(fits, jnp.take(local_mask.reshape(-1), flat), 0).astype(jnp.bfloat16)
    got_tiles, got_mask = (
        lax.all_to_all(send_tiles, "aux", split_axis=0, concat_axis=0, tiled=True),
        lax.all_to_all(send_mask, "aux", split_axis=0, concat_axis=0, tiled=True),
    )
    unit = jnp.arange(blocks_dev, dtype=jnp.int32)[:, None, None]
    slot_ids = jnp.arange(band, dtype=jnp.int32)[None, :, None]
    member_ids = members[None, None, :]
    position = unit + slot_ids
    source = (aux_pos * blocks_dev + position) % n_aux
    pick = ((source * repeats + position // n_aux) * band + slot_ids) * per_centre + member_ids
    mine = jnp.take(got_tiles.reshape(-1, aux_rows, pair_rows), pick, axis=0)
    mine_mask = jnp.take(got_mask.reshape(-1), pick)
    centre = aux_pos * blocks_dev + unit
    gaps, region, number = pair_gaps(
        centre, member_ids, blocks_dev, pair_col, n_pair, occ_energy, virt_energy, pair_rows
    )
    gaps = jnp.broadcast_to(gaps, (blocks_dev, band, per_centre, pair_rows))
    present = (
        (centre + slot_ids < n_blocks) & (mine_mask > 0) & (number < live_blocks[0, 0])
    ).astype(jnp.float32)
    scaled = weigh(mine, present, gaps, frequencies)
    bands = []
    for delta in range(band):
        total = jnp.zeros((freq_count, span, aux_rows, aux_rows), jnp.float32)
        for slot in range(band - delta):
            product = jnp.einsum(
                "fukxr,fukyr->fuxy",
                scaled[:, :, slot],
                scaled[:, :, slot + delta],
                preferred_element_type=jnp.float32,
            )
            total = total + jnp.pad(product, ((0, 0), (slot, band - 1 - slot), (0, 0), (0, 0)))
        bands.append(total)
    partial_value = jnp.stack(bands, axis=2)
    outgoing = route_out(partial_value, aux_pos, blocks_dev, n_aux, repeats, n_blocks)
    received = lax.all_to_all(outgoing, "aux", split_axis=1, concat_axis=1, tiled=True)
    owned = route_in(received, aux_pos, blocks_dev, n_aux, repeats, n_blocks, span)
    owned = owned.reshape(freq_count, blocks_dev, aux_rows, band * aux_rows)
    summed = lax.psum_scatter(owned, "pair", scatter_dimension=2, tiled=True)
    return summed.reshape(freq_count, blocks_dev, 1, rows_dev, band * aux_rows)


def solution(mesh):
    return jax.shard_map(
        on_device,
        mesh=mesh,
        in_specs=(
            P(("grp", "aux"), "pair", None, None, None, None, None),
            P(("grp", "aux"), "pair", None, None, None),
            P(("grp", "aux"), "pair"),
            P("grp"),
            P("grp"),
            P("grp"),
        ),
        out_specs=P(None, None, ("grp", "aux"), "pair", None),
        check_vma=False,
    )
```

profile of v0, /device:TPU:1, one launch (start us, length us, event | category | flops | bytes accessed | tf_op | source)
XLA Modules:
  0.0 275.8 jit_solution(13251607103429517561)
XLA Ops:
  7.0 0.8 copy.56
  7.8 0.8 gather_fusion.4
  8.8 0.6 copy.58
  9.4 4.3 %all-to-all-start.1 = ((bf16[4,3,3,1]{2,1,3,0:T(4,128)(2,1)}), bf16[4,3,3,1]{2,1,3,0:T(4,128)(2,1)S(1)}, u32[]{:S(2)}, u32[]{:S(2)}) async-start(bf16[4,3,3,1]{2,1,3,0:T(4,128)(2,1)} %copy.58), calls=%async_computation.1 | async-start | bytes 8192 | tf_op jit(solution)/shard_map/all_to_all | solution.py:82
  13.7 7.4 %gather_fusion = bf16[36,128,640]{2,1,0:T(8,128)(2,1)} fusion(bf16[24,128,640]{2,1,0:T(8,128)(2,1)} %bitcast.64, s32[1024]{0:T(1024)S(1)} %pad_clamp_fusion.4), kind=kCustom, calls=%fused_computation | custom fusion | bytes 11796624 | tf_op jit(solution)/shard_map/jit(_take)/gather | solution.py:78
  21.2 5.9 %broadcast_select_fusion = bf16[4,3,3,1,128,640]{5,4,2,1,3,0:T(8,128)(2,1)} fusion(bf16[4,3,3,1,128,640]{5,4,2,1,3,0:T(8,128)(2,1)} %bitcast.60, pred[4,3,3]{2,1,0:T(4,128)(4,1)S(1)} %fusion.17), kind=kLoop, calls=%fused_computation.8 | loop fusion | flops 2949120 | bytes 11796516 | tf_op jit(solution)/shard_map/jit(_take)/select_n | solution.py:78
  27.1 5.3 %all-to-all-start = ((bf16[4,3,3,1,128,640]{5,4,2,1,3,0:T(8,128)(2,1)}), bf16[4,3,3,1,128,640]{5,4,2,1,3,0:T(8,128)(2,1)}, u32[]{:S(2)}, u32[]{:S(2)}) async-start(bf16[4,3,3,1,128,640]{5,4,2,1,3,0:T(8,128)(2,1)} %broadcast_select_fusion), calls=%async_computation | async-start | bytes 11796480 | tf_op jit(solution)/shard_map/all_to_all | solution.py:81
  32.4 0.2 reduce-scatter.2.cloned.1.call-start
  33.9 0.6 gather_fusion.3
  34.5 0.6 gather_fusion.2
  35.5 0.7 gather_fusion.5
  36.4 61.7 %all-to-all-done = bf16[4,3,3,1,128,640]{5,4,2,1,3,0:T(8,128)(2,1)} async-done(((bf16[4,3,3,1,128,640]{5,4,2,1,3,0:T(8,128)(2,1)}), bf16[4,3,3,1,128,640]{5,4,2,1,3,0:T(8,128)(2,1)}, u32[]{:S(2)}, u32[]{:S(2)}) %all-to-all-start) | async-done | bytes 5898272 | tf_op jit(solution)/shard_map/all_to_all | solution.py:81
  98.1 5.9 %gather_fusion.1 = bf16[24,128,640]{2,1,0:T(8,128)(2,1)} fusion(bf16[36,128,640]{2,1,0:T(8,128)(2,1)} %bitcast.4, s32[1024]{0:T(1024)S(1)} %pad_clamp_fusion.3), kind=kCustom, calls=%fused_computation.1 | custom fusion | bytes 7864416 | tf_op jit(solution)/shard_map/jit(_take)/gather | solution.py:90
  104.0 8.4 %multiply_convert_fusion = bf16[2,8,3,1,128,640]{5,4,1,0,3,2:T(8,128)(2,1)} fusion(f32[8,3]{0,1:T(4,128)S(1)} %copy.59, f32[2,8,3,640]{3,1,0,2:T(8,128)S(1)} %divide_sqrt_fusion, bf16[8,3,128,640]{3,2,1,0:T(8,128)(2,1)} %bitcast.62, pred[8,3]{1,0:T(8,128)(4,1)S(1)} %compare_and_fusion), kind=kLoop, calls=%fused_computation.7 | loop fusion | flops 15728640 | bytes 11919480 | tf_op jit(solution)/shard_map/convert_element_type | solution.py:12
  112.4 3.8 %fusion.6 = f32[2,8,128,128]{3,2,1,0:T(8,128)S(1)} fusion(bf16[2,8,3,1,128,640]{5,4,1,0,3,2:T(8,128)(2,1)} %multiply_convert_fusion), kind=kOutput, calls=%fused_computation.21 | convolution fusion | flops 335544320 | bytes 3670016 | tf_op jit(solution)/shard_map/fukxr,fukyr->fuxy/dot_general | solution.py:105
  116.2 3.6 %fusion.8 = f32[2,8,128,128]{3,2,1,0:T(8,128)S(1)} fusion(bf16[2,8,3,1,128,640]{5,4,1,0,3,2:T(8,128)(2,1)} %multiply_convert_fusion), kind=kOutput, calls=%fused_computation.23 | convolution fusion | flops 335544320 | bytes 3670016 | tf_op jit(solution)/shard_map/fukxr,fukyr->fuxy/dot_general | solution.py:105
  119.8 1.1 fusion.9
  120.9 1.1 fusion.5
  122.0 1.1 fusion.7
  123.1 1.1 fusion.4
  124.2 0.1 pad_bitcast_fusion
  124.3 0.1 add_bitcast_fusion
  124.4 0.2 add_bitcast_fusion.1
  124.6 2.4 pad_maximum_fusion
  127.0 5.1 %gather_fusion.6 = f32[12,2,3,128,128]{4,3,1,2,0:T(8,128)} fusion(f32[2,10,3,128,128]{4,3,1,0,2:T(8,128)} %pad_maximum_fusion, s32[1024]{0:T(1024)S(1)} %pad_clamp_fusion), kind=kCustom, calls=%fused_computation.6 | custom fusion | bytes 9437232 | tf_op jit(solution)/shard_map/jit(_take)/gather | solution.py:34
  132.1 3.4 %fusion.3 = f32[2,4,3,3,128,128]{5,4,3,2,0,1:T(8,128)S(1)} fusion(f32[4,3,2,3,128,128]{5,4,2,3,1,0:T(8,128)} %bitcast.61, pred[4,3]{1,0:T(4,128)(4,1)S(1)} %copy.51, pred[4,3]{1,0:T(4,128)(4,1)S(1)} %copy.52), kind=kLoop, calls=%fused_computation.13 | loop fusion | flops 2359296 | bytes 9437208 | tf_op jit(solution)/shard_map/jit(_where)/select_n | solution.py:36
  135.5 56.2 %all_to_all.15 = f32[2,4,3,3,128,128]{5,4,3,2,0,1:T(8,128)S(1)} all-to-all(f32[2,4,3,3,128,128]{5,4,3,2,0,1:T(8,128)S(1)} %fusion.3), channel_id=1, replica_groups=mesh['grp'=2,'aux'=4,'pair'=4] {'aux'}, dimensions={1} | all-to-all | bytes 9437184 | tf_op jit(solution)/shard_map/all_to_all | solution.py:115
  191.7 7.5 %fusion.10 = f32[2,8,128,3,128]{4,1,2,3,0:T(8,128)S(1)} fusion(f32[2,4,3,3,128,128]{5,4,3,2,0,1:T(8,128)S(1)} %all_to_all.15, s32[4,3]{0,1:T(4,128)S(1)} %get-tuple-element.10, pred[4,3]{0,1:T(4,128)(4,1)S(1)} %get-tuple-element.15), kind=kOutput, calls=%fused_computation.25 | convolution fusion | flops 113246400 | bytes 7864380 | tf_op jit(solution)/shard_map/fqtdxy,qtm->fmxdy/dot_general | solution.py:47
  199.2 2.4 copy.62
  201.6 3.7 %copy.63 = f32[2,8,128,384]{3,1,0,2:T(8,128)} copy(f32[2,8,128,384]{2,3,1,0:T(8,128)} %bitcast.63) | data formatting | bytes 6291456 | tf_op jit(solution)/shard_map/reshape | solution.py:117
  205.3 61.4 %reduce-scatter.2.cloned.1.call-done = f32[2,8,32,384]{3,1,0,2:T(8,128)} async-done(((f32[2,8,128,384]{3,1,0,2:T(8,128)}), f32[2,8,32,384]{3,1,0,2:T(8,128)}) %reduce-scatter.2.cloned.1.call-update) | async-done | bytes 786448 | tf_op jit(solution)/shard_map/reduce_scatter | solution.py:118
  266.7 2.3 copy.64
  (48 shorter events, 1.9 us)
Async XLA Ops:
  6.5 27.3 %copy-start = (f32[8]{0:T(128)S(1)}, f32[8]{0:T(128)}, u32[]{:S(2)}) copy-start(f32[8]{0:T(128)} %param.9) | copy-start | bytes 100
  9.4 17.7 %all-to-all-start.1 = ((bf16[4,3,3,1]{2,1,3,0:T(4,128)(2,1)}), bf16[4,3,3,1]{2,1,3,0:T(4,128)(2,1)S(1)}, u32[]{:S(2)}, u32[]{:S(2)}) async-start(bf16[4,3,3,1]{2,1,3,0:T(4,128)(2,1)} %copy.58), calls=%async_computation.1 | async-start | bytes 8192 | tf_op jit(solution)/shard_map/all_to_all | solution.py:82
  27.1 5.6 %copy-start.3 = (f32[10240]{0:T(1024)S(1)}, f32[10240]{0:T(1024)}, u32[]{:S(2)}) copy-start(f32[10240]{0:T(1024)} %param.10) | copy-start | bytes 122884
  27.1 6.2 %copy-start.4 = (f32[2]{0:T(128)S(1)}, f32[2]{0:T(128)}, u32[]{:S(2)}) copy-start(f32[2]{0:T(128)} %param.11) | copy-start | bytes 28
  27.1 71.0 %all-to-all-start = ((bf16[4,3,3,1,128,640]{5,4,2,1,3,0:T(8,128)(2,1)}), bf16[4,3,3,1,128,640]{5,4,2,1,3,0:T(8,128)(2,1)}, u32[]{:S(2)}, u32[]{:S(2)}) async-start(bf16[4,3,3,1,128,640]{5,4,2,1,3,0:T(8,128)(2,1)} %broadcast_select_fusion), calls=%async_computation | async-start | bytes 11796480 | tf_op jit(solution)/shard_map/all_to_all | solution.py:81
  32.4 234.3 %reduce-scatter.2.cloned.1.call-start = ((), (), s32[]{:S(2)}) async-start(), calls=%async_computation.4 | async-start | bytes 3932160 | tf_op jit(solution)/shard_map/reduce_scatter | solution.py:118
  112.4 7.4 %copy-start.2 = (bf16[2,8,3,1,128,640]{5,4,1,0,3,2:T(8,128)(2,1)S(1)}, bf16[2,8,3,1,128,640]{5,4,1,0,3,2:T(8,128)(2,1)}, u32[]{:S(2)}) copy-start(bf16[2,8,3,1,128,640]{5,4,1,0,3,2:T(8,128)(2,1)} %multiply_convert_fusion) | copy-start | bytes 23592964
  201.6 67.4 %copy-start.1 = (f32[8]{0:T(128)S(1)}, f32[8]{0:T(128)}, u32[]{:S(2)}) copy-start(f32[8]{0:T(128)} %param.9) | copy-start | bytes 100
Sparse Core Ops, SparseCore 0:
  205.5 61.2 reduce-scatter.1
where the time goes:
time: 277 us; the launch traced here: 276 us
  waiting for transfers between devices  123 us (44%)
  blocking collectives  56.2 us (20%)
  local copies, waits for them, and re-layouts  31.9 us (12%)
  other arithmetic  21.4 us (8%)
  matrix products  19.2 us (7%)
  between operations  14.3 us (5%)
  starting transfers between devices  9.78 us (4%)
    all_to_all x1, waiting for transfers between devices, on_device(): lax.all_to_all(send_tiles, 'aux', split_axis=0, concat_axis=0, tiled=True)  61.7 us
    reduce_scatter x1, waiting for transfers between devices, on_device(): summed = lax.psum_scatter(owned, 'pair', scatter_dimension=2, tiled=True)  61.4 us
    all_to_all x1, blocking collectives, on_device(): lax.all_to_all(outgoing, 'aux', split_axis=1, concat_axis=1, tiled=True)  56.2 us
    dot_general x6, matrix products, on_device(): jnp.einsum('fukxr,fukyr->fuxy', scaled[:, :, slot], scaled[:, :, slot + d...  11.7 us
    convert_element_type x1, other arithmetic, weigh(): return (scaled * present[None, ..., None, None]).astype(jnp.bfloat16)  8.45 us
    dot_general x1, matrix products, route_in(): jnp.einsum('fqtdxy,qtm->fmxdy', received, onehot, precision=lax.Precision...  7.53 us
    gather x1, local copies, waits for them, and re-layouts, on_device(): send_tiles = jnp.take(tiles.reshape(-1, aux_rows, pair_rows), flat, axis=0)  7.41 us
    select_n x2, other arithmetic, on_device(): send_tiles = jnp.take(tiles.reshape(-1, aux_rows, pair_rows), flat, axis=0)  5.99 us
  transfers between devices with their start and end apart: 3, of which 2 were waited for; matrix products, arithmetic and copies ran while one was open for 6% of the time, Pallas kernels for 0%

commit v1 on v0

v1 whole, which is shorter than its diff:
```python
import functools

import jax
import jax.numpy as jnp
from jax import lax
from jax.experimental import pallas as pl
from jax.experimental.pallas import tpu as pltpu
from jax.sharding import PartitionSpec as P

HEAD = 2


def band_kernel(dims, first, delta, slots, n_own, *refs):
    n_aux, n_pair, blocks_dev, band, freq_count = dims
    meta, occ, freq, table, own = refs[:5]
    others = refs[5:-1]
    out = refs[-1]
    virt_blocks = table.shape[0]
    record = blocks_dev * band + 1
    aux_pos, pair_col = meta[0], meta[1]
    shift = ((aux_pos + delta) >= n_aux).astype(jnp.int32)
    there = pl.program_id(0) + first
    here = there - shift
    block = here * n_aux + aux_pos
    far = lax.rem(aux_pos + delta, n_aux)
    sums = [None] * freq_count
    for slot in slots:
        centre = block - slot
        safe = jnp.maximum(centre, 0)
        region = safe // blocks_dev
        number = lax.rem(safe, blocks_dev)
        own_row = jnp.maximum(here, 0)
        live = meta[HEAD + region * record + blocks_dev * band]
        left_on = meta[HEAD + aux_pos * record + own_row * band + slot]
        right_on = meta[HEAD + far * record + there * band + slot + delta]
        keep = (centre >= 0) & (number < live) & (left_on > 0) & (right_on > 0)
        present = keep.astype(jnp.float32)
        pair_block = (region * n_pair + pair_col) * blocks_dev + number
        gap = table[pl.ds(lax.rem(pair_block, virt_blocks), 1), :] - occ[pair_block // virt_blocks]
        left = own[0, slot].astype(jnp.float32)
        right = None if delta == 0 else others[slot][0].astype(jnp.float32)
        for w in range(freq_count):
            omega = freq[w]
            root = jnp.sqrt(2.0 * gap / (gap * gap + omega * omega))
            a = (left * (root * present)).astype(jnp.bfloat16)
            b = a if right is None else (right * root).astype(jnp.bfloat16)
            term = lax.dot_general(a, b, (((1,), (1,)), ((), ())), preferred_element_type=jnp.float32)
            sums[w] = term if sums[w] is None else sums[w] + term
    for w in range(freq_count):
        out[w, 0] = sums[w]


def band_rows(dims, first, count, delta, meta, occ, freq, table, tiles, others):
    n_aux, n_pair, blocks_dev, band, freq_count = dims
    aux_rows, pair_rows = tiles.shape[-2:]
    slots = range(band - delta)

    def own_index(i, meta):
        shift = ((meta[0] + delta) >= n_aux).astype(jnp.int32)
        return (jnp.maximum(i + first - shift, 0), 0, 0, 0)

    def far_index(offset):
        return lambda i, meta: (i + offset, 0, 0)

    smem = pl.BlockSpec(memory_space=pltpu.SMEM)
    return pl.pallas_call(
        functools.partial(band_kernel, dims, first, delta, slots, len(others)),
        out_shape=jax.ShapeDtypeStruct((freq_count, count, aux_rows, aux_rows), jnp.float32),
        grid_spec=pltpu.PrefetchScalarGridSpec(
            num_scalar_prefetch=1,
            grid=(count,),
            in_specs=[
                smem,
                smem,
                pl.BlockSpec(table.shape, lambda i, meta: (0, 0)),
                pl.BlockSpec((1, band - delta, aux_rows, pair_rows), own_index),
            ]
            + [pl.BlockSpec((1, aux_rows, pair_rows), far_index(offset)) for _, offset in others],
            out_specs=pl.BlockSpec((freq_count, 1, aux_rows, aux_rows), lambda i, meta: (0, i, 0, 0)),
        ),
        cost_estimate=pl.CostEstimate(
            flops=4 * count * len(slots) * aux_rows * aux_rows * pair_rows,
            bytes_accessed=count * len(slots) * aux_rows * pair_rows * 4,
            transcendentals=0,
        ),
    )(meta, occ, freq, table, tiles, *[array for array, _ in others])


def spread(rows, pair_col, n_pair, scale):
    height = rows.shape[2] // n_pair
    parts = []
    for k in range(1, n_pair):
        start = lax.rem(pair_col + k, n_pair) * height
        part = (lax.dynamic_slice_in_dim(rows, start, height, 2) * scale).astype(jnp.float16)
        parts.append(lax.ppermute(part, "pair", [(s, (s + k) % n_pair) for s in range(n_pair)]))
    return lax.dynamic_slice_in_dim(rows, pair_col * height, height, 2), parts


def gather_sum(pieces, scale):
    own, parts = pieces
    far = sum(part.astype(jnp.float32) for part in parts)
    return own + far * (1.0 / scale)


def on_device(three_centre, locality, live_blocks, occ_energy, virt_energy, frequencies):
    n_aux = lax.axis_size("aux")
    n_pair = lax.axis_size("pair")
    aux_pos = lax.axis_index("aux")
    pair_col = lax.axis_index("pair")
    tiles = three_centre[0, 0, :, :, 0]
    blocks_dev, band, aux_rows, pair_rows = tiles.shape
    freq_count = frequencies.shape[0]
    dims = (n_aux, n_pair, blocks_dev, band, freq_count)
    half = blocks_dev // 2
    scale = 128.0 / n_pair
    table = virt_energy.reshape(-1, pair_rows)
    record = jnp.concatenate([locality[0, 0].reshape(-1), live_blocks[0]])
    records = lax.all_gather(record, "aux", tiled=True)
    meta = jnp.concatenate([jnp.stack([aux_pos, pair_col]).astype(jnp.int32), records])

    down1 = [(s, (s - 1) % n_aux) for s in range(n_aux)]
    down2 = [(s, (s - 2) % n_aux) for s in range(n_aux)]
    swap = [(s, s ^ 1) for s in range(n_aux)]
    c2 = [lax.ppermute(tiles[h : h + half, 2], "aux", down2) for h in (0, half)]
    b1 = [lax.ppermute(tiles[h : h + half, 1], "aux", down1) for h in (0, half)]
    args = (meta, occ_energy, frequencies, table, tiles)
    z0 = spread(band_rows(dims, 0, blocks_dev, 0, *args, []), pair_col, n_pair, scale)
    even = aux_pos % 2 == 0
    z2, b2 = [], []
    for n, h in enumerate((0, half)):
        b2.append(lax.ppermute(jnp.where(even, c2[n], tiles[h : h + half, 2]), "aux", swap))
        z2.append(spread(band_rows(dims, h, half, 2, *args, [(c2[n], 0)]), pair_col, n_pair, scale))
    z1 = []
    for n, h in enumerate((0, half)):
        z1.append(
            spread(band_rows(dims, h, half, 1, *args, [(b1[n], 0), (b2[n], 0)]), pair_col, n_pair, scale)
        )

    def settle(pieces, delta):
        rows = jnp.concatenate([gather_sum(piece, scale) for piece in pieces], axis=1)
        return jnp.where(aux_pos + delta >= n_aux, jnp.roll(rows, -1, axis=1), rows) if delta else rows

    out = jnp.concatenate([settle([z0], 0), settle(z1, 1), settle(z2, 2)], axis=-1)
    return out[:, :, None]


def solution(mesh):
    return jax.shard_map(
        on_device,
        mesh=mesh,
        in_specs=(
            P(("grp", "aux"), "pair", None, None, None, None, None),
            P(("grp", "aux"), "pair", None, None, None),
            P(("grp", "aux"), "pair"),
            P("grp"),
            P("grp"),
            P("grp"),
        ),
        out_specs=P(None, None, ("grp", "aux"), "pair", None),
        check_vma=False,
    )
```

time: 277 us -> 128 us (0.46)
  waiting for transfers between devices: 123 us -> 16.2 us
  blocking collectives: 56.2 us -> 26.2 us
  Pallas kernels: 0 us -> 28.2 us
  local copies, waits for them, and re-layouts: 31.9 us -> 11.2 us
  matrix products: 19.2 us -> 0 us
  starting transfers between devices: 9.78 us -> 25.5 us
  between operations: 14.3 us -> 1.53 us
  other arithmetic: 21.4 us -> 16.2 us
    all_to_all x2 -> x0, waiting for transfers between devices: 61.7 us -> none  [the longest x1 61.7 us: on_device(): lax.all_to_all(send_tiles, 'aux', split_axis=0, concat_axis=0, tiled=True)]
    reduce_scatter x1 -> x0, waiting for transfers between devices: 61.4 us -> none  [on_device(): summed = lax.psum_scatter(owned, 'pair', scatter_dimension=2, tiled=True)]
    all_to_all x1 -> x0, blocking collectives: 56.2 us -> none  [on_device(): lax.all_to_all(outgoing, 'aux', split_axis=1, concat_axis=1, tiled=True)]
    pallas_call x0 -> x5, Pallas kernels: none -> 28.2 us  [band_rows(): pl.pallas_call(functools.partial(band_kernel, dims, first, delta, slots,...]
    unnamed x0 -> x1, blocking collectives: none -> 26.2 us
    ppermute x0 -> x21, starting transfers between devices: none -> 25.5 us  [the longest x15 19.7 us: spread(): lax.ppermute(part, 'pair', [(s, (s + k) % n_pair) for s in range(n_pair)])]
    gather x9 -> x0, local copies, waits for them, and re-layouts: 21.3 us -> none  [the longest x1 7.41 us: on_device(): send_tiles = jnp.take(tiles.reshape(-1, aux_rows, pair_rows), flat, axis=0)]
    dot_general x7 -> x0, matrix products: 19.2 us -> none  [the longest x6 11.7 us: on_device(): jnp.einsum('fukxr,fukyr->fuxy', scaled[:, :, slot], scaled[:, :, slot + d...]
  transfers between devices with their start and end apart: 3 -> 21, of which waited for: 2 -> 6; matrix products, arithmetic and copies ran while one was open for 6% -> 13% of each run, Pallas kernels for 0% -> 23%
where the time goes in v1:
time: 128 us; the launch traced here: 125 us
  Pallas kernels  28.2 us (22%)
  blocking collectives  26.2 us (20%)
  starting transfers between devices  25.5 us (20%)
  other arithmetic  16.2 us (13%)
  waiting for transfers between devices  16.2 us (13%)
  local copies, waits for them, and re-layouts  11.2 us (9%)
  between operations  1.53 us (1%)
    pallas_call x5, Pallas kernels, band_rows(): pl.pallas_call(functools.partial(band_kernel, dims, first, delta, slots,...  28.2 us
    unnamed x1, blocking collectives  26.2 us
    ppermute x15, starting transfers between devices, spread(): lax.ppermute(part, 'pair', [(s, (s + k) % n_pair) for s in range(n_pair)])  19.7 us
    ppermute x15, waiting for transfers between devices, spread(): lax.ppermute(part, 'pair', [(s, (s + k) % n_pair) for s in range(n_pair)])  12.7 us
    unnamed x26, local copies, waits for them, and re-layouts  9.34 us
    convert_element_type x5, other arithmetic, spread(): (lax.dynamic_slice_in_dim(rows, start, height, 2) * scale).astype(jnp.flo...  6.93 us
    add x5, other arithmetic, gather_sum(): return own + far * (1.0 / scale)  5.08 us
    ppermute x2, waiting for transfers between devices, on_device(): b1 = [lax.ppermute(tiles[h:h + half, 1], 'aux', down1) for h in (0, half)]  3.48 us
  transfers between devices with their start and end apart: 21, of which 6 were waited for; matrix products, arithmetic and copies ran while one was open for 13% of the time, Pallas kernels for 23%

profile of v1, /device:TPU:1, one launch (start us, length us, event | category | flops | bytes accessed | tf_op | source)
XLA Modules:
  0.0 125.1 jit_solution(10094646887799496812)
XLA Ops:
  0.0 2.5 %copy.25 = bf16[1,1,8,3,1,128,640]{6,5,2,3,4,1,0:T(8,128)(2,1)S(1)} copy(bf16[1,1,8,3,1,128,640]{6,5,4,3,2,1,0:T(8,128)(2,1)} %param.6) | data formatting | bytes 7864320 | tf_op args[0]
  2.6 1.8 %copy-done = bf16[1,1,8,3,1,128,640]{6,5,2,3,4,1,0:T(8,128)(2,1)} copy-done((bf16[1,1,8,3,1,128,640]{6,5,2,3,4,1,0:T(8,128)(2,1)}, bf16[1,1,8,3,1,128,640]{6,5,2,3,4,1,0:T(8,128)(2,1)S(1)}, u32[]{:S(2)}) %copy-start) | copy-done | bytes 3932184
  4.4 1.1 slice_bitcast_fusion.3
  5.5 2.0 %collective-permute-start.10 = (bf16[4,128,640]{2,1,0:T(8,128)(2,1)S(1)}, bf16[4,128,640]{2,1,0:T(8,128)(2,1)S(1)}, u32[]{:S(2)}, u32[]{:S(2)}) collective-permute-start(bf16[4,128,640]{2,1,0:T(8,128)(2,1)S(1)} %get-tuple-element.8), channel_id=1, source_target_pairs={{0,8},{4,12},{8,0},{12,4},{1,9},{5,13},{9,1},{13,5},{2,10},{6,14},... | collective-permute-start | bytes 1966088 | tf_op jit(solution)/shard_map/ppermute | solution.py:124
  10.0 26.2 %all-reduce = s32[100]{0:T(128)S(1)} all-reduce(s32[100]{0:T(128)S(1)} %add_dynamic-update-slice_fusion), channel_id=1, replica_groups=mesh['grp'=2,'aux'=4,'pair'=4] {'aux'}, use_global_device_ids=true, to_apply=%add | all-reduce | flops 100 | bytes 800
  37.5 8.6 %shard_map.64 = f32[2,8,128,128]{3,2,1,0:T(8,128)} custom-call(s32[102]{0:T(128)} %pad_add_fusion.refs_0_, f32[8]{0:T(128)} %refs_1_.9, f32[2]{0:T(128)} %refs_2_.9, f32[16,640]{1,0:T(8,128)} %reshape.3.refs_3_, bf16[8,3,128,640]{3,2,1,0:T(8,128)(2,1)} %bitcast.29), custom_call_target="tpu_custom_call" | custom-call | flops 1006632960 | bytes 7864320 | tf_op jit(solution)/shard_map/pallas_call | solution.py:66
  46.1 1.9 %multiply_convert_fusion.2 = (f16[2,8,32,128]{3,2,1,0:T(8,128)(2,1)}, f16[2,8,32,128]{3,2,1,0:T(8,128)(2,1)S(1)}, f16[2,8,32,128]{3,2,1,0:T(8,128)(2,1)}) fusion(f32[2,8,128,128]{3,2,1,0:T(8,128)} %shard_map.64, s32[]{:T(128)S(6)} %select_n.62, s32[]{:T(128)S(6)} %select_n.64, s32[]{:T(128)S(6)} %select_n.63), kind=kLoop, calls=%fused_computation.19 | loop fusion | flops 393216 | bytes 1179660 | tf_op jit(solution)/shard_map/convert_element_type | solution.py:94
  48.0 1.2 collective-permute-start
  49.2 2.3 %collective-permute-start.1 = (f16[2,8,32,128]{3,2,1,0:T(8,128)(2,1)}, f16[2,8,32,128]{3,2,1,0:T(8,128)(2,1)}, u32[]{:S(2)}, u32[]{:S(2)}) collective-permute-start(f16[2,8,32,128]{3,2,1,0:T(8,128)(2,1)} %get-tuple-element.13), channel_id=1, source_target_pairs={{0,2},{1,3},{2,0},{3,1},{4,6},{5,7},{6,4},{7,5},{8,10},{9,11},{10,... | collective-permute-start | bytes 393224 | tf_op jit(solution)/shard_map/ppermute | solution.py:95
  52.6 1.3 %collective-permute-done = f16[2,8,32,128]{3,2,1,0:T(8,128)(2,1)S(1)} collective-permute-done((f16[2,8,32,128]{3,2,1,0:T(8,128)(2,1)}, f16[2,8,32,128]{3,2,1,0:T(8,128)(2,1)S(1)}, u32[]{:S(2)}, u32[]{:S(2)}) %collective-permute-start) | collective-permute-done | bytes 131104 | tf_op jit(solution)/shard_map/ppermute | solution.py:95
  53.9 7.2 %collective-permute-done.1 = f16[2,8,32,128]{3,2,1,0:T(8,128)(2,1)} collective-permute-done((f16[2,8,32,128]{3,2,1,0:T(8,128)(2,1)}, f16[2,8,32,128]{3,2,1,0:T(8,128)(2,1)}, u32[]{:S(2)}, u32[]{:S(2)}) %collective-permute-start.1) | collective-permute-done | bytes 131104 | tf_op jit(solution)/shard_map/ppermute | solution.py:95
  61.1 1.2 multiply_add_fusion
  63.2 4.7 %shard_map.67 = f32[2,4,128,128]{3,2,1,0:T(8,128)} custom-call(s32[102]{0:T(128)} %pad_add_fusion.refs_0_, f32[8]{0:T(128)} %refs_1_.9, f32[2]{0:T(128)} %refs_2_.9, f32[16,640]{1,0:T(8,128)} %reshape.3.refs_3_, bf16[8,3,128,640]{3,2,1,0:T(8,128)(2,1)} %bitcast.30, bf16[4,128,640]{2,1,0:T(8,128)(2,1)} %copy-done.2), custom_call_target="tpu_custom_call" | custom-call | flops 167772160 | bytes 1310720 | tf_op jit(solution)/shard_map/pallas_call | solution.py:66
  67.9 1.8 %multiply_convert_fusion.8 = (f16[2,4,32,128]{3,2,1,0:T(8,128)(2,1)}, f16[2,4,32,128]{3,2,1,0:T(8,128)(2,1)}, f16[2,4,32,128]{3,2,1,0:T(8,128)(2,1)}) fusion(f32[2,4,128,128]{3,2,1,0:T(8,128)} %shard_map.67, s32[]{:T(128)S(6)} %select_n.62, s32[]{:T(128)S(6)} %select_n.64, s32[]{:T(128)S(6)} %select_n.63), kind=kLoop, calls=%fused_computation.29 | loop fusion | flops 196608 | bytes 589836 | tf_op jit(solution)/shard_map/convert_element_type | solution.py:94
  69.7 3.1 %collective-permute-start.15 = (f16[2,4,32,128]{3,2,1,0:T(8,128)(2,1)}, f16[2,4,32,128]{3,2,1,0:T(8,128)(2,1)}, u32[]{:S(2)}, u32[]{:S(2)}) collective-permute-start(f16[2,4,32,128]{3,2,1,0:T(8,128)(2,1)} %get-tuple-element.20), channel_id=1, source_target_pairs={{0,1},{1,2},{2,3},{3,0},{4,5},{5,6},{6,7},{7,4},{8,9},{9,10},{10,1... | collective-permute-start | bytes 196616 | tf_op jit(solution)/shard_map/ppermute | solution.py:95
  72.8 2.1 %collective-permute-start.17 = (f16[2,4,32,128]{3,2,1,0:T(8,128)(2,1)}, f16[2,4,32,128]{3,2,1,0:T(8,128)(2,1)}, u32[]{:S(2)}, u32[]{:S(2)}) collective-permute-start(f16[2,4,32,128]{3,2,1,0:T(8,128)(2,1)} %get-tuple-element.21), channel_id=1, source_target_pairs={{0,3},{1,0},{2,1},{3,2},{4,7},{5,4},{6,5},{7,6},{8,11},{9,8},{10,9... | collective-permute-start | bytes 196616 | tf_op jit(solution)/shard_map/ppermute | solution.py:95
  75.7 4.7 %shard_map.68 = f32[2,4,128,128]{3,2,1,0:T(8,128)} custom-call(s32[102]{0:T(128)} %pad_add_fusion.refs_0_, f32[8]{0:T(128)} %refs_1_.9, f32[2]{0:T(128)} %refs_2_.9, f32[16,640]{1,0:T(8,128)} %reshape.3.refs_3_, bf16[8,3,128,640]{3,2,1,0:T(8,128)(2,1)} %bitcast.31, bf16[4,128,640]{2,1,0:T(8,128)(2,1)} %copy-done.1), custom_call_target="tpu_custom_call" | custom-call | flops 167772160 | bytes 1310720 | tf_op jit(solution)/shard_map/pallas_call | solution.py:66
  80.4 1.1 multiply_convert_fusion.5
  81.6 1.7 %collective-permute-start.19 = (f16[2,4,32,128]{3,2,1,0:T(8,128)(2,1)S(1)}, f16[2,4,32,128]{3,2,1,0:T(8,128)(2,1)S(1)}, u32[]{:S(2)}, u32[]{:S(2)}) collective-permute-start(f16[2,4,32,128]{3,2,1,0:T(8,128)(2,1)S(1)} %get-tuple-element.25), channel_id=1, source_target_pairs={{0,2},{1,3},{2,0},{3,1},{4,6},{5,7},{6,4},{7,5},{8,10},{9,11},{10,... | collective-permute-start | bytes 196616 | tf_op jit(solution)/shard_map/ppermute | solution.py:95
  83.3 2.3 %broadcast_select_fusion.1 = (bf16[4,128,640]{2,1,0:T(8,128)(2,1)S(1)}, bf16[4,128,640]{2,1,0:T(8,128)(2,1)}) fusion(bf16[4,128,640]{2,1,0:T(8,128)(2,1)S(1)} %copy-done.3, pred[]{:T(512)S(6)} %eq.5, bf16[8,3,128,640]{3,2,0,1:T(8,128)(2,1)} %bitcast.35, bf16[4,128,640]{2,1,0:T(8,128)(2,1)} %copy-done.1), kind=kLoop, calls=%fused_computation.7 | loop fusion | flops 655360 | bytes 3932161 | tf_op jit(solution)/shard_map/jit(_where)/select_n | solution.py:131
  85.6 2.1 %collective-permute-start.3 = (bf16[4,128,640]{2,1,0:T(8,128)(2,1)S(1)}, bf16[4,128,640]{2,1,0:T(8,128)(2,1)S(1)}, u32[]{:S(2)}, u32[]{:S(2)}) collective-permute-start(bf16[4,128,640]{2,1,0:T(8,128)(2,1)S(1)} %get-tuple-element.7), channel_id=1, source_target_pairs={{0,12},{4,0},{8,4},{12,8},{1,13},{5,1},{9,5},{13,9},{2,14},{6,2},{... | collective-permute-start | bytes 1966088 | tf_op jit(solution)/shard_map/ppermute | solution.py:125
  87.8 1.5 %collective-permute-start.5 = (bf16[4,128,640]{2,1,0:T(8,128)(2,1)S(1)}, bf16[4,128,640]{2,1,0:T(8,128)(2,1)}, u32[]{:S(2)}, u32[]{:S(2)}) collective-permute-start(bf16[4,128,640]{2,1,0:T(8,128)(2,1)S(1)} %get-tuple-element.5), channel_id=1, source_target_pairs={{0,4},{4,0},{8,12},{12,8},{1,5},{5,1},{9,13},{13,9},{2,6},{6,2},{1... | collective-permute-start | bytes 1966088 | tf_op jit(solution)/shard_map/ppermute | solution.py:131
  91.4 1.2 collective-permute-done.20
  93.6 3.5 %collective-permute-done.3.refs_5_ = bf16[4,128,640]{2,1,0:T(8,128)(2,1)S(1)} collective-permute-done((bf16[4,128,640]{2,1,0:T(8,128)(2,1)S(1)}, bf16[4,128,640]{2,1,0:T(8,128)(2,1)S(1)}, u32[]{:S(2)}, u32[]{:S(2)}) %collective-permute-start.3) | collective-permute-done | bytes 655392 | tf_op jit(solution)/shard_map/ppermute | solution.py:125
  97.9 5.1 %shard_map.65 = f32[2,4,128,128]{3,2,1,0:T(8,128)} custom-call(s32[102]{0:T(128)} %pad_add_fusion.refs_0_, f32[8]{0:T(128)} %refs_1_.9, f32[2]{0:T(128)} %refs_2_.9, f32[16,640]{1,0:T(8,128)} %reshape.3.refs_3_, bf16[8,3,128,640]{3,2,1,0:T(8,128)(2,1)} %bitcast.32, bf16[4,128,640]{2,1,0:T(8,128)(2,1)} %copy-done.6, ...), custom_call_target="tpu_custom_call" | custom-call | flops 335544320 | bytes 2621440 | tf_op jit(solution)/shard_map/pallas_call | solution.py:66
  104.1 1.6 %collective-permute-start.6 = (f16[2,4,32,128]{3,2,1,0:T(8,128)(2,1)S(1)}, f16[2,4,32,128]{3,2,1,0:T(8,128)(2,1)S(1)}, u32[]{:S(2)}, u32[]{:S(2)}) collective-permute-start(f16[2,4,32,128]{3,2,1,0:T(8,128)(2,1)S(1)} %get-tuple-element.14), channel_id=1, source_target_pairs={{0,1},{1,2},{2,3},{3,0},{4,5},{5,6},{6,7},{7,4},{8,9},{9,10},{10,1... | collective-permute-start | bytes 196616 | tf_op jit(solution)/shard_map/ppermute | solution.py:95
  105.7 2.2 %collective-permute-start.8 = (f16[2,4,32,128]{3,2,1,0:T(8,128)(2,1)S(1)}, f16[2,4,32,128]{3,2,1,0:T(8,128)(2,1)S(1)}, u32[]{:S(2)}, u32[]{:S(2)}) collective-permute-start(f16[2,4,32,128]{3,2,1,0:T(8,128)(2,1)S(1)} %get-tuple-element.15), channel_id=1, source_target_pairs={{0,3},{1,0},{2,1},{3,2},{4,7},{5,4},{6,5},{7,6},{8,11},{9,8},{10,9... | collective-permute-start | bytes 196616 | tf_op jit(solution)/shard_map/ppermute | solution.py:95
  109.5 5.1 %shard_map.66 = f32[2,4,128,128]{3,2,1,0:T(8,128)} custom-call(s32[102]{0:T(128)} %pad_add_fusion.refs_0_, f32[8]{0:T(128)} %refs_1_.9, f32[2]{0:T(128)} %refs_2_.9, f32[16,640]{1,0:T(8,128)} %reshape.3.refs_3_, bf16[8,3,128,640]{3,2,1,0:T(8,128)(2,1)} %bitcast.33, bf16[4,128,640]{2,1,0:T(8,128)(2,1)} %copy-done.4, bf16[4,128,640]{2,1,0:T(8,128)(2,1)} %copy-done.5), custom_call_target="tpu_custom_call" | custom-call | flops 335544320 | bytes 2621440 | tf_op jit(solution)/shard_map/pallas_call | solution.py:66
  115.8 1.6 %collective-permute-start.13 = (f16[2,4,32,128]{3,2,1,0:T(8,128)(2,1)S(1)}, f16[2,4,32,128]{3,2,1,0:T(8,128)(2,1)S(1)}, u32[]{:S(2)}, u32[]{:S(2)}) collective-permute-start(f16[2,4,32,128]{3,2,1,0:T(8,128)(2,1)S(1)} %get-tuple-element.19), channel_id=1, source_target_pairs={{0,2},{1,3},{2,0},{3,1},{4,6},{5,7},{6,4},{7,5},{8,10},{9,11},{10,... | collective-permute-start | bytes 196616 | tf_op jit(solution)/shard_map/ppermute | solution.py:95
  117.4 1.7 %collective-permute-start.14 = (f16[2,4,32,128]{3,2,1,0:T(8,128)(2,1)S(1)}, f16[2,4,32,128]{3,2,1,0:T(8,128)(2,1)S(1)}, u32[]{:S(2)}, u32[]{:S(2)}) collective-permute-start(f16[2,4,32,128]{3,2,1,0:T(8,128)(2,1)S(1)} %get-tuple-element.18), channel_id=1, source_target_pairs={{0,3},{1,0},{2,1},{3,2},{4,7},{5,4},{6,5},{7,6},{8,11},{9,8},{10,9... | collective-permute-start | bytes 196616 | tf_op jit(solution)/shard_map/ppermute | solution.py:95
  120.1 1.5 %collective-permute-done.12 = f16[2,4,32,128]{3,2,1,0:T(8,128)(2,1)S(1)} collective-permute-done((f16[2,4,32,128]{3,2,1,0:T(8,128)(2,1)S(1)}, f16[2,4,32,128]{3,2,1,0:T(8,128)(2,1)S(1)}, u32[]{:S(2)}, u32[]{:S(2)}) %collective-permute-start.12) | collective-permute-done | bytes 65568 | tf_op jit(solution)/shard_map/ppermute | solution.py:95
  121.6 1.5 %collective-permute-done.14 = f16[2,4,32,128]{3,2,1,0:T(8,128)(2,1)S(1)} collective-permute-done((f16[2,4,32,128]{3,2,1,0:T(8,128)(2,1)S(1)}, f16[2,4,32,128]{3,2,1,0:T(8,128)(2,1)S(1)}, u32[]{:S(2)}, u32[]{:S(2)}) %collective-permute-start.14) | collective-permute-done | bytes 65568 | tf_op jit(solution)/shard_map/ppermute | solution.py:95
  (65 shorter events, 16.0 us)
Async XLA Ops:
  2.6 1.9 %copy-start = (bf16[1,1,8,3,1,128,640]{6,5,2,3,4,1,0:T(8,128)(2,1)}, bf16[1,1,8,3,1,128,640]{6,5,2,3,4,1,0:T(8,128)(2,1)S(1)}, u32[]{:S(2)}) copy-start(bf16[1,1,8,3,1,128,640]{6,5,2,3,4,1,0:T(8,128)(2,1)S(1)} %copy.25) | copy-start | bytes 11796484
  2.6 5.0 %copy-start.9 = (s32[1,1,8,3,1]{2,4,3,1,0:T(1,128)S(1)}, s32[1,1,8,3,1]{2,4,3,1,0:T(1,128)}, u32[]{:S(2)}) copy-start(s32[1,1,8,3,1]{2,4,3,1,0:T(1,128)} %param.7) | copy-start | bytes 292
  2.6 5.9 %copy-start.10 = (u32[32]{0:T(128)S(1)}, u32[32]{0:T(128)}, u32[]{:S(2)}) copy-start(u32[32]{0:T(128)} %constant.47) | copy-start | bytes 388
  2.6 33.6 %copy-start.8 = (f32[10240]{0:T(1024)S(1)}, f32[10240]{0:T(1024)}, u32[]{:S(2)}) copy-start(f32[10240]{0:T(1024)} %param.10) | copy-start | bytes 122884
  5.5 69.4 %collective-permute-start.10 = (bf16[4,128,640]{2,1,0:T(8,128)(2,1)S(1)}, bf16[4,128,640]{2,1,0:T(8,128)(2,1)S(1)}, u32[]{:S(2)}, u32[]{:S(2)}) collective-permute-start(bf16[4,128,640]{2,1,0:T(8,128)(2,1)S(1)} %get-tuple-element.8), channel_id=1, source_target_pairs={{0,8},{4,12},{8,0},{12,4},{1,9},{5,13},{9,1},{13,5},{2,10},{6,14},... | collective-permute-start | bytes 1966088 | tf_op jit(solution)/shard_map/ppermute | solution.py:124
  7.6 54.8 %collective-permute-start.4 = (bf16[4,128,640]{2,1,0:T(8,128)(2,1)}, bf16[4,128,640]{2,1,0:T(8,128)(2,1)S(1)}, u32[]{:S(2)}, u32[]{:S(2)}) collective-permute-start(bf16[4,128,640]{2,1,0:T(8,128)(2,1)} %get-tuple-element.9), channel_id=1, source_target_pairs={{0,8},{4,12},{8,0},{12,4},{1,9},{5,13},{9,1},{13,5},{2,10},{6,14},... | collective-permute-start | bytes 1966088 | tf_op jit(solution)/shard_map/ppermute | solution.py:124
  48.0 5.9 %collective-permute-start = (f16[2,8,32,128]{3,2,1,0:T(8,128)(2,1)}, f16[2,8,32,128]{3,2,1,0:T(8,128)(2,1)S(1)}, u32[]{:S(2)}, u32[]{:S(2)}) collective-permute-start(f16[2,8,32,128]{3,2,1,0:T(8,128)(2,1)} %get-tuple-element.11), channel_id=1, source_target_pairs={{0,1},{1,2},{2,3},{3,0},{4,5},{5,6},{6,7},{7,4},{8,9},{9,10},{10,1... | collective-permute-start | bytes 393224 | tf_op jit(solution)/shard_map/ppermute | solution.py:95
  49.2 11.9 %collective-permute-start.1 = (f16[2,8,32,128]{3,2,1,0:T(8,128)(2,1)}, f16[2,8,32,128]{3,2,1,0:T(8,128)(2,1)}, u32[]{:S(2)}, u32[]{:S(2)}) collective-permute-start(f16[2,8,32,128]{3,2,1,0:T(8,128)(2,1)} %get-tuple-element.13), channel_id=1, source_target_pairs={{0,2},{1,3},{2,0},{3,1},{4,6},{5,7},{6,4},{7,5},{8,10},{9,11},{10,... | collective-permute-start | bytes 393224 | tf_op jit(solution)/shard_map/ppermute | solution.py:95
  51.5 9.6 %collective-permute-start.2 = (f16[2,8,32,128]{3,2,1,0:T(8,128)(2,1)S(1)}, f16[2,8,32,128]{3,2,1,0:T(8,128)(2,1)}, u32[]{:S(2)}, u32[]{:S(2)}) collective-permute-start(f16[2,8,32,128]{3,2,1,0:T(8,128)(2,1)S(1)} %get-tuple-element.12), channel_id=1, source_target_pairs={{0,3},{1,0},{2,1},{3,2},{4,7},{5,4},{6,5},{7,6},{8,11},{9,8},{10,9... | collective-permute-start | bytes 393224 | tf_op jit(solution)/shard_map/ppermute | solution.py:95
  53.9 7.2 %copy-start.7 = (f16[2,8,32,128]{3,2,1,0:T(8,128)(2,1)}, f16[2,8,32,128]{3,2,1,0:T(8,128)(2,1)S(1)}, u32[]{:S(2)}) copy-start(f16[2,8,32,128]{3,2,1,0:T(8,128)(2,1)S(1)} %collective-permute-done) | copy-start | bytes 393220
  62.4 0.9 copy-start.2
  67.9 15.4 %copy-start.3 = (bf16[4,128,640]{2,1,0:T(8,128)(2,1)S(1)}, bf16[4,128,640]{2,1,0:T(8,128)(2,1)}, u32[]{:S(2)}) copy-start(bf16[4,128,640]{2,1,0:T(8,128)(2,1)} %copy-done.2) | copy-start | bytes 1966084
  69.7 15.9 %collective-permute-start.15 = (f16[2,4,32,128]{3,2,1,0:T(8,128)(2,1)}, f16[2,4,32,128]{3,2,1,0:T(8,128)(2,1)}, u32[]{:S(2)}, u32[]{:S(2)}) collective-permute-start(f16[2,4,32,128]{3,2,1,0:T(8,128)(2,1)} %get-tuple-element.20), channel_id=1, source_target_pairs={{0,1},{1,2},{2,3},{3,0},{4,5},{5,6},{6,7},{7,4},{8,9},{9,10},{10,1... | collective-permute-start | bytes 196616 | tf_op jit(solution)/shard_map/ppermute | solution.py:95
  72.8 14.9 %collective-permute-start.16 = (f16[2,4,32,128]{3,2,1,0:T(8,128)(2,1)}, f16[2,4,32,128]{3,2,1,0:T(8,128)(2,1)}, u32[]{:S(2)}, u32[]{:S(2)}) collective-permute-start(f16[2,4,32,128]{3,2,1,0:T(8,128)(2,1)} %get-tuple-element.22), channel_id=1, source_target_pairs={{0,2},{1,3},{2,0},{3,1},{4,6},{5,7},{6,4},{7,5},{8,10},{9,11},{10,... | collective-permute-start | bytes 196616 | tf_op jit(solution)/shard_map/ppermute | solution.py:95
  72.8 14.9 %collective-permute-start.17 = (f16[2,4,32,128]{3,2,1,0:T(8,128)(2,1)}, f16[2,4,32,128]{3,2,1,0:T(8,128)(2,1)}, u32[]{:S(2)}, u32[]{:S(2)}) collective-permute-start(f16[2,4,32,128]{3,2,1,0:T(8,128)(2,1)} %get-tuple-element.21), channel_id=1, source_target_pairs={{0,3},{1,0},{2,1},{3,2},{4,7},{5,4},{6,5},{7,6},{8,11},{9,8},{10,9... | collective-permute-start | bytes 196616 | tf_op jit(solution)/shard_map/ppermute | solution.py:95
  74.9 0.8 copy-start.1
  81.5 7.8 %collective-permute-start.18 = (f16[2,4,32,128]{3,2,1,0:T(8,128)(2,1)S(1)}, f16[2,4,32,128]{3,2,1,0:T(8,128)(2,1)S(1)}, u32[]{:S(2)}, u32[]{:S(2)}) collective-permute-start(f16[2,4,32,128]{3,2,1,0:T(8,128)(2,1)S(1)} %get-tuple-element.23), channel_id=1, source_target_pairs={{0,1},{1,2},{2,3},{3,0},{4,5},{5,6},{6,7},{7,4},{8,9},{9,10},{10,1... | collective-permute-start | bytes 196616 | tf_op jit(solution)/shard_map/ppermute | solution.py:95
  81.6 7.8 %collective-permute-start.19 = (f16[2,4,32,128]{3,2,1,0:T(8,128)(2,1)S(1)}, f16[2,4,32,128]{3,2,1,0:T(8,128)(2,1)S(1)}, u32[]{:S(2)}, u32[]{:S(2)}) collective-permute-start(f16[2,4,32,128]{3,2,1,0:T(8,128)(2,1)S(1)} %get-tuple-element.25), channel_id=1, source_target_pairs={{0,2},{1,3},{2,0},{3,1},{4,6},{5,7},{6,4},{7,5},{8,10},{9,11},{10,... | collective-permute-start | bytes 196616 | tf_op jit(solution)/shard_map/ppermute | solution.py:95
  85.6 11.5 %collective-permute-start.3 = (bf16[4,128,640]{2,1,0:T(8,128)(2,1)S(1)}, bf16[4,128,640]{2,1,0:T(8,128)(2,1)S(1)}, u32[]{:S(2)}, u32[]{:S(2)}) collective-permute-start(bf16[4,128,640]{2,1,0:T(8,128)(2,1)S(1)} %get-tuple-element.7), channel_id=1, source_target_pairs={{0,12},{4,0},{8,4},{12,8},{1,13},{5,1},{9,5},{13,9},{2,14},{6,2},{... | collective-permute-start | bytes 1966088 | tf_op jit(solution)/shard_map/ppermute | solution.py:125
  87.7 20.1 %collective-permute-start.9 = (bf16[4,128,640]{2,1,0:T(8,128)(2,1)S(1)}, bf16[4,128,640]{2,1,0:T(8,128)(2,1)S(1)}, u32[]{:S(2)}, u32[]{:S(2)}) collective-permute-start(bf16[4,128,640]{2,1,0:T(8,128)(2,1)S(1)} %get-tuple-element.10), channel_id=1, source_target_pairs={{0,12},{4,0},{8,4},{12,8},{1,13},{5,1},{9,5},{13,9},{2,14},{6,2},{... | collective-permute-start | bytes 1966088 | tf_op jit(solution)/shard_map/ppermute | solution.py:125
  87.8 10.1 %collective-permute-start.5 = (bf16[4,128,640]{2,1,0:T(8,128)(2,1)S(1)}, bf16[4,128,640]{2,1,0:T(8,128)(2,1)}, u32[]{:S(2)}, u32[]{:S(2)}) collective-permute-start(bf16[4,128,640]{2,1,0:T(8,128)(2,1)S(1)} %get-tuple-element.5), channel_id=1, source_target_pairs={{0,4},{4,0},{8,12},{12,8},{1,5},{5,1},{9,13},{13,9},{2,6},{6,2},{1... | collective-permute-start | bytes 1966088 | tf_op jit(solution)/shard_map/ppermute | solution.py:131
  89.3 18.5 %collective-permute-start.11 = (bf16[4,128,640]{2,1,0:T(8,128)(2,1)}, bf16[4,128,640]{2,1,0:T(8,128)(2,1)S(1)}, u32[]{:S(2)}, u32[]{:S(2)}) collective-permute-start(bf16[4,128,640]{2,1,0:T(8,128)(2,1)} %get-tuple-element.6), channel_id=1, source_target_pairs={{0,4},{4,0},{8,12},{12,8},{1,5},{5,1},{9,13},{13,9},{2,6},{6,2},{1... | collective-permute-start | bytes 1966088 | tf_op jit(solution)/shard_map/ppermute | solution.py:131
  89.4 3.2 %collective-permute-start.20 = (f16[2,4,32,128]{3,2,1,0:T(8,128)(2,1)S(1)}, f16[2,4,32,128]{3,2,1,0:T(8,128)(2,1)S(1)}, u32[]{:S(2)}, u32[]{:S(2)}) collective-permute-start(f16[2,4,32,128]{3,2,1,0:T(8,128)(2,1)S(1)} %get-tuple-element.24), channel_id=1, source_target_pairs={{0,3},{1,0},{2,1},{3,2},{4,7},{5,4},{6,5},{7,6},{8,11},{9,8},{10,9... | collective-permute-start | bytes 196616 | tf_op jit(solution)/shard_map/ppermute | solution.py:95
  97.1 0.8 copy-start.6
  104.1 13.3 %collective-permute-start.6 = (f16[2,4,32,128]{3,2,1,0:T(8,128)(2,1)S(1)}, f16[2,4,32,128]{3,2,1,0:T(8,128)(2,1)S(1)}, u32[]{:S(2)}, u32[]{:S(2)}) collective-permute-start(f16[2,4,32,128]{3,2,1,0:T(8,128)(2,1)S(1)} %get-tuple-element.14), channel_id=1, source_target_pairs={{0,1},{1,2},{2,3},{3,0},{4,5},{5,6},{6,7},{7,4},{8,9},{9,10},{10,1... | collective-permute-start | bytes 196616 | tf_op jit(solution)/shard_map/ppermute | solution.py:95
  105.7 13.5 %collective-permute-start.7 = (f16[2,4,32,128]{3,2,1,0:T(8,128)(2,1)S(1)}, f16[2,4,32,128]{3,2,1,0:T(8,128)(2,1)S(1)}, u32[]{:S(2)}, u32[]{:S(2)}) collective-permute-start(f16[2,4,32,128]{3,2,1,0:T(8,128)(2,1)S(1)} %get-tuple-element.16), channel_id=1, source_target_pairs={{0,2},{1,3},{2,0},{3,1},{4,6},{5,7},{6,4},{7,5},{8,10},{9,11},{10,... | collective-permute-start | bytes 196616 | tf_op jit(solution)/shard_map/ppermute | solution.py:95
  105.7 13.5 %collective-permute-start.8 = (f16[2,4,32,128]{3,2,1,0:T(8,128)(2,1)S(1)}, f16[2,4,32,128]{3,2,1,0:T(8,128)(2,1)S(1)}, u32[]{:S(2)}, u32[]{:S(2)}) collective-permute-start(f16[2,4,32,128]{3,2,1,0:T(8,128)(2,1)S(1)} %get-tuple-element.15), channel_id=1, source_target_pairs={{0,3},{1,0},{2,1},{3,2},{4,7},{5,4},{6,5},{7,6},{8,11},{9,8},{10,9... | collective-permute-start | bytes 196616 | tf_op jit(solution)/shard_map/ppermute | solution.py:95
  107.8 0.8 copy-start.4
  108.7 0.9 copy-start.5
  115.7 5.9 %collective-permute-start.12 = (f16[2,4,32,128]{3,2,1,0:T(8,128)(2,1)S(1)}, f16[2,4,32,128]{3,2,1,0:T(8,128)(2,1)S(1)}, u32[]{:S(2)}, u32[]{:S(2)}) collective-permute-start(f16[2,4,32,128]{3,2,1,0:T(8,128)(2,1)S(1)} %get-tuple-element.17), channel_id=1, source_target_pairs={{0,1},{1,2},{2,3},{3,0},{4,5},{5,6},{6,7},{7,4},{8,9},{9,10},{10,1... | collective-permute-start | bytes 196616 | tf_op jit(solution)/shard_map/ppermute | solution.py:95
  115.8 5.8 %collective-permute-start.13 = (f16[2,4,32,128]{3,2,1,0:T(8,128)(2,1)S(1)}, f16[2,4,32,128]{3,2,1,0:T(8,128)(2,1)S(1)}, u32[]{:S(2)}, u32[]{:S(2)}) collective-permute-start(f16[2,4,32,128]{3,2,1,0:T(8,128)(2,1)S(1)} %get-tuple-element.19), channel_id=1, source_target_pairs={{0,2},{1,3},{2,0},{3,1},{4,6},{5,7},{6,4},{7,5},{8,10},{9,11},{10,... | collective-permute-start | bytes 196616 | tf_op jit(solution)/shard_map/ppermute | solution.py:95
  117.4 5.7 %collective-permute-start.14 = (f16[2,4,32,128]{3,2,1,0:T(8,128)(2,1)S(1)}, f16[2,4,32,128]{3,2,1,0:T(8,128)(2,1)S(1)}, u32[]{:S(2)}, u32[]{:S(2)}) collective-permute-start(f16[2,4,32,128]{3,2,1,0:T(8,128)(2,1)S(1)} %get-tuple-element.18), channel_id=1, source_target_pairs={{0,3},{1,0},{2,1},{3,2},{4,7},{5,4},{6,5},{7,6},{8,11},{9,8},{10,9... | collective-permute-start | bytes 196616 | tf_op jit(solution)/shard_map/ppermute | solution.py:95

commit v2 on v1

v2 whole, which is shorter than its diff:
```python
import functools

import jax
import jax.numpy as jnp
from jax import lax
from jax.experimental import pallas as pl
from jax.experimental.pallas import tpu as pltpu
from jax.sharding import PartitionSpec as P

HEAD = 2
ANY = pl.BlockSpec(memory_space=pl.ANY)
SMEM = pl.BlockSpec(memory_space=pltpu.SMEM)
VMEM = pl.BlockSpec(memory_space=pltpu.VMEM)


def chunks_of(count, sizes):
    ends = [count * sum(sizes[: n + 1]) // sum(sizes) for n in range(len(sizes))]
    return [(a, b - a) for a, b in zip([0] + ends[:-1], ends)]


def pack_kernel(plan, n_aux, tiles, *refs):
    outs, sem = refs[:-1], refs[-1]
    aux_pos = lax.axis_index("aux")
    blocks_dev = tiles.shape[0]
    copies = []
    for out, (slot, back, first) in zip(outs, plan):
        shift = (aux_pos < back).astype(jnp.int32)
        for i in range(out.shape[0]):
            row = jnp.minimum(first + i + shift, blocks_dev - 1)
            copies.append(pltpu.make_async_copy(tiles.at[row, slot], out.at[i], sem.at[len(copies)]))
    for copy in copies:
        copy.start()
    for copy in copies:
        copy.wait()


def pack(tiles, n_aux, plan, counts):
    return pl.pallas_call(
        functools.partial(pack_kernel, plan, n_aux),
        out_shape=[jax.ShapeDtypeStruct((count,) + tiles.shape[-2:], tiles.dtype) for count in counts],
        in_specs=[ANY],
        out_specs=[ANY] * len(counts),
        scratch_shapes=[pltpu.SemaphoreType.DMA((sum(counts),))],
    )(tiles)


def band_kernel(dims, first, delta, *refs):
    n_aux, n_pair, blocks_dev, band, freq_count = dims
    meta, occ, freq, table, own = refs[:5]
    far = refs[5:-4]
    out, own_buf, far_buf, sem = refs[-4:]
    count = out.shape[1]
    slots = band - delta
    virt_blocks = table.shape[0]
    record = blocks_dev * band + 1
    aux_pos, pair_col = meta[0], meta[1]
    shift = ((aux_pos + delta) >= n_aux).astype(jnp.int32)
    behind = lax.rem(2 * n_aux - delta, n_aux)
    even = lax.rem(aux_pos, 2) == 0

    def own_copy(i):
        return pltpu.make_async_copy(own.at[first + i, pl.ds(0, slots)], own_buf.at[i], sem.at[0, i])

    def far_copy(i, slot, array):
        return pltpu.make_async_copy(array.at[i], far_buf.at[i, slot], sem.at[1 + slot, i])

    for i in range(count):
        own_copy(i).start()
        if delta > 0:
            far_copy(i, 0, far[0]).start()
        if delta == 1:
            even_from, odd_from = far[1], far[2]

            @pl.when(even)
            def _():
                far_copy(i, 1, even_from.at[pl.ds(first, count)]).start()

            @pl.when(jnp.logical_not(even))
            def _():
                far_copy(i, 1, odd_from.at[pl.ds(first, count)]).start()

    for i in range(count):
        here = first + i
        block = here * n_aux + aux_pos
        there = here + shift
        safe_there = jnp.minimum(there, blocks_dev - 1)
        own_copy(i).wait()
        sums = [None] * freq_count
        for slot in range(slots):
            if delta > 0:
                far_copy(i, slot, far[0]).wait()
            centre = block - slot
            safe = jnp.maximum(centre, 0)
            region = safe // blocks_dev
            number = lax.rem(safe, blocks_dev)
            live = meta[HEAD + lax.rem(aux_pos - region + n_aux, n_aux) * record + blocks_dev * band]
            left_on = meta[HEAD + here * band + slot]
            right_on = meta[HEAD + behind * record + safe_there * band + slot + delta]
            keep = (centre >= 0) & (number < live) & (left_on > 0) & (right_on > 0) & (there < blocks_dev)
            present = keep.astype(jnp.float32)
            pair_block = (region * n_pair + pair_col) * blocks_dev + number
            gap = table[pl.ds(lax.rem(pair_block, virt_blocks), 1), :] - occ[pair_block // virt_blocks]
            left = own_buf[i, slot].astype(jnp.float32)
            right = None if delta == 0 else far_buf[i, slot].astype(jnp.float32)
            for w in range(freq_count):
                omega = freq[w]
                root = jnp.sqrt(2.0 * gap / (gap * gap + omega * omega))
                a = (left * (root * present)).astype(jnp.bfloat16)
                b = a if right is None else (right * root).astype(jnp.bfloat16)
                term = lax.dot_general(a, b, (((1,), (1,)), ((), ())), preferred_element_type=jnp.float32)
                sums[w] = term if sums[w] is None else sums[w] + term
        for w in range(freq_count):
            out[w, i] = sums[w]


def band_rows(dims, first, count, delta, meta, occ, freq, table, tiles, far):
    n_aux, n_pair, blocks_dev, band, freq_count = dims
    aux_rows, pair_rows = tiles.shape[-2:]
    slots = band - delta
    far_shape = (count, slots, aux_rows, pair_rows) if far else (1, 1, 16, 128)
    return pl.pallas_call(
        functools.partial(band_kernel, dims, first, delta),
        out_shape=jax.ShapeDtypeStruct((freq_count, count, aux_rows, aux_rows), jnp.float32),
        in_specs=[SMEM, SMEM, SMEM, VMEM, ANY] + [ANY] * len(far),
        out_specs=VMEM,
        scratch_shapes=[
            pltpu.VMEM((count, slots, aux_rows, pair_rows), tiles.dtype),
            pltpu.VMEM(far_shape, tiles.dtype),
            pltpu.SemaphoreType.DMA((1 + slots, count)),
        ],
        compiler_params=pltpu.CompilerParams(vmem_limit_bytes=24 << 20),
        cost_estimate=pl.CostEstimate(flops=1000, bytes_accessed=1000, transcendentals=0),
    )(meta, occ, freq, table, tiles, *far)


def spread(rows, pair_col, n_pair, scale):
    freq_count, count, aux_rows, width = rows.shape
    height = aux_rows // n_pair
    keep = rows.reshape(freq_count, count, n_pair, height, width)
    step = 1
    while step < n_pair:
        half = keep.shape[2] // 2
        keep = keep.reshape(freq_count, count, half, 2, height, width)
        bit = (pair_col // step) % 2
        part = lax.dynamic_index_in_dim(keep, 1 - bit, 3, keepdims=False)
        mine = lax.dynamic_index_in_dim(keep, bit, 3, keepdims=False)
        sent = (part * scale).astype(jnp.float16)
        got = lax.ppermute(sent, "pair", [(s, s ^ step) for s in range(n_pair)])
        keep = mine + got.astype(jnp.float32) * (1.0 / scale)
        step *= 2
    return keep[:, :, 0]


def on_device(three_centre, locality, live_blocks, occ_energy, virt_energy, frequencies):
    n_aux = lax.axis_size("aux")
    n_pair = lax.axis_size("pair")
    aux_pos = lax.axis_index("aux")
    pair_col = lax.axis_index("pair")
    tiles = three_centre[0, 0, :, :, 0]
    blocks_dev, band, aux_rows, pair_rows = tiles.shape
    freq_count = frequencies.shape[0]
    dims = (n_aux, n_pair, blocks_dev, band, freq_count)
    scale = 128.0 / n_pair
    table = virt_energy.reshape(-1, pair_rows)
    record = jnp.concatenate([locality[0, 0].reshape(-1), live_blocks[0]])
    records = [record] + [
        lax.ppermute(record, "aux", [(s, (s + k) % n_aux) for s in range(n_aux)]) for k in range(1, n_aux)
    ]
    meta = jnp.concatenate([jnp.stack([aux_pos, pair_col]).astype(jnp.int32)] + records)

    two = chunks_of(blocks_dev, (4, 4))
    one = chunks_of(blocks_dev, (5, 3))
    plan = [(2, 2, f) for f, _ in two] + [(1, 1, f) for f, _ in one] + [(2, 0, 0)]
    packed = pack(tiles, n_aux, plan, [c for _, c in two + one] + [blocks_dev])
    packed, meta = lax.optimization_barrier((packed, meta))
    down1 = [(s, (s - 1) % n_aux) for s in range(n_aux)]
    down2 = [(s, (s - 2) % n_aux) for s in range(n_aux)]
    c2 = [lax.ppermute(packed[n], "aux", down2) for n in range(2)]
    b1 = [lax.ppermute(packed[2 + n], "aux", down1) for n in range(2)]
    to_even = lax.ppermute(packed[4], "aux", [(s, s - 1) for s in range(1, n_aux, 2)])
    args = (meta, occ_energy, frequencies, table, tiles)
    z0 = spread(band_rows(dims, 0, blocks_dev, 0, *args, []), pair_col, n_pair, scale)
    to_odd, z2 = [], []
    for n, (first, count) in enumerate(two):
        to_odd.append(lax.ppermute(c2[n], "aux", [(s, s + 1) for s in range(0, n_aux, 2)]))
        z2.append(spread(band_rows(dims, first, count, 2, *args, [c2[n]]), pair_col, n_pair, scale))
    to_odd = jnp.concatenate(to_odd)
    z1 = []
    for n, (first, count) in enumerate(one):
        far = [b1[n], to_even, to_odd]
        z1.append(spread(band_rows(dims, first, count, 1, *args, far), pair_col, n_pair, scale))
    out = jnp.concatenate([z0, jnp.concatenate(z1, axis=1), jnp.concatenate(z2, axis=1)], axis=-1)
    return out[:, :, None]


def solution(mesh):
    return jax.shard_map(
        on_device,
        mesh=mesh,
        in_specs=(
            P(("grp", "aux"), "pair", None, None, None, None, None),
            P(("grp", "aux"), "pair", None, None, None),
            P(("grp", "aux"), "pair"),
            P("grp"),
            P("grp"),
            P("grp"),
        ),
        out_specs=P(None, None, ("grp", "aux"), "pair", None),
        check_vma=False,
    )
```

time: 128 us -> 223 us (1.74)
  Pallas kernels: 28.2 us -> 145 us
  blocking collectives: 26.2 us -> 0 us
  waiting for transfers between devices: 16.2 us -> 39.7 us
  other arithmetic: 16.2 us -> 1.7 us
  local copies, waits for them, and re-layouts: 11.2 us -> 5.59 us
  starting transfers between devices: 25.5 us -> 28.6 us
    pallas_call x5 -> x6, Pallas kernels: 28.2 us -> 145 us  [the longest x1 120 us: pack(): pl.pallas_call(functools.partial(pack_kernel, plan, n_aux), out_shape=[ja...]
    unnamed x1 -> x0, blocking collectives: 26.2 us -> none
    ppermute x21 -> x20, waiting for transfers between devices: 16.2 us -> 39.7 us  [the longest x10 21.9 us: spread(): got = lax.ppermute(sent, 'pair', [(s, s ^ step) for s in range(n_pair)])]
    convert_element_type x5 -> x10, other arithmetic: 6.93 us -> 0.33 us  [spread(): sent = (part * scale).astype(jnp.float16)]
    add x5, other arithmetic: 5.08 us -> 0.24 us  [spread(): keep = mine + got.astype(jnp.float32) * (1.0 / scale)]
    unnamed x26 -> x16, local copies, waits for them, and re-layouts: 9.34 us -> 5.06 us
    ppermute x21 -> x20, starting transfers between devices: 25.5 us -> 28.6 us  [the longest x10 11.4 us: spread(): got = lax.ppermute(sent, 'pair', [(s, s ^ step) for s in range(n_pair)])]
    select_n x3 -> x0, other arithmetic: 2.38 us -> none  [the longest x1 2.28 us: on_device(): jnp.where(even, c2[n], tiles[h:h + half, 2])]
  transfers between devices with their start and end apart: 21 -> 20, of which waited for: 6 -> 9; matrix products, arithmetic and copies ran while one was open for 13% -> 0% of each run, Pallas kernels for 23% -> 62%
where the time goes in v2:
time: 223 us; the launch traced here: 222 us
  Pallas kernels  145 us (65%)
  waiting for transfers between devices  39.7 us (18%)
  starting transfers between devices  28.6 us (13%)
  local copies, waits for them, and re-layouts  5.59 us (3%)
    pallas_call x1, Pallas kernels, pack(): pl.pallas_call(functools.partial(pack_kernel, plan, n_aux), out_shape=[ja...  120 us
    pallas_call x5, Pallas kernels, band_rows(): pl.pallas_call(functools.partial(band_kernel, dims, first, delta), out_sh...  24.9 us
    ppermute x10, waiting for transfers between devices, spread(): got = lax.ppermute(sent, 'pair', [(s, s ^ step) for s in range(n_pair)])  21.9 us
    ppermute x10, starting transfers between devices, spread(): got = lax.ppermute(sent, 'pair', [(s, s ^ step) for s in range(n_pair)])  11.4 us
    ppermute x2, waiting for transfers between devices, on_device(): c2 = [lax.ppermute(packed[n], 'aux', down2) for n in range(2)]  10.9 us
    ppermute x2, starting transfers between devices, on_device(): b1 = [lax.ppermute(packed[2 + n], 'aux', down1) for n in range(2)]  8.16 us
    ppermute x2, waiting for transfers between devices, on_device(): b1 = [lax.ppermute(packed[2 + n], 'aux', down1) for n in range(2)]  6.84 us
    unnamed x16, local copies, waits for them, and re-layouts  5.06 us
  transfers between devices with their start and end apart: 20, of which 9 were waited for; matrix products, arithmetic and copies ran while one was open for 0% of the time, Pallas kernels for 62%

profile of v2, /device:TPU:1, one launch (start us, length us, event | category | flops | bytes accessed | tf_op | source)
XLA Modules:
  0.0 221.9 jit_solution(7134353881157841971)
XLA Ops:
  0.0 0.8 copy.18
  1.6 2.6 %collective-permute-start = (s32[25]{0:T(128)S(1)}, s32[25]{0:T(128)S(1)}, u32[]{:S(2)}, u32[]{:S(2)}) collective-permute-start(s32[25]{0:T(128)S(1)} %pad_add_fusion), channel_id=1, source_target_pairs={{0,4},{4,8},{8,12},{12,0},{1,5},{5,9},{9,13},{13,1},{2,6},{6,10},{... | collective-permute-start | bytes 308 | tf_op jit(solution)/shard_map/ppermute | solution.py:167
  4.6 120.4 %shard_map.64 = (bf16[4,128,640]{2,1,0:T(8,128)(2,1)}, bf16[4,128,640]{2,1,0:T(8,128)(2,1)}, bf16[5,128,640]{2,1,0:T(8,128)(2,1)}, bf16[3,128,640]{2,1,0:T(8,128)(2,1)}, bf16[8,128,640]{2,1,0:T(8,128)(2,1)}) custom-call(bf16[8,3,128,640]{3,2,1,0:T(8,128)(2,1)} %bitcast.47), custom_call_target="tpu_custom_call" | custom-call | tf_op jit(solution)/shard_map/pallas_call | solution.py:38
  125.3 2.1 copy-done
  127.4 7.7 %shard_map.65 = f32[2,8,128,128]{3,2,1,0:T(8,128)S(1)} custom-call(s32[102]{0:T(128)S(1)} %concatenate.20.refs_0_, f32[8]{0:T(128)S(1)} %copy-done.2, f32[2]{0:T(128)S(1)} %copy-done.3, f32[16,640]{1,0:T(8,128)S(1)} %reshape.58.refs_3_, bf16[8,3,128,640]{3,2,1,0:T(8,128)(2,1)S(1)} %bitcast.48), custom_call_target="tpu_custom_call" | custom-call | flops 1000 | bytes 1000 | tf_op jit(solution)/shard_map/pallas_call | solution.py:121
  135.2 1.4 collective-permute-start.3
  136.6 1.0 collective-permute-start.9
  138.0 3.6 %collective-permute-done.3 = f16[2,8,2,32,128]{4,3,1,0,2:T(8,128)(2,1)S(1)} collective-permute-done((f16[2,8,2,32,128]{4,3,1,0,2:T(8,128)(2,1)S(1)}, f16[2,8,2,32,128]{4,3,1,0,2:T(8,128)(2,1)S(1)}, u32[]{:S(2)}, u32[]{:S(2)}) %collective-permute-start.3) | collective-permute-done | bytes 262176 | tf_op jit(solution)/shard_map/ppermute | solution.py:148
  141.8 2.4 %collective-permute-start.4 = (f16[2,8,1,32,128]{4,3,1,0,2:T(8,128)(2,1)S(1)}, f16[2,8,1,32,128]{4,3,1,0,2:T(8,128)(2,1)S(1)}, u32[]{:S(2)}, u32[]{:S(2)}) collective-permute-start(f16[2,8,1,32,128]{4,3,1,0,2:T(8,128)(2,1)S(1)} %multiply_convert_fusion), channel_id=1, source_target_pairs={{0,2},{1,3},{2,0},{3,1},{4,6},{5,7},{6,4},{7,5},{8,10},{9,11},{10,... | collective-permute-start | bytes 393224 | tf_op jit(solution)/shard_map/ppermute | solution.py:148
  144.2 2.6 %collective-permute-start.13 = (bf16[3,128,640]{2,1,0:T(8,128)(2,1)}, bf16[3,128,640]{2,1,0:T(8,128)(2,1)S(1)}, u32[]{:S(2)}, u32[]{:S(2)}) collective-permute-start(bf16[3,128,640]{2,1,0:T(8,128)(2,1)} %get-tuple-element.26), channel_id=1, source_target_pairs={{0,12},{4,0},{8,4},{12,8},{1,13},{5,1},{9,5},{13,9},{2,14},{6,2},{... | collective-permute-start | bytes 1474568 | tf_op jit(solution)/shard_map/ppermute | solution.py:179
  146.8 2.0 collective-permute-start.6
  148.8 2.5 %collective-permute-done.9.refs_5_ = bf16[4,128,640]{2,1,0:T(8,128)(2,1)S(1)} collective-permute-done((bf16[4,128,640]{2,1,0:T(8,128)(2,1)}, bf16[4,128,640]{2,1,0:T(8,128)(2,1)S(1)}, u32[]{:S(2)}, u32[]{:S(2)}) %collective-permute-start.9) | collective-permute-done | bytes 655392 | tf_op jit(solution)/shard_map/ppermute | solution.py:178
  151.3 2.1 copy-done.1
  153.4 3.5 %shard_map.69 = f32[2,4,128,128]{3,2,1,0:T(8,128)S(1)} custom-call(s32[102]{0:T(128)S(1)} %concatenate.20.refs_0_, f32[8]{0:T(128)S(1)} %copy-done.2, f32[2]{0:T(128)S(1)} %copy-done.3, f32[16,640]{1,0:T(8,128)S(1)} %reshape.58.refs_3_, bf16[8,3,128,640]{3,2,1,0:T(8,128)(2,1)S(1)} %bitcast.49, bf16[4,128,640]{2,1,0:T(8,128)(2,1)S(1)} %collective-permute-done.9.refs_5_), custom_call_target="tpu_custom_call" | custom-call | flops 1000 | bytes 1000 | tf_op jit(solution)/shard_map/pallas_call | solution.py:121
  157.0 8.4 %collective-permute-done.7.refs_5_ = bf16[4,128,640]{2,1,0:T(8,128)(2,1)S(1)} collective-permute-done((bf16[4,128,640]{2,1,0:T(8,128)(2,1)S(1)}, bf16[4,128,640]{2,1,0:T(8,128)(2,1)S(1)}, u32[]{:S(2)}, u32[]{:S(2)}) %collective-permute-start.7) | collective-permute-done | bytes 655392 | tf_op jit(solution)/shard_map/ppermute | solution.py:178
  165.4 3.5 %shard_map.68 = f32[2,4,128,128]{3,2,1,0:T(8,128)S(1)} custom-call(s32[102]{0:T(128)S(1)} %concatenate.20.refs_0_, f32[8]{0:T(128)S(1)} %copy-done.2, f32[2]{0:T(128)S(1)} %copy-done.3, f32[16,640]{1,0:T(8,128)S(1)} %reshape.58.refs_3_, bf16[8,3,128,640]{3,2,1,0:T(8,128)(2,1)S(1)} %bitcast.50, bf16[4,128,640]{2,1,0:T(8,128)(2,1)S(1)} %collective-permute-done.7.refs_5_), custom_call_target="tpu_custom_call" | custom-call | flops 1000 | bytes 1000 | tf_op jit(solution)/shard_map/pallas_call | solution.py:121
  169.3 1.4 collective-permute-start.16
  170.7 1.3 collective-permute-start.8
  172.0 1.0 collective-permute-done.18
  172.9 1.3 collective-permute-start.10
  174.3 2.3 %collective-permute-start.19 = (f16[2,4,1,32,128]{4,3,1,0,2:T(8,128)(2,1)S(1)}, f16[2,4,1,32,128]{4,3,1,0,2:T(8,128)(2,1)S(1)}, u32[]{:S(2)}, u32[]{:S(2)}) collective-permute-start(f16[2,4,1,32,128]{4,3,1,0,2:T(8,128)(2,1)S(1)} %multiply_convert_fusion.2), channel_id=1, source_target_pairs={{0,2},{1,3},{2,0},{3,1},{4,6},{5,7},{6,4},{7,5},{8,10},{9,11},{10,... | collective-permute-start | bytes 196616 | tf_op jit(solution)/shard_map/ppermute | solution.py:148
  176.8 2.3 %collective-permute-done.19 = f16[2,4,1,32,128]{4,3,1,0,2:T(8,128)(2,1)S(1)} collective-permute-done((f16[2,4,1,32,128]{4,3,1,0,2:T(8,128)(2,1)S(1)}, f16[2,4,1,32,128]{4,3,1,0,2:T(8,128)(2,1)S(1)}, u32[]{:S(2)}, u32[]{:S(2)}) %collective-permute-start.19) | collective-permute-done | bytes 65568 | tf_op jit(solution)/shard_map/ppermute | solution.py:148
  179.0 1.7 collective-permute-start.17
  180.7 4.4 %collective-permute-done.17 = f16[2,4,1,32,128]{4,3,1,0,2:T(8,128)(2,1)S(1)} collective-permute-done((f16[2,4,1,32,128]{4,3,1,0,2:T(8,128)(2,1)S(1)}, f16[2,4,1,32,128]{4,3,1,0,2:T(8,128)(2,1)S(1)}, u32[]{:S(2)}, u32[]{:S(2)}) %collective-permute-start.17) | collective-permute-done | bytes 65568 | tf_op jit(solution)/shard_map/ppermute | solution.py:148
  185.1 5.6 %collective-permute-start.5 = (bf16[5,128,640]{2,1,0:T(8,128)(2,1)S(1)}, bf16[5,128,640]{2,1,0:T(8,128)(2,1)S(1)}, u32[]{:S(2)}, u32[]{:S(2)}) collective-permute-start(bf16[5,128,640]{2,1,0:T(8,128)(2,1)S(1)} %copy-done.5), channel_id=1, source_target_pairs={{0,12},{4,0},{8,4},{12,8},{1,13},{5,1},{9,5},{13,9},{2,14},{6,2},{... | collective-permute-start | bytes 2457608 | tf_op jit(solution)/shard_map/ppermute | solution.py:179
  190.9 3.9 %shard_map.67 = f32[2,3,128,128]{3,2,1,0:T(8,128)S(1)} custom-call(s32[102]{0:T(128)S(1)} %concatenate.20.refs_0_, f32[8]{0:T(128)S(1)} %copy-done.2, f32[2]{0:T(128)S(1)} %copy-done.3, f32[16,640]{1,0:T(8,128)S(1)} %reshape.58.refs_3_, bf16[8,3,128,640]{3,2,1,0:T(8,128)(2,1)S(1)} %bitcast.51, bf16[3,128,640]{2,1,0:T(8,128)(2,1)S(1)} %collective-permute-done.13.refs_5_, ...), custom_call_target="tpu_custom_call" | custom-call | flops 1000 | bytes 1000 | tf_op jit(solution)/shard_map/pallas_call | solution.py:121
  195.0 6.8 %collective-permute-done.5.refs_5_ = bf16[5,128,640]{2,1,0:T(8,128)(2,1)S(1)} collective-permute-done((bf16[5,128,640]{2,1,0:T(8,128)(2,1)S(1)}, bf16[5,128,640]{2,1,0:T(8,128)(2,1)S(1)}, u32[]{:S(2)}, u32[]{:S(2)}) %collective-permute-start.5) | collective-permute-done | bytes 819232 | tf_op jit(solution)/shard_map/ppermute | solution.py:179
  201.8 6.3 %shard_map.66 = f32[2,5,128,128]{3,2,1,0:T(8,128)S(1)} custom-call(s32[102]{0:T(128)S(1)} %concatenate.20.refs_0_, f32[8]{0:T(128)S(1)} %copy-done.2, f32[2]{0:T(128)S(1)} %copy-done.3, f32[16,640]{1,0:T(8,128)S(1)} %reshape.58.refs_3_, bf16[8,3,128,640]{3,2,1,0:T(8,128)(2,1)S(1)} %bitcast.52, bf16[5,128,640]{2,1,0:T(8,128)(2,1)S(1)} %collective-permute-done.5.refs_5_, ...), custom_call_target="tpu_custom_call" | custom-call | flops 1000 | bytes 1000 | tf_op jit(solution)/shard_map/pallas_call | solution.py:121
  208.3 1.1 collective-permute-start.15
  209.5 5.0 %collective-permute-done.11 = f16[2,5,2,32,128]{4,3,1,0,2:T(8,128)(2,1)S(1)} collective-permute-done((f16[2,5,2,32,128]{4,3,1,0,2:T(8,128)(2,1)S(1)}, f16[2,5,2,32,128]{4,3,1,0,2:T(8,128)(2,1)S(1)}, u32[]{:S(2)}, u32[]{:S(2)}) %collective-permute-start.11) | collective-permute-done | bytes 163872 | tf_op jit(solution)/shard_map/ppermute | solution.py:148
  215.3 5.7 %collective-permute-done.12 = f16[2,5,1,32,128]{4,3,1,0,2:T(8,128)(2,1)S(1)} collective-permute-done((f16[2,5,1,32,128]{4,3,1,0,2:T(8,128)(2,1)S(1)}, f16[2,5,1,32,128]{4,3,1,0,2:T(8,128)(2,1)S(1)}, u32[]{:S(2)}, u32[]{:S(2)}) %collective-permute-start.12) | collective-permute-done | bytes 81952 | tf_op jit(solution)/shard_map/ppermute | solution.py:148
  221.0 0.9 maximum_bitcast_fusion
  (60 shorter events, 3.5 us)
Async XLA Ops:
  1.6 123.6 %collective-permute-start = (s32[25]{0:T(128)S(1)}, s32[25]{0:T(128)S(1)}, u32[]{:S(2)}, u32[]{:S(2)}) collective-permute-start(s32[25]{0:T(128)S(1)} %pad_add_fusion), channel_id=1, source_target_pairs={{0,4},{4,8},{8,12},{12,0},{1,5},{5,9},{9,13},{13,1},{2,6},{6,10},{... | collective-permute-start | bytes 308 | tf_op jit(solution)/shard_map/ppermute | solution.py:167
  4.2 121.0 %collective-permute-start.1 = (s32[25]{0:T(128)S(1)}, s32[25]{0:T(128)S(1)}, u32[]{:S(2)}, u32[]{:S(2)}) collective-permute-start(s32[25]{0:T(128)S(1)} %pad_add_fusion), channel_id=1, source_target_pairs={{0,8},{4,12},{8,0},{12,4},{1,9},{5,13},{9,1},{13,5},{2,10},{6,14},... | collective-permute-start | bytes 308 | tf_op jit(solution)/shard_map/ppermute | solution.py:167
  4.2 121.0 %collective-permute-start.2 = (s32[25]{0:T(128)S(1)}, s32[25]{0:T(128)S(1)}, u32[]{:S(2)}, u32[]{:S(2)}) collective-permute-start(s32[25]{0:T(128)S(1)} %pad_add_fusion), channel_id=1, source_target_pairs={{0,12},{4,0},{8,4},{12,8},{1,13},{5,1},{9,5},{13,9},{2,14},{6,2},{... | collective-permute-start | bytes 308 | tf_op jit(solution)/shard_map/ppermute | solution.py:167
  4.6 120.5 %copy-start.4 = (f32[10240]{0:T(1024)S(1)}, f32[10240]{0:T(1024)}, u32[]{:S(2)}) copy-start(f32[10240]{0:T(1024)} %param.10) | copy-start | bytes 122884
  4.6 120.6 %copy-start.2 = (f32[8]{0:T(128)S(1)}, f32[8]{0:T(128)}, u32[]{:S(2)}) copy-start(f32[8]{0:T(128)} %refs_1_.9) | copy-start | bytes 100
  4.6 120.6 %copy-start.3 = (f32[2]{0:T(128)S(1)}, f32[2]{0:T(128)}, u32[]{:S(2)}) copy-start(f32[2]{0:T(128)} %refs_2_.9) | copy-start | bytes 28
  125.2 2.1 copy-start
  135.0 2.6 %copy-start.6 = (bf16[4,128,640]{2,1,0:T(8,128)(2,1)S(1)}, bf16[4,128,640]{2,1,0:T(8,128)(2,1)}, u32[]{:S(2)}) copy-start(bf16[4,128,640]{2,1,0:T(8,128)(2,1)} %get-tuple-element.24) | copy-start | bytes 1966084
  135.2 6.5 %collective-permute-start.3 = (f16[2,8,2,32,128]{4,3,1,0,2:T(8,128)(2,1)S(1)}, f16[2,8,2,32,128]{4,3,1,0,2:T(8,128)(2,1)S(1)}, u32[]{:S(2)}, u32[]{:S(2)}) collective-permute-start(f16[2,8,2,32,128]{4,3,1,0,2:T(8,128)(2,1)S(1)} %fusion.2), channel_id=1, source_target_pairs={{0,1},{1,0},{2,3},{3,2},{4,5},{5,4},{6,7},{7,6},{8,9},{9,8},{10,11... | collective-permute-start | bytes 786440 | tf_op jit(solution)/shard_map/ppermute | solution.py:148
  136.6 14.8 %collective-permute-start.9 = (bf16[4,128,640]{2,1,0:T(8,128)(2,1)}, bf16[4,128,640]{2,1,0:T(8,128)(2,1)S(1)}, u32[]{:S(2)}, u32[]{:S(2)}) collective-permute-start(bf16[4,128,640]{2,1,0:T(8,128)(2,1)} %get-tuple-element.25), channel_id=1, source_target_pairs={{0,8},{4,12},{8,0},{12,4},{1,9},{5,13},{9,1},{13,5},{2,10},{6,14},... | collective-permute-start | bytes 1966088 | tf_op jit(solution)/shard_map/ppermute | solution.py:178
  137.6 27.8 %collective-permute-start.7 = (bf16[4,128,640]{2,1,0:T(8,128)(2,1)S(1)}, bf16[4,128,640]{2,1,0:T(8,128)(2,1)S(1)}, u32[]{:S(2)}, u32[]{:S(2)}) collective-permute-start(bf16[4,128,640]{2,1,0:T(8,128)(2,1)S(1)} %copy-done.6), channel_id=1, source_target_pairs={{0,8},{4,12},{8,0},{12,4},{1,9},{5,13},{9,1},{13,5},{2,10},{6,14},... | collective-permute-start | bytes 1966088 | tf_op jit(solution)/shard_map/ppermute | solution.py:178
  141.8 7.0 %collective-permute-start.4 = (f16[2,8,1,32,128]{4,3,1,0,2:T(8,128)(2,1)S(1)}, f16[2,8,1,32,128]{4,3,1,0,2:T(8,128)(2,1)S(1)}, u32[]{:S(2)}, u32[]{:S(2)}) collective-permute-start(f16[2,8,1,32,128]{4,3,1,0,2:T(8,128)(2,1)S(1)} %multiply_convert_fusion), channel_id=1, source_target_pairs={{0,2},{1,3},{2,0},{3,1},{4,6},{5,7},{6,4},{7,5},{8,10},{9,11},{10,... | collective-permute-start | bytes 393224 | tf_op jit(solution)/shard_map/ppermute | solution.py:148
  144.2 46.7 %collective-permute-start.13 = (bf16[3,128,640]{2,1,0:T(8,128)(2,1)}, bf16[3,128,640]{2,1,0:T(8,128)(2,1)S(1)}, u32[]{:S(2)}, u32[]{:S(2)}) collective-permute-start(bf16[3,128,640]{2,1,0:T(8,128)(2,1)} %get-tuple-element.26), channel_id=1, source_target_pairs={{0,12},{4,0},{8,4},{12,8},{1,13},{5,1},{9,5},{13,9},{2,14},{6,2},{... | collective-permute-start | bytes 1474568 | tf_op jit(solution)/shard_map/ppermute | solution.py:179
  146.8 44.1 %collective-permute-start.6 = (bf16[8,128,640]{2,1,0:T(8,128)(2,1)}, bf16[8,128,640]{2,1,0:T(8,128)(2,1)S(1)}, u32[]{:S(2)}, u32[]{:S(2)}) collective-permute-start(bf16[8,128,640]{2,1,0:T(8,128)(2,1)} %get-tuple-element.23), channel_id=1, source_target_pairs={{4,0},{12,8},{5,1},{13,9},{6,2},{14,10},{7,3},{15,11},{20,16},{28,... | collective-permute-start | bytes 3932168 | tf_op jit(solution)/shard_map/ppermute | solution.py:180
  151.3 2.1 copy-start.1
  169.0 16.1 %copy-start.5 = (bf16[5,128,640]{2,1,0:T(8,128)(2,1)S(1)}, bf16[5,128,640]{2,1,0:T(8,128)(2,1)}, u32[]{:S(2)}) copy-start(bf16[5,128,640]{2,1,0:T(8,128)(2,1)} %get-tuple-element.22) | copy-start | bytes 2457604
  169.0 3.9 %collective-permute-start.18 = (f16[2,4,2,32,128]{4,3,1,0,2:T(8,128)(2,1)S(1)}, f16[2,4,2,32,128]{4,3,1,0,2:T(8,128)(2,1)S(1)}, u32[]{:S(2)}, u32[]{:S(2)}) collective-permute-start(f16[2,4,2,32,128]{4,3,1,0,2:T(8,128)(2,1)S(1)} %fusion.8), channel_id=1, source_target_pairs={{0,1},{1,0},{2,3},{3,2},{4,5},{5,4},{6,7},{7,6},{8,9},{9,8},{10,11... | collective-permute-start | bytes 393224 | tf_op jit(solution)/shard_map/ppermute | solution.py:148
  169.3 5.0 %collective-permute-start.16 = (f16[2,4,2,32,128]{4,3,1,0,2:T(8,128)(2,1)S(1)}, f16[2,4,2,32,128]{4,3,1,0,2:T(8,128)(2,1)S(1)}, u32[]{:S(2)}, u32[]{:S(2)}) collective-permute-start(f16[2,4,2,32,128]{4,3,1,0,2:T(8,128)(2,1)S(1)} %fusion.7), channel_id=1, source_target_pairs={{0,1},{1,0},{2,3},{3,2},{4,5},{5,4},{6,7},{7,6},{8,9},{9,8},{10,11... | collective-permute-start | bytes 393224 | tf_op jit(solution)/shard_map/ppermute | solution.py:148
  170.7 20.0 %collective-permute-start.8 = (bf16[4,128,640]{2,1,0:T(8,128)(2,1)S(1)}, bf16[4,128,640]{2,1,0:T(8,128)(2,1)S(1)}, u32[]{:S(2)}, u32[]{:S(2)}) collective-permute-start(bf16[4,128,640]{2,1,0:T(8,128)(2,1)S(1)} %collective-permute-done.7.refs_5_), channel_id=1, source_target_pairs={{0,4},{8,12},{1,5},{9,13},{2,6},{10,14},{3,7},{11,15},{16,20},{24,... | collective-permute-start | bytes 1966088 | tf_op jit(solution)/shard_map/ppermute | solution.py:185
  172.9 17.8 %collective-permute-start.10 = (bf16[4,128,640]{2,1,0:T(8,128)(2,1)S(1)}, bf16[4,128,640]{2,1,0:T(8,128)(2,1)S(1)}, u32[]{:S(2)}, u32[]{:S(2)}) collective-permute-start(bf16[4,128,640]{2,1,0:T(8,128)(2,1)S(1)} %collective-permute-done.9.refs_5_), channel_id=1, source_target_pairs={{0,4},{8,12},{1,5},{9,13},{2,6},{10,14},{3,7},{11,15},{16,20},{24,... | collective-permute-start | bytes 1966088 | tf_op jit(solution)/shard_map/ppermute | solution.py:185
  174.3 4.7 %collective-permute-start.19 = (f16[2,4,1,32,128]{4,3,1,0,2:T(8,128)(2,1)S(1)}, f16[2,4,1,32,128]{4,3,1,0,2:T(8,128)(2,1)S(1)}, u32[]{:S(2)}, u32[]{:S(2)}) collective-permute-start(f16[2,4,1,32,128]{4,3,1,0,2:T(8,128)(2,1)S(1)} %multiply_convert_fusion.2), channel_id=1, source_target_pairs={{0,2},{1,3},{2,0},{3,1},{4,6},{5,7},{6,4},{7,5},{8,10},{9,11},{10,... | collective-permute-start | bytes 196616 | tf_op jit(solution)/shard_map/ppermute | solution.py:148
  179.0 6.1 %collective-permute-start.17 = (f16[2,4,1,32,128]{4,3,1,0,2:T(8,128)(2,1)S(1)}, f16[2,4,1,32,128]{4,3,1,0,2:T(8,128)(2,1)S(1)}, u32[]{:S(2)}, u32[]{:S(2)}) collective-permute-start(f16[2,4,1,32,128]{4,3,1,0,2:T(8,128)(2,1)S(1)} %multiply_convert_fusion.3), channel_id=1, source_target_pairs={{0,2},{1,3},{2,0},{3,1},{4,6},{5,7},{6,4},{7,5},{8,10},{9,11},{10,... | collective-permute-start | bytes 196616 | tf_op jit(solution)/shard_map/ppermute | solution.py:148
  185.1 16.7 %collective-permute-start.5 = (bf16[5,128,640]{2,1,0:T(8,128)(2,1)S(1)}, bf16[5,128,640]{2,1,0:T(8,128)(2,1)S(1)}, u32[]{:S(2)}, u32[]{:S(2)}) collective-permute-start(bf16[5,128,640]{2,1,0:T(8,128)(2,1)S(1)} %copy-done.5), channel_id=1, source_target_pairs={{0,12},{4,0},{8,4},{12,8},{1,13},{5,1},{9,5},{13,9},{2,14},{6,2},{... | collective-permute-start | bytes 2457608 | tf_op jit(solution)/shard_map/ppermute | solution.py:179
  194.9 13.4 %collective-permute-start.14 = (f16[2,3,2,32,128]{4,3,1,0,2:T(8,128)(2,1)S(1)}, f16[2,3,2,32,128]{4,3,1,0,2:T(8,128)(2,1)S(1)}, u32[]{:S(2)}, u32[]{:S(2)}) collective-permute-start(f16[2,3,2,32,128]{4,3,1,0,2:T(8,128)(2,1)S(1)} %fusion.9), channel_id=1, source_target_pairs={{0,1},{1,0},{2,3},{3,2},{4,5},{5,4},{6,7},{7,6},{8,9},{9,8},{10,11... | collective-permute-start | bytes 294920 | tf_op jit(solution)/shard_map/ppermute | solution.py:148
  208.2 6.3 %collective-permute-start.11 = (f16[2,5,2,32,128]{4,3,1,0,2:T(8,128)(2,1)S(1)}, f16[2,5,2,32,128]{4,3,1,0,2:T(8,128)(2,1)S(1)}, u32[]{:S(2)}, u32[]{:S(2)}) collective-permute-start(f16[2,5,2,32,128]{4,3,1,0,2:T(8,128)(2,1)S(1)} %fusion.6), channel_id=1, source_target_pairs={{0,1},{1,0},{2,3},{3,2},{4,5},{5,4},{6,7},{7,6},{8,9},{9,8},{10,11... | collective-permute-start | bytes 491528 | tf_op jit(solution)/shard_map/ppermute | solution.py:148
  208.3 6.9 %collective-permute-start.15 = (f16[2,3,1,32,128]{4,3,1,0,2:T(8,128)(2,1)S(1)}, f16[2,3,1,32,128]{4,3,1,0,2:T(8,128)(2,1)S(1)}, u32[]{:S(2)}, u32[]{:S(2)}) collective-permute-start(f16[2,3,1,32,128]{4,3,1,0,2:T(8,128)(2,1)S(1)} %multiply_convert_fusion.4), channel_id=1, source_target_pairs={{0,2},{1,3},{2,0},{3,1},{4,6},{5,7},{6,4},{7,5},{8,10},{9,11},{10,... | collective-permute-start | bytes 147464 | tf_op jit(solution)/shard_map/ppermute | solution.py:148
  214.5 6.4 %collective-permute-start.12 = (f16[2,5,1,32,128]{4,3,1,0,2:T(8,128)(2,1)S(1)}, f16[2,5,1,32,128]{4,3,1,0,2:T(8,128)(2,1)S(1)}, u32[]{:S(2)}, u32[]{:S(2)}) collective-permute-start(f16[2,5,1,32,128]{4,3,1,0,2:T(8,128)(2,1)S(1)} %multiply_convert_fusion.1), channel_id=1, source_target_pairs={{0,2},{1,3},{2,0},{3,1},{4,6},{5,7},{6,4},{7,5},{8,10},{9,11},{10,... | collective-permute-start | bytes 245768 | tf_op jit(solution)/shard_map/ppermute | solution.py:148

commit v3 on v2

v3 whole, which is shorter than its diff:
```python
import functools

import jax
import jax.numpy as jnp
from jax import lax
from jax.experimental import pallas as pl
from jax.experimental.pallas import tpu as pltpu
from jax.sharding import PartitionSpec as P

HEAD = 2
LIMIT = 61 << 20
COST = pl.CostEstimate(flops=1000, bytes_accessed=1000, transcendentals=0)
ANY = pl.BlockSpec(memory_space=pl.ANY)
HBM = pl.BlockSpec(memory_space=pltpu.HBM)
SMEM = pl.BlockSpec(memory_space=pltpu.SMEM)
VMEM = pl.BlockSpec(memory_space=pltpu.VMEM)


def chunks_of(count, sizes):
    ends = [count * sum(sizes[: n + 1]) // sum(sizes) for n in range(len(sizes))]
    return [(a, b - a) for a, b in zip([0] + ends[:-1], ends)]


def pack_kernel(plan, tiles, *refs):
    outs, held, sem_in, sem_out = refs[:-3], refs[-3], refs[-2], refs[-1]
    aux_pos = lax.axis_index("aux")
    blocks_dev = tiles.shape[0]
    loads = [pltpu.make_async_copy(tiles.at[m], held.at[m], sem_in.at[m]) for m in range(blocks_dev)]
    copies = []
    for out, (slot, back, first) in zip(outs, plan):
        shift = (aux_pos < back).astype(jnp.int32)
        for i in range(out.shape[0]):
            row = jnp.minimum(first + i + shift, blocks_dev - 1)
            copies.append(pltpu.make_async_copy(held.at[row, slot], out.at[i], sem_out.at[len(copies)]))
    for load in loads:
        load.start()
    for load in loads:
        load.wait()
    for copy in copies:
        copy.start()
    for copy in copies:
        copy.wait()


def pack(tiles, plan, counts):
    return pl.pallas_call(
        functools.partial(pack_kernel, plan),
        out_shape=[jax.ShapeDtypeStruct((count,) + tiles.shape[-2:], tiles.dtype) for count in counts],
        in_specs=[HBM],
        out_specs=[HBM] * len(counts),
        scratch_shapes=[
            pltpu.VMEM(tiles.shape, tiles.dtype),
            pltpu.SemaphoreType.DMA((tiles.shape[0],)),
            pltpu.SemaphoreType.DMA((sum(counts),)),
        ],
        compiler_params=pltpu.CompilerParams(vmem_limit_bytes=LIMIT),
        cost_estimate=COST,
    )(tiles)


def band_kernel(dims, first, delta, pick, *refs):
    n_aux, n_pair, blocks_dev, band, freq_count = dims
    meta, occ, freq, table, own = refs[:5]
    far = refs[5:-4]
    out, mark, held, sem = refs[-4:]
    count = out.shape[1]
    slots = band - delta
    loads = [
        pltpu.make_async_copy(own.at[first + i, pl.ds(0, slots)], held.at[i], sem.at[i]) for i in range(count)
    ]
    for load in loads:
        load.start()
    virt_blocks = table.shape[0]
    record = blocks_dev * band + 1
    aux_pos, pair_col = meta[0], meta[1]
    shift = ((aux_pos + delta) >= n_aux).astype(jnp.int32)
    behind = lax.rem(2 * n_aux - delta, n_aux)
    even = lax.rem(aux_pos, 2) == 0
    mark[0] = pair_col
    for load in loads:
        load.wait()
    for i in range(count):
        here = first + i
        block = here * n_aux + aux_pos
        there = here + shift
        safe_there = jnp.minimum(there, blocks_dev - 1)
        sums = [None] * freq_count
        for slot in range(slots):
            centre = block - slot
            safe = jnp.maximum(centre, 0)
            region = safe // blocks_dev
            number = lax.rem(safe, blocks_dev)
            live = meta[HEAD + lax.rem(aux_pos - region + n_aux, n_aux) * record + blocks_dev * band]
            left_on = meta[HEAD + here * band + slot]
            right_on = meta[HEAD + behind * record + safe_there * band + slot + delta]
            keep = (centre >= 0) & (number < live) & (left_on > 0) & (right_on > 0) & (there < blocks_dev)
            present = keep.astype(jnp.float32)
            pair_block = (region * n_pair + pair_col) * blocks_dev + number
            gap = table[pl.ds(lax.rem(pair_block, virt_blocks), 1), :] - occ[pair_block // virt_blocks]
            left = held[i, slot].astype(jnp.float32)
            right = None
            if delta > 0:
                places = [far[n][row] for n, row in pick[i][slot]]
                right = places[0] if len(places) == 1 else jnp.where(even, places[0], places[1])
                right = right.astype(jnp.float32)
            for w in range(freq_count):
                omega = freq[w]
                root = jnp.sqrt(2.0 * gap / (gap * gap + omega * omega))
                a = (left * (root * present)).astype(jnp.bfloat16)
                b = a if right is None else (right * root).astype(jnp.bfloat16)
                term = lax.dot_general(a, b, (((1,), (1,)), ((), ())), preferred_element_type=jnp.float32)
                sums[w] = term if sums[w] is None else sums[w] + term
        for w in range(freq_count):
            out[w, i] = sums[w]


def band_rows(dims, first, count, delta, args, far=(), pick=None, after=()):
    meta, occ, freq, table, tiles = args
    n_aux, n_pair, blocks_dev, band, freq_count = dims
    aux_rows, pair_rows = tiles.shape[-2:]

    def body(*refs):
        ins = refs[: 5 + len(far)]
        band_kernel(dims, first, delta, pick, *ins, *refs[-4:])

    return pl.pallas_call(
        body,
        out_shape=[
            jax.ShapeDtypeStruct((freq_count, count, aux_rows, aux_rows), jnp.float32),
            jax.ShapeDtypeStruct((1,), jnp.int32),
        ],
        in_specs=[SMEM, SMEM, SMEM, VMEM, HBM] + [VMEM] * len(far) + [ANY] * len(after),
        out_specs=[VMEM, SMEM],
        scratch_shapes=[
            pltpu.VMEM((count, band - delta, aux_rows, pair_rows), tiles.dtype),
            pltpu.SemaphoreType.DMA((count,)),
        ],
        compiler_params=pltpu.CompilerParams(vmem_limit_bytes=LIMIT),
        cost_estimate=COST,
    )(meta, occ, freq, table, tiles, *far, *after)


def trade(keep, pair_col, step, n_pair, scale):
    freq_count, count, shares, height, width = keep.shape
    keep = keep.reshape(freq_count, count, shares // 2, 2, height, width)
    bit = (pair_col // step) % 2
    part = lax.dynamic_index_in_dim(keep, 1 - bit, 3, keepdims=False)
    mine = lax.dynamic_index_in_dim(keep, bit, 3, keepdims=False)
    sent = (part * scale).astype(jnp.float16)
    got = lax.ppermute(sent, "pair", [(s, s ^ step) for s in range(n_pair)])
    return mine, got


class Sum:
    def __init__(self, rows, n_pair, scale):
        freq_count, count, aux_rows, width = rows.shape
        self.keep = rows.reshape(freq_count, count, n_pair, aux_rows // n_pair, width)
        self.n_pair, self.scale, self.step = n_pair, scale, 1

    def advance(self, mark):
        if self.step < self.n_pair:
            mine, got = trade(self.keep, mark[0], self.step, self.n_pair, self.scale)
            self.keep = mine + got.astype(jnp.float32) * (1.0 / self.scale)
            self.step *= 2

    def finish(self, mark):
        while self.step < self.n_pair:
            self.advance(mark)
        return self.keep[:, :, 0]


def on_device(three_centre, locality, live_blocks, occ_energy, virt_energy, frequencies):
    n_aux = lax.axis_size("aux")
    n_pair = lax.axis_size("pair")
    aux_pos = lax.axis_index("aux")
    pair_col = lax.axis_index("pair")
    tiles = three_centre[0, 0, :, :, 0]
    blocks_dev, band, aux_rows, pair_rows = tiles.shape
    freq_count = frequencies.shape[0]
    dims = (n_aux, n_pair, blocks_dev, band, freq_count)
    scale = 128.0 / n_pair
    table = virt_energy.reshape(-1, pair_rows)
    record = jnp.concatenate([locality[0, 0].reshape(-1), live_blocks[0]])
    records = [record] + [
        lax.ppermute(record, "aux", [(s, (s + k) % n_aux) for s in range(n_aux)]) for k in range(1, n_aux)
    ]
    meta = jnp.concatenate([jnp.stack([aux_pos, pair_col]).astype(jnp.int32)] + records)

    two = chunks_of(blocks_dev, (4, 4))
    one = chunks_of(blocks_dev, (5, 3))
    plan = [(2, 2, f) for f, _ in two] + [(1, 1, f) for f, _ in one] + [(2, 0, 0)]
    packed = pack(tiles, plan, [c for _, c in two + one] + [blocks_dev])
    down1 = [(s, (s - 1) % n_aux) for s in range(n_aux)]
    down2 = [(s, (s - 2) % n_aux) for s in range(n_aux)]
    c2 = [lax.ppermute(packed[n], "aux", down2) for n in range(2)]
    b1 = [lax.ppermute(packed[2 + n], "aux", down1) for n in range(2)]
    to_even = lax.ppermute(packed[4], "aux", [(s, s - 1) for s in range(1, n_aux, 2)])
    to_odd = [lax.ppermute(c, "aux", [(s, s + 1) for s in range(0, n_aux, 2)]) for c in c2]
    args = (meta, occ_energy, frequencies, table, tiles)
    rows, mark = band_rows(dims, 0, blocks_dev, 0, args)
    sums = [Sum(rows, n_pair, scale)]
    sums[0].advance(mark)
    for n, (first, count) in enumerate(two):
        pick = [[[(0, i)]] for i in range(count)]
        rows, mark = band_rows(dims, first, count, 2, args, [c2[n]], pick, [rows])
        sums.append(Sum(rows, n_pair, scale))
        for part in sums:
            part.advance(mark)
    where = [(n, i) for n, (_, count) in enumerate(two) for i in range(count)]
    for n, (first, count) in enumerate(one):
        pick = []
        for i in range(count):
            piece, row = where[first + i]
            pick.append([[(0, i)], [(1, first + i), (2 + piece, row)]])
        rows, mark = band_rows(dims, first, count, 1, args, [b1[n], to_even, *to_odd], pick, [rows])
        sums.append(Sum(rows, n_pair, scale))
        for part in sums:
            part.advance(mark)
    done = [part.finish(mark) for part in sums]
    out = jnp.concatenate(
        [done[0], jnp.concatenate(done[3:], axis=1), jnp.concatenate(done[1:3], axis=1)], axis=-1
    )
    return out[:, :, None]


def solution(mesh):
    return jax.shard_map(
        on_device,
        mesh=mesh,
        in_specs=(
            P(("grp", "aux"), "pair", None, None, None, None, None),
            P(("grp", "aux"), "pair", None, None, None),
            P(("grp", "aux"), "pair"),
            P("grp"),
            P("grp"),
            P("grp"),
        ),
        out_specs=P(None, None, ("grp", "aux"), "pair", None),
        check_vma=False,
    )
```

time: 223 us -> 104 us (0.47)
  the two profiles are of different devices: /device:TPU:1 before, /device:TPU:0 now
where the time goes in v3:
time: 104 us; the launch traced here: 103 us
  Pallas kernels  29.7 us (29%)
  waiting for transfers between devices  28.7 us (28%)
  starting transfers between devices  22.5 us (22%)
  between operations  12.9 us (12%)
  local copies, waits for them, and re-layouts  5.75 us (6%)
  other arithmetic  3.38 us (3%)
    ppermute x10, waiting for transfers between devices, trade(): got = lax.ppermute(sent, 'pair', [(s, s ^ step) for s in range(n_pair)])  26.4 us
    pallas_call x5, Pallas kernels, band_rows(): pl.pallas_call(body, out_shape=[jax.ShapeDtypeStruct((freq_count, count,...  25.4 us
    ppermute x10, starting transfers between devices, trade(): got = lax.ppermute(sent, 'pair', [(s, s ^ step) for s in range(n_pair)])  12.5 us
    pallas_call x1, Pallas kernels, pack(): pl.pallas_call(functools.partial(pack_kernel, plan), out_shape=[jax.Shape...  4.25 us
    ppermute x3, starting transfers between devices, on_device(): lax.ppermute(record, 'aux', [(s, (s + k) % n_aux) for s in range(n_aux)])  3.17 us
    unnamed x25, local copies, waits for them, and re-layouts  2.9 us
    ppermute x2, starting transfers between devices, on_device(): lax.ppermute(c, 'aux', [(s, s + 1) for s in range(0, n_aux, 2)])  2.77 us
    ppermute x2, waiting for transfers between devices, on_device(): c2 = [lax.ppermute(packed[n], 'aux', down2) for n in range(2)]  2.22 us
  transfers between devices with their start and end apart: 20, of which 10 were waited for; matrix products, arithmetic and copies ran while one was open for 5% of the time, Pallas kernels for 24%

profile of v3, /device:TPU:0, one launch (start us, length us, event | category | flops | bytes accessed | tf_op | source)
XLA Modules:
  0.0 102.9 jit_solution(6435274623473304163)
XLA Ops:
  1.6 2.4 %collective-permute-start.2 = (s32[25]{0:T(128)S(1)}, s32[25]{0:T(128)S(1)}, u32[]{:S(2)}, u32[]{:S(2)}) collective-permute-start(s32[25]{0:T(128)S(1)} %pad_add_fusion), channel_id=1, source_target_pairs={{0,12},{4,0},{8,4},{12,8},{1,13},{5,1},{9,5},{13,9},{2,14},{6,2},{... | collective-permute-start | bytes 308 | tf_op jit(solution)/shard_map/ppermute | solution.py:185
  4.7 4.3 %shard_map.65 = (bf16[4,128,640]{2,1,0:T(8,128)(2,1)}, bf16[4,128,640]{2,1,0:T(8,128)(2,1)}, bf16[5,128,640]{2,1,0:T(8,128)(2,1)}, bf16[3,128,640]{2,1,0:T(8,128)(2,1)}, bf16[8,128,640]{2,1,0:T(8,128)(2,1)}) custom-call(bf16[8,3,128,640]{3,2,1,0:T(8,128)(2,1)} %bitcast.52), custom_call_target="tpu_custom_call" | custom-call | flops 1000 | bytes 1000 | tf_op jit(solution)/shard_map/pallas_call | solution.py:46
  9.0 1.3 %collective-permute-start.4 = (bf16[4,128,640]{2,1,0:T(8,128)(2,1)}, bf16[4,128,640]{2,1,0:T(8,128)(2,1)}, u32[]{:S(2)}, u32[]{:S(2)}) collective-permute-start(bf16[4,128,640]{2,1,0:T(8,128)(2,1)} %get-tuple-element.22), channel_id=1, source_target_pairs={{0,8},{4,12},{8,0},{12,4},{1,9},{5,13},{9,1},{13,5},{2,10},{6,14},... | collective-permute-start | bytes 1966088 | tf_op jit(solution)/shard_map/ppermute | solution.py:195
  12.4 6.9 %shard_map.64 = (f32[2,8,128,128]{3,2,1,0:T(8,128)}, s32[1]{0:T(128)}) custom-call(s32[102]{0:T(128)} %concatenate.17.refs_0_, f32[8]{0:T(128)} %refs_1_.9, f32[2]{0:T(128)} %refs_2_.9, f32[16,640]{1,0:T(8,128)} %reshape.58.refs_3_, bf16[8,3,128,640]{3,2,1,0:T(8,128)(2,1)} %bitcast.53), custom_call_target="tpu_custom_call" | custom-call | flops 1000 | bytes 1000 | tf_op jit(solution)/shard_map/pallas_call | solution.py:126
  21.4 1.3 %constant_dynamic-slice_fusion.8 = (f32[2,8,2,1,32,128]{5,4,3,2,1,0:T(8,128)S(1)}, f32[2,8,2,1,32,128]{5,4,3,2,1,0:T(8,128)S(1)}) fusion(f32[2,8,2,2,32,128]{5,4,3,2,1,0:T(8,128)} %bitcast.58, s32[]{:T(128)S(6)} %select_n.126, s32[]{:T(128)S(6)} %select_n.125), kind=kLoop, calls=%fused_computation.39 | loop fusion | bytes 2097160 | tf_op jit(solution)/shard_map/jit(dynamic_index_in_dim)/dynamic_slice | solution.py:147
  22.8 1.6 %collective-permute-start.3 = (f16[2,8,2,32,128]{4,3,1,0,2:T(8,128)(2,1)S(1)}, f16[2,8,2,32,128]{4,3,1,0,2:T(8,128)(2,1)S(1)}, u32[]{:S(2)}, u32[]{:S(2)}) collective-permute-start(f16[2,8,2,32,128]{4,3,1,0,2:T(8,128)(2,1)S(1)} %fusion.2), channel_id=1, source_target_pairs={{0,1},{1,0},{2,3},{3,2},{4,5},{5,4},{6,7},{7,6},{8,9},{9,8},{10,11... | collective-permute-start | bytes 786440 | tf_op jit(solution)/shard_map/ppermute | solution.py:150
  25.2 1.3 %collective-permute-start.7 = (bf16[8,128,640]{2,1,0:T(8,128)(2,1)}, bf16[8,128,640]{2,1,0:T(8,128)(2,1)S(1)}, u32[]{:S(2)}, u32[]{:S(2)}) collective-permute-start(bf16[8,128,640]{2,1,0:T(8,128)(2,1)} %get-tuple-element.25), channel_id=1, source_target_pairs={{4,0},{12,8},{5,1},{13,9},{6,2},{14,10},{7,3},{15,11},{20,16},{28,... | collective-permute-start | bytes 3932168 | tf_op jit(solution)/shard_map/ppermute | solution.py:197
  26.5 5.4 %collective-permute-done.3 = f16[2,8,2,32,128]{4,3,1,0,2:T(8,128)(2,1)S(1)} collective-permute-done((f16[2,8,2,32,128]{4,3,1,0,2:T(8,128)(2,1)S(1)}, f16[2,8,2,32,128]{4,3,1,0,2:T(8,128)(2,1)S(1)}, u32[]{:S(2)}, u32[]{:S(2)}) %collective-permute-start.3) | collective-permute-done | bytes 262176 | tf_op jit(solution)/shard_map/ppermute | solution.py:150
  32.0 4.0 %shard_map.66 = (f32[2,4,128,128]{3,2,1,0:T(8,128)}, s32[1]{0:T(128)}) custom-call(s32[102]{0:T(128)} %concatenate.17.refs_0_, f32[8]{0:T(128)} %refs_1_.9, f32[2]{0:T(128)} %refs_2_.9, f32[16,640]{1,0:T(8,128)} %reshape.58.refs_3_, bf16[8,3,128,640]{3,2,1,0:T(8,128)(2,1)} %bitcast.54, bf16[4,128,640]{2,1,0:T(8,128)(2,1)} %collective-permute-done.4.refs_5_, ...), custom_call_target="tpu_custom_call" | custom-call | flops 1000 | bytes 1000 | tf_op jit(solution)/shard_map/pallas_call | solution.py:126
  38.5 2.2 %collective-permute-done.9.refs_5_ = bf16[4,128,640]{2,1,0:T(8,128)(2,1)} collective-permute-done((bf16[4,128,640]{2,1,0:T(8,128)(2,1)}, bf16[4,128,640]{2,1,0:T(8,128)(2,1)}, u32[]{:S(2)}, u32[]{:S(2)}) %collective-permute-start.9) | collective-permute-done | bytes 655392 | tf_op jit(solution)/shard_map/ppermute | solution.py:195
  40.7 3.9 %shard_map.67 = (f32[2,4,128,128]{3,2,1,0:T(8,128)}, s32[1]{0:T(128)}) custom-call(s32[102]{0:T(128)} %concatenate.17.refs_0_, f32[8]{0:T(128)} %refs_1_.9, f32[2]{0:T(128)} %refs_2_.9, f32[16,640]{1,0:T(8,128)} %reshape.58.refs_3_, bf16[8,3,128,640]{3,2,1,0:T(8,128)(2,1)} %bitcast.55, bf16[4,128,640]{2,1,0:T(8,128)(2,1)} %collective-permute-done.9.refs_5_, ...), custom_call_target="tpu_custom_call" | custom-call | flops 1000 | bytes 1000 | tf_op jit(solution)/shard_map/pallas_call | solution.py:126
  47.0 2.7 %collective-permute-start.5 = (f16[2,8,1,32,128]{4,3,1,0,2:T(8,128)(2,1)S(1)}, f16[2,8,1,32,128]{4,3,1,0,2:T(8,128)(2,1)S(1)}, u32[]{:S(2)}, u32[]{:S(2)}) collective-permute-start(f16[2,8,1,32,128]{4,3,1,0,2:T(8,128)(2,1)S(1)} %multiply_convert_fusion), channel_id=1, source_target_pairs={{0,2},{1,3},{2,0},{3,1},{4,6},{5,7},{6,4},{7,5},{8,10},{9,11},{10,... | collective-permute-start | bytes 393224 | tf_op jit(solution)/shard_map/ppermute | solution.py:150
  49.8 1.6 %collective-permute-start.16 = (f16[2,4,2,32,128]{4,3,1,0,2:T(8,128)(2,1)S(1)}, f16[2,4,2,32,128]{4,3,1,0,2:T(8,128)(2,1)S(1)}, u32[]{:S(2)}, u32[]{:S(2)}) collective-permute-start(f16[2,4,2,32,128]{4,3,1,0,2:T(8,128)(2,1)S(1)} %fusion.7), channel_id=1, source_target_pairs={{0,1},{1,0},{2,3},{3,2},{4,5},{5,4},{6,7},{7,6},{8,9},{9,8},{10,11... | collective-permute-start | bytes 393224 | tf_op jit(solution)/shard_map/ppermute | solution.py:150
  52.0 5.9 %collective-permute-done.16 = f16[2,4,2,32,128]{4,3,1,0,2:T(8,128)(2,1)S(1)} collective-permute-done((f16[2,4,2,32,128]{4,3,1,0,2:T(8,128)(2,1)S(1)}, f16[2,4,2,32,128]{4,3,1,0,2:T(8,128)(2,1)S(1)}, u32[]{:S(2)}, u32[]{:S(2)}) %collective-permute-start.16) | collective-permute-done | bytes 131104 | tf_op jit(solution)/shard_map/ppermute | solution.py:150
  57.9 0.9 collective-permute-start.17
  58.9 1.7 %collective-permute-done.18 = f16[2,4,2,32,128]{4,3,1,0,2:T(8,128)(2,1)S(1)} collective-permute-done((f16[2,4,2,32,128]{4,3,1,0,2:T(8,128)(2,1)S(1)}, f16[2,4,2,32,128]{4,3,1,0,2:T(8,128)(2,1)S(1)}, u32[]{:S(2)}, u32[]{:S(2)}) %collective-permute-start.18) | collective-permute-done | bytes 131104 | tf_op jit(solution)/shard_map/ppermute | solution.py:150
  60.6 1.5 %collective-permute-start.8 = (bf16[4,128,640]{2,1,0:T(8,128)(2,1)}, bf16[4,128,640]{2,1,0:T(8,128)(2,1)S(1)}, u32[]{:S(2)}, u32[]{:S(2)}) collective-permute-start(bf16[4,128,640]{2,1,0:T(8,128)(2,1)} %collective-permute-done.4.refs_5_), channel_id=1, source_target_pairs={{0,4},{8,12},{1,5},{9,13},{2,6},{10,14},{3,7},{11,15},{16,20},{24,... | collective-permute-start | bytes 1966088 | tf_op jit(solution)/shard_map/ppermute | solution.py:198
  62.0 1.8 %collective-permute-done.17 = f16[2,4,1,32,128]{4,3,1,0,2:T(8,128)(2,1)S(1)} collective-permute-done((f16[2,4,1,32,128]{4,3,1,0,2:T(8,128)(2,1)S(1)}, f16[2,4,1,32,128]{4,3,1,0,2:T(8,128)(2,1)S(1)}, u32[]{:S(2)}, u32[]{:S(2)}) %collective-permute-start.17) | collective-permute-done | bytes 65568 | tf_op jit(solution)/shard_map/ppermute | solution.py:150
  63.9 1.3 %collective-permute-start.10 = (bf16[4,128,640]{2,1,0:T(8,128)(2,1)}, bf16[4,128,640]{2,1,0:T(8,128)(2,1)S(1)}, u32[]{:S(2)}, u32[]{:S(2)}) collective-permute-start(bf16[4,128,640]{2,1,0:T(8,128)(2,1)} %collective-permute-done.9.refs_5_), channel_id=1, source_target_pairs={{0,4},{8,12},{1,5},{9,13},{2,6},{10,14},{3,7},{11,15},{16,20},{24,... | collective-permute-start | bytes 1966088 | tf_op jit(solution)/shard_map/ppermute | solution.py:198
  65.2 1.7 %add_bitcast_fusion = f32[2,8,32,128]{3,2,1,0:T(8,128)} fusion(f16[2,8,1,32,128]{4,3,1,0,2:T(8,128)(2,1)S(1)} %collective-permute-done.5, f32[2,8,2,32,128]{4,3,1,0,2:T(8,128)} %copy-done.6, s32[]{:T(128)S(6)} %select_n.129), kind=kLoop, calls=%fused_computation.14 | loop fusion | flops 196608 | bytes 655364 | tf_op jit(solution)/shard_map/squeeze | solution.py:169
  68.1 1.1 %copy-done = bf16[8,128,640]{2,1,0:T(8,128)(2,1)} copy-done((bf16[8,128,640]{2,1,0:T(8,128)(2,1)}, bf16[8,128,640]{2,1,0:T(8,128)(2,1)S(1)}, u32[]{:S(2)}) %copy-start) | copy-done | bytes 1310744
  69.2 5.8 %shard_map.68 = (f32[2,5,128,128]{3,2,1,0:T(8,128)}, s32[1]{0:T(128)}) custom-call(s32[102]{0:T(128)} %concatenate.17.refs_0_, f32[8]{0:T(128)} %refs_1_.9, f32[2]{0:T(128)} %refs_2_.9, f32[16,640]{1,0:T(8,128)} %reshape.58.refs_3_, bf16[8,3,128,640]{3,2,1,0:T(8,128)(2,1)} %bitcast.56, bf16[5,128,640]{2,1,0:T(8,128)(2,1)} %collective-permute-done.6.refs_5_, ...), custom_call_target="tpu_custom_call" | custom-call | flops 1000 | bytes 1000 | tf_op jit(solution)/shard_map/pallas_call | solution.py:126
  77.3 4.9 %shard_map.69 = (f32[2,3,128,128]{3,2,1,0:T(8,128)}, s32[1]{0:T(128)}) custom-call(s32[102]{0:T(128)} %concatenate.17.refs_0_, f32[8]{0:T(128)} %refs_1_.9, f32[2]{0:T(128)} %refs_2_.9, f32[16,640]{1,0:T(8,128)} %reshape.58.refs_3_, bf16[8,3,128,640]{3,2,1,0:T(8,128)(2,1)} %bitcast.57, bf16[3,128,640]{2,1,0:T(8,128)(2,1)} %collective-permute-done.12.refs_5_, ...), custom_call_target="tpu_custom_call" | custom-call | flops 1000 | bytes 1000 | tf_op jit(solution)/shard_map/pallas_call | solution.py:126
  85.2 2.2 %collective-permute-start.14 = (f16[2,3,2,32,128]{4,3,1,0,2:T(8,128)(2,1)S(1)}, f16[2,3,2,32,128]{4,3,1,0,2:T(8,128)(2,1)S(1)}, u32[]{:S(2)}, u32[]{:S(2)}) collective-permute-start(f16[2,3,2,32,128]{4,3,1,0,2:T(8,128)(2,1)S(1)} %fusion.9), channel_id=1, source_target_pairs={{0,1},{1,0},{2,3},{3,2},{4,5},{5,4},{6,7},{7,6},{8,9},{9,8},{10,11... | collective-permute-start | bytes 294920 | tf_op jit(solution)/shard_map/ppermute | solution.py:150
  87.5 3.2 %collective-permute-done.19 = f16[2,4,1,32,128]{4,3,1,0,2:T(8,128)(2,1)S(1)} collective-permute-done((f16[2,4,1,32,128]{4,3,1,0,2:T(8,128)(2,1)S(1)}, f16[2,4,1,32,128]{4,3,1,0,2:T(8,128)(2,1)S(1)}, u32[]{:S(2)}, u32[]{:S(2)}) %collective-permute-start.19) | collective-permute-done | bytes 65568 | tf_op jit(solution)/shard_map/ppermute | solution.py:150
  90.8 1.6 %collective-permute-done.14 = f16[2,3,2,32,128]{4,3,1,0,2:T(8,128)(2,1)S(1)} collective-permute-done((f16[2,3,2,32,128]{4,3,1,0,2:T(8,128)(2,1)S(1)}, f16[2,3,2,32,128]{4,3,1,0,2:T(8,128)(2,1)S(1)}, u32[]{:S(2)}, u32[]{:S(2)}) %collective-permute-start.14) | collective-permute-done | bytes 98336 | tf_op jit(solution)/shard_map/ppermute | solution.py:150
  92.4 1.4 %collective-permute-start.15 = (f16[2,3,1,32,128]{4,3,1,0,2:T(8,128)(2,1)S(1)}, f16[2,3,1,32,128]{4,3,1,0,2:T(8,128)(2,1)S(1)}, u32[]{:S(2)}, u32[]{:S(2)}) collective-permute-start(f16[2,3,1,32,128]{4,3,1,0,2:T(8,128)(2,1)S(1)} %multiply_convert_fusion.4), channel_id=1, source_target_pairs={{0,2},{1,3},{2,0},{3,1},{4,6},{5,7},{6,4},{7,5},{8,10},{9,11},{10,... | collective-permute-start | bytes 147464 | tf_op jit(solution)/shard_map/ppermute | solution.py:150
  93.9 1.8 %collective-permute-done.11 = f16[2,5,2,32,128]{4,3,1,0,2:T(8,128)(2,1)S(1)} collective-permute-done((f16[2,5,2,32,128]{4,3,1,0,2:T(8,128)(2,1)S(1)}, f16[2,5,2,32,128]{4,3,1,0,2:T(8,128)(2,1)S(1)}, u32[]{:S(2)}, u32[]{:S(2)}) %collective-permute-start.11) | collective-permute-done | bytes 163872 | tf_op jit(solution)/shard_map/ppermute | solution.py:150
  95.7 1.1 %collective-permute-start.13 = (f16[2,5,1,32,128]{4,3,1,0,2:T(8,128)(2,1)S(1)}, f16[2,5,1,32,128]{4,3,1,0,2:T(8,128)(2,1)S(1)}, u32[]{:S(2)}, u32[]{:S(2)}) collective-permute-start(f16[2,5,1,32,128]{4,3,1,0,2:T(8,128)(2,1)S(1)} %multiply_convert_fusion.1), channel_id=1, source_target_pairs={{0,2},{1,3},{2,0},{3,1},{4,6},{5,7},{6,4},{7,5},{8,10},{9,11},{10,... | collective-permute-start | bytes 245768 | tf_op jit(solution)/shard_map/ppermute | solution.py:150
  96.9 1.1 %collective-permute-done.15 = f16[2,3,1,32,128]{4,3,1,0,2:T(8,128)(2,1)S(1)} collective-permute-done((f16[2,3,1,32,128]{4,3,1,0,2:T(8,128)(2,1)S(1)}, f16[2,3,1,32,128]{4,3,1,0,2:T(8,128)(2,1)S(1)}, u32[]{:S(2)}, u32[]{:S(2)}) %collective-permute-start.15) | collective-permute-done | bytes 49184 | tf_op jit(solution)/shard_map/ppermute | solution.py:150
  98.0 3.9 %collective-permute-done.13 = f16[2,5,1,32,128]{4,3,1,0,2:T(8,128)(2,1)S(1)} collective-permute-done((f16[2,5,1,32,128]{4,3,1,0,2:T(8,128)(2,1)S(1)}, f16[2,5,1,32,128]{4,3,1,0,2:T(8,128)(2,1)S(1)}, u32[]{:S(2)}, u32[]{:S(2)}) %collective-permute-start.13) | collective-permute-done | bytes 81952 | tf_op jit(solution)/shard_map/ppermute | solution.py:150
  102.0 0.9 maximum_bitcast_fusion
  (69 shorter events, 7.2 us)
Async XLA Ops:
  1.6 10.2 %collective-permute-start.2 = (s32[25]{0:T(128)S(1)}, s32[25]{0:T(128)S(1)}, u32[]{:S(2)}, u32[]{:S(2)}) collective-permute-start(s32[25]{0:T(128)S(1)} %pad_add_fusion), channel_id=1, source_target_pairs={{0,12},{4,0},{8,4},{12,8},{1,13},{5,1},{9,5},{13,9},{2,14},{6,2},{... | collective-permute-start | bytes 308 | tf_op jit(solution)/shard_map/ppermute | solution.py:185
  3.9 7.8 %collective-permute-start.1 = (s32[25]{0:T(128)S(1)}, s32[25]{0:T(128)S(1)}, u32[]{:S(2)}, u32[]{:S(2)}) collective-permute-start(s32[25]{0:T(128)S(1)} %pad_add_fusion), channel_id=1, source_target_pairs={{0,8},{4,12},{8,0},{12,4},{1,9},{5,13},{9,1},{13,5},{2,10},{6,14},... | collective-permute-start | bytes 308 | tf_op jit(solution)/shard_map/ppermute | solution.py:185
  4.6 7.2 %collective-permute-start = (s32[25]{0:T(128)S(1)}, s32[25]{0:T(128)S(1)}, u32[]{:S(2)}, u32[]{:S(2)}) collective-permute-start(s32[25]{0:T(128)S(1)} %pad_add_fusion), channel_id=1, source_target_pairs={{0,4},{4,8},{8,12},{12,0},{1,5},{5,9},{9,13},{13,1},{2,6},{6,10},{... | collective-permute-start | bytes 308 | tf_op jit(solution)/shard_map/ppermute | solution.py:185
  4.7 6.4 %copy-start.11 = (f32[10240]{0:T(1024)S(1)}, f32[10240]{0:T(1024)}, u32[]{:S(2)}) copy-start(f32[10240]{0:T(1024)} %param.10) | copy-start | bytes 122884
  9.0 23.0 %collective-permute-start.4 = (bf16[4,128,640]{2,1,0:T(8,128)(2,1)}, bf16[4,128,640]{2,1,0:T(8,128)(2,1)}, u32[]{:S(2)}, u32[]{:S(2)}) collective-permute-start(bf16[4,128,640]{2,1,0:T(8,128)(2,1)} %get-tuple-element.22), channel_id=1, source_target_pairs={{0,8},{4,12},{8,0},{12,4},{1,9},{5,13},{9,1},{13,5},{2,10},{6,14},... | collective-permute-start | bytes 1966088 | tf_op jit(solution)/shard_map/ppermute | solution.py:195
  10.3 30.4 %collective-permute-start.9 = (bf16[4,128,640]{2,1,0:T(8,128)(2,1)}, bf16[4,128,640]{2,1,0:T(8,128)(2,1)}, u32[]{:S(2)}, u32[]{:S(2)}) collective-permute-start(bf16[4,128,640]{2,1,0:T(8,128)(2,1)} %get-tuple-element.26), channel_id=1, source_target_pairs={{0,8},{4,12},{8,0},{12,4},{1,9},{5,13},{9,1},{13,5},{2,10},{6,14},... | collective-permute-start | bytes 1966088 | tf_op jit(solution)/shard_map/ppermute | solution.py:195
  22.8 9.1 %collective-permute-start.3 = (f16[2,8,2,32,128]{4,3,1,0,2:T(8,128)(2,1)S(1)}, f16[2,8,2,32,128]{4,3,1,0,2:T(8,128)(2,1)S(1)}, u32[]{:S(2)}, u32[]{:S(2)}) collective-permute-start(f16[2,8,2,32,128]{4,3,1,0,2:T(8,128)(2,1)S(1)} %fusion.2), channel_id=1, source_target_pairs={{0,1},{1,0},{2,3},{3,2},{4,5},{5,4},{6,7},{7,6},{8,9},{9,8},{10,11... | collective-permute-start | bytes 786440 | tf_op jit(solution)/shard_map/ppermute | solution.py:150
  24.4 42.6 %collective-permute-start.6 = (bf16[5,128,640]{2,1,0:T(8,128)(2,1)}, bf16[5,128,640]{2,1,0:T(8,128)(2,1)}, u32[]{:S(2)}, u32[]{:S(2)}) collective-permute-start(bf16[5,128,640]{2,1,0:T(8,128)(2,1)} %get-tuple-element.24), channel_id=1, source_target_pairs={{0,12},{4,0},{8,4},{12,8},{1,13},{5,1},{9,5},{13,9},{2,14},{6,2},{... | collective-permute-start | bytes 2457608 | tf_op jit(solution)/shard_map/ppermute | solution.py:196
  25.2 41.9 %collective-permute-start.7 = (bf16[8,128,640]{2,1,0:T(8,128)(2,1)}, bf16[8,128,640]{2,1,0:T(8,128)(2,1)S(1)}, u32[]{:S(2)}, u32[]{:S(2)}) collective-permute-start(bf16[8,128,640]{2,1,0:T(8,128)(2,1)} %get-tuple-element.25), channel_id=1, source_target_pairs={{4,0},{12,8},{5,1},{13,9},{6,2},{14,10},{7,3},{15,11},{20,16},{28,... | collective-permute-start | bytes 3932168 | tf_op jit(solution)/shard_map/ppermute | solution.py:197
  31.9 15.0 %copy-start.6 = (f32[2,8,2,32,128]{4,3,1,0,2:T(8,128)}, f32[2,8,2,32,128]{4,3,1,0,2:T(8,128)S(1)}, u32[]{:S(2)}) copy-start(f32[2,8,2,32,128]{4,3,1,0,2:T(8,128)S(1)} %bitcast_add_fusion) | copy-start | bytes 1572868
  40.7 8.9 %copy-start.5 = (f32[2,4,128,128]{3,2,1,0:T(8,128)S(1)}, f32[2,4,128,128]{3,2,1,0:T(8,128)}, u32[]{:S(2)}) copy-start(f32[2,4,128,128]{3,2,1,0:T(8,128)} %get-tuple-element.27.refs_6_) | copy-start | bytes 1572868
  44.6 6.8 %copy-start.4 = (f32[2,4,128,128]{3,2,1,0:T(8,128)S(1)}, f32[2,4,128,128]{3,2,1,0:T(8,128)}, u32[]{:S(2)}) copy-start(f32[2,4,128,128]{3,2,1,0:T(8,128)} %get-tuple-element.28.refs_9_) | copy-start | bytes 1572868
  47.0 11.9 %collective-permute-start.5 = (f16[2,8,1,32,128]{4,3,1,0,2:T(8,128)(2,1)S(1)}, f16[2,8,1,32,128]{4,3,1,0,2:T(8,128)(2,1)S(1)}, u32[]{:S(2)}, u32[]{:S(2)}) collective-permute-start(f16[2,8,1,32,128]{4,3,1,0,2:T(8,128)(2,1)S(1)} %multiply_convert_fusion), channel_id=1, source_target_pairs={{0,2},{1,3},{2,0},{3,1},{4,6},{5,7},{6,4},{7,5},{8,10},{9,11},{10,... | collective-permute-start | bytes 393224 | tf_op jit(solution)/shard_map/ppermute | solution.py:150
  49.8 8.1 %collective-permute-start.16 = (f16[2,4,2,32,128]{4,3,1,0,2:T(8,128)(2,1)S(1)}, f16[2,4,2,32,128]{4,3,1,0,2:T(8,128)(2,1)S(1)}, u32[]{:S(2)}, u32[]{:S(2)}) collective-permute-start(f16[2,4,2,32,128]{4,3,1,0,2:T(8,128)(2,1)S(1)} %fusion.7), channel_id=1, source_target_pairs={{0,1},{1,0},{2,3},{3,2},{4,5},{5,4},{6,7},{7,6},{8,9},{9,8},{10,11... | collective-permute-start | bytes 393224 | tf_op jit(solution)/shard_map/ppermute | solution.py:150
  51.5 9.1 %collective-permute-start.18 = (f16[2,4,2,32,128]{4,3,1,0,2:T(8,128)(2,1)S(1)}, f16[2,4,2,32,128]{4,3,1,0,2:T(8,128)(2,1)S(1)}, u32[]{:S(2)}, u32[]{:S(2)}) collective-permute-start(f16[2,4,2,32,128]{4,3,1,0,2:T(8,128)(2,1)S(1)} %fusion.8), channel_id=1, source_target_pairs={{0,1},{1,0},{2,3},{3,2},{4,5},{5,4},{6,7},{7,6},{8,9},{9,8},{10,11... | collective-permute-start | bytes 393224 | tf_op jit(solution)/shard_map/ppermute | solution.py:150
  57.9 1.0 copy-start.7
  57.9 5.9 %collective-permute-start.17 = (f16[2,4,1,32,128]{4,3,1,0,2:T(8,128)(2,1)S(1)}, f16[2,4,1,32,128]{4,3,1,0,2:T(8,128)(2,1)S(1)}, u32[]{:S(2)}, u32[]{:S(2)}) collective-permute-start(f16[2,4,1,32,128]{4,3,1,0,2:T(8,128)(2,1)S(1)} %multiply_convert_fusion.3), channel_id=1, source_target_pairs={{0,2},{1,3},{2,0},{3,1},{4,6},{5,7},{6,4},{7,5},{8,10},{9,11},{10,... | collective-permute-start | bytes 196616 | tf_op jit(solution)/shard_map/ppermute | solution.py:150
  58.9 18.4 %collective-permute-start.12 = (bf16[3,128,640]{2,1,0:T(8,128)(2,1)}, bf16[3,128,640]{2,1,0:T(8,128)(2,1)}, u32[]{:S(2)}, u32[]{:S(2)}) collective-permute-start(bf16[3,128,640]{2,1,0:T(8,128)(2,1)} %get-tuple-element.31), channel_id=1, source_target_pairs={{0,12},{4,0},{8,4},{12,8},{1,13},{5,1},{9,5},{13,9},{2,14},{6,2},{... | collective-permute-start | bytes 1474568 | tf_op jit(solution)/shard_map/ppermute | solution.py:196
  60.6 6.4 %copy-start.8 = (f32[2,4,2,32,128]{4,3,1,0,2:T(8,128)S(1)}, f32[2,4,2,32,128]{4,3,1,0,2:T(8,128)}, u32[]{:S(2)}) copy-start(f32[2,4,2,32,128]{4,3,1,0,2:T(8,128)} %copy-done.7) | copy-start | bytes 786436
  60.6 6.4 %collective-permute-start.8 = (bf16[4,128,640]{2,1,0:T(8,128)(2,1)}, bf16[4,128,640]{2,1,0:T(8,128)(2,1)S(1)}, u32[]{:S(2)}, u32[]{:S(2)}) collective-permute-start(bf16[4,128,640]{2,1,0:T(8,128)(2,1)} %collective-permute-done.4.refs_5_), channel_id=1, source_target_pairs={{0,4},{8,12},{1,5},{9,13},{2,6},{10,14},{3,7},{11,15},{16,20},{24,... | collective-permute-start | bytes 1966088 | tf_op jit(solution)/shard_map/ppermute | solution.py:198
  63.9 3.2 %collective-permute-start.10 = (bf16[4,128,640]{2,1,0:T(8,128)(2,1)}, bf16[4,128,640]{2,1,0:T(8,128)(2,1)S(1)}, u32[]{:S(2)}, u32[]{:S(2)}) collective-permute-start(bf16[4,128,640]{2,1,0:T(8,128)(2,1)} %collective-permute-done.9.refs_5_), channel_id=1, source_target_pairs={{0,4},{8,12},{1,5},{9,13},{2,6},{10,14},{3,7},{11,15},{16,20},{24,... | collective-permute-start | bytes 1966088 | tf_op jit(solution)/shard_map/ppermute | solution.py:198
  67.0 0.8 copy-start.1
  67.1 1.0 copy-start.2
  68.1 1.1 %copy-start = (bf16[8,128,640]{2,1,0:T(8,128)(2,1)}, bf16[8,128,640]{2,1,0:T(8,128)(2,1)S(1)}, u32[]{:S(2)}) copy-start(bf16[8,128,640]{2,1,0:T(8,128)(2,1)S(1)} %collective-permute-done.7.refs_6_) | copy-start | bytes 3932164
  77.3 6.9 %copy-start.3 = (f32[2,5,128,128]{3,2,1,0:T(8,128)S(1)}, f32[2,5,128,128]{3,2,1,0:T(8,128)}, u32[]{:S(2)}) copy-start(f32[2,5,128,128]{3,2,1,0:T(8,128)} %get-tuple-element.29.refs_9_) | copy-start | bytes 1966084
  82.2 2.3 %copy-start.10 = (f32[2,3,128,128]{3,2,1,0:T(8,128)S(1)}, f32[2,3,128,128]{3,2,1,0:T(8,128)}, u32[]{:S(2)}) copy-start(f32[2,3,128,128]{3,2,1,0:T(8,128)} %get-tuple-element.33) | copy-start | bytes 1179652
  84.3 6.5 %collective-permute-start.19 = (f16[2,4,1,32,128]{4,3,1,0,2:T(8,128)(2,1)S(1)}, f16[2,4,1,32,128]{4,3,1,0,2:T(8,128)(2,1)S(1)}, u32[]{:S(2)}, u32[]{:S(2)}) collective-permute-start(f16[2,4,1,32,128]{4,3,1,0,2:T(8,128)(2,1)S(1)} %multiply_convert_fusion.2), channel_id=1, source_target_pairs={{0,2},{1,3},{2,0},{3,1},{4,6},{5,7},{6,4},{7,5},{8,10},{9,11},{10,... | collective-permute-start | bytes 196616 | tf_op jit(solution)/shard_map/ppermute | solution.py:150
  85.2 7.1 %collective-permute-start.14 = (f16[2,3,2,32,128]{4,3,1,0,2:T(8,128)(2,1)S(1)}, f16[2,3,2,32,128]{4,3,1,0,2:T(8,128)(2,1)S(1)}, u32[]{:S(2)}, u32[]{:S(2)}) collective-permute-start(f16[2,3,2,32,128]{4,3,1,0,2:T(8,128)(2,1)S(1)} %fusion.9), channel_id=1, source_target_pairs={{0,1},{1,0},{2,3},{3,2},{4,5},{5,4},{6,7},{7,6},{8,9},{9,8},{10,11... | collective-permute-start | bytes 294920 | tf_op jit(solution)/shard_map/ppermute | solution.py:150
  87.5 8.2 %collective-permute-start.11 = (f16[2,5,2,32,128]{4,3,1,0,2:T(8,128)(2,1)S(1)}, f16[2,5,2,32,128]{4,3,1,0,2:T(8,128)(2,1)S(1)}, u32[]{:S(2)}, u32[]{:S(2)}) collective-permute-start(f16[2,5,2,32,128]{4,3,1,0,2:T(8,128)(2,1)S(1)} %fusion.6), channel_id=1, source_target_pairs={{0,1},{1,0},{2,3},{3,2},{4,5},{5,4},{6,7},{7,6},{8,9},{9,8},{10,11... | collective-permute-start | bytes 491528 | tf_op jit(solution)/shard_map/ppermute | solution.py:150
  87.5 14.4 %copy-start.9 = (f32[2,8,32,128]{3,2,1,0:T(8,128)S(1)}, f32[2,8,32,128]{3,2,1,0:T(8,128)}, u32[]{:S(2)}) copy-start(f32[2,8,32,128]{3,2,1,0:T(8,128)} %add_bitcast_fusion) | copy-start | bytes 786436
  92.4 5.6 %collective-permute-start.15 = (f16[2,3,1,32,128]{4,3,1,0,2:T(8,128)(2,1)S(1)}, f16[2,3,1,32,128]{4,3,1,0,2:T(8,128)(2,1)S(1)}, u32[]{:S(2)}, u32[]{:S(2)}) collective-permute-start(f16[2,3,1,32,128]{4,3,1,0,2:T(8,128)(2,1)S(1)} %multiply_convert_fusion.4), channel_id=1, source_target_pairs={{0,2},{1,3},{2,0},{3,1},{4,6},{5,7},{6,4},{7,5},{8,10},{9,11},{10,... | collective-permute-start | bytes 147464 | tf_op jit(solution)/shard_map/ppermute | solution.py:150
  95.7 6.2 %collective-permute-start.13 = (f16[2,5,1,32,128]{4,3,1,0,2:T(8,128)(2,1)S(1)}, f16[2,5,1,32,128]{4,3,1,0,2:T(8,128)(2,1)S(1)}, u32[]{:S(2)}, u32[]{:S(2)}) collective-permute-start(f16[2,5,1,32,128]{4,3,1,0,2:T(8,128)(2,1)S(1)} %multiply_convert_fusion.1), channel_id=1, source_target_pairs={{0,2},{1,3},{2,0},{3,1},{4,6},{5,7},{6,4},{7,5},{8,10},{9,11},{10,... | collective-permute-start | bytes 245768 | tf_op jit(solution)/shard_map/ppermute | solution.py:150

commit v4 on v2

v4 whole, which is shorter than its diff:
```python
import functools

import jax
import jax.numpy as jnp
from jax import lax
from jax.experimental import pallas as pl
from jax.experimental.pallas import tpu as pltpu
from jax.sharding import PartitionSpec as P

LIMIT = 61 << 20
COST = pl.CostEstimate(flops=1000, bytes_accessed=1000, transcendentals=0)
PARAMS = pltpu.CompilerParams(vmem_limit_bytes=LIMIT)
ANY = pl.BlockSpec(memory_space=pl.ANY)
HBM = pl.BlockSpec(memory_space=pltpu.HBM)
SMEM = pl.BlockSpec(memory_space=pltpu.SMEM)
VMEM = pl.BlockSpec(memory_space=pltpu.VMEM)
DMA = pltpu.SemaphoreType.DMA


def chunks_of(count, sizes):
    ends = [count * sum(sizes[: n + 1]) // sum(sizes) for n in range(len(sizes))]
    return [(a, b - a) for a, b in zip([0] + ends[:-1], ends)]


def dot(a, b):
    return lax.dot_general(a, b, (((1,), (1,)), ((), ())), preferred_element_type=jnp.float32)


def pack_kernel(plan, n_after, tiles, *refs):
    outs, held, sem_in, sem_out = refs[n_after:-3], refs[-3], refs[-2], refs[-1]
    aux_pos = lax.axis_index("aux")
    blocks_dev = tiles.shape[0]
    loads, stores = [], []
    for out, (slot, back, first) in zip(outs, plan):
        shift = (aux_pos < back).astype(jnp.int32)
        for i in range(out.shape[0]):
            n = len(loads)
            row = jnp.minimum(first + i + shift, blocks_dev - 1)
            loads.append(pltpu.make_async_copy(tiles.at[row, slot], held.at[n], sem_in.at[n]))
            stores.append(pltpu.make_async_copy(held.at[n], out.at[i], sem_out.at[n]))
    for load in loads:
        load.start()
    for load, store in zip(loads, stores):
        load.wait()
        store.start()
    for store in stores:
        store.wait()


def pack(tiles, plan, counts, after):
    total = sum(counts)
    return pl.pallas_call(
        functools.partial(pack_kernel, plan, len(after)),
        out_shape=[jax.ShapeDtypeStruct((count,) + tiles.shape[-2:], tiles.dtype) for count in counts],
        in_specs=[HBM] + [ANY] * len(after),
        out_specs=[HBM] * len(counts),
        scratch_shapes=[pltpu.VMEM((total,) + tiles.shape[-2:], tiles.dtype), DMA((total,)), DMA((total,))],
        compiler_params=PARAMS,
        cost_estimate=COST,
    )(tiles, *after)


def root_row(band, freq_count, delta, slot, w):
    before = 0 if delta is None else band + sum(band - d for d in range(1, delta))
    return (before + slot) * freq_count + w


def root_rows(band, freq_count):
    rows = freq_count * (band + sum(band - d for d in range(1, band)))
    return -(-rows // 8) * 8


def first_kernel(dims, *refs):
    n_aux, n_pair, blocks_dev, band, freq_count = dims
    records = refs[:n_aux]
    occ, freq, table, own = refs[n_aux : n_aux + 4]
    out, roots, last, held, sem, sem_out = refs[-6:]
    pair_rows = own.shape[-1]
    virt_blocks = table.shape[1] // pair_rows
    aux_pos, pair_col = lax.axis_index("aux"), lax.axis_index("pair")
    loads = [pltpu.make_async_copy(own.at[m], held.at[m], sem.at[m]) for m in range(blocks_dev)]
    stores = [pltpu.make_async_copy(held.at[m, band - 1], last.at[m], sem_out.at[m]) for m in range(blocks_dev)]
    for load in loads:
        load.start()

    def of_region(region):
        live = records[0][blocks_dev * band]
        for k in range(1, n_aux):
            live = jnp.where(lax.rem(aux_pos - region + n_aux, n_aux) == k, records[k][blocks_dev * band], live)
        return live

    masked = {}
    for m in range(blocks_dev):
        block = m * n_aux + aux_pos
        for slot in range(band):
            centre = block - slot
            safe = jnp.maximum(centre, 0)
            region = safe // blocks_dev
            number = lax.rem(safe, blocks_dev)
            pair_block = (region * n_pair + pair_col) * blocks_dev + number
            start = pl.multiple_of(lax.rem(pair_block, virt_blocks) * pair_rows, pair_rows)
            gap = table[:, pl.ds(start, pair_rows)] - occ[pair_block // virt_blocks]
            alive = (centre >= 0) & (number < of_region(region)) & (records[0][m * band + slot] > 0)
            for w in range(freq_count):
                omega = freq[w]
                root = jnp.sqrt(2.0 * gap / (gap * gap + omega * omega))
                roots[m, pl.ds(root_row(band, freq_count, None, slot, w), 1), :] = root
                masked[m, slot, w] = root * alive.astype(jnp.float32)
                for delta in range(1, band - slot):
                    there = m + ((aux_pos + delta) >= n_aux).astype(jnp.int32)
                    row = jnp.minimum(there, blocks_dev - 1) * band + slot + delta
                    both = alive & (there < blocks_dev) & (records[(n_aux - delta) % n_aux][row] > 0)
                    spot = root_row(band, freq_count, delta, slot, w)
                    roots[m, pl.ds(spot, 1), :] = root * both.astype(jnp.float32)
    for load in loads:
        load.wait()
    for store in stores:
        store.start()
    for m in range(blocks_dev):
        for w in range(freq_count):
            total = None
            for slot in range(band):
                a = (held[m, slot].astype(jnp.float32) * masked[m, slot, w]).astype(jnp.bfloat16)
                term = dot(a, a)
                total = term if total is None else total + term
            out[w, m] = total
    for store in stores:
        store.wait()


def first_rows(dims, records, occ, freq, table, tiles, after):
    n_aux, n_pair, blocks_dev, band, freq_count = dims
    aux_rows, pair_rows = tiles.shape[-2:]
    return pl.pallas_call(
        functools.partial(first_kernel, dims),
        out_shape=[
            jax.ShapeDtypeStruct((freq_count, blocks_dev, aux_rows, aux_rows), jnp.float32),
            jax.ShapeDtypeStruct((blocks_dev, root_rows(band, freq_count), pair_rows), jnp.float32),
            jax.ShapeDtypeStruct((blocks_dev, aux_rows, pair_rows), tiles.dtype),
        ],
        in_specs=[SMEM] * (n_aux + 2) + [VMEM, HBM] + [ANY] * len(after),
        out_specs=[VMEM, VMEM, HBM],
        scratch_shapes=[pltpu.VMEM(tiles.shape, tiles.dtype), DMA((blocks_dev,)), DMA((blocks_dev,))],
        compiler_params=PARAMS,
        cost_estimate=COST,
    )(*records, occ, freq, table, tiles, *after)


def pieces_of(arrays, first, count):
    parts, start = [], 0
    for n, array in enumerate(arrays):
        low, high = max(first, start), min(first + count, start + array.shape[0])
        if low < high:
            parts.append((n, low - start, low - first, high - low))
        start += array.shape[0]
    return parts


def band_kernel(dims, first, delta, groups, roots, own, *refs):
    n_aux, n_pair, blocks_dev, band, freq_count = dims
    out, held, held_far, sem, sem_far = refs[-5:]
    count, slots = out.shape[1], band - delta
    even = lax.rem(lax.axis_index("aux"), 2) == 0

    def far_copies(slot, group):
        return [
            pltpu.make_async_copy(
                refs[n].at[pl.ds(low, length)], held_far.at[slot, pl.ds(to, length)], sem_far.at[slot, k]
            )
            for k, (n, low, to, length) in enumerate(group)
        ]

    near = [
        pltpu.make_async_copy(own.at[first + i, pl.ds(0, slots)], held.at[i], sem.at[i]) for i in range(count)
    ]
    for copy in near + far_copies(0, groups[0]):
        copy.start()
    if slots > 1:

        @pl.when(even)
        def _():
            for copy in far_copies(1, groups[1]):
                copy.start()
            for copy in far_copies(1, groups[1]):
                copy.wait()

        @pl.when(jnp.logical_not(even))
        def _():
            for copy in far_copies(1, groups[2]):
                copy.start()
            for copy in far_copies(1, groups[2]):
                copy.wait()

    for copy in near + far_copies(0, groups[0]):
        copy.wait()
    for i in range(count):
        m = first + i
        sums = [None] * freq_count
        for slot in range(slots):
            left = held[i, slot].astype(jnp.float32)
            right = held_far[slot, i].astype(jnp.float32)
            for w in range(freq_count):
                kept = roots[m, pl.ds(root_row(band, freq_count, delta, slot, w), 1), :]
                root = roots[m, pl.ds(root_row(band, freq_count, None, slot, w), 1), :]
                term = dot((left * kept).astype(jnp.bfloat16), (right * root).astype(jnp.bfloat16))
                sums[w] = term if sums[w] is None else sums[w] + term
        for w in range(freq_count):
            out[w, i] = sums[w]


def band_rows(dims, first, count, delta, roots, tiles, far, after):
    n_aux, n_pair, blocks_dev, band, freq_count = dims
    aux_rows, pair_rows = tiles.shape[-2:]
    slots = band - delta
    groups, arrays = [], []
    for group in far:
        parts = pieces_of(group, first, count)
        groups.append([(len(arrays) + n, low, to, length) for n, low, to, length in parts])
        arrays += group
    return pl.pallas_call(
        functools.partial(band_kernel, dims, first, delta, groups),
        out_shape=jax.ShapeDtypeStruct((freq_count, count, aux_rows, aux_rows), jnp.float32),
        in_specs=[VMEM, HBM] + [HBM] * len(arrays) + [ANY] * len(after),
        out_specs=VMEM,
        scratch_shapes=[
            pltpu.VMEM((count, slots, aux_rows, pair_rows), tiles.dtype),
            pltpu.VMEM((slots, count, aux_rows, pair_rows), tiles.dtype),
            DMA((count,)),
            DMA((slots, max(len(group) for group in groups))),
        ],
        compiler_params=PARAMS,
        cost_estimate=COST,
    )(roots, tiles, *arrays, *after)


def halve(keep, pair_col, step, n_pair, scale):
    freq_count, count, shares, height, width = keep.shape
    keep = keep.reshape(freq_count, count, shares // 2, 2, height, width)
    bit = (pair_col // step) & 1
    part = lax.dynamic_index_in_dim(keep, 1 - bit, 3, keepdims=False)
    mine = lax.dynamic_index_in_dim(keep, bit, 3, keepdims=False)
    sent = (part * scale).astype(jnp.float16)
    got = lax.ppermute(sent, "pair", [(s, s ^ step) for s in range(n_pair)])
    return mine + got.astype(jnp.float32) * (1.0 / scale), got


def totals(rows, pair_col, n_pair, scale):
    freq_count, count, aux_rows, width = rows.shape
    keep = rows.reshape(freq_count, count, n_pair, aux_rows // n_pair, width)
    stages, step = [], 1
    while step < n_pair:
        keep, got = halve(keep, pair_col, step, n_pair, scale)
        stages.append(got[0, 0, 0].astype(jnp.float32))
        step *= 2
    return stages[0], keep[:, :, 0]


def on_device(three_centre, locality, live_blocks, occ_energy, virt_energy, frequencies):
    n_aux = lax.axis_size("aux")
    n_pair = lax.axis_size("pair")
    pair_col = lax.axis_index("pair").astype(jnp.uint32).astype(jnp.int32)
    tiles = three_centre[0, 0, :, :, 0]
    blocks_dev, band, aux_rows, pair_rows = tiles.shape
    freq_count = frequencies.shape[0]
    dims = (n_aux, n_pair, blocks_dev, band, freq_count)
    scale = 128.0 / n_pair
    record = jnp.concatenate([locality[0, 0].reshape(-1), live_blocks[0]])
    records = [record] + [
        lax.ppermute(record, "aux", [(s, (s + k) % n_aux) for s in range(n_aux)]) for k in range(1, n_aux)
    ]
    two = chunks_of(blocks_dev, (4, 4))
    one = chunks_of(blocks_dev, (8,))
    plan = [(2, 2, first) for first, _ in two] + [(1, 1, first) for first, _ in one]
    packed = pack(tiles, plan, [count for _, count in two + one], records[1:])
    down = [[(s, (s - d) % n_aux) for s in range(n_aux)] for d in range(3)]
    c2 = [lax.ppermute(p, "aux", down[2]) for p in packed[: len(two)]]
    b1 = [lax.ppermute(p, "aux", down[1]) for p in packed[len(two) :]]
    table = virt_energy.reshape(1, -1)
    rows0, roots, last = first_rows(dims, records, occ_energy, frequencies, table, tiles, packed[:1])
    z0 = totals(rows0, pair_col, n_pair, scale)
    to_even = [lax.ppermute(last, "aux", [(s, s - 1) for s in range(1, n_aux, 2)])]
    to_odd = [lax.ppermute(c, "aux", [(s, s + 1) for s in range(0, n_aux, 2)]) for c in c2]
    rows2 = band_rows(dims, 0, blocks_dev, 2, roots, tiles, [c2], [z0[0]])
    z2 = totals(rows2, pair_col, n_pair, scale)
    z1, after = [], z2[0]
    for first, count in one:
        rows1 = band_rows(dims, first, count, 1, roots, tiles, [b1, to_even, to_odd], [after])
        z1.append(totals(rows1, pair_col, n_pair, scale))
        after = rows1
    out = jnp.concatenate([z0[1], jnp.concatenate([z[1] for z in z1], axis=1), z2[1]], axis=-1)
    return out[:, :, None]


def solution(mesh):
    return jax.shard_map(
        on_device,
        mesh=mesh,
        in_specs=(
            P(("grp", "aux"), "pair", None, None, None, None, None),
            P(("grp", "aux"), "pair", None, None, None),
            P(("grp", "aux"), "pair"),
            P("grp"),
            P("grp"),
            P("grp"),
        ),
        out_specs=P(None, None, ("grp", "aux"), "pair", None),
        check_vma=False,
    )
```

time: 223 us -> 87.2 us (0.39)
  the two profiles are of different devices: /device:TPU:1 before, /device:TPU:0 now
where the time goes in v4:
time: 87.2 us; the launch traced here: 86.6 us
  waiting for transfers between devices  29.4 us (34%)
  starting transfers between devices  24.1 us (28%)
  Pallas kernels  22 us (25%)
  local copies, waits for them, and re-layouts  5.46 us (6%)
  other arithmetic  4.87 us (6%)
  between operations  0.9 us (1%)
    ppermute x6, waiting for transfers between devices, halve(): got = lax.ppermute(sent, 'pair', [(s, s ^ step) for s in range(n_pair)])  19.6 us
    ppermute x6, starting transfers between devices, halve(): got = lax.ppermute(sent, 'pair', [(s, s ^ step) for s in range(n_pair)])  12.2 us
    pallas_call x2, Pallas kernels, band_rows(): pl.pallas_call(functools.partial(band_kernel, dims, first, delta, groups)...  11.8 us
    ppermute x2, waiting for transfers between devices, on_device(): c2 = [lax.ppermute(p, 'aux', down[2]) for p in packed[:len(two)]]  8.46 us
    pallas_call x1, Pallas kernels, first_rows(): pl.pallas_call(functools.partial(first_kernel, dims), out_shape=[jax.Shap...  7.07 us
    ppermute x3, starting transfers between devices, on_device(): lax.ppermute(record, 'aux', [(s, (s + k) % n_aux) for s in range(n_aux)])  4.41 us
    ppermute x2, starting transfers between devices, on_device(): lax.ppermute(c, 'aux', [(s, s + 1) for s in range(0, n_aux, 2)])  3.63 us
    pallas_call x1, Pallas kernels, pack(): pl.pallas_call(functools.partial(pack_kernel, plan, len(after)), out_shap...  3.12 us
  transfers between devices with their start and end apart: 15, of which 7 were waited for; matrix products, arithmetic and copies ran while one was open for 6% of the time, Pallas kernels for 14%

profile of v4, /device:TPU:0, one launch (start us, length us, event | category | flops | bytes accessed | tf_op | source)
XLA Modules:
  0.0 86.6 jit_solution(7993663901987424706)
XLA Ops:
  0.7 0.8 copy.13
  2.0 2.6 %collective-permute-start.1 = (s32[25]{0:T(128)S(1)}, s32[25]{0:T(128)S(1)}, u32[]{:S(2)}, u32[]{:S(2)}) collective-permute-start(s32[25]{0:T(128)S(1)} %pad_add_fusion.refs_0_), channel_id=1, source_target_pairs={{0,8},{4,12},{8,0},{12,4},{1,9},{5,13},{9,1},{13,5},{2,10},{6,14},... | collective-permute-start | bytes 308 | tf_op jit(solution)/shard_map/ppermute | solution.py:269
  4.6 1.4 %collective-permute-start.2 = (s32[25]{0:T(128)S(1)}, s32[25]{0:T(128)S(1)}, u32[]{:S(2)}, u32[]{:S(2)}) collective-permute-start(s32[25]{0:T(128)S(1)} %pad_add_fusion.refs_0_), channel_id=1, source_target_pairs={{0,12},{4,0},{8,4},{12,8},{1,13},{5,1},{9,5},{13,9},{2,14},{6,2},{... | collective-permute-start | bytes 308 | tf_op jit(solution)/shard_map/ppermute | solution.py:269
  6.1 1.2 %collective-permute-done.2.refs_2_.refs_3_ = s32[25]{0:T(128)S(1)} collective-permute-done((s32[25]{0:T(128)S(1)}, s32[25]{0:T(128)S(1)}, u32[]{:S(2)}, u32[]{:S(2)}) %collective-permute-start.2) | collective-permute-done | bytes 132 | tf_op jit(solution)/shard_map/ppermute | solution.py:269
  7.3 0.6 copy-done.5
  7.9 3.1 %shard_map.64 = (bf16[4,128,640]{2,1,0:T(8,128)(2,1)}, bf16[4,128,640]{2,1,0:T(8,128)(2,1)}, bf16[8,128,640]{2,1,0:T(8,128)(2,1)}) custom-call(bf16[8,3,128,640]{3,2,1,0:T(8,128)(2,1)} %bitcast.53, s32[25]{0:T(128)} %copy-done.3, s32[25]{0:T(128)} %copy-done.4, s32[25]{0:T(128)} %copy-done.5), custom_call_target="tpu_custom_call" | custom-call | flops 1000 | bytes 1000 | tf_op jit(solution)/shard_map/pallas_call | solution.py:52
  11.6 1.5 %collective-permute-start.9 = (bf16[4,128,640]{2,1,0:T(8,128)(2,1)}, bf16[4,128,640]{2,1,0:T(8,128)(2,1)}, u32[]{:S(2)}, u32[]{:S(2)}) collective-permute-start(bf16[4,128,640]{2,1,0:T(8,128)(2,1)} %get-tuple-element.16), channel_id=1, source_target_pairs={{0,8},{4,12},{8,0},{12,4},{1,9},{5,13},{9,1},{13,5},{2,10},{6,14},... | collective-permute-start | bytes 1966088 | tf_op jit(solution)/shard_map/ppermute | solution.py:276
  13.1 7.1 %shard_map.65 = (f32[2,8,128,128]{3,2,1,0:T(8,128)}, f32[8,16,640]{2,1,0:T(8,128)}, bf16[8,128,640]{2,1,0:T(8,128)(2,1)}) custom-call(s32[25]{0:T(128)} %copy-done.6, s32[25]{0:T(128)} %copy-done.3, s32[25]{0:T(128)} %copy-done.4, s32[25]{0:T(128)} %copy-done.5, f32[8]{0:T(128)} %refs_4_.1, f32[2]{0:T(128)} %refs_5_.1, f32[1,10240]{1,0:T(1,128)} %bitcast.61, ...), custom_call_target="tpu_custom_call" | custom-call | flops 1000 | bytes 1000 | tf_op jit(solution)/shard_map/pallas_call | solution.py:134
  20.2 1.3 %constant_dynamic-slice_fusion.4 = (f32[2,8,2,1,32,128]{5,4,3,2,1,0:T(8,128)S(1)}, f32[2,8,2,1,32,128]{5,4,3,2,1,0:T(8,128)S(1)}) fusion(f32[2,8,2,2,32,128]{5,4,3,2,1,0:T(8,128)} %bitcast.60, s32[]{:T(128)S(6)} %select_n.32, s32[]{:T(128)S(6)} %select_n.33), kind=kLoop, calls=%fused_computation.30 | loop fusion | bytes 2097160 | tf_op jit(solution)/shard_map/jit(dynamic_index_in_dim)/dynamic_slice | solution.py:241
  21.6 1.6 %collective-permute-start.3 = (f16[2,8,2,32,128]{4,3,1,0,2:T(8,128)(2,1)S(1)}, f16[2,8,2,32,128]{4,3,1,0,2:T(8,128)(2,1)S(1)}, u32[]{:S(2)}, u32[]{:S(2)}) collective-permute-start(f16[2,8,2,32,128]{4,3,1,0,2:T(8,128)(2,1)S(1)} %fusion.3), channel_id=1, source_target_pairs={{0,1},{1,0},{2,3},{3,2},{4,5},{5,4},{6,7},{7,6},{8,9},{9,8},{10,11... | collective-permute-start | bytes 786440 | tf_op jit(solution)/shard_map/ppermute | solution.py:243
  23.7 1.3 %collective-permute-start.6 = (bf16[8,128,640]{2,1,0:T(8,128)(2,1)}, bf16[8,128,640]{2,1,0:T(8,128)(2,1)}, u32[]{:S(2)}, u32[]{:S(2)}) collective-permute-start(bf16[8,128,640]{2,1,0:T(8,128)(2,1)} %get-tuple-element.15), channel_id=1, source_target_pairs={{4,0},{12,8},{5,1},{13,9},{6,2},{14,10},{7,3},{15,11},{20,16},{28,... | collective-permute-start | bytes 3932168 | tf_op jit(solution)/shard_map/ppermute | solution.py:281
  25.0 4.7 %collective-permute-done.3 = f16[2,8,2,32,128]{4,3,1,0,2:T(8,128)(2,1)S(1)} collective-permute-done((f16[2,8,2,32,128]{4,3,1,0,2:T(8,128)(2,1)S(1)}, f16[2,8,2,32,128]{4,3,1,0,2:T(8,128)(2,1)S(1)}, u32[]{:S(2)}, u32[]{:S(2)}) %collective-permute-start.3) | collective-permute-done | bytes 262176 | tf_op jit(solution)/shard_map/ppermute | solution.py:243
  29.8 2.8 %collective-permute-start.4 = (f16[2,8,1,32,128]{4,3,1,0,2:T(8,128)(2,1)S(1)}, f16[2,8,1,32,128]{4,3,1,0,2:T(8,128)(2,1)}, u32[]{:S(2)}, u32[]{:S(2)}) collective-permute-start(f16[2,8,1,32,128]{4,3,1,0,2:T(8,128)(2,1)S(1)} %multiply_convert_fusion.1), channel_id=1, source_target_pairs={{0,2},{1,3},{2,0},{3,1},{4,6},{5,7},{6,4},{7,5},{8,10},{9,11},{10,... | collective-permute-start | bytes 393224 | tf_op jit(solution)/shard_map/ppermute | solution.py:243
  32.6 1.3 %collective-permute-start.8 = (bf16[4,128,640]{2,1,0:T(8,128)(2,1)}, bf16[4,128,640]{2,1,0:T(8,128)(2,1)S(1)}, u32[]{:S(2)}, u32[]{:S(2)}) collective-permute-start(bf16[4,128,640]{2,1,0:T(8,128)(2,1)} %collective-permute-done.7.refs_0_), channel_id=1, source_target_pairs={{0,4},{8,12},{1,5},{9,13},{2,6},{10,14},{3,7},{11,15},{16,20},{24,... | collective-permute-start | bytes 1966088 | tf_op jit(solution)/shard_map/ppermute | solution.py:282
  34.0 8.5 %collective-permute-done.9.refs_1_ = bf16[4,128,640]{2,1,0:T(8,128)(2,1)} collective-permute-done((bf16[4,128,640]{2,1,0:T(8,128)(2,1)}, bf16[4,128,640]{2,1,0:T(8,128)(2,1)}, u32[]{:S(2)}, u32[]{:S(2)}) %collective-permute-start.9) | collective-permute-done | bytes 655392 | tf_op jit(solution)/shard_map/ppermute | solution.py:276
  42.4 2.3 %collective-permute-start.10 = (bf16[4,128,640]{2,1,0:T(8,128)(2,1)}, bf16[4,128,640]{2,1,0:T(8,128)(2,1)}, u32[]{:S(2)}, u32[]{:S(2)}) collective-permute-start(bf16[4,128,640]{2,1,0:T(8,128)(2,1)} %collective-permute-done.9.refs_1_), channel_id=1, source_target_pairs={{0,4},{8,12},{1,5},{9,13},{2,6},{10,14},{3,7},{11,15},{16,20},{24,... | collective-permute-start | bytes 1966088 | tf_op jit(solution)/shard_map/ppermute | solution.py:282
  44.7 0.6 fusion.10.refs_2_
  45.3 5.0 %shard_map.66 = f32[2,8,128,128]{3,2,1,0:T(8,128)} custom-call(f32[8,16,640]{2,1,0:T(8,128)} %get-tuple-element.13.roots, bf16[8,3,128,640]{3,2,1,0:T(8,128)(2,1)} %bitcast.55, bf16[4,128,640]{2,1,0:T(8,128)(2,1)} %collective-permute-done.7.refs_0_, bf16[4,128,640]{2,1,0:T(8,128)(2,1)} %collective-permute-done.9.refs_1_, f32[32,128]{1,0:T(8,128)} %fusion.10.refs_2_), custom_call_target="tpu_custom_call" | custom-call | flops 1000 | bytes 1000 | tf_op jit(solution)/shard_map/pallas_call | solution.py:220
  50.3 1.1 %fusion.4 = f16[2,8,2,32,128]{4,3,1,0,2:T(8,128)(2,1)S(1)} fusion(f32[2,8,2,2,32,128]{5,4,3,2,1,0:T(8,128)} %bitcast.57, s32[]{:T(128)S(6)} %select_n.33), kind=kLoop, calls=%fused_computation.11 | loop fusion | flops 262144 | bytes 786436 | tf_op jit(solution)/shard_map/convert_element_type | solution.py:242
  51.5 2.1 %collective-permute-start.11 = (f16[2,8,2,32,128]{4,3,2,1,0:T(8,128)(2,1)S(1)}, f16[2,8,2,32,128]{4,3,2,1,0:T(8,128)(2,1)S(1)}, u32[]{:S(2)}, u32[]{:S(2)}) collective-permute-start(f16[2,8,2,32,128]{4,3,2,1,0:T(8,128)(2,1)S(1)} %copy.17), channel_id=1, source_target_pairs={{0,1},{1,0},{2,3},{3,2},{4,5},{5,4},{6,7},{7,6},{8,9},{9,8},{10,11... | collective-permute-start | bytes 786440 | tf_op jit(solution)/shard_map/ppermute | solution.py:243
  53.6 0.9 %add_bitcast_fusion.1 = f32[2,8,32,128]{3,2,1,0:T(8,128)S(1)} fusion(f16[2,8,1,32,128]{4,3,1,0,2:T(8,128)(2,1)} %collective-permute-done.4, f32[2,8,2,32,128]{4,3,1,0,2:T(8,128)S(1)} %bitcast_add_fusion.2, s32[]{:T(128)S(6)} %select_n.35), kind=kLoop, calls=%fused_computation.20 | loop fusion | flops 196608 | bytes 655364 | tf_op jit(solution)/shard_map/squeeze | solution.py:255
  54.6 4.0 %collective-permute-done.11 = f16[2,8,2,32,128]{4,3,2,1,0:T(8,128)(2,1)S(1)} collective-permute-done((f16[2,8,2,32,128]{4,3,2,1,0:T(8,128)(2,1)S(1)}, f16[2,8,2,32,128]{4,3,2,1,0:T(8,128)(2,1)S(1)}, u32[]{:S(2)}, u32[]{:S(2)}) %collective-permute-start.11) | collective-permute-done | bytes 262176 | tf_op jit(solution)/shard_map/ppermute | solution.py:243
  58.6 0.6 fusion.9.refs_4_
  59.3 0.8 copy-done.2
  60.5 6.8 %shard_map.67 = f32[2,8,128,128]{3,2,1,0:T(8,128)} custom-call(f32[8,16,640]{2,1,0:T(8,128)} %get-tuple-element.13.roots, bf16[8,3,128,640]{3,2,1,0:T(8,128)(2,1)} %bitcast.56, bf16[8,128,640]{2,1,0:T(8,128)(2,1)} %copy-done.1, bf16[8,128,640]{2,1,0:T(8,128)(2,1)} %collective-permute-done.6.refs_1_, bf16[4,128,640]{2,1,0:T(8,128)(2,1)} %copy-done.2, ...), custom_call_target="tpu_custom_call" | custom-call | flops 1000 | bytes 1000 | tf_op jit(solution)/shard_map/pallas_call | solution.py:220
  67.3 1.4 %constant_dynamic-slice_fusion = (f32[2,8,2,1,32,128]{5,4,3,2,1,0:T(8,128)S(1)}, f32[2,8,2,1,32,128]{5,4,3,2,1,0:T(8,128)S(1)}) fusion(f32[2,8,2,2,32,128]{5,4,3,2,1,0:T(8,128)} %bitcast.59, s32[]{:T(128)S(6)} %select_n.33, s32[]{:T(128)S(6)} %select_n.32), kind=kLoop, calls=%fused_computation.26 | loop fusion | bytes 2097160 | tf_op jit(solution)/shard_map/jit(dynamic_index_in_dim)/dynamic_slice | solution.py:240
  68.8 1.8 %collective-permute-start.12 = (f16[2,8,2,32,128]{4,3,1,0,2:T(8,128)(2,1)S(1)}, f16[2,8,2,32,128]{4,3,1,0,2:T(8,128)(2,1)S(1)}, u32[]{:S(2)}, u32[]{:S(2)}) collective-permute-start(f16[2,8,2,32,128]{4,3,1,0,2:T(8,128)(2,1)S(1)} %fusion.5), channel_id=1, source_target_pairs={{0,1},{1,0},{2,3},{3,2},{4,5},{5,4},{6,7},{7,6},{8,9},{9,8},{10,11... | collective-permute-start | bytes 786440 | tf_op jit(solution)/shard_map/ppermute | solution.py:243
  70.8 2.7 %collective-permute-start.14 = (f16[2,8,1,32,128]{4,3,2,1,0:T(8,128)(2,1)S(1)}, f16[2,8,1,32,128]{4,3,2,1,0:T(8,128)(2,1)S(1)}, u32[]{:S(2)}, u32[]{:S(2)}) collective-permute-start(f16[2,8,1,32,128]{4,3,2,1,0:T(8,128)(2,1)S(1)} %fusion.8), channel_id=1, source_target_pairs={{0,2},{1,3},{2,0},{3,1},{4,6},{5,7},{6,4},{7,5},{8,10},{9,11},{10,... | collective-permute-start | bytes 393224 | tf_op jit(solution)/shard_map/ppermute | solution.py:243
  73.4 4.8 %collective-permute-done.12 = f16[2,8,2,32,128]{4,3,1,0,2:T(8,128)(2,1)S(1)} collective-permute-done((f16[2,8,2,32,128]{4,3,1,0,2:T(8,128)(2,1)S(1)}, f16[2,8,2,32,128]{4,3,1,0,2:T(8,128)(2,1)S(1)}, u32[]{:S(2)}, u32[]{:S(2)}) %collective-permute-start.12) | collective-permute-done | bytes 262176 | tf_op jit(solution)/shard_map/ppermute | solution.py:243
  78.3 1.2 %collective-permute-start.13 = (f16[2,8,1,32,128]{4,3,1,0,2:T(8,128)(2,1)S(1)}, f16[2,8,1,32,128]{4,3,1,0,2:T(8,128)(2,1)S(1)}, u32[]{:S(2)}, u32[]{:S(2)}) collective-permute-start(f16[2,8,1,32,128]{4,3,1,0,2:T(8,128)(2,1)S(1)} %multiply_convert_fusion), channel_id=1, source_target_pairs={{0,2},{1,3},{2,0},{3,1},{4,6},{5,7},{6,4},{7,5},{8,10},{9,11},{10,... | collective-permute-start | bytes 393224 | tf_op jit(solution)/shard_map/ppermute | solution.py:243
  79.6 6.1 %collective-permute-done.13 = f16[2,8,1,32,128]{4,3,1,0,2:T(8,128)(2,1)S(1)} collective-permute-done((f16[2,8,1,32,128]{4,3,1,0,2:T(8,128)(2,1)S(1)}, f16[2,8,1,32,128]{4,3,1,0,2:T(8,128)(2,1)S(1)}, u32[]{:S(2)}, u32[]{:S(2)}) %collective-permute-start.13) | collective-permute-done | bytes 131104 | tf_op jit(solution)/shard_map/ppermute | solution.py:243
  85.7 0.9 %maximum_bitcast_fusion = f32[2,8,1,32,384]{4,3,2,1,0:T(8,128)} fusion(f32[2,8,32,128]{3,2,1,0:T(8,128)S(1)} %fusion.7, f32[2,8,32,128]{3,2,1,0:T(8,128)S(1)} %add_bitcast_fusion, f32[2,8,32,128]{3,2,1,0:T(8,128)S(1)} %add_bitcast_fusion.1), kind=kLoop, calls=%fused_computation | loop fusion | flops 393216 | bytes 1572864 | tf_op jit(solution)/shard_map/broadcast_in_dim | solution.py:291
  (37 shorter events, 2.9 us)
Async XLA Ops:
  1.6 9.4 %copy-start.6 = (s32[25]{0:T(128)}, s32[25]{0:T(128)S(1)}, u32[]{:S(2)}) copy-start(s32[25]{0:T(128)S(1)} %pad_add_fusion.refs_0_) | copy-start | bytes 304
  1.6 4.4 %collective-permute-start = (s32[25]{0:T(128)S(1)}, s32[25]{0:T(128)S(1)}, u32[]{:S(2)}, u32[]{:S(2)}) collective-permute-start(s32[25]{0:T(128)S(1)} %pad_add_fusion.refs_0_), channel_id=1, source_target_pairs={{0,4},{4,8},{8,12},{12,0},{1,5},{5,9},{9,13},{13,1},{2,6},{6,10},{... | collective-permute-start | bytes 308 | tf_op jit(solution)/shard_map/ppermute | solution.py:269
  2.0 4.1 %collective-permute-start.1 = (s32[25]{0:T(128)S(1)}, s32[25]{0:T(128)S(1)}, u32[]{:S(2)}, u32[]{:S(2)}) collective-permute-start(s32[25]{0:T(128)S(1)} %pad_add_fusion.refs_0_), channel_id=1, source_target_pairs={{0,8},{4,12},{8,0},{12,4},{1,9},{5,13},{9,1},{13,5},{2,10},{6,14},... | collective-permute-start | bytes 308 | tf_op jit(solution)/shard_map/ppermute | solution.py:269
  4.6 2.7 %collective-permute-start.2 = (s32[25]{0:T(128)S(1)}, s32[25]{0:T(128)S(1)}, u32[]{:S(2)}, u32[]{:S(2)}) collective-permute-start(s32[25]{0:T(128)S(1)} %pad_add_fusion.refs_0_), channel_id=1, source_target_pairs={{0,12},{4,0},{8,4},{12,8},{1,13},{5,1},{9,5},{13,9},{2,14},{6,2},{... | collective-permute-start | bytes 308 | tf_op jit(solution)/shard_map/ppermute | solution.py:269
  6.0 1.3 %copy-start.3 = (s32[25]{0:T(128)}, s32[25]{0:T(128)S(1)}, u32[]{:S(2)}) copy-start(s32[25]{0:T(128)S(1)} %collective-permute-done.refs_0_.refs_1_) | copy-start | bytes 304
  6.1 1.2 %copy-start.4 = (s32[25]{0:T(128)}, s32[25]{0:T(128)S(1)}, u32[]{:S(2)}) copy-start(s32[25]{0:T(128)S(1)} %collective-permute-done.1.refs_1_.refs_2_) | copy-start | bytes 304
  7.3 0.6 copy-start.5
  11.0 21.6 %collective-permute-start.7 = (bf16[4,128,640]{2,1,0:T(8,128)(2,1)}, bf16[4,128,640]{2,1,0:T(8,128)(2,1)}, u32[]{:S(2)}, u32[]{:S(2)}) collective-permute-start(bf16[4,128,640]{2,1,0:T(8,128)(2,1)} %get-tuple-element.11.refs_8_), channel_id=1, source_target_pairs={{0,8},{4,12},{8,0},{12,4},{1,9},{5,13},{9,1},{13,5},{2,10},{6,14},... | collective-permute-start | bytes 1966088 | tf_op jit(solution)/shard_map/ppermute | solution.py:276
  11.6 30.9 %collective-permute-start.9 = (bf16[4,128,640]{2,1,0:T(8,128)(2,1)}, bf16[4,128,640]{2,1,0:T(8,128)(2,1)}, u32[]{:S(2)}, u32[]{:S(2)}) collective-permute-start(bf16[4,128,640]{2,1,0:T(8,128)(2,1)} %get-tuple-element.16), channel_id=1, source_target_pairs={{0,8},{4,12},{8,0},{12,4},{1,9},{5,13},{9,1},{13,5},{2,10},{6,14},... | collective-permute-start | bytes 1966088 | tf_op jit(solution)/shard_map/ppermute | solution.py:276
  21.6 8.1 %collective-permute-start.3 = (f16[2,8,2,32,128]{4,3,1,0,2:T(8,128)(2,1)S(1)}, f16[2,8,2,32,128]{4,3,1,0,2:T(8,128)(2,1)S(1)}, u32[]{:S(2)}, u32[]{:S(2)}) collective-permute-start(f16[2,8,2,32,128]{4,3,1,0,2:T(8,128)(2,1)S(1)} %fusion.3), channel_id=1, source_target_pairs={{0,1},{1,0},{2,3},{3,2},{4,5},{5,4},{6,7},{7,6},{8,9},{9,8},{10,11... | collective-permute-start | bytes 786440 | tf_op jit(solution)/shard_map/ppermute | solution.py:243
  23.2 36.1 %collective-permute-start.5 = (bf16[8,128,640]{2,1,0:T(8,128)(2,1)}, bf16[8,128,640]{2,1,0:T(8,128)(2,1)S(1)}, u32[]{:S(2)}, u32[]{:S(2)}) collective-permute-start(bf16[8,128,640]{2,1,0:T(8,128)(2,1)} %get-tuple-element.14), channel_id=1, source_target_pairs={{0,12},{4,0},{8,4},{12,8},{1,13},{5,1},{9,5},{13,9},{2,14},{6,2},{... | collective-permute-start | bytes 3932168 | tf_op jit(solution)/shard_map/ppermute | solution.py:277
  23.7 35.6 %collective-permute-start.6 = (bf16[8,128,640]{2,1,0:T(8,128)(2,1)}, bf16[8,128,640]{2,1,0:T(8,128)(2,1)}, u32[]{:S(2)}, u32[]{:S(2)}) collective-permute-start(bf16[8,128,640]{2,1,0:T(8,128)(2,1)} %get-tuple-element.15), channel_id=1, source_target_pairs={{4,0},{12,8},{5,1},{13,9},{6,2},{14,10},{7,3},{15,11},{20,16},{28,... | collective-permute-start | bytes 3932168 | tf_op jit(solution)/shard_map/ppermute | solution.py:281
  29.8 21.7 %collective-permute-start.4 = (f16[2,8,1,32,128]{4,3,1,0,2:T(8,128)(2,1)S(1)}, f16[2,8,1,32,128]{4,3,1,0,2:T(8,128)(2,1)}, u32[]{:S(2)}, u32[]{:S(2)}) collective-permute-start(f16[2,8,1,32,128]{4,3,1,0,2:T(8,128)(2,1)S(1)} %multiply_convert_fusion.1), channel_id=1, source_target_pairs={{0,2},{1,3},{2,0},{3,1},{4,6},{5,7},{6,4},{7,5},{8,10},{9,11},{10,... | collective-permute-start | bytes 393224 | tf_op jit(solution)/shard_map/ppermute | solution.py:243
  32.6 26.6 %collective-permute-start.8 = (bf16[4,128,640]{2,1,0:T(8,128)(2,1)}, bf16[4,128,640]{2,1,0:T(8,128)(2,1)S(1)}, u32[]{:S(2)}, u32[]{:S(2)}) collective-permute-start(bf16[4,128,640]{2,1,0:T(8,128)(2,1)} %collective-permute-done.7.refs_0_), channel_id=1, source_target_pairs={{0,4},{8,12},{1,5},{9,13},{2,6},{10,14},{3,7},{11,15},{16,20},{24,... | collective-permute-start | bytes 1966088 | tf_op jit(solution)/shard_map/ppermute | solution.py:282
  42.4 16.8 %collective-permute-start.10 = (bf16[4,128,640]{2,1,0:T(8,128)(2,1)}, bf16[4,128,640]{2,1,0:T(8,128)(2,1)}, u32[]{:S(2)}, u32[]{:S(2)}) collective-permute-start(bf16[4,128,640]{2,1,0:T(8,128)(2,1)} %collective-permute-done.9.refs_1_), channel_id=1, source_target_pairs={{0,4},{8,12},{1,5},{9,13},{2,6},{10,14},{3,7},{11,15},{16,20},{24,... | collective-permute-start | bytes 1966088 | tf_op jit(solution)/shard_map/ppermute | solution.py:282
  51.5 7.1 %collective-permute-start.11 = (f16[2,8,2,32,128]{4,3,2,1,0:T(8,128)(2,1)S(1)}, f16[2,8,2,32,128]{4,3,2,1,0:T(8,128)(2,1)S(1)}, u32[]{:S(2)}, u32[]{:S(2)}) collective-permute-start(f16[2,8,2,32,128]{4,3,2,1,0:T(8,128)(2,1)S(1)} %copy.17), channel_id=1, source_target_pairs={{0,1},{1,0},{2,3},{3,2},{4,5},{5,4},{6,7},{7,6},{8,9},{9,8},{10,11... | collective-permute-start | bytes 786440 | tf_op jit(solution)/shard_map/ppermute | solution.py:243
  59.2 0.8 copy-start.2
  59.3 1.3 %copy-start.1 = (bf16[8,128,640]{2,1,0:T(8,128)(2,1)}, bf16[8,128,640]{2,1,0:T(8,128)(2,1)S(1)}, u32[]{:S(2)}) copy-start(bf16[8,128,640]{2,1,0:T(8,128)(2,1)S(1)} %collective-permute-done.5.refs_0_) | copy-start | bytes 3932164
  67.3 3.3 %copy-start = (f32[2,8,128,128]{3,2,1,0:T(8,128)S(1)}, f32[2,8,128,128]{3,2,1,0:T(8,128)}, u32[]{:S(2)}) copy-start(f32[2,8,128,128]{3,2,1,0:T(8,128)} %shard_map.66) | copy-start | bytes 3145732
  68.8 9.4 %collective-permute-start.12 = (f16[2,8,2,32,128]{4,3,1,0,2:T(8,128)(2,1)S(1)}, f16[2,8,2,32,128]{4,3,1,0,2:T(8,128)(2,1)S(1)}, u32[]{:S(2)}, u32[]{:S(2)}) collective-permute-start(f16[2,8,2,32,128]{4,3,1,0,2:T(8,128)(2,1)S(1)} %fusion.5), channel_id=1, source_target_pairs={{0,1},{1,0},{2,3},{3,2},{4,5},{5,4},{6,7},{7,6},{8,9},{9,8},{10,11... | collective-permute-start | bytes 786440 | tf_op jit(solution)/shard_map/ppermute | solution.py:243
  70.8 8.7 %collective-permute-start.14 = (f16[2,8,1,32,128]{4,3,2,1,0:T(8,128)(2,1)S(1)}, f16[2,8,1,32,128]{4,3,2,1,0:T(8,128)(2,1)S(1)}, u32[]{:S(2)}, u32[]{:S(2)}) collective-permute-start(f16[2,8,1,32,128]{4,3,2,1,0:T(8,128)(2,1)S(1)} %fusion.8), channel_id=1, source_target_pairs={{0,2},{1,3},{2,0},{3,1},{4,6},{5,7},{6,4},{7,5},{8,10},{9,11},{10,... | collective-permute-start | bytes 393224 | tf_op jit(solution)/shard_map/ppermute | solution.py:243
  78.3 7.3 %collective-permute-start.13 = (f16[2,8,1,32,128]{4,3,1,0,2:T(8,128)(2,1)S(1)}, f16[2,8,1,32,128]{4,3,1,0,2:T(8,128)(2,1)S(1)}, u32[]{:S(2)}, u32[]{:S(2)}) collective-permute-start(f16[2,8,1,32,128]{4,3,1,0,2:T(8,128)(2,1)S(1)} %multiply_convert_fusion), channel_id=1, source_target_pairs={{0,2},{1,3},{2,0},{3,1},{4,6},{5,7},{6,4},{7,5},{8,10},{9,11},{10,... | collective-permute-start | bytes 393224 | tf_op jit(solution)/shard_map/ppermute | solution.py:243

commit v5 on v4

v5 whole, which is shorter than its diff:
```python
import functools

import jax
import jax.numpy as jnp
from jax import lax
from jax.experimental import pallas as pl
from jax.experimental.pallas import tpu as pltpu
from jax.sharding import PartitionSpec as P

LIMIT = 61 << 20
COST = pl.CostEstimate(flops=1000, bytes_accessed=1000, transcendentals=0)
PARAMS = pltpu.CompilerParams(vmem_limit_bytes=LIMIT)
ANY = pl.BlockSpec(memory_space=pl.ANY)
HBM = pl.BlockSpec(memory_space=pltpu.HBM)
SMEM = pl.BlockSpec(memory_space=pltpu.SMEM)
VMEM = pl.BlockSpec(memory_space=pltpu.VMEM)
DMA = pltpu.SemaphoreType.DMA


def chunks_of(count, sizes):
    ends = [count * sum(sizes[: n + 1]) // sum(sizes) for n in range(len(sizes))]
    return [(a, b - a) for a, b in zip([0] + ends[:-1], ends)]


def dot(a, b):
    return lax.dot_general(a, b, (((1,), (1,)), ((), ())), preferred_element_type=jnp.float32)


def pack_kernel(plan, tiles, *refs):
    outs, held, sem_in, sem_out = refs[:-3], refs[-3], refs[-2], refs[-1]
    aux_pos = lax.axis_index("aux")
    blocks_dev = tiles.shape[0]
    loads, stores = [], []
    for out, parts in zip(outs, plan):
        rows = [(slot, back, first + i) for slot, back, first, count in parts for i in range(count)]
        for at, (slot, back, m) in enumerate(rows):
            n = len(loads)
            row = jnp.minimum(m + (aux_pos < back).astype(jnp.int32), blocks_dev - 1)
            loads.append(pltpu.make_async_copy(tiles.at[row, slot], held.at[n], sem_in.at[n]))
            stores.append(pltpu.make_async_copy(held.at[n], out.at[at], sem_out.at[n]))
    for load in loads:
        load.start()
    for load, store in zip(loads, stores):
        load.wait()
        store.start()
    for store in stores:
        store.wait()


def pack(tiles, plan):
    counts = [sum(part[3] for part in parts) for parts in plan]
    total = sum(counts)
    return pl.pallas_call(
        functools.partial(pack_kernel, plan),
        out_shape=[jax.ShapeDtypeStruct((count,) + tiles.shape[-2:], tiles.dtype) for count in counts],
        in_specs=[HBM],
        out_specs=[HBM] * len(counts),
        scratch_shapes=[pltpu.VMEM((total,) + tiles.shape[-2:], tiles.dtype), DMA((total,)), DMA((total,))],
        compiler_params=PARAMS,
        cost_estimate=COST,
    )(tiles)


def tie(arrays, after):
    return pl.pallas_call(
        lambda *refs: None,
        out_shape=[jax.ShapeDtypeStruct(array.shape, array.dtype) for array in arrays],
        in_specs=[HBM] * len(arrays) + [ANY] * len(after),
        out_specs=[HBM] * len(arrays),
        input_output_aliases={n: n for n in range(len(arrays))},
        compiler_params=PARAMS,
        cost_estimate=COST,
    )(*arrays, *after)


def root_row(band, freq_count, delta, slot, w):
    before = 0 if delta is None else band + sum(band - d for d in range(1, delta))
    return (before + slot) * freq_count + w


def root_rows(band, freq_count):
    rows = freq_count * (band + sum(band - d for d in range(1, band)))
    return -(-rows // 8) * 8


def first_kernel(dims, *refs):
    n_aux, n_pair, blocks_dev, band, freq_count = dims
    records = refs[:n_aux]
    occ, freq, table, own = refs[n_aux : n_aux + 4]
    out, roots, held, sem = refs[-4:]
    pair_rows = own.shape[-1]
    virt_blocks = table.shape[1] // pair_rows
    aux_pos, pair_col = lax.axis_index("aux"), lax.axis_index("pair")
    loads = [pltpu.make_async_copy(own.at[m], held.at[m], sem.at[m]) for m in range(blocks_dev)]
    for load in loads:
        load.start()

    def of_region(region):
        live = records[0][blocks_dev * band]
        for k in range(1, n_aux):
            live = jnp.where(lax.rem(aux_pos - region + n_aux, n_aux) == k, records[k][blocks_dev * band], live)
        return live

    masked = {}
    for m in range(blocks_dev):
        block = m * n_aux + aux_pos
        for slot in range(band):
            centre = block - slot
            safe = jnp.maximum(centre, 0)
            region = safe // blocks_dev
            number = lax.rem(safe, blocks_dev)
            pair_block = (region * n_pair + pair_col) * blocks_dev + number
            start = pl.multiple_of(lax.rem(pair_block, virt_blocks) * pair_rows, pair_rows)
            gap = table[:, pl.ds(start, pair_rows)] - occ[pair_block // virt_blocks]
            alive = (centre >= 0) & (number < of_region(region)) & (records[0][m * band + slot] > 0)
            for w in range(freq_count):
                omega = freq[w]
                root = jnp.sqrt(2.0 * gap / (gap * gap + omega * omega))
                roots[m, pl.ds(root_row(band, freq_count, None, slot, w), 1), :] = root
                masked[m, slot, w] = root * alive.astype(jnp.float32)
                for delta in range(1, band - slot):
                    there = m + ((aux_pos + delta) >= n_aux).astype(jnp.int32)
                    row = jnp.minimum(there, blocks_dev - 1) * band + slot + delta
                    both = alive & (there < blocks_dev) & (records[(n_aux - delta) % n_aux][row] > 0)
                    spot = root_row(band, freq_count, delta, slot, w)
                    roots[m, pl.ds(spot, 1), :] = root * both.astype(jnp.float32)
    for load in loads:
        load.wait()
    for m in range(blocks_dev):
        for w in range(freq_count):
            total = None
            for slot in range(band):
                a = (held[m, slot].astype(jnp.float32) * masked[m, slot, w]).astype(jnp.bfloat16)
                term = dot(a, a)
                total = term if total is None else total + term
            out[w, m] = total


def first_rows(dims, records, occ, freq, table, tiles, after):
    n_aux, n_pair, blocks_dev, band, freq_count = dims
    aux_rows, pair_rows = tiles.shape[-2:]
    return pl.pallas_call(
        functools.partial(first_kernel, dims),
        out_shape=[
            jax.ShapeDtypeStruct((freq_count, blocks_dev, aux_rows, aux_rows), jnp.float32),
            jax.ShapeDtypeStruct((blocks_dev, root_rows(band, freq_count), pair_rows), jnp.float32),
        ],
        in_specs=[SMEM] * (n_aux + 2) + [VMEM, HBM] + [ANY] * len(after),
        out_specs=[VMEM, VMEM],
        scratch_shapes=[pltpu.VMEM(tiles.shape, tiles.dtype), DMA((blocks_dev,))],
        compiler_params=PARAMS,
        cost_estimate=COST,
    )(*records, occ, freq, table, tiles, *after)


def pieces_of(arrays, first, count):
    parts, start = [], 0
    for n, array in enumerate(arrays):
        low, high = max(first, start), min(first + count, start + array.shape[0])
        if low < high:
            parts.append((n, low - start, low - first, high - low))
        start += array.shape[0]
    return parts


def band_kernel(dims, first, delta, slots, groups, add, roots, own, *refs):
    n_aux, n_pair, blocks_dev, band, freq_count = dims
    out, held, held_far, sem, sem_far = refs[-5:]
    count = out.shape[1]
    low, high = min(slots), max(slots) + 1
    copies = [
        pltpu.make_async_copy(own.at[first + i, pl.ds(low, high - low)], held.at[i], sem.at[i])
        for i in range(count)
    ]
    for s, group in enumerate(groups):
        for k, (n, at, to, length) in enumerate(group):
            copies.append(
                pltpu.make_async_copy(
                    refs[n].at[pl.ds(at, length)], held_far.at[s, pl.ds(to, length)], sem_far.at[s, k]
                )
            )
    for copy in copies:
        copy.start()
    for copy in copies:
        copy.wait()
    for i in range(count):
        m = first + i
        sums = [refs[add][w, i] if add is not None else None for w in range(freq_count)]
        for s, slot in enumerate(slots):
            left = held[i, slot - low].astype(jnp.float32)
            right = held_far[s, i].astype(jnp.float32)
            for w in range(freq_count):
                kept = roots[m, pl.ds(root_row(band, freq_count, delta, slot, w), 1), :]
                root = roots[m, pl.ds(root_row(band, freq_count, None, slot, w), 1), :]
                term = dot((left * kept).astype(jnp.bfloat16), (right * root).astype(jnp.bfloat16))
                sums[w] = term if sums[w] is None else sums[w] + term
        for w in range(freq_count):
            out[w, i] = sums[w]


def band_rows(dims, first, count, delta, slots, roots, tiles, far, after, add=None):
    n_aux, n_pair, blocks_dev, band, freq_count = dims
    aux_rows, pair_rows = tiles.shape[-2:]
    groups, arrays = [], []
    for group, offset in far:
        parts = pieces_of(group, first + offset, count)
        groups.append([(len(arrays) + n, low, to, length) for n, low, to, length in parts])
        arrays += group
    extra = [] if add is None else [add]
    spot = None if add is None else len(arrays)
    return pl.pallas_call(
        functools.partial(band_kernel, dims, first, delta, slots, groups, spot),
        out_shape=jax.ShapeDtypeStruct((freq_count, count, aux_rows, aux_rows), jnp.float32),
        in_specs=[VMEM, HBM] + [HBM] * len(arrays) + [VMEM] * len(extra) + [ANY] * len(after),
        out_specs=VMEM,
        scratch_shapes=[
            pltpu.VMEM((count, max(slots) + 1 - min(slots), aux_rows, pair_rows), tiles.dtype),
            pltpu.VMEM((len(slots), count, aux_rows, pair_rows), tiles.dtype),
            DMA((count,)),
            DMA((len(slots), max(len(group) for group in groups))),
        ],
        compiler_params=PARAMS,
        cost_estimate=COST,
    )(roots, tiles, *arrays, *extra, *after)


def halve(keep, pair_col, step, n_pair, rings, scale):
    freq_count, count, shares, height, width = keep.shape
    keep = keep.reshape(freq_count, count, shares // 2, 2, height, width)
    bit = (pair_col // step) & 1
    part = lax.dynamic_index_in_dim(keep, 1 - bit, 3, keepdims=False)
    mine = lax.dynamic_index_in_dim(keep, bit, 3, keepdims=False)
    sent = (part * scale).astype(jnp.float16)
    pairs = [(ring * n_pair + s, ring * n_pair + (s ^ step)) for ring in rings for s in range(n_pair)]
    got = lax.ppermute(sent, ("aux", "pair"), pairs)
    return mine + got.astype(jnp.float32) * (1.0 / scale), got


def totals(rows, pair_col, n_pair, rings, scale):
    freq_count, count, aux_rows, width = rows.shape
    keep = rows.reshape(freq_count, count, n_pair, aux_rows // n_pair, width)
    stages, step = [], 1
    while step < n_pair:
        keep, got = halve(keep, pair_col, step, n_pair, rings, scale)
        stages.append(got[0, 0, 0].astype(jnp.float32))
        step *= 2
    return stages[0], keep[:, :, 0]


def on_device(three_centre, locality, live_blocks, occ_energy, virt_energy, frequencies):
    n_aux = lax.axis_size("aux")
    n_pair = lax.axis_size("pair")
    pair_col = lax.axis_index("pair").astype(jnp.uint32).astype(jnp.int32)
    tiles = three_centre[0, 0, :, :, 0]
    blocks_dev, band, aux_rows, pair_rows = tiles.shape
    freq_count = frequencies.shape[0]
    dims = (n_aux, n_pair, blocks_dev, band, freq_count)
    scale = 128.0 / n_pair
    record = jnp.concatenate([locality[0, 0].reshape(-1), live_blocks[0]])
    records = [record] + [
        lax.ppermute(record, "aux", [(s, (s + k) % n_aux) for s in range(n_aux)]) for k in range(1, n_aux)
    ]
    two = chunks_of(blocks_dev, (4, 4))
    whole = list(range(n_aux))
    evens, odds = whole[::2], whole[1::2]
    plan = [[(2, 2, first, count)] for first, count in two] + [[(1, 1, 0, blocks_dev)]]
    plan.append([(1, 0, 0, blocks_dev), (2, 0, 0, blocks_dev)])
    *to_two, to_one, lower = tie(pack(tiles, plan), records[1:])
    c2 = [lax.ppermute(p, "aux", [(s, (s - 2) % n_aux) for s in whole]) for p in to_two]
    b1 = lax.ppermute(to_one, "aux", [(s, (s - 1) % n_aux) for s in evens])
    to_even = lax.ppermute(lower, "aux", [(s, s - 1) for s in odds])
    table = virt_energy.reshape(1, -1)
    rows0, roots = first_rows(dims, records, occ_energy, frequencies, table, tiles, to_two[:1])

    def rows_of(delta, slots, far, after, add=None):
        return band_rows(dims, 0, blocks_dev, delta, slots, roots, tiles, far, after, add)

    z0 = totals(rows0, pair_col, n_pair, whole, scale)
    rows_even = rows_of(1, [0, 1], [([to_even], 0), ([to_even], blocks_dev)], [rows0])
    z_even = totals(rows_even, pair_col, n_pair, evens, scale)
    rows2 = rows_of(2, [0], [(c2, 0)], [z0[0], z_even[0]])
    z2 = totals(rows2, pair_col, n_pair, whole, scale)
    to_odd = [lax.ppermute(c, "aux", [(s, s + 1) for s in evens]) for c in tie(c2, [rows2])]
    part = rows_of(1, [1], [(to_odd, 0)], [rows2])
    rows_odd = rows_of(1, [0], [([b1], 0)], [z2[0]], part)
    z_odd = totals(rows_odd, pair_col, n_pair, odds, scale)
    even = lax.axis_index("aux") % 2 == 0
    out = jnp.concatenate([z0[1], jnp.where(even, z_even[1], z_odd[1]), z2[1]], axis=-1)
    return out[:, :, None]


def solution(mesh):
    return jax.shard_map(
        on_device,
        mesh=mesh,
        in_specs=(
            P(("grp", "aux"), "pair", None, None, None, None, None),
            P(("grp", "aux"), "pair", None, None, None),
            P(("grp", "aux"), "pair"),
            P("grp"),
            P("grp"),
            P("grp"),
        ),
        out_specs=P(None, None, ("grp", "aux"), "pair", None),
        check_vma=False,
    )
```

time: 87.2 us -> 95.2 us (1.092)
  the two profiles are of different devices: /device:TPU:0 before, /device:TPU:1 now
where the time goes in v5:
time: 95.2 us; the launch traced here: 94.5 us
  Pallas kernels  34.3 us (36%)
  starting transfers between devices  27.2 us (29%)
  waiting for transfers between devices  20.1 us (21%)
  local copies, waits for them, and re-layouts  6.19 us (7%)
  other arithmetic  5.74 us (6%)
  between operations  1.06 us (1%)
    pallas_call x4, Pallas kernels, band_rows(): pl.pallas_call(functools.partial(band_kernel, dims, first, delta, slots,...  22.2 us
    ppermute x8, waiting for transfers between devices, halve(): got = lax.ppermute(sent, ('aux', 'pair'), pairs)  16.3 us
    ppermute x8, starting transfers between devices, halve(): got = lax.ppermute(sent, ('aux', 'pair'), pairs)  15.2 us
    pallas_call x1, Pallas kernels, first_rows(): pl.pallas_call(functools.partial(first_kernel, dims), out_shape=[jax.Shap...  6.88 us
    pallas_call x1, Pallas kernels, pack(): pl.pallas_call(functools.partial(pack_kernel, plan), out_shape=[jax.Shape...  5.22 us
    ppermute x2, waiting for transfers between devices, on_device(): lax.ppermute(p, 'aux', [(s, (s - 2) % n_aux) for s in whole])  3.71 us
    ppermute x1, starting transfers between devices, on_device(): to_even = lax.ppermute(lower, 'aux', [(s, s - 1) for s in odds])  3.5 us
    ppermute x3, starting transfers between devices, on_device(): lax.ppermute(record, 'aux', [(s, (s + k) % n_aux) for s in range(n_aux)])  3.07 us
  transfers between devices with their start and end apart: 17, of which 7 were waited for; matrix products, arithmetic and copies ran while one was open for 8% of the time, Pallas kernels for 36%

profile of v5, /device:TPU:1, one launch (start us, length us, event | category | flops | bytes accessed | tf_op | source)
XLA Modules:
  0.0 94.5 jit_solution(5573554705764914286)
XLA Ops:
  0.0 0.8 copy.19
  1.6 2.6 %collective-permute-start = (s32[25]{0:T(128)S(1)}, s32[25]{0:T(128)S(1)}, u32[]{:S(2)}, u32[]{:S(2)}) collective-permute-start(s32[25]{0:T(128)S(1)} %pad_add_fusion.refs_0_), channel_id=1, source_target_pairs={{0,4},{4,8},{8,12},{12,0},{1,5},{5,9},{9,13},{13,1},{2,6},{6,10},{... | collective-permute-start | bytes 308 | tf_op jit(solution)/shard_map/ppermute | solution.py:261
  4.6 5.2 %shard_map.64 = (bf16[4,128,640]{2,1,0:T(8,128)(2,1)}, bf16[4,128,640]{2,1,0:T(8,128)(2,1)}, bf16[8,128,640]{2,1,0:T(8,128)(2,1)}, bf16[16,128,640]{2,1,0:T(8,128)(2,1)}) custom-call(bf16[8,3,128,640]{3,2,1,0:T(8,128)(2,1)} %bitcast.63), custom_call_target="tpu_custom_call" | custom-call | flops 1000 | bytes 1000 | tf_op jit(solution)/shard_map/pallas_call | solution.py:53
  10.5 3.5 %collective-permute-start.5 = (bf16[16,128,640]{2,1,0:T(8,128)(2,1)}, bf16[16,128,640]{2,1,0:T(8,128)(2,1)S(1)}, u32[]{:S(2)}, u32[]{:S(2)}) collective-permute-start(bf16[16,128,640]{2,1,0:T(8,128)(2,1)} %get-tuple-element.24), channel_id=1, source_target_pairs={{4,0},{12,8},{5,1},{13,9},{6,2},{14,10},{7,3},{15,11},{20,16},{28,... | collective-permute-start | bytes 7864328 | tf_op jit(solution)/shard_map/ppermute | solution.py:271
  14.1 1.5 %collective-permute-start.10 = (bf16[4,128,640]{2,1,0:T(8,128)(2,1)}, bf16[4,128,640]{2,1,0:T(8,128)(2,1)}, u32[]{:S(2)}, u32[]{:S(2)}) collective-permute-start(bf16[4,128,640]{2,1,0:T(8,128)(2,1)} %get-tuple-element.26), channel_id=1, source_target_pairs={{0,8},{4,12},{8,0},{12,4},{1,9},{5,13},{9,1},{13,5},{2,10},{6,14},... | collective-permute-start | bytes 1966088 | tf_op jit(solution)/shard_map/ppermute | solution.py:269
  15.5 6.9 %shard_map.66 = (f32[2,8,128,128]{3,2,1,0:T(8,128)}, f32[8,16,640]{2,1,0:T(8,128)}) custom-call(s32[25]{0:T(128)} %copy-done.7, s32[25]{0:T(128)} %copy-done.4, s32[25]{0:T(128)} %copy-done.5, s32[25]{0:T(128)} %copy-done.6, f32[8]{0:T(128)} %refs_4_.1, f32[2]{0:T(128)} %refs_5_.1, f32[1,10240]{1,0:T(1,128)} %bitcast.74, bf16[8,3,128,640]{3,2,1,0:T(8,128)(2,1)} %bitcast.64, ...), custom_call_target="tpu_custom_call" | custom-call | flops 1000 | bytes 1000 | tf_op jit(solution)/shard_map/pallas_call | solution.py:142
  22.4 1.5 %copy-done.2 = bf16[16,128,640]{2,1,0:T(8,128)(2,1)} copy-done((bf16[16,128,640]{2,1,0:T(8,128)(2,1)}, bf16[16,128,640]{2,1,0:T(8,128)(2,1)S(1)}, u32[]{:S(2)}) %copy-start.2) | copy-done | bytes 2621464
  24.0 6.8 %shard_map.67 = f32[2,8,128,128]{3,2,1,0:T(8,128)} custom-call(f32[8,16,640]{2,1,0:T(8,128)} %get-tuple-element.23.roots, bf16[8,3,128,640]{3,2,1,0:T(8,128)(2,1)} %bitcast.65, bf16[16,128,640]{2,1,0:T(8,128)(2,1)} %copy-done.2, bf16[16,128,640]{2,1,0:T(8,128)(2,1)} %copy-done.2, f32[2,8,128,128]{3,2,1,0:T(8,128)} %get-tuple-element.22.refs_2_), custom_call_target="tpu_custom_call" | custom-call | flops 1000 | bytes 1000 | tf_op jit(solution)/shard_map/pallas_call | solution.py:211
  30.8 1.8 %constant_dynamic-slice_fusion.4 = (f32[2,8,2,1,32,128]{5,4,3,2,1,0:T(8,128)S(1)}, f32[2,8,2,1,32,128]{5,4,3,2,1,0:T(8,128)S(1)}, f32[2,8,2,1,32,128]{5,4,3,2,1,0:T(8,128)S(1)}, f32[2,8,2,1,32,128]{5,4,3,2,1,0:T(8,128)S(1)}) fusion(f32[2,8,2,2,32,128]{5,4,3,2,1,0:T(8,128)} %bitcast.72, s32[]{:T(128)S(6)} %select_n.55, s32[]{:T(128)S(6)} %select_n.56, ...), kind=kLoop, calls=%fused_computation.37 | loop fusion | bytes 4194312 | tf_op jit(solution)/shard_map/jit(dynamic_index_in_dim)/dynamic_slice | solution.py:232
  32.6 0.7 collective-permute-start.6
  33.4 1.4 %collective-permute-start.3 = (f16[2,8,2,32,128]{4,3,1,0,2:T(8,128)(2,1)S(1)}, f16[2,8,2,32,128]{4,3,1,0,2:T(8,128)(2,1)S(1)}, u32[]{:S(2)}, u32[]{:S(2)}) collective-permute-start(f16[2,8,2,32,128]{4,3,1,0,2:T(8,128)(2,1)S(1)} %fusion.4), channel_id=1, source_target_pairs={{0,1},{1,0},{2,3},{3,2},{4,5},{5,4},{6,7},{7,6},{8,9},{9,8},{10,11... | collective-permute-start | bytes 786440 | tf_op jit(solution)/shard_map/ppermute | solution.py:235
  34.8 1.3 %collective-permute-start.8 = (bf16[8,128,640]{2,1,0:T(8,128)(2,1)}, bf16[8,128,640]{2,1,0:T(8,128)(2,1)}, u32[]{:S(2)}, u32[]{:S(2)}) collective-permute-start(bf16[8,128,640]{2,1,0:T(8,128)(2,1)} %get-tuple-element.25), channel_id=1, source_target_pairs={{0,12},{8,4},{1,13},{9,5},{2,14},{10,6},{3,15},{11,7},{16,28},{24,... | collective-permute-start | bytes 3932168 | tf_op jit(solution)/shard_map/ppermute | solution.py:270
  36.7 3.9 %collective-permute-done.3 = f16[2,8,2,32,128]{4,3,1,0,2:T(8,128)(2,1)S(1)} collective-permute-done((f16[2,8,2,32,128]{4,3,1,0,2:T(8,128)(2,1)S(1)}, f16[2,8,2,32,128]{4,3,1,0,2:T(8,128)(2,1)S(1)}, u32[]{:S(2)}, u32[]{:S(2)}) %collective-permute-start.3) | collective-permute-done | bytes 262176 | tf_op jit(solution)/shard_map/ppermute | solution.py:235
  41.2 3.7 %collective-permute-done.10.refs_1_ = bf16[4,128,640]{2,1,0:T(8,128)(2,1)} collective-permute-done((bf16[4,128,640]{2,1,0:T(8,128)(2,1)}, bf16[4,128,640]{2,1,0:T(8,128)(2,1)}, u32[]{:S(2)}, u32[]{:S(2)}) %collective-permute-start.10) | collective-permute-done | bytes 655392 | tf_op jit(solution)/shard_map/ppermute | solution.py:269
  44.9 5.0 %shard_map.68.refs_2_ = f32[2,8,128,128]{3,2,1,0:T(8,128)} custom-call(f32[8,16,640]{2,1,0:T(8,128)} %get-tuple-element.23.roots, bf16[8,3,128,640]{3,2,1,0:T(8,128)(2,1)} %bitcast.66, bf16[4,128,640]{2,1,0:T(8,128)(2,1)} %collective-permute-done.9.refs_0_, bf16[4,128,640]{2,1,0:T(8,128)(2,1)} %collective-permute-done.10.refs_1_, f32[32,128]{1,0:T(8,128)} %fusion.13.refs_2_, ...), custom_call_target="tpu_custom_call" | custom-call | flops 1000 | bytes 1000 | tf_op jit(solution)/shard_map/pallas_call | solution.py:211
  49.9 1.1 %bitcast_add_fusion.3 = f32[2,8,2,32,128]{4,3,1,0,2:T(8,128)S(1)} fusion(f32[2,8,2,1,32,128]{5,4,3,2,1,0:T(8,128)S(1)} %get-tuple-element.36, f16[2,8,2,32,128]{4,3,1,0,2:T(8,128)(2,1)} %copy-done.3), kind=kLoop, calls=%fused_computation.12 | loop fusion | flops 393216 | bytes 1310720 | tf_op jit(solution)/shard_map/add | solution.py:236
  51.1 2.4 %collective-permute-start.4 = (f16[2,8,1,32,128]{4,3,1,0,2:T(8,128)(2,1)S(1)}, f16[2,8,1,32,128]{4,3,1,0,2:T(8,128)(2,1)}, u32[]{:S(2)}, u32[]{:S(2)}) collective-permute-start(f16[2,8,1,32,128]{4,3,1,0,2:T(8,128)(2,1)S(1)} %multiply_convert_fusion.2), channel_id=1, source_target_pairs={{0,2},{1,3},{2,0},{3,1},{4,6},{5,7},{6,4},{7,5},{8,10},{9,11},{10,... | collective-permute-start | bytes 393224 | tf_op jit(solution)/shard_map/ppermute | solution.py:235
  53.5 1.3 %collective-permute-start.11 = (bf16[4,128,640]{2,1,0:T(8,128)(2,1)}, bf16[4,128,640]{2,1,0:T(8,128)(2,1)}, u32[]{:S(2)}, u32[]{:S(2)}) collective-permute-start(bf16[4,128,640]{2,1,0:T(8,128)(2,1)} %get-tuple-element.27), channel_id=1, source_target_pairs={{0,4},{8,12},{1,5},{9,13},{2,6},{10,14},{3,7},{11,15},{16,20},{24,... | collective-permute-start | bytes 1966088 | tf_op jit(solution)/shard_map/ppermute | solution.py:283
  54.8 1.3 %collective-permute-start.12 = (bf16[4,128,640]{2,1,0:T(8,128)(2,1)}, bf16[4,128,640]{2,1,0:T(8,128)(2,1)}, u32[]{:S(2)}, u32[]{:S(2)}) collective-permute-start(bf16[4,128,640]{2,1,0:T(8,128)(2,1)} %get-tuple-element.28), channel_id=1, source_target_pairs={{0,4},{8,12},{1,5},{9,13},{2,6},{10,14},{3,7},{11,15},{16,20},{24,... | collective-permute-start | bytes 1966088 | tf_op jit(solution)/shard_map/ppermute | solution.py:283
  56.2 1.4 %collective-permute-start.13 = (f16[2,8,2,32,128]{4,3,2,1,0:T(8,128)(2,1)S(1)}, f16[2,8,2,32,128]{4,3,2,1,0:T(8,128)(2,1)S(1)}, u32[]{:S(2)}, u32[]{:S(2)}) collective-permute-start(f16[2,8,2,32,128]{4,3,2,1,0:T(8,128)(2,1)S(1)} %copy.25), channel_id=1, source_target_pairs={{0,1},{1,0},{2,3},{3,2},{4,5},{5,4},{6,7},{7,6},{8,9},{9,8},{10,11... | collective-permute-start | bytes 786440 | tf_op jit(solution)/shard_map/ppermute | solution.py:235
  57.7 1.6 %collective-permute-done.4 = f16[2,8,1,32,128]{4,3,1,0,2:T(8,128)(2,1)} collective-permute-done((f16[2,8,1,32,128]{4,3,1,0,2:T(8,128)(2,1)S(1)}, f16[2,8,1,32,128]{4,3,1,0,2:T(8,128)(2,1)}, u32[]{:S(2)}, u32[]{:S(2)}) %collective-permute-start.4) | collective-permute-done | bytes 131104 | tf_op jit(solution)/shard_map/ppermute | solution.py:235
  60.0 0.9 %add_bitcast_fusion = f32[2,8,32,128]{3,2,1,0:T(8,128)S(1)} fusion(f16[2,8,1,32,128]{4,3,1,0,2:T(8,128)(2,1)} %collective-permute-done.4, f32[2,8,2,32,128]{4,3,1,0,2:T(8,128)S(1)} %bitcast_add_fusion.3, s32[]{:T(128)S(6)} %select_n.58), kind=kLoop, calls=%fused_computation.25 | loop fusion | flops 196608 | bytes 655364 | tf_op jit(solution)/shard_map/squeeze | solution.py:247
  61.0 3.1 %collective-permute-done.13 = f16[2,8,2,32,128]{4,3,2,1,0:T(8,128)(2,1)S(1)} collective-permute-done((f16[2,8,2,32,128]{4,3,2,1,0:T(8,128)(2,1)S(1)}, f16[2,8,2,32,128]{4,3,2,1,0:T(8,128)(2,1)S(1)}, u32[]{:S(2)}, u32[]{:S(2)}) %collective-permute-start.13) | collective-permute-done | bytes 262176 | tf_op jit(solution)/shard_map/ppermute | solution.py:235
  64.6 5.0 %shard_map.70.refs_1_ = f32[2,8,128,128]{3,2,1,0:T(8,128)} custom-call(f32[8,16,640]{2,1,0:T(8,128)} %get-tuple-element.23.roots, bf16[8,3,128,640]{3,2,1,0:T(8,128)(2,1)} %bitcast.67, bf16[4,128,640]{2,1,0:T(8,128)(2,1)} %collective-permute-done.11.refs_0_, bf16[4,128,640]{2,1,0:T(8,128)(2,1)} %collective-permute-done.12.refs_1_, ...), custom_call_target="tpu_custom_call" | custom-call | flops 1000 | bytes 1000 | tf_op jit(solution)/shard_map/pallas_call | solution.py:211
  69.6 5.4 %shard_map.71 = f32[2,8,128,128]{3,2,1,0:T(8,128)} custom-call(f32[8,16,640]{2,1,0:T(8,128)} %get-tuple-element.23.roots, bf16[8,3,128,640]{3,2,1,0:T(8,128)(2,1)} %bitcast.68, bf16[8,128,640]{2,1,0:T(8,128)(2,1)} %collective-permute-done.8.refs_0_, f32[2,8,128,128]{3,2,1,0:T(8,128)} %shard_map.70.refs_1_, f32[32,128]{1,0:T(8,128)} %fusion.11.refs_2_), custom_call_target="tpu_custom_call" | custom-call | flops 1000 | bytes 1000 | tf_op jit(solution)/shard_map/pallas_call | solution.py:211
  75.0 1.4 %constant_dynamic-slice_fusion = (f32[2,8,2,1,32,128]{5,4,3,2,1,0:T(8,128)S(1)}, f32[2,8,2,1,32,128]{5,4,3,2,1,0:T(8,128)S(1)}) fusion(f32[2,8,2,2,32,128]{5,4,3,2,1,0:T(8,128)} %bitcast.73, s32[]{:T(128)S(6)} %select_n.56, s32[]{:T(128)S(6)} %select_n.55), kind=kLoop, calls=%fused_computation.33 | loop fusion | bytes 2097160 | tf_op jit(solution)/shard_map/jit(dynamic_index_in_dim)/dynamic_slice | solution.py:231
  76.5 1.9 %collective-permute-start.14 = (f16[2,8,2,32,128]{4,3,1,0,2:T(8,128)(2,1)S(1)}, f16[2,8,2,32,128]{4,3,1,0,2:T(8,128)(2,1)S(1)}, u32[]{:S(2)}, u32[]{:S(2)}) collective-permute-start(f16[2,8,2,32,128]{4,3,1,0,2:T(8,128)(2,1)S(1)} %fusion.7), channel_id=1, source_target_pairs={{4,5},{5,4},{6,7},{7,6},{12,13},{13,12},{14,15},{15,14},{20,21},{2... | collective-permute-start | bytes 786440 | tf_op jit(solution)/shard_map/ppermute | solution.py:235
  78.6 3.7 %collective-permute-start.16 = (f16[2,8,1,32,128]{4,3,2,1,0:T(8,128)(2,1)S(1)}, f16[2,8,1,32,128]{4,3,2,1,0:T(8,128)(2,1)S(1)}, u32[]{:S(2)}, u32[]{:S(2)}) collective-permute-start(f16[2,8,1,32,128]{4,3,2,1,0:T(8,128)(2,1)S(1)} %fusion.10), channel_id=1, source_target_pairs={{0,2},{1,3},{2,0},{3,1},{4,6},{5,7},{6,4},{7,5},{8,10},{9,11},{10,... | collective-permute-start | bytes 393224 | tf_op jit(solution)/shard_map/ppermute | solution.py:235
  82.3 3.2 %collective-permute-done.14 = f16[2,8,2,32,128]{4,3,1,0,2:T(8,128)(2,1)S(1)} collective-permute-done((f16[2,8,2,32,128]{4,3,1,0,2:T(8,128)(2,1)S(1)}, f16[2,8,2,32,128]{4,3,1,0,2:T(8,128)(2,1)S(1)}, u32[]{:S(2)}, u32[]{:S(2)}) %collective-permute-start.14) | collective-permute-done | bytes 262176 | tf_op jit(solution)/shard_map/ppermute | solution.py:235
  85.7 3.2 %collective-permute-start.15 = (f16[2,8,1,32,128]{4,3,1,0,2:T(8,128)(2,1)S(1)}, f16[2,8,1,32,128]{4,3,1,0,2:T(8,128)(2,1)S(1)}, u32[]{:S(2)}, u32[]{:S(2)}) collective-permute-start(f16[2,8,1,32,128]{4,3,1,0,2:T(8,128)(2,1)S(1)} %multiply_convert_fusion), channel_id=1, source_target_pairs={{4,6},{5,7},{6,4},{7,5},{12,14},{13,15},{14,12},{15,13},{20,22},{2... | collective-permute-start | bytes 393224 | tf_op jit(solution)/shard_map/ppermute | solution.py:235
  89.0 4.5 %collective-permute-done.15 = f16[2,8,1,32,128]{4,3,1,0,2:T(8,128)(2,1)S(1)} collective-permute-done((f16[2,8,1,32,128]{4,3,1,0,2:T(8,128)(2,1)S(1)}, f16[2,8,1,32,128]{4,3,1,0,2:T(8,128)(2,1)S(1)}, u32[]{:S(2)}, u32[]{:S(2)}) %collective-permute-start.15) | collective-permute-done | bytes 131104 | tf_op jit(solution)/shard_map/ppermute | solution.py:235
  93.6 0.9 maximum_bitcast_fusion
  (51 shorter events, 4.7 us)
Async XLA Ops:
  1.6 8.9 %copy-start.7 = (s32[25]{0:T(128)}, s32[25]{0:T(128)S(1)}, u32[]{:S(2)}) copy-start(s32[25]{0:T(128)S(1)} %pad_add_fusion.refs_0_) | copy-start | bytes 304
  1.6 8.3 %collective-permute-start = (s32[25]{0:T(128)S(1)}, s32[25]{0:T(128)S(1)}, u32[]{:S(2)}, u32[]{:S(2)}) collective-permute-start(s32[25]{0:T(128)S(1)} %pad_add_fusion.refs_0_), channel_id=1, source_target_pairs={{0,4},{4,8},{8,12},{12,0},{1,5},{5,9},{9,13},{13,1},{2,6},{6,10},{... | collective-permute-start | bytes 308 | tf_op jit(solution)/shard_map/ppermute | solution.py:261
  4.2 5.7 %collective-permute-start.1 = (s32[25]{0:T(128)S(1)}, s32[25]{0:T(128)S(1)}, u32[]{:S(2)}, u32[]{:S(2)}) collective-permute-start(s32[25]{0:T(128)S(1)} %pad_add_fusion.refs_0_), channel_id=1, source_target_pairs={{0,8},{4,12},{8,0},{12,4},{1,9},{5,13},{9,1},{13,5},{2,10},{6,14},... | collective-permute-start | bytes 308 | tf_op jit(solution)/shard_map/ppermute | solution.py:261
  4.2 5.7 %collective-permute-start.2 = (s32[25]{0:T(128)S(1)}, s32[25]{0:T(128)S(1)}, u32[]{:S(2)}, u32[]{:S(2)}) collective-permute-start(s32[25]{0:T(128)S(1)} %pad_add_fusion.refs_0_), channel_id=1, source_target_pairs={{0,12},{4,0},{8,4},{12,8},{1,13},{5,1},{9,5},{13,9},{2,14},{6,2},{... | collective-permute-start | bytes 308 | tf_op jit(solution)/shard_map/ppermute | solution.py:261
  9.9 0.5 copy-start.4
  9.9 0.6 copy-start.5
  9.9 0.6 copy-start.6
  10.5 11.9 %collective-permute-start.5 = (bf16[16,128,640]{2,1,0:T(8,128)(2,1)}, bf16[16,128,640]{2,1,0:T(8,128)(2,1)S(1)}, u32[]{:S(2)}, u32[]{:S(2)}) collective-permute-start(bf16[16,128,640]{2,1,0:T(8,128)(2,1)} %get-tuple-element.24), channel_id=1, source_target_pairs={{4,0},{12,8},{5,1},{13,9},{6,2},{14,10},{7,3},{15,11},{20,16},{28,... | collective-permute-start | bytes 7864328 | tf_op jit(solution)/shard_map/ppermute | solution.py:271
  14.0 27.2 %collective-permute-start.9 = (bf16[4,128,640]{2,1,0:T(8,128)(2,1)}, bf16[4,128,640]{2,1,0:T(8,128)(2,1)}, u32[]{:S(2)}, u32[]{:S(2)}) collective-permute-start(bf16[4,128,640]{2,1,0:T(8,128)(2,1)} %get-tuple-element.21.refs_8_), channel_id=1, source_target_pairs={{0,8},{4,12},{8,0},{12,4},{1,9},{5,13},{9,1},{13,5},{2,10},{6,14},... | collective-permute-start | bytes 1966088 | tf_op jit(solution)/shard_map/ppermute | solution.py:269
  14.1 30.8 %collective-permute-start.10 = (bf16[4,128,640]{2,1,0:T(8,128)(2,1)}, bf16[4,128,640]{2,1,0:T(8,128)(2,1)}, u32[]{:S(2)}, u32[]{:S(2)}) collective-permute-start(bf16[4,128,640]{2,1,0:T(8,128)(2,1)} %get-tuple-element.26), channel_id=1, source_target_pairs={{0,8},{4,12},{8,0},{12,4},{1,9},{5,13},{9,1},{13,5},{2,10},{6,14},... | collective-permute-start | bytes 1966088 | tf_op jit(solution)/shard_map/ppermute | solution.py:269
  22.4 1.5 %copy-start.2 = (bf16[16,128,640]{2,1,0:T(8,128)(2,1)}, bf16[16,128,640]{2,1,0:T(8,128)(2,1)S(1)}, u32[]{:S(2)}) copy-start(bf16[16,128,640]{2,1,0:T(8,128)(2,1)S(1)} %collective-permute-done.5.refs_0_.refs_1_) | copy-start | bytes 7864324
  32.6 3.4 %collective-permute-start.6 = (f16[2,8,2,32,128]{4,3,1,0,2:T(8,128)(2,1)S(1)}, f16[2,8,2,32,128]{4,3,1,0,2:T(8,128)(2,1)S(1)}, u32[]{:S(2)}, u32[]{:S(2)}) collective-permute-start(f16[2,8,2,32,128]{4,3,1,0,2:T(8,128)(2,1)S(1)} %fusion.5), channel_id=1, source_target_pairs={{0,1},{1,0},{2,3},{3,2},{8,9},{9,8},{10,11},{11,10},{16,17},{17,16... | collective-permute-start | bytes 786440 | tf_op jit(solution)/shard_map/ppermute | solution.py:235
  33.4 7.1 %collective-permute-start.3 = (f16[2,8,2,32,128]{4,3,1,0,2:T(8,128)(2,1)S(1)}, f16[2,8,2,32,128]{4,3,1,0,2:T(8,128)(2,1)S(1)}, u32[]{:S(2)}, u32[]{:S(2)}) collective-permute-start(f16[2,8,2,32,128]{4,3,1,0,2:T(8,128)(2,1)S(1)} %fusion.4), channel_id=1, source_target_pairs={{0,1},{1,0},{2,3},{3,2},{4,5},{5,4},{6,7},{7,6},{8,9},{9,8},{10,11... | collective-permute-start | bytes 786440 | tf_op jit(solution)/shard_map/ppermute | solution.py:235
  34.8 34.9 %collective-permute-start.8 = (bf16[8,128,640]{2,1,0:T(8,128)(2,1)}, bf16[8,128,640]{2,1,0:T(8,128)(2,1)}, u32[]{:S(2)}, u32[]{:S(2)}) collective-permute-start(bf16[8,128,640]{2,1,0:T(8,128)(2,1)} %get-tuple-element.25), channel_id=1, source_target_pairs={{0,12},{8,4},{1,13},{9,5},{2,14},{10,6},{3,15},{11,7},{16,28},{24,... | collective-permute-start | bytes 3932168 | tf_op jit(solution)/shard_map/ppermute | solution.py:270
  40.5 9.4 %copy-start.3 = (f16[2,8,2,32,128]{4,3,1,0,2:T(8,128)(2,1)}, f16[2,8,2,32,128]{4,3,1,0,2:T(8,128)(2,1)S(1)}, u32[]{:S(2)}) copy-start(f16[2,8,2,32,128]{4,3,1,0,2:T(8,128)(2,1)S(1)} %collective-permute-done.3) | copy-start | bytes 786436
  49.9 6.2 %copy-start = (f32[2,8,128,128]{3,2,1,0:T(8,128)S(1)}, f32[2,8,128,128]{3,2,1,0:T(8,128)}, u32[]{:S(2)}) copy-start(f32[2,8,128,128]{3,2,1,0:T(8,128)} %shard_map.68.refs_2_) | copy-start | bytes 3145732
  51.1 8.3 %collective-permute-start.4 = (f16[2,8,1,32,128]{4,3,1,0,2:T(8,128)(2,1)S(1)}, f16[2,8,1,32,128]{4,3,1,0,2:T(8,128)(2,1)}, u32[]{:S(2)}, u32[]{:S(2)}) collective-permute-start(f16[2,8,1,32,128]{4,3,1,0,2:T(8,128)(2,1)S(1)} %multiply_convert_fusion.2), channel_id=1, source_target_pairs={{0,2},{1,3},{2,0},{3,1},{4,6},{5,7},{6,4},{7,5},{8,10},{9,11},{10,... | collective-permute-start | bytes 393224 | tf_op jit(solution)/shard_map/ppermute | solution.py:235
  53.5 11.2 %collective-permute-start.11 = (bf16[4,128,640]{2,1,0:T(8,128)(2,1)}, bf16[4,128,640]{2,1,0:T(8,128)(2,1)}, u32[]{:S(2)}, u32[]{:S(2)}) collective-permute-start(bf16[4,128,640]{2,1,0:T(8,128)(2,1)} %get-tuple-element.27), channel_id=1, source_target_pairs={{0,4},{8,12},{1,5},{9,13},{2,6},{10,14},{3,7},{11,15},{16,20},{24,... | collective-permute-start | bytes 1966088 | tf_op jit(solution)/shard_map/ppermute | solution.py:283
  54.8 9.9 %collective-permute-start.12 = (bf16[4,128,640]{2,1,0:T(8,128)(2,1)}, bf16[4,128,640]{2,1,0:T(8,128)(2,1)}, u32[]{:S(2)}, u32[]{:S(2)}) collective-permute-start(bf16[4,128,640]{2,1,0:T(8,128)(2,1)} %get-tuple-element.28), channel_id=1, source_target_pairs={{0,4},{8,12},{1,5},{9,13},{2,6},{10,14},{3,7},{11,15},{16,20},{24,... | collective-permute-start | bytes 1966088 | tf_op jit(solution)/shard_map/ppermute | solution.py:283
  56.2 7.8 %collective-permute-start.13 = (f16[2,8,2,32,128]{4,3,2,1,0:T(8,128)(2,1)S(1)}, f16[2,8,2,32,128]{4,3,2,1,0:T(8,128)(2,1)S(1)}, u32[]{:S(2)}, u32[]{:S(2)}) collective-permute-start(f16[2,8,2,32,128]{4,3,2,1,0:T(8,128)(2,1)S(1)} %copy.25), channel_id=1, source_target_pairs={{0,1},{1,0},{2,3},{3,2},{4,5},{5,4},{6,7},{7,6},{8,9},{9,8},{10,11... | collective-permute-start | bytes 786440 | tf_op jit(solution)/shard_map/ppermute | solution.py:235
  59.3 29.6 %collective-permute-start.7 = (f16[2,8,1,32,128]{4,3,1,0,2:T(8,128)(2,1)S(1)}, f16[2,8,1,32,128]{4,3,1,0,2:T(8,128)(2,1)S(1)}, u32[]{:S(2)}, u32[]{:S(2)}) collective-permute-start(f16[2,8,1,32,128]{4,3,1,0,2:T(8,128)(2,1)S(1)} %multiply_convert_fusion.1), channel_id=1, source_target_pairs={{0,2},{1,3},{2,0},{3,1},{8,10},{9,11},{10,8},{11,9},{16,18},{17,19... | collective-permute-start | bytes 393224 | tf_op jit(solution)/shard_map/ppermute | solution.py:235
  75.0 3.4 %copy-start.1 = (f32[2,8,128,128]{3,2,1,0:T(8,128)S(1)}, f32[2,8,128,128]{3,2,1,0:T(8,128)}, u32[]{:S(2)}) copy-start(f32[2,8,128,128]{3,2,1,0:T(8,128)} %shard_map.68.refs_2_) | copy-start | bytes 3145732
  76.5 9.0 %collective-permute-start.14 = (f16[2,8,2,32,128]{4,3,1,0,2:T(8,128)(2,1)S(1)}, f16[2,8,2,32,128]{4,3,1,0,2:T(8,128)(2,1)S(1)}, u32[]{:S(2)}, u32[]{:S(2)}) collective-permute-start(f16[2,8,2,32,128]{4,3,1,0,2:T(8,128)(2,1)S(1)} %fusion.7), channel_id=1, source_target_pairs={{4,5},{5,4},{6,7},{7,6},{12,13},{13,12},{14,15},{15,14},{20,21},{2... | collective-permute-start | bytes 786440 | tf_op jit(solution)/shard_map/ppermute | solution.py:235
  78.6 10.3 %collective-permute-start.16 = (f16[2,8,1,32,128]{4,3,2,1,0:T(8,128)(2,1)S(1)}, f16[2,8,1,32,128]{4,3,2,1,0:T(8,128)(2,1)S(1)}, u32[]{:S(2)}, u32[]{:S(2)}) collective-permute-start(f16[2,8,1,32,128]{4,3,2,1,0:T(8,128)(2,1)S(1)} %fusion.10), channel_id=1, source_target_pairs={{0,2},{1,3},{2,0},{3,1},{4,6},{5,7},{6,4},{7,5},{8,10},{9,11},{10,... | collective-permute-start | bytes 393224 | tf_op jit(solution)/shard_map/ppermute | solution.py:235
  85.7 7.8 %collective-permute-start.15 = (f16[2,8,1,32,128]{4,3,1,0,2:T(8,128)(2,1)S(1)}, f16[2,8,1,32,128]{4,3,1,0,2:T(8,128)(2,1)S(1)}, u32[]{:S(2)}, u32[]{:S(2)}) collective-permute-start(f16[2,8,1,32,128]{4,3,1,0,2:T(8,128)(2,1)S(1)} %multiply_convert_fusion), channel_id=1, source_target_pairs={{4,6},{5,7},{6,4},{7,5},{12,14},{13,15},{14,12},{15,13},{20,22},{2... | collective-permute-start | bytes 393224 | tf_op jit(solution)/shard_map/ppermute | solution.py:235

commit v6 on v5

v6 whole, which is shorter than its diff:
```python
import functools

import jax
import jax.numpy as jnp
from jax import lax
from jax.experimental import pallas as pl
from jax.experimental.pallas import tpu as pltpu
from jax.sharding import PartitionSpec as P

LIMIT = 16 << 20
COST = pl.CostEstimate(flops=1000, bytes_accessed=1000, transcendentals=0)
PARAMS = pltpu.CompilerParams(vmem_limit_bytes=LIMIT)
ANY = pl.BlockSpec(memory_space=pl.ANY)
HBM = pl.BlockSpec(memory_space=pltpu.HBM)
SMEM = pl.BlockSpec(memory_space=pltpu.SMEM)
VMEM = pl.BlockSpec(memory_space=pltpu.VMEM)
DMA = pltpu.SemaphoreType.DMA


def chunks_of(count, sizes):
    ends = [count * sum(sizes[: n + 1]) // sum(sizes) for n in range(len(sizes))]
    return [(a, b - a) for a, b in zip([0] + ends[:-1], ends)]


def dot(a, b):
    return lax.dot_general(a, b, (((1,), (1,)), ((), ())), preferred_element_type=jnp.float32)


def pack_kernel(plan, tiles, *refs):
    blocks_dev, band = tiles.shape[:2]
    own, outs, sem_in, sem_out = refs[:band], refs[band:-2], refs[-2], refs[-1]
    aux_pos = lax.axis_index("aux")
    loads = {
        slot: [
            pltpu.make_async_copy(tiles.at[m, slot], own[slot].at[m], sem_in.at[slot, m]) for m in range(blocks_dev)
        ]
        for slot in range(band)
    }
    for slot in reversed(range(band)):
        for load in loads[slot]:
            load.start()
    stores = []
    ready = set()
    for out, (slot, back, first, count) in zip(outs, plan):
        if slot not in ready:
            ready.add(slot)
            for load in loads[slot]:
                load.wait()
        for i in range(count):
            row = jnp.minimum(first + i + (aux_pos < back).astype(jnp.int32), blocks_dev - 1)
            store = pltpu.make_async_copy(own[slot].at[row], out.at[i], sem_out.at[len(stores)])
            store.start()
            stores.append(store)
    for slot in range(band):
        if slot not in ready:
            for load in loads[slot]:
                load.wait()
    for store in stores:
        store.wait()


def pack(tiles, plan):
    counts = [part[3] for part in plan]
    blocks_dev, band, aux_rows, pair_rows = tiles.shape
    return pl.pallas_call(
        functools.partial(pack_kernel, plan),
        out_shape=[
            jax.ShapeDtypeStruct((count, aux_rows, pair_rows), tiles.dtype)
            for count in [blocks_dev] * band + counts
        ],
        in_specs=[ANY],
        out_specs=[VMEM] * band + [ANY] * len(counts),
        scratch_shapes=[DMA((band, blocks_dev)), DMA((sum(counts),))],
        compiler_params=PARAMS,
        cost_estimate=COST,
    )(tiles)


def tie(arrays, after):
    return pl.pallas_call(
        lambda *refs: None,
        out_shape=[jax.ShapeDtypeStruct(array.shape, array.dtype) for array in arrays],
        in_specs=[ANY] * (len(arrays) + len(after)),
        out_specs=[ANY] * len(arrays),
        input_output_aliases={n: n for n in range(len(arrays))},
        compiler_params=PARAMS,
        cost_estimate=COST,
    )(*arrays, *after)


def root_row(band, freq_count, delta, slot, w):
    before = 0 if delta is None else band + sum(band - d for d in range(1, delta))
    return (before + slot) * freq_count + w


def root_rows(band, freq_count):
    rows = freq_count * (band + sum(band - d for d in range(1, band)))
    return -(-rows // 8) * 8


def first_kernel(dims, *refs):
    n_aux, n_pair, blocks_dev, band, freq_count = dims
    records = refs[:n_aux]
    occ, freq, table = refs[n_aux : n_aux + 3]
    own = refs[n_aux + 3 : n_aux + 3 + band]
    out, roots = refs[-2:]
    pair_rows = own[0].shape[-1]
    virt_blocks = table.shape[1] // pair_rows
    aux_pos, pair_col = lax.axis_index("aux"), lax.axis_index("pair")

    def of_region(region):
        live = records[0][blocks_dev * band]
        for k in range(1, n_aux):
            live = jnp.where(lax.rem(aux_pos - region + n_aux, n_aux) == k, records[k][blocks_dev * band], live)
        return live

    masked = {}
    for m in range(blocks_dev):
        block = m * n_aux + aux_pos
        for slot in range(band):
            centre = block - slot
            safe = jnp.maximum(centre, 0)
            region = safe // blocks_dev
            number = lax.rem(safe, blocks_dev)
            pair_block = (region * n_pair + pair_col) * blocks_dev + number
            start = pl.multiple_of(lax.rem(pair_block, virt_blocks) * pair_rows, pair_rows)
            gap = table[:, pl.ds(start, pair_rows)] - occ[pair_block // virt_blocks]
            alive = (centre >= 0) & (number < of_region(region)) & (records[0][m * band + slot] > 0)
            for w in range(freq_count):
                omega = freq[w]
                root = jnp.sqrt(2.0 * gap / (gap * gap + omega * omega))
                roots[m, pl.ds(root_row(band, freq_count, None, slot, w), 1), :] = root
                masked[m, slot, w] = root * alive.astype(jnp.float32)
                for delta in range(1, band - slot):
                    there = m + ((aux_pos + delta) >= n_aux).astype(jnp.int32)
                    row = jnp.minimum(there, blocks_dev - 1) * band + slot + delta
                    both = alive & (there < blocks_dev) & (records[(n_aux - delta) % n_aux][row] > 0)
                    spot = root_row(band, freq_count, delta, slot, w)
                    roots[m, pl.ds(spot, 1), :] = root * both.astype(jnp.float32)
    for m in range(blocks_dev):
        for w in range(freq_count):
            total = None
            for slot in range(band):
                a = (own[slot][m].astype(jnp.float32) * masked[m, slot, w]).astype(jnp.bfloat16)
                term = dot(a, a)
                total = term if total is None else total + term
            out[w, m] = total


def first_rows(dims, records, occ, freq, table, own, after):
    n_aux, n_pair, blocks_dev, band, freq_count = dims
    aux_rows, pair_rows = own[0].shape[-2:]
    return pl.pallas_call(
        functools.partial(first_kernel, dims),
        out_shape=[
            jax.ShapeDtypeStruct((freq_count, blocks_dev, aux_rows, aux_rows), jnp.float32),
            jax.ShapeDtypeStruct((blocks_dev, root_rows(band, freq_count), pair_rows), jnp.float32),
        ],
        in_specs=[SMEM] * (n_aux + 2) + [VMEM] * (1 + band) + [ANY] * len(after),
        out_specs=[VMEM, VMEM],
        compiler_params=PARAMS,
        cost_estimate=COST,
    )(*records, occ, freq, table, *own, *after)


def band_kernel(dims, delta, slots, rights, add, roots, *refs):
    n_aux, n_pair, blocks_dev, band, freq_count = dims
    out = refs[-1]
    for m in range(blocks_dev):
        sums = [refs[add][w, m] if add is not None else None for w in range(freq_count)]
        for s, slot in enumerate(slots):
            n, row = rights[s][m]
            left = refs[s][m].astype(jnp.float32)
            right = refs[n][row].astype(jnp.float32)
            for w in range(freq_count):
                kept = roots[m, pl.ds(root_row(band, freq_count, delta, slot, w), 1), :]
                root = roots[m, pl.ds(root_row(band, freq_count, None, slot, w), 1), :]
                term = dot((left * kept).astype(jnp.bfloat16), (right * root).astype(jnp.bfloat16))
                sums[w] = term if sums[w] is None else sums[w] + term
        for w in range(freq_count):
            out[w, m] = sums[w]


def band_rows(dims, delta, slots, roots, own, far, after, add=None):
    n_aux, n_pair, blocks_dev, band, freq_count = dims
    aux_rows = own[0].shape[-2]
    arrays = [own[slot] for slot in slots]
    rights = []
    for group in far:
        rights.append([(len(arrays) + n, row) for n, array in enumerate(group) for row in range(array.shape[0])])
        arrays += group
    spot = None if add is None else len(arrays)
    arrays += [] if add is None else [add]
    return pl.pallas_call(
        functools.partial(band_kernel, dims, delta, slots, rights, spot),
        out_shape=jax.ShapeDtypeStruct((freq_count, blocks_dev, aux_rows, aux_rows), jnp.float32),
        in_specs=[VMEM] * (1 + len(arrays)) + [ANY] * len(after),
        out_specs=VMEM,
        compiler_params=PARAMS,
        cost_estimate=COST,
    )(roots, *arrays, *after)


def halve(keep, pair_col, step, n_pair, rings, scale):
    freq_count, count, shares, height, width = keep.shape
    keep = keep.reshape(freq_count, count, shares // 2, 2, height, width)
    bit = (pair_col // step) & 1
    part = lax.dynamic_index_in_dim(keep, 1 - bit, 3, keepdims=False)
    mine = lax.dynamic_index_in_dim(keep, bit, 3, keepdims=False)
    sent = (part * scale).astype(jnp.float16)
    pairs = [(ring * n_pair + s, ring * n_pair + (s ^ step)) for ring in rings for s in range(n_pair)]
    got = lax.ppermute(sent, ("aux", "pair"), pairs)
    return mine + got.astype(jnp.float32) * (1.0 / scale), got


def totals(rows, pair_col, n_pair, rings, scale):
    freq_count, count, aux_rows, width = rows.shape
    keep = rows.reshape(freq_count, count, n_pair, aux_rows // n_pair, width)
    stages, step = [], 1
    while step < n_pair:
        keep, got = halve(keep, pair_col, step, n_pair, rings, scale)
        stages.append(got[0, 0, 0].astype(jnp.float32))
        step *= 2
    return stages[0], keep[:, :, 0]


def on_device(three_centre, locality, live_blocks, occ_energy, virt_energy, frequencies):
    n_aux = lax.axis_size("aux")
    n_pair = lax.axis_size("pair")
    pair_col = lax.axis_index("pair").astype(jnp.uint32).astype(jnp.int32)
    tiles = three_centre[0, 0, :, :, 0]
    blocks_dev, band, aux_rows, pair_rows = tiles.shape
    freq_count = frequencies.shape[0]
    dims = (n_aux, n_pair, blocks_dev, band, freq_count)
    scale = 128.0 / n_pair
    record = jnp.concatenate([locality[0, 0].reshape(-1), live_blocks[0]])
    records = [record] + [
        lax.ppermute(record, "aux", [(s, (s + k) % n_aux) for s in range(n_aux)]) for k in range(1, n_aux)
    ]
    two = chunks_of(blocks_dev, (4, 4))
    whole = list(range(n_aux))
    evens, odds = whole[::2], whole[1::2]
    plan = [(2, 2, first, count) for first, count in two]
    plan += [(2, 0, 0, blocks_dev), (1, 1, 0, blocks_dev), (1, 0, 0, blocks_dev)]
    packed = pack(tiles, plan)
    own, packed = packed[:band], packed[band:]
    *to_two, lower2, to_one, lower1 = tie(packed, records[1:])
    c2 = [lax.ppermute(p, "aux", [(s, (s - 2) % n_aux) for s in whole]) for p in to_two]
    b1 = lax.ppermute(to_one, "aux", [(s, (s - 1) % n_aux) for s in evens])
    to_even = [lax.ppermute(p, "aux", [(s, s - 1) for s in odds]) for p in (lower1, lower2)]
    table = virt_energy.reshape(1, -1)
    rows0, roots = first_rows(dims, records, occ_energy, frequencies, table, own, to_two[:1])

    def rows_of(delta, slots, far, after, add=None):
        return band_rows(dims, delta, slots, roots, own, far, after, add)

    z0 = totals(rows0, pair_col, n_pair, whole, scale)
    rows_even = rows_of(1, [0, 1], [[p] for p in to_even], [rows0])
    z_even = totals(rows_even, pair_col, n_pair, evens, scale)
    rows2 = rows_of(2, [0], [c2], [z0[0], z_even[0]])
    z2 = totals(rows2, pair_col, n_pair, whole, scale)
    to_odd = [lax.ppermute(c, "aux", [(s, s + 1) for s in evens]) for c in tie(c2, [rows2])]
    part = rows_of(1, [1], [to_odd], [rows2])
    rows_odd = rows_of(1, [0], [[b1]], [z2[0]], part)
    z_odd = totals(rows_odd, pair_col, n_pair, odds, scale)
    even = lax.axis_index("aux") % 2 == 0
    out = jnp.concatenate([z0[1], jnp.where(even, z_even[1], z_odd[1]), z2[1]], axis=-1)
    return out[:, :, None]


def solution(mesh):
    return jax.shard_map(
        on_device,
        mesh=mesh,
        in_specs=(
            P(("grp", "aux"), "pair", None, None, None, None, None),
            P(("grp", "aux"), "pair", None, None, None),
            P(("grp", "aux"), "pair"),
            P("grp"),
            P("grp"),
            P("grp"),
        ),
        out_specs=P(None, None, ("grp", "aux"), "pair", None),
        check_vma=False,
    )
```

time: 95.2 us -> 96.3 us (1.012)
  Pallas kernels: 34.3 us -> 21.8 us
  waiting for transfers between devices: 20.1 us -> 30 us
  local copies, waits for them, and re-layouts: 6.19 us -> 8.49 us
    pallas_call x4, Pallas kernels: 22.2 us -> 8.94 us  [band_rows(): pl.pallas_call(functools.partial(band_kernel, dims, delta, slots, rights,...]
    ppermute x2, waiting for transfers between devices: 3.71 us -> 8.89 us  [on_device(): lax.ppermute(p, 'aux', [(s, (s - 2) % n_aux) for s in whole])]
    ppermute x8, waiting for transfers between devices: 16.3 us -> 21.1 us  [halve(): got = lax.ppermute(sent, ('aux', 'pair'), pairs)]
    unnamed x17 -> x19, local copies, waits for them, and re-layouts: 2.83 us -> 7.23 us
    pallas_call x1, Pallas kernels: 5.22 us -> 9.18 us  [pack(): pl.pallas_call(functools.partial(pack_kernel, plan), out_shape=[jax.Shape...]
    ppermute x1 -> x2, starting transfers between devices: 3.5 us -> 6.78 us  [on_device(): lax.ppermute(p, 'aux', [(s, s - 1) for s in odds])]
    pallas_call x1, Pallas kernels: 6.88 us -> 3.63 us  [first_rows(): pl.pallas_call(functools.partial(first_kernel, dims), out_shape=[jax.Shap...]
    ppermute x8, starting transfers between devices: 15.2 us -> 12.6 us  [halve(): got = lax.ppermute(sent, ('aux', 'pair'), pairs)]
  transfers between devices with their start and end apart: 17 -> 18, of which waited for: 7 -> 5; matrix products, arithmetic and copies ran while one was open for 8% -> 7% of each run, Pallas kernels for 36% -> 23%
where the time goes in v6:
time: 96.3 us; the launch traced here: 95.7 us
  waiting for transfers between devices  30 us (31%)
  starting transfers between devices  27.8 us (29%)
  Pallas kernels  21.8 us (23%)
  local copies, waits for them, and re-layouts  8.49 us (9%)
  other arithmetic  6.68 us (7%)
  between operations  1.01 us (1%)
    ppermute x8, waiting for transfers between devices, halve(): got = lax.ppermute(sent, ('aux', 'pair'), pairs)  21.1 us
    ppermute x8, starting transfers between devices, halve(): got = lax.ppermute(sent, ('aux', 'pair'), pairs)  12.6 us
    pallas_call x1, Pallas kernels, pack(): pl.pallas_call(functools.partial(pack_kernel, plan), out_shape=[jax.Shape...  9.18 us
    pallas_call x4, Pallas kernels, band_rows(): pl.pallas_call(functools.partial(band_kernel, dims, delta, slots, rights,...  8.94 us
    ppermute x2, waiting for transfers between devices, on_device(): lax.ppermute(p, 'aux', [(s, (s - 2) % n_aux) for s in whole])  8.89 us
    unnamed x19, local copies, waits for them, and re-layouts  7.23 us
    ppermute x2, starting transfers between devices, on_device(): lax.ppermute(p, 'aux', [(s, s - 1) for s in odds])  6.78 us
    pallas_call x1, Pallas kernels, first_rows(): pl.pallas_call(functools.partial(first_kernel, dims), out_shape=[jax.Shap...  3.63 us
  transfers between devices with their start and end apart: 18, of which 5 were waited for; matrix products, arithmetic and copies ran while one was open for 7% of the time, Pallas kernels for 23%

profile of v6, /device:TPU:1, one launch (start us, length us, event | category | flops | bytes accessed | tf_op | source)
XLA Modules:
  0.0 95.7 jit_solution(15794409024609179171)
XLA Ops:
  1.6 2.6 %collective-permute-start = (s32[25]{0:T(128)S(1)}, s32[25]{0:T(128)S(1)}, u32[]{:S(2)}, u32[]{:S(2)}) collective-permute-start(s32[25]{0:T(128)S(1)} %pad_add_fusion.refs_0_), channel_id=1, source_target_pairs={{0,4},{4,8},{8,12},{12,0},{1,5},{5,9},{9,13},{13,1},{2,6},{6,10},{... | collective-permute-start | bytes 308 | tf_op jit(solution)/shard_map/ppermute | solution.py:238
  4.6 2.1 %copy-done = bf16[1,1,8,3,1,128,640]{6,5,4,3,2,1,0:T(8,128)(2,1)S(1)} copy-done((bf16[1,1,8,3,1,128,640]{6,5,4,3,2,1,0:T(8,128)(2,1)S(1)}, bf16[1,1,8,3,1,128,640]{6,5,4,3,2,1,0:T(8,128)(2,1)}, u32[]{:S(2)}) %copy-start) | copy-done | bytes 3932184
  6.7 9.2 %shard_map.64 = (bf16[8,128,640]{2,1,0:T(8,128)(2,1)S(1)}, bf16[8,128,640]{2,1,0:T(8,128)(2,1)S(1)}, bf16[8,128,640]{2,1,0:T(8,128)(2,1)S(1)}, bf16[4,128,640]{2...) custom-call(bf16[8,3,128,640]{3,2,1,0:T(8,128)(2,1)S(1)} %bitcast.68), custom_call_target="tpu_custom_call" | custom-call | flops 1000 | bytes 1000 | tf_op jit(solution)/shard_map/pallas_call | solution.py:65
  15.9 1.1 %copy-done.1 = bf16[8,128,640]{2,1,0:T(8,128)(2,1)} copy-done((bf16[8,128,640]{2,1,0:T(8,128)(2,1)}, bf16[8,128,640]{2,1,0:T(8,128)(2,1)S(1)}, u32[]{:S(2)}) %copy-start.1) | copy-done | bytes 1310744
  17.1 1.1 %copy-done.3 = bf16[8,128,640]{2,1,0:T(8,128)(2,1)} copy-done((bf16[8,128,640]{2,1,0:T(8,128)(2,1)}, bf16[8,128,640]{2,1,0:T(8,128)(2,1)S(1)}, u32[]{:S(2)}) %copy-start.3) | copy-done | bytes 1310744
  19.0 4.4 %collective-permute-start.5 = (bf16[8,128,640]{2,1,0:T(8,128)(2,1)}, bf16[8,128,640]{2,1,0:T(8,128)(2,1)}, u32[]{:S(2)}, u32[]{:S(2)}) collective-permute-start(bf16[8,128,640]{2,1,0:T(8,128)(2,1)} %get-tuple-element.33), channel_id=1, source_target_pairs={{4,0},{12,8},{5,1},{13,9},{6,2},{14,10},{7,3},{15,11},{20,16},{28,... | collective-permute-start | bytes 3932168 | tf_op jit(solution)/shard_map/ppermute | solution.py:250
  23.4 2.4 %collective-permute-start.6 = (bf16[8,128,640]{2,1,0:T(8,128)(2,1)}, bf16[8,128,640]{2,1,0:T(8,128)(2,1)}, u32[]{:S(2)}, u32[]{:S(2)}) collective-permute-start(bf16[8,128,640]{2,1,0:T(8,128)(2,1)} %get-tuple-element.34), channel_id=1, source_target_pairs={{4,0},{12,8},{5,1},{13,9},{6,2},{14,10},{7,3},{15,11},{20,16},{28,... | collective-permute-start | bytes 3932168 | tf_op jit(solution)/shard_map/ppermute | solution.py:250
  25.9 1.4 %collective-permute-start.11 = (bf16[4,128,640]{2,1,0:T(8,128)(2,1)}, bf16[4,128,640]{2,1,0:T(8,128)(2,1)}, u32[]{:S(2)}, u32[]{:S(2)}) collective-permute-start(bf16[4,128,640]{2,1,0:T(8,128)(2,1)} %copy-done.4), channel_id=1, source_target_pairs={{0,8},{4,12},{8,0},{12,4},{1,9},{5,13},{9,1},{13,5},{2,10},{6,14},... | collective-permute-start | bytes 1966088 | tf_op jit(solution)/shard_map/ppermute | solution.py:248
  27.3 1.3 %copy-done.2 = bf16[8,128,640]{2,1,0:T(8,128)(2,1)S(1)} copy-done((bf16[8,128,640]{2,1,0:T(8,128)(2,1)S(1)}, bf16[8,128,640]{2,1,0:T(8,128)(2,1)}, u32[]{:S(2)}) %copy-start.2) | copy-done | bytes 1310744
  28.6 3.6 %shard_map.66 = (f32[2,8,128,128]{3,2,1,0:T(8,128)S(1)}, f32[8,16,640]{2,1,0:T(8,128)S(1)}) custom-call(s32[25]{0:T(128)S(1)} %pad_add_fusion.refs_0_, s32[25]{0:T(128)S(1)} %collective-permute-done.refs_5_.refs_1_, s32[25]{0:T(128)S(1)} %collective-permute-done.1.refs_6_.refs_2_, s32[25]{0:T(128)S(1)} %collective-permute-done.2.refs_7_.refs_3_, ...), custom_call_target="tpu_custom_call" | custom-call | flops 1000 | bytes 1000 | tf_op jit(solution)/shard_map/pallas_call | solution.py:153
  32.3 4.1 %shard_map.67 = f32[2,8,128,128]{3,2,1,0:T(8,128)S(1)} custom-call(f32[8,16,640]{2,1,0:T(8,128)S(1)} %get-tuple-element.32.roots, bf16[8,128,640]{2,1,0:T(8,128)(2,1)S(1)} %get-tuple-element.22.refs_7_.refs_0_, bf16[8,128,640]{2,1,0:T(8,128)(2,1)S(1)} %get-tuple-element.23.refs_8_.refs_1_.refs_0_, bf16[8,128,640]{2,1,0:T(8,128)(2,1)} %collective-permute-done.5.refs_2_, ...), custom_call_target="tpu_custom_call" | custom-call | flops 1000 | bytes 1000 | tf_op jit(solution)/shard_map/pallas_call | solution.py:194
  36.3 1.0 %constant_dynamic-slice_fusion.4 = (f32[2,8,2,1,32,128]{5,4,3,2,1,0:T(8,128)S(1)}, f32[2,8,2,1,32,128]{5,4,3,2,1,0:T(8,128)S(1)}, f32[2,8,2,1,32,128]{5,4,3,2,1,0:T(8,128)S(1)}, f32[2,8,2,1,32,128]{5,4,3,2,1,0:T(8,128)}) fusion(f32[2,8,2,2,32,128]{5,4,3,2,1,0:T(8,128)S(1)} %bitcast.67, s32[]{:T(128)S(6)} %select_n.55, s32[]{:T(128)S(6)} %select_n.56, ...), kind=kLoop, calls=%fused_computation.37 | loop fusion | bytes 4194312 | tf_op jit(solution)/shard_map/jit(dynamic_index_in_dim)/dynamic_slice | solution.py:209
  38.2 1.3 %collective-permute-start.3 = (f16[2,8,2,32,128]{4,3,1,0,2:T(8,128)(2,1)}, f16[2,8,2,32,128]{4,3,1,0,2:T(8,128)(2,1)}, u32[]{:S(2)}, u32[]{:S(2)}) collective-permute-start(f16[2,8,2,32,128]{4,3,1,0,2:T(8,128)(2,1)} %fusion.4), channel_id=1, source_target_pairs={{0,1},{1,0},{2,3},{3,2},{4,5},{5,4},{6,7},{7,6},{8,9},{9,8},{10,11... | collective-permute-start | bytes 786440 | tf_op jit(solution)/shard_map/ppermute | solution.py:212
  40.3 1.4 %collective-permute-start.7 = (f16[2,8,2,32,128]{4,3,1,0,2:T(8,128)(2,1)}, f16[2,8,2,32,128]{4,3,1,0,2:T(8,128)(2,1)}, u32[]{:S(2)}, u32[]{:S(2)}) collective-permute-start(f16[2,8,2,32,128]{4,3,1,0,2:T(8,128)(2,1)} %fusion.5), channel_id=1, source_target_pairs={{0,1},{1,0},{2,3},{3,2},{8,9},{9,8},{10,11},{11,10},{16,17},{17,16... | collective-permute-start | bytes 786440 | tf_op jit(solution)/shard_map/ppermute | solution.py:212
  41.6 1.3 %collective-permute-start.9 = (bf16[8,128,640]{2,1,0:T(8,128)(2,1)}, bf16[8,128,640]{2,1,0:T(8,128)(2,1)S(1)}, u32[]{:S(2)}, u32[]{:S(2)}) collective-permute-start(bf16[8,128,640]{2,1,0:T(8,128)(2,1)} %copy-done.3), channel_id=1, source_target_pairs={{0,12},{8,4},{1,13},{9,5},{2,14},{10,6},{3,15},{11,7},{16,28},{24,... | collective-permute-start | bytes 3932168 | tf_op jit(solution)/shard_map/ppermute | solution.py:249
  42.9 3.5 %collective-permute-done.3 = f16[2,8,2,32,128]{4,3,1,0,2:T(8,128)(2,1)} collective-permute-done((f16[2,8,2,32,128]{4,3,1,0,2:T(8,128)(2,1)}, f16[2,8,2,32,128]{4,3,1,0,2:T(8,128)(2,1)}, u32[]{:S(2)}, u32[]{:S(2)}) %collective-permute-start.3) | collective-permute-done | bytes 262176 | tf_op jit(solution)/shard_map/ppermute | solution.py:212
  47.8 8.9 %collective-permute-done.11.refs_2_.refs_1_ = bf16[4,128,640]{2,1,0:T(8,128)(2,1)} collective-permute-done((bf16[4,128,640]{2,1,0:T(8,128)(2,1)}, bf16[4,128,640]{2,1,0:T(8,128)(2,1)}, u32[]{:S(2)}, u32[]{:S(2)}) %collective-permute-start.11) | collective-permute-done | bytes 655392 | tf_op jit(solution)/shard_map/ppermute | solution.py:248
  56.7 2.5 %shard_map.68.refs_2_.refs_3_ = f32[2,8,128,128]{3,2,1,0:T(8,128)S(1)} custom-call(f32[8,16,640]{2,1,0:T(8,128)S(1)} %get-tuple-element.32.roots, bf16[8,128,640]{2,1,0:T(8,128)(2,1)S(1)} %get-tuple-element.22.refs_7_.refs_0_, bf16[4,128,640]{2,1,0:T(8,128)(2,1)} %collective-permute-done.10.refs_1_.refs_0_, ...), custom_call_target="tpu_custom_call" | custom-call | flops 1000 | bytes 1000 | tf_op jit(solution)/shard_map/pallas_call | solution.py:194
  59.3 1.4 %collective-permute-start.14 = (f16[2,8,2,32,128]{4,3,2,1,0:T(8,128)(2,1)S(1)}, f16[2,8,2,32,128]{4,3,2,1,0:T(8,128)(2,1)S(1)}, u32[]{:S(2)}, u32[]{:S(2)}) collective-permute-start(f16[2,8,2,32,128]{4,3,2,1,0:T(8,128)(2,1)S(1)} %copy.26), channel_id=1, source_target_pairs={{0,1},{1,0},{2,3},{3,2},{4,5},{5,4},{6,7},{7,6},{8,9},{9,8},{10,11... | collective-permute-start | bytes 786440 | tf_op jit(solution)/shard_map/ppermute | solution.py:212
  60.7 1.3 %collective-permute-start.12 = (bf16[4,128,640]{2,1,0:T(8,128)(2,1)}, bf16[4,128,640]{2,1,0:T(8,128)(2,1)S(1)}, u32[]{:S(2)}, u32[]{:S(2)}) collective-permute-start(bf16[4,128,640]{2,1,0:T(8,128)(2,1)} %get-tuple-element.37), channel_id=1, source_target_pairs={{0,4},{8,12},{1,5},{9,13},{2,6},{10,14},{3,7},{11,15},{16,20},{24,... | collective-permute-start | bytes 1966088 | tf_op jit(solution)/shard_map/ppermute | solution.py:262
  62.0 1.3 %collective-permute-start.13 = (bf16[4,128,640]{2,1,0:T(8,128)(2,1)}, bf16[4,128,640]{2,1,0:T(8,128)(2,1)S(1)}, u32[]{:S(2)}, u32[]{:S(2)}) collective-permute-start(bf16[4,128,640]{2,1,0:T(8,128)(2,1)} %get-tuple-element.38), channel_id=1, source_target_pairs={{0,4},{8,12},{1,5},{9,13},{2,6},{10,14},{3,7},{11,15},{16,20},{24,... | collective-permute-start | bytes 1966088 | tf_op jit(solution)/shard_map/ppermute | solution.py:262
  63.3 1.0 %bitcast_add_fusion.3 = f32[2,8,2,32,128]{4,3,1,0,2:T(8,128)S(1)} fusion(f32[2,8,2,1,32,128]{5,4,3,2,1,0:T(8,128)S(1)} %copy-done.8, f16[2,8,2,32,128]{4,3,1,0,2:T(8,128)(2,1)} %collective-permute-done.3), kind=kLoop, calls=%fused_computation.12 | loop fusion | flops 393216 | bytes 1310720 | tf_op jit(solution)/shard_map/add | solution.py:213
  64.4 2.4 %collective-permute-start.4 = (f16[2,8,1,32,128]{4,3,1,0,2:T(8,128)(2,1)S(1)}, f16[2,8,1,32,128]{4,3,1,0,2:T(8,128)(2,1)S(1)}, u32[]{:S(2)}, u32[]{:S(2)}) collective-permute-start(f16[2,8,1,32,128]{4,3,1,0,2:T(8,128)(2,1)S(1)} %multiply_convert_fusion.2), channel_id=1, source_target_pairs={{0,2},{1,3},{2,0},{3,1},{4,6},{5,7},{6,4},{7,5},{8,10},{9,11},{10,... | collective-permute-start | bytes 393224 | tf_op jit(solution)/shard_map/ppermute | solution.py:212
  66.7 1.0 %bitcast_add_fusion.2 = f32[2,8,2,32,128]{4,3,1,0,2:T(8,128)S(1)} fusion(f32[2,8,2,1,32,128]{5,4,3,2,1,0:T(8,128)S(1)} %get-tuple-element.41, f16[2,8,2,32,128]{4,3,1,0,2:T(8,128)(2,1)} %collective-permute-done.7), kind=kLoop, calls=%fused_computation.11 | loop fusion | flops 393216 | bytes 1310720 | tf_op jit(solution)/shard_map/add | solution.py:213
  67.8 5.5 %collective-permute-done.4 = f16[2,8,1,32,128]{4,3,1,0,2:T(8,128)(2,1)S(1)} collective-permute-done((f16[2,8,1,32,128]{4,3,1,0,2:T(8,128)(2,1)S(1)}, f16[2,8,1,32,128]{4,3,1,0,2:T(8,128)(2,1)S(1)}, u32[]{:S(2)}, u32[]{:S(2)}) %collective-permute-start.4) | collective-permute-done | bytes 131104 | tf_op jit(solution)/shard_map/ppermute | solution.py:212
  74.0 1.2 %shard_map.70.refs_2_ = f32[2,8,128,128]{3,2,1,0:T(8,128)S(1)} custom-call(f32[8,16,640]{2,1,0:T(8,128)S(1)} %get-tuple-element.32.roots, bf16[8,128,640]{2,1,0:T(8,128)(2,1)S(1)} %get-tuple-element.23.refs_8_.refs_1_.refs_0_, bf16[4,128,640]{2,1,0:T(8,128)(2,1)S(1)} %collective-permute-done.12.refs_1_, ...), custom_call_target="tpu_custom_call" | custom-call | flops 1000 | bytes 1000 | tf_op jit(solution)/shard_map/pallas_call | solution.py:194
  75.3 1.2 %shard_map.71 = f32[2,8,128,128]{3,2,1,0:T(8,128)S(1)} custom-call(f32[8,16,640]{2,1,0:T(8,128)S(1)} %get-tuple-element.32.roots, bf16[8,128,640]{2,1,0:T(8,128)(2,1)S(1)} %get-tuple-element.22.refs_7_.refs_0_, bf16[8,128,640]{2,1,0:T(8,128)(2,1)S(1)} %collective-permute-done.9.refs_1_, f32[2,8,128,128]{3,2,1,0:T(8,128)S(1)} %shard_map.70.refs_2_, ...), custom_call_target="tpu_custom_call" | custom-call | flops 1000 | bytes 1000 | tf_op jit(solution)/shard_map/pallas_call | solution.py:194
  76.7 1.9 %collective-permute-start.15 = (f16[2,8,2,32,128]{4,3,1,0,2:T(8,128)(2,1)S(1)}, f16[2,8,2,32,128]{4,3,1,0,2:T(8,128)(2,1)S(1)}, u32[]{:S(2)}, u32[]{:S(2)}) collective-permute-start(f16[2,8,2,32,128]{4,3,1,0,2:T(8,128)(2,1)S(1)} %fusion.7), channel_id=1, source_target_pairs={{4,5},{5,4},{6,7},{7,6},{12,13},{13,12},{14,15},{15,14},{20,21},{2... | collective-permute-start | bytes 786440 | tf_op jit(solution)/shard_map/ppermute | solution.py:212
  78.7 1.7 %collective-permute-start.17 = (f16[2,8,1,32,128]{4,3,2,1,0:T(8,128)(2,1)S(1)}, f16[2,8,1,32,128]{4,3,2,1,0:T(8,128)(2,1)S(1)}, u32[]{:S(2)}, u32[]{:S(2)}) collective-permute-start(f16[2,8,1,32,128]{4,3,2,1,0:T(8,128)(2,1)S(1)} %fusion.10), channel_id=1, source_target_pairs={{0,2},{1,3},{2,0},{3,1},{4,6},{5,7},{6,4},{7,5},{8,10},{9,11},{10,... | collective-permute-start | bytes 393224 | tf_op jit(solution)/shard_map/ppermute | solution.py:212
  80.5 7.1 %collective-permute-done.15 = f16[2,8,2,32,128]{4,3,1,0,2:T(8,128)(2,1)S(1)} collective-permute-done((f16[2,8,2,32,128]{4,3,1,0,2:T(8,128)(2,1)S(1)}, f16[2,8,2,32,128]{4,3,1,0,2:T(8,128)(2,1)S(1)}, u32[]{:S(2)}, u32[]{:S(2)}) %collective-permute-start.15) | collective-permute-done | bytes 262176 | tf_op jit(solution)/shard_map/ppermute | solution.py:212
  87.7 1.9 %collective-permute-start.16 = (f16[2,8,1,32,128]{4,3,1,0,2:T(8,128)(2,1)S(1)}, f16[2,8,1,32,128]{4,3,1,0,2:T(8,128)(2,1)S(1)}, u32[]{:S(2)}, u32[]{:S(2)}) collective-permute-start(f16[2,8,1,32,128]{4,3,1,0,2:T(8,128)(2,1)S(1)} %multiply_convert_fusion), channel_id=1, source_target_pairs={{4,6},{5,7},{6,4},{7,5},{12,14},{13,15},{14,12},{15,13},{20,22},{2... | collective-permute-start | bytes 393224 | tf_op jit(solution)/shard_map/ppermute | solution.py:212
  89.7 5.0 %collective-permute-done.16 = f16[2,8,1,32,128]{4,3,1,0,2:T(8,128)(2,1)S(1)} collective-permute-done((f16[2,8,1,32,128]{4,3,1,0,2:T(8,128)(2,1)S(1)}, f16[2,8,1,32,128]{4,3,1,0,2:T(8,128)(2,1)S(1)}, u32[]{:S(2)}, u32[]{:S(2)}) %collective-permute-start.16) | collective-permute-done | bytes 131104 | tf_op jit(solution)/shard_map/ppermute | solution.py:212
  (55 shorter events, 7.7 us)
Async XLA Ops:
  1.6 15.4 %collective-permute-start = (s32[25]{0:T(128)S(1)}, s32[25]{0:T(128)S(1)}, u32[]{:S(2)}, u32[]{:S(2)}) collective-permute-start(s32[25]{0:T(128)S(1)} %pad_add_fusion.refs_0_), channel_id=1, source_target_pairs={{0,4},{4,8},{8,12},{12,0},{1,5},{5,9},{9,13},{13,1},{2,6},{6,10},{... | collective-permute-start | bytes 308 | tf_op jit(solution)/shard_map/ppermute | solution.py:238
  4.2 12.8 %collective-permute-start.1 = (s32[25]{0:T(128)S(1)}, s32[25]{0:T(128)S(1)}, u32[]{:S(2)}, u32[]{:S(2)}) collective-permute-start(s32[25]{0:T(128)S(1)} %pad_add_fusion.refs_0_), channel_id=1, source_target_pairs={{0,8},{4,12},{8,0},{12,4},{1,9},{5,13},{9,1},{13,5},{2,10},{6,14},... | collective-permute-start | bytes 308 | tf_op jit(solution)/shard_map/ppermute | solution.py:238
  4.2 12.8 %collective-permute-start.2 = (s32[25]{0:T(128)S(1)}, s32[25]{0:T(128)S(1)}, u32[]{:S(2)}, u32[]{:S(2)}) collective-permute-start(s32[25]{0:T(128)S(1)} %pad_add_fusion.refs_0_), channel_id=1, source_target_pairs={{0,12},{4,0},{8,4},{12,8},{1,13},{5,1},{9,5},{13,9},{2,14},{6,2},{... | collective-permute-start | bytes 308 | tf_op jit(solution)/shard_map/ppermute | solution.py:238
  4.6 2.1 %copy-start = (bf16[1,1,8,3,1,128,640]{6,5,4,3,2,1,0:T(8,128)(2,1)S(1)}, bf16[1,1,8,3,1,128,640]{6,5,4,3,2,1,0:T(8,128)(2,1)}, u32[]{:S(2)}) copy-start(bf16[1,1,8,3,1,128,640]{6,5,4,3,2,1,0:T(8,128)(2,1)} %param.6) | copy-start | bytes 11796484
  15.9 1.1 %copy-start.1 = (bf16[8,128,640]{2,1,0:T(8,128)(2,1)}, bf16[8,128,640]{2,1,0:T(8,128)(2,1)S(1)}, u32[]{:S(2)}) copy-start(bf16[8,128,640]{2,1,0:T(8,128)(2,1)S(1)} %get-tuple-element.24.refs_9_) | copy-start | bytes 3932164
  17.0 10.3 %copy-start.5 = (f32[10240]{0:T(1024)S(1)}, f32[10240]{0:T(1024)}, u32[]{:S(2)}) copy-start(f32[10240]{0:T(1024)} %param.10) | copy-start | bytes 122884
  17.0 10.3 %copy-start.6 = (f32[8]{0:T(128)S(1)}, f32[8]{0:T(128)}, u32[]{:S(2)}) copy-start(f32[8]{0:T(128)} %refs_4_.1) | copy-start | bytes 100
  17.0 10.2 %copy-start.7 = (f32[2]{0:T(128)S(1)}, f32[2]{0:T(128)}, u32[]{:S(2)}) copy-start(f32[2]{0:T(128)} %refs_5_.1) | copy-start | bytes 28
  17.1 1.1 %copy-start.3 = (bf16[8,128,640]{2,1,0:T(8,128)(2,1)}, bf16[8,128,640]{2,1,0:T(8,128)(2,1)S(1)}, u32[]{:S(2)}) copy-start(bf16[8,128,640]{2,1,0:T(8,128)(2,1)S(1)} %get-tuple-element.35) | copy-start | bytes 3932164
  18.2 0.9 copy-start.4
  19.0 13.2 %collective-permute-start.5 = (bf16[8,128,640]{2,1,0:T(8,128)(2,1)}, bf16[8,128,640]{2,1,0:T(8,128)(2,1)}, u32[]{:S(2)}, u32[]{:S(2)}) collective-permute-start(bf16[8,128,640]{2,1,0:T(8,128)(2,1)} %get-tuple-element.33), channel_id=1, source_target_pairs={{4,0},{12,8},{5,1},{13,9},{6,2},{14,10},{7,3},{15,11},{20,16},{28,... | collective-permute-start | bytes 3932168 | tf_op jit(solution)/shard_map/ppermute | solution.py:250
  23.4 8.8 %collective-permute-start.6 = (bf16[8,128,640]{2,1,0:T(8,128)(2,1)}, bf16[8,128,640]{2,1,0:T(8,128)(2,1)}, u32[]{:S(2)}, u32[]{:S(2)}) collective-permute-start(bf16[8,128,640]{2,1,0:T(8,128)(2,1)} %get-tuple-element.34), channel_id=1, source_target_pairs={{4,0},{12,8},{5,1},{13,9},{6,2},{14,10},{7,3},{15,11},{20,16},{28,... | collective-permute-start | bytes 3932168 | tf_op jit(solution)/shard_map/ppermute | solution.py:250
  25.8 22.0 %collective-permute-start.10 = (bf16[4,128,640]{2,1,0:T(8,128)(2,1)}, bf16[4,128,640]{2,1,0:T(8,128)(2,1)}, u32[]{:S(2)}, u32[]{:S(2)}) collective-permute-start(bf16[4,128,640]{2,1,0:T(8,128)(2,1)} %get-tuple-element.30.refs_10_), channel_id=1, source_target_pairs={{0,8},{4,12},{8,0},{12,4},{1,9},{5,13},{9,1},{13,5},{2,10},{6,14},... | collective-permute-start | bytes 1966088 | tf_op jit(solution)/shard_map/ppermute | solution.py:248
  25.9 30.8 %collective-permute-start.11 = (bf16[4,128,640]{2,1,0:T(8,128)(2,1)}, bf16[4,128,640]{2,1,0:T(8,128)(2,1)}, u32[]{:S(2)}, u32[]{:S(2)}) collective-permute-start(bf16[4,128,640]{2,1,0:T(8,128)(2,1)} %copy-done.4), channel_id=1, source_target_pairs={{0,8},{4,12},{8,0},{12,4},{1,9},{5,13},{9,1},{13,5},{2,10},{6,14},... | collective-permute-start | bytes 1966088 | tf_op jit(solution)/shard_map/ppermute | solution.py:248
  27.3 1.3 %copy-start.2 = (bf16[8,128,640]{2,1,0:T(8,128)(2,1)S(1)}, bf16[8,128,640]{2,1,0:T(8,128)(2,1)}, u32[]{:S(2)}) copy-start(bf16[8,128,640]{2,1,0:T(8,128)(2,1)} %copy-done.1) | copy-start | bytes 3932164
  38.2 8.2 %collective-permute-start.3 = (f16[2,8,2,32,128]{4,3,1,0,2:T(8,128)(2,1)}, f16[2,8,2,32,128]{4,3,1,0,2:T(8,128)(2,1)}, u32[]{:S(2)}, u32[]{:S(2)}) collective-permute-start(f16[2,8,2,32,128]{4,3,1,0,2:T(8,128)(2,1)} %fusion.4), channel_id=1, source_target_pairs={{0,1},{1,0},{2,3},{3,2},{4,5},{5,4},{6,7},{7,6},{8,9},{9,8},{10,11... | collective-permute-start | bytes 786440 | tf_op jit(solution)/shard_map/ppermute | solution.py:212
  40.3 6.8 %collective-permute-start.7 = (f16[2,8,2,32,128]{4,3,1,0,2:T(8,128)(2,1)}, f16[2,8,2,32,128]{4,3,1,0,2:T(8,128)(2,1)}, u32[]{:S(2)}, u32[]{:S(2)}) collective-permute-start(f16[2,8,2,32,128]{4,3,1,0,2:T(8,128)(2,1)} %fusion.5), channel_id=1, source_target_pairs={{0,1},{1,0},{2,3},{3,2},{8,9},{9,8},{10,11},{11,10},{16,17},{17,16... | collective-permute-start | bytes 786440 | tf_op jit(solution)/shard_map/ppermute | solution.py:212
  41.6 33.6 %collective-permute-start.9 = (bf16[8,128,640]{2,1,0:T(8,128)(2,1)}, bf16[8,128,640]{2,1,0:T(8,128)(2,1)S(1)}, u32[]{:S(2)}, u32[]{:S(2)}) collective-permute-start(bf16[8,128,640]{2,1,0:T(8,128)(2,1)} %copy-done.3), channel_id=1, source_target_pairs={{0,12},{8,4},{1,13},{9,5},{2,14},{10,6},{3,15},{11,7},{16,28},{24,... | collective-permute-start | bytes 3932168 | tf_op jit(solution)/shard_map/ppermute | solution.py:249
  59.3 4.0 %copy-start.8 = (f32[2,8,2,1,32,128]{5,4,3,2,1,0:T(8,128)S(1)}, f32[2,8,2,1,32,128]{5,4,3,2,1,0:T(8,128)}, u32[]{:S(2)}) copy-start(f32[2,8,2,1,32,128]{5,4,3,2,1,0:T(8,128)} %get-tuple-element.46) | copy-start | bytes 1572868
  59.3 14.7 %collective-permute-start.14 = (f16[2,8,2,32,128]{4,3,2,1,0:T(8,128)(2,1)S(1)}, f16[2,8,2,32,128]{4,3,2,1,0:T(8,128)(2,1)S(1)}, u32[]{:S(2)}, u32[]{:S(2)}) collective-permute-start(f16[2,8,2,32,128]{4,3,2,1,0:T(8,128)(2,1)S(1)} %copy.26), channel_id=1, source_target_pairs={{0,1},{1,0},{2,3},{3,2},{4,5},{5,4},{6,7},{7,6},{8,9},{9,8},{10,11... | collective-permute-start | bytes 786440 | tf_op jit(solution)/shard_map/ppermute | solution.py:212
  60.7 13.3 %collective-permute-start.12 = (bf16[4,128,640]{2,1,0:T(8,128)(2,1)}, bf16[4,128,640]{2,1,0:T(8,128)(2,1)S(1)}, u32[]{:S(2)}, u32[]{:S(2)}) collective-permute-start(bf16[4,128,640]{2,1,0:T(8,128)(2,1)} %get-tuple-element.37), channel_id=1, source_target_pairs={{0,4},{8,12},{1,5},{9,13},{2,6},{10,14},{3,7},{11,15},{16,20},{24,... | collective-permute-start | bytes 1966088 | tf_op jit(solution)/shard_map/ppermute | solution.py:262
  62.0 12.1 %collective-permute-start.13 = (bf16[4,128,640]{2,1,0:T(8,128)(2,1)}, bf16[4,128,640]{2,1,0:T(8,128)(2,1)S(1)}, u32[]{:S(2)}, u32[]{:S(2)}) collective-permute-start(bf16[4,128,640]{2,1,0:T(8,128)(2,1)} %get-tuple-element.38), channel_id=1, source_target_pairs={{0,4},{8,12},{1,5},{9,13},{2,6},{10,14},{3,7},{11,15},{16,20},{24,... | collective-permute-start | bytes 1966088 | tf_op jit(solution)/shard_map/ppermute | solution.py:262
  64.4 8.9 %collective-permute-start.4 = (f16[2,8,1,32,128]{4,3,1,0,2:T(8,128)(2,1)S(1)}, f16[2,8,1,32,128]{4,3,1,0,2:T(8,128)(2,1)S(1)}, u32[]{:S(2)}, u32[]{:S(2)}) collective-permute-start(f16[2,8,1,32,128]{4,3,1,0,2:T(8,128)(2,1)S(1)} %multiply_convert_fusion.2), channel_id=1, source_target_pairs={{0,2},{1,3},{2,0},{3,1},{4,6},{5,7},{6,4},{7,5},{8,10},{9,11},{10,... | collective-permute-start | bytes 393224 | tf_op jit(solution)/shard_map/ppermute | solution.py:212
  73.3 16.4 %collective-permute-start.8 = (f16[2,8,1,32,128]{4,3,1,0,2:T(8,128)(2,1)S(1)}, f16[2,8,1,32,128]{4,3,1,0,2:T(8,128)(2,1)S(1)}, u32[]{:S(2)}, u32[]{:S(2)}) collective-permute-start(f16[2,8,1,32,128]{4,3,1,0,2:T(8,128)(2,1)S(1)} %multiply_convert_fusion.1), channel_id=1, source_target_pairs={{0,2},{1,3},{2,0},{3,1},{8,10},{9,11},{10,8},{11,9},{16,18},{17,19... | collective-permute-start | bytes 393224 | tf_op jit(solution)/shard_map/ppermute | solution.py:212
  76.7 10.9 %collective-permute-start.15 = (f16[2,8,2,32,128]{4,3,1,0,2:T(8,128)(2,1)S(1)}, f16[2,8,2,32,128]{4,3,1,0,2:T(8,128)(2,1)S(1)}, u32[]{:S(2)}, u32[]{:S(2)}) collective-permute-start(f16[2,8,2,32,128]{4,3,1,0,2:T(8,128)(2,1)S(1)} %fusion.7), channel_id=1, source_target_pairs={{4,5},{5,4},{6,7},{7,6},{12,13},{13,12},{14,15},{15,14},{20,21},{2... | collective-permute-start | bytes 786440 | tf_op jit(solution)/shard_map/ppermute | solution.py:212
  78.7 10.9 %collective-permute-start.17 = (f16[2,8,1,32,128]{4,3,2,1,0:T(8,128)(2,1)S(1)}, f16[2,8,1,32,128]{4,3,2,1,0:T(8,128)(2,1)S(1)}, u32[]{:S(2)}, u32[]{:S(2)}) collective-permute-start(f16[2,8,1,32,128]{4,3,2,1,0:T(8,128)(2,1)S(1)} %fusion.10), channel_id=1, source_target_pairs={{0,2},{1,3},{2,0},{3,1},{4,6},{5,7},{6,4},{7,5},{8,10},{9,11},{10,... | collective-permute-start | bytes 393224 | tf_op jit(solution)/shard_map/ppermute | solution.py:212
  87.7 7.0 %collective-permute-start.16 = (f16[2,8,1,32,128]{4,3,1,0,2:T(8,128)(2,1)S(1)}, f16[2,8,1,32,128]{4,3,1,0,2:T(8,128)(2,1)S(1)}, u32[]{:S(2)}, u32[]{:S(2)}) collective-permute-start(f16[2,8,1,32,128]{4,3,1,0,2:T(8,128)(2,1)S(1)} %multiply_convert_fusion), channel_id=1, source_target_pairs={{4,6},{5,7},{6,4},{7,5},{12,14},{13,15},{14,12},{15,13},{20,22},{2... | collective-permute-start | bytes 393224 | tf_op jit(solution)/shard_map/ppermute | solution.py:212

commit v7 on v6

--- a/solution.py
+++ b/solution.py
@@ -8,6 +8,7 @@
 from jax.sharding import PartitionSpec as P
 
 LIMIT = 16 << 20
+SPLIT = (2, 6)
 COST = pl.CostEstimate(flops=1000, bytes_accessed=1000, transcendentals=0)
 PARAMS = pltpu.CompilerParams(vmem_limit_bytes=LIMIT)
 ANY = pl.BlockSpec(memory_space=pl.ANY)
@@ -26,51 +27,27 @@
     return lax.dot_general(a, b, (((1,), (1,)), ((), ())), preferred_element_type=jnp.float32)
 
 
-def pack_kernel(plan, tiles, *refs):
+def pack_kernel(plan, tiles, first_slot, rest, *outs):
     blocks_dev, band = tiles.shape[:2]
-    own, outs, sem_in, sem_out = refs[:band], refs[band:-2], refs[-2], refs[-1]
     aux_pos = lax.axis_index("aux")
-    loads = {
-        slot: [
-            pltpu.make_async_copy(tiles.at[m, slot], own[slot].at[m], sem_in.at[slot, m]) for m in range(blocks_dev)
-        ]
-        for slot in range(band)
-    }
-    for slot in reversed(range(band)):
-        for load in loads[slot]:
-            load.start()
-    stores = []
-    ready = set()
     for out, (slot, back, first, count) in zip(outs, plan):
-        if slot not in ready:
-            ready.add(slot)
-            for load in loads[slot]:
-                load.wait()
+        shift = (aux_pos < back).astype(jnp.int32)
         for i in range(count):
-            row = jnp.minimum(first + i + (aux_pos < back).astype(jnp.int32), blocks_dev - 1)
-            store = pltpu.make_async_copy(own[slot].at[row], out.at[i], sem_out.at[len(stores)])
-            store.start()
-            stores.append(store)
-    for slot in range(band):
-        if slot not in ready:
-            for load in loads[slot]:
-                load.wait()
-    for store in stores:
-        store.wait()
+            out[i] = tiles[jnp.minimum(first + i + shift, blocks_dev - 1), slot]
+    for m in range(blocks_dev):
+        first_slot[m] = tiles[m, 0]
+        for slot in range(1, band):
+            rest[(slot - 1) * blocks_dev + m] = tiles[m, slot]
 
 
 def pack(tiles, plan):
-    counts = [part[3] for part in plan]
     blocks_dev, band, aux_rows, pair_rows = tiles.shape
+    counts = [blocks_dev, (band - 1) * blocks_dev] + [part[3] for part in plan]
     return pl.pallas_call(
         functools.partial(pack_kernel, plan),
-        out_shape=[
-            jax.ShapeDtypeStruct((count, aux_rows, pair_rows), tiles.dtype)
-            for count in [blocks_dev] * band + counts
-        ],
-        in_specs=[ANY],
-        out_specs=[VMEM] * band + [ANY] * len(counts),
-        scratch_shapes=[DMA((band, blocks_dev)), DMA((sum(counts),))],
+        out_shape=[jax.ShapeDtypeStruct((count, aux_rows, pair_rows), tiles.dtype) for count in counts],
+        in_specs=[VMEM],
+        out_specs=[VMEM] * len(counts),
         compiler_params=PARAMS,
         cost_estimate=COST,
     )(tiles)
@@ -98,11 +75,15 @@
     return -(-rows // 8) * 8
 
 
+def own_tile(own, slot, m, blocks_dev):
+    return own[0][m] if slot == 0 else own[1][(slot - 1) * blocks_dev + m]
+
+
 def first_kernel(dims, *refs):
     n_aux, n_pair, blocks_dev, band, freq_count = dims
     records = refs[:n_aux]
     occ, freq, table = refs[n_aux : n_aux + 3]
-    own = refs[n_aux + 3 : n_aux + 3 + band]
+    own = refs[n_aux + 3 : n_aux + 5]
     out, roots = refs[-2:]
     pair_rows = own[0].shape[-1]
     virt_blocks = table.shape[1] // pair_rows
@@ -141,7 +122,7 @@
         for w in range(freq_count):
             total = None
             for slot in range(band):
-                a = (own[slot][m].astype(jnp.float32) * masked[m, slot, w]).astype(jnp.bfloat16)
+                a = (own_tile(own, slot, m, blocks_dev).astype(jnp.float32) * masked[m, slot, w]).astype(jnp.bfloat16)
                 term = dot(a, a)
                 total = term if total is None else total + term
             out[w, m] = total
@@ -156,7 +137,7 @@
             jax.ShapeDtypeStruct((freq_count, blocks_dev, aux_rows, aux_rows), jnp.float32),
             jax.ShapeDtypeStruct((blocks_dev, root_rows(band, freq_count), pair_rows), jnp.float32),
         ],
-        in_specs=[SMEM] * (n_aux + 2) + [VMEM] * (1 + band) + [ANY] * len(after),
+        in_specs=[SMEM] * (n_aux + 2) + [VMEM] * 3 + [ANY] * len(after),
         out_specs=[VMEM, VMEM],
         compiler_params=PARAMS,
         cost_estimate=COST,
@@ -170,7 +151,7 @@
         sums = [refs[add][w, m] if add is not None else None for w in range(freq_count)]
         for s, slot in enumerate(slots):
             n, row = rights[s][m]
-            left = refs[s][m].astype(jnp.float32)
+            left = own_tile(refs, slot, m, blocks_dev).astype(jnp.float32)
             right = refs[n][row].astype(jnp.float32)
             for w in range(freq_count):
                 kept = roots[m, pl.ds(root_row(band, freq_count, delta, slot, w), 1), :]
@@ -184,10 +165,11 @@
 def band_rows(dims, delta, slots, roots, own, far, after, add=None):
     n_aux, n_pair, blocks_dev, band, freq_count = dims
     aux_rows = own[0].shape[-2]
-    arrays = [own[slot] for slot in slots]
+    arrays = list(own)
     rights = []
     for group in far:
-        rights.append([(len(arrays) + n, row) for n, array in enumerate(group) for row in range(array.shape[0])])
+        rows = [(len(arrays) + n, row) for n, array in enumerate(group) for row in range(array.shape[0])]
+        rights.append(rows[-blocks_dev:] if len(rights) > 0 else rows[:blocks_dev])
         arrays += group
     spot = None if add is None else len(arrays)
     arrays += [] if add is None else [add]
@@ -237,32 +219,33 @@
     records = [record] + [
         lax.ppermute(record, "aux", [(s, (s + k) % n_aux) for s in range(n_aux)]) for k in range(1, n_aux)
     ]
-    two = chunks_of(blocks_dev, (4, 4))
+    two = chunks_of(blocks_dev, SPLIT)
     whole = list(range(n_aux))
     evens, odds = whole[::2], whole[1::2]
-    plan = [(2, 2, first, count) for first, count in two]
-    plan += [(2, 0, 0, blocks_dev), (1, 1, 0, blocks_dev), (1, 0, 0, blocks_dev)]
-    packed = pack(tiles, plan)
-    own, packed = packed[:band], packed[band:]
-    *to_two, lower2, to_one, lower1 = tie(packed, records[1:])
-    c2 = [lax.ppermute(p, "aux", [(s, (s - 2) % n_aux) for s in whole]) for p in to_two]
+    plan = [(2, 2, first, count) for first, count in two] + [(1, 1, 0, blocks_dev)]
+    first_slot, rest, near_two, far_two, to_one = pack(tiles, plan)
+    own = (first_slot, rest)
+    down2 = [(s, (s - 2) % n_aux) for s in whole]
+    c2 = [lax.ppermute(near_two, "aux", down2)]
+    (far_two,) = tie([far_two], records[1:] + c2)
+    c2.append(lax.ppermute(far_two, "aux", down2))
     b1 = lax.ppermute(to_one, "aux", [(s, (s - 1) % n_aux) for s in evens])
-    to_even = [lax.ppermute(p, "aux", [(s, s - 1) for s in odds]) for p in (lower1, lower2)]
+    to_even = lax.ppermute(rest, "aux", [(s, s - 1) for s in odds])
     table = virt_energy.reshape(1, -1)
-    rows0, roots = first_rows(dims, records, occ_energy, frequencies, table, own, to_two[:1])
+    rows0, roots = first_rows(dims, records, occ_energy, frequencies, table, own, [far_two])
 
     def rows_of(delta, slots, far, after, add=None):
         return band_rows(dims, delta, slots, roots, own, far, after, add)
 
     z0 = totals(rows0, pair_col, n_pair, whole, scale)
-    rows_even = rows_of(1, [0, 1], [[p] for p in to_even], [rows0])
+    rows_even = rows_of(1, [0, 1], [[to_even], [to_even]], [rows0])
     z_even = totals(rows_even, pair_col, n_pair, evens, scale)
     rows2 = rows_of(2, [0], [c2], [z0[0], z_even[0]])
     z2 = totals(rows2, pair_col, n_pair, whole, scale)
     to_odd = [lax.ppermute(c, "aux", [(s, s + 1) for s in evens]) for c in tie(c2, [rows2])]
     part = rows_of(1, [1], [to_odd], [rows2])
-    rows_odd = rows_of(1, [0], [[b1]], [z2[0]], part)
-    z_odd = totals(rows_odd, pair_col, n_pair, odds, scale)
+    rows_odd = rows_of(1, [0], [[b1]], [z2[0]])
+    z_odd = totals(rows_odd + part, pair_col, n_pair, odds, scale)
     even = lax.axis_index("aux") % 2 == 0
     out = jnp.concatenate([z0[1], jnp.where(even, z_even[1], z_odd[1]), z2[1]], axis=-1)
     return out[:, :, None]

time: 96.3 us -> 82.9 us (0.86)
  Pallas kernels: 21.8 us -> 16.5 us
  waiting for transfers between devices: 30 us -> 25.6 us
  starting transfers between devices: 27.8 us -> 25.7 us
  other arithmetic: 6.68 us -> 5.25 us
    pallas_call x1, Pallas kernels: 9.18 us -> 1.88 us  [pack(): pl.pallas_call(functools.partial(pack_kernel, plan), out_shape=[jax.Shape...]
    ppermute x4 -> x3, waiting for transfers between devices: 8.9 us -> 2.4 us  [the longest x1 2.39 us: on_device(): c2.append(lax.ppermute(far_two, 'aux', down2))]
    ppermute x3, waiting for transfers between devices: 0.01 us -> 4.5 us  [on_device(): lax.ppermute(record, 'aux', [(s, (s + k) % n_aux) for s in range(n_aux)])]
    ppermute x8, waiting for transfers between devices: 21.1 us -> 18.7 us  [halve(): got = lax.ppermute(sent, ('aux', 'pair'), pairs)]
    ppermute x3, starting transfers between devices: 3.06 us -> 0.78 us  [on_device(): lax.ppermute(record, 'aux', [(s, (s + k) % n_aux) for s in range(n_aux)])]
    pallas_call x4, Pallas kernels: 8.94 us -> 11 us  [band_rows(): pl.pallas_call(functools.partial(band_kernel, dims, delta, slots, rights,...]
    unnamed x19 -> x29, local copies, waits for them, and re-layouts: 7.23 us -> 6.88 us
    ppermute x4 -> x3, starting transfers between devices: 8.25 us -> 7.91 us  [the longest x1 3.45 us: on_device(): to_even = lax.ppermute(rest, 'aux', [(s, s - 1) for s in odds])]
  transfers between devices with their start and end apart: 18 -> 17, of which waited for: 5 -> 8; matrix products, arithmetic and copies ran while one was open for 7% -> 7% of each run, Pallas kernels for 23% -> 18%
where the time goes in v7:
time: 82.9 us; the launch traced here: 82.4 us
  starting transfers between devices  25.7 us (31%)
  waiting for transfers between devices  25.6 us (31%)
  Pallas kernels  16.5 us (20%)
  local copies, waits for them, and re-layouts  8.3 us (10%)
  other arithmetic  5.25 us (6%)
  between operations  1 us (1%)
    ppermute x8, waiting for transfers between devices, halve(): got = lax.ppermute(sent, ('aux', 'pair'), pairs)  18.7 us
    ppermute x8, starting transfers between devices, halve(): got = lax.ppermute(sent, ('aux', 'pair'), pairs)  13 us
    pallas_call x4, Pallas kernels, band_rows(): pl.pallas_call(functools.partial(band_kernel, dims, delta, slots, rights,...  11 us
    unnamed x29, local copies, waits for them, and re-layouts  6.88 us
    ppermute x3, waiting for transfers between devices, on_device(): lax.ppermute(record, 'aux', [(s, (s + k) % n_aux) for s in range(n_aux)])  4.5 us
    pallas_call x1, Pallas kernels, first_rows(): pl.pallas_call(functools.partial(first_kernel, dims), out_shape=[jax.Shap...  3.66 us
    ppermute x1, starting transfers between devices, on_device(): to_even = lax.ppermute(rest, 'aux', [(s, s - 1) for s in odds])  3.45 us
    ppermute x2, starting transfers between devices, on_device(): lax.ppermute(c, 'aux', [(s, s + 1) for s in evens])  2.69 us
  transfers between devices with their start and end apart: 17, of which 8 were waited for; matrix products, arithmetic and copies ran while one was open for 7% of the time, Pallas kernels for 18%

profile of v7, /device:TPU:1, one launch (start us, length us, event | category | flops | bytes accessed | tf_op | source)
XLA Modules:
  0.0 82.4 jit_solution(2011147058023495645)
XLA Ops:
  0.0 2.1 %copy-done.7 = bf16[1,1,8,3,1,128,640]{6,5,4,3,2,1,0:T(8,128)(2,1)S(1)} copy-done((bf16[1,1,8,3,1,128,640]{6,5,4,3,2,1,0:T(8,128)(2,1)S(1)}, bf16[1,1,8,3,1,128,640]{6,5,4,3,2,1,0:T(8,128)(2,1)}, u32[]{:S(2)}) %copy-start.7) | copy-done | bytes 3932184
  2.1 1.9 %shard_map.64 = (bf16[8,128,640]{2,1,0:T(8,128)(2,1)S(1)}, bf16[16,128,640]{2,1,0:T(8,128)(2,1)S(1)}, bf16[2,128,640]{2,1,0:T(8,128)(2,1)S(1)}, bf16[6,128,640]{2,1,0:T(8,128)(2,1)}, bf16[8,128,640]{2,1,0:T(8,128)(2,1)}) custom-call(bf16[8,3,128,640]{3,2,1,0:T(8,128)(2,1)S(1)} %bitcast.67), custom_call_target="tpu_custom_call" | custom-call | flops 1000 | bytes 1000 | tf_op jit(solution)/shard_map/pallas_call | solution.py:46
  4.0 1.1 %copy-done = bf16[8,128,640]{2,1,0:T(8,128)(2,1)} copy-done((bf16[8,128,640]{2,1,0:T(8,128)(2,1)}, bf16[8,128,640]{2,1,0:T(8,128)(2,1)S(1)}, u32[]{:S(2)}) %copy-start) | copy-done | bytes 1310744
  5.1 3.4 %collective-permute-start.6 = (bf16[16,128,640]{2,1,0:T(8,128)(2,1)S(1)}, bf16[16,128,640]{2,1,0:T(8,128)(2,1)}, u32[]{:S(2)}, u32[]{:S(2)}) collective-permute-start(bf16[16,128,640]{2,1,0:T(8,128)(2,1)S(1)} %get-tuple-element.15.refs_8_.refs_1_), channel_id=1, source_target_pairs={{4,0},{12,8},{5,1},{13,9},{6,2},{14,10},{7,3},{15,11},{20,16},{28,... | collective-permute-start | bytes 7864328 | tf_op jit(solution)/shard_map/ppermute | solution.py:233
  8.6 2.7 %collective-permute-start.3 = (bf16[2,128,640]{2,1,0:T(8,128)(2,1)S(1)}, bf16[2,128,640]{2,1,0:T(8,128)(2,1)S(1)}, u32[]{:S(2)}, u32[]{:S(2)}) collective-permute-start(bf16[2,128,640]{2,1,0:T(8,128)(2,1)S(1)} %get-tuple-element.17), channel_id=1, source_target_pairs={{0,8},{4,12},{8,0},{12,4},{1,9},{5,13},{9,1},{13,5},{2,10},{6,14},... | collective-permute-start | bytes 983048 | tf_op jit(solution)/shard_map/ppermute | solution.py:229
  12.9 4.3 %collective-permute-done.refs_1_ = s32[25]{0:T(128)S(1)} collective-permute-done((s32[25]{0:T(128)S(1)}, s32[25]{0:T(128)S(1)}, u32[]{:S(2)}, u32[]{:S(2)}) %collective-permute-start) | collective-permute-done | bytes 132 | tf_op jit(solution)/shard_map/ppermute | solution.py:220
  17.4 1.8 %collective-permute-start.10 = (bf16[6,128,640]{2,1,0:T(8,128)(2,1)}, bf16[6,128,640]{2,1,0:T(8,128)(2,1)}, u32[]{:S(2)}, u32[]{:S(2)}) collective-permute-start(bf16[6,128,640]{2,1,0:T(8,128)(2,1)} %shard_map.65.refs_9_), channel_id=1, source_target_pairs={{0,8},{4,12},{8,0},{12,4},{1,9},{5,13},{9,1},{13,5},{2,10},{6,14},... | collective-permute-start | bytes 2949128 | tf_op jit(solution)/shard_map/ppermute | solution.py:231
  19.3 3.7 %shard_map.66 = (f32[2,8,128,128]{3,2,1,0:T(8,128)S(1)}, f32[8,16,640]{2,1,0:T(8,128)S(1)}) custom-call(s32[25]{0:T(128)S(1)} %pad_add_fusion.refs_0_, s32[25]{0:T(128)S(1)} %collective-permute-done.refs_1_, s32[25]{0:T(128)S(1)} %collective-permute-done.1.refs_2_, s32[25]{0:T(128)S(1)} %collective-permute-done.2.refs_3_, f32[8]{0:T(128)S(1)} %copy-done.9, ...), custom_call_target="tpu_custom_call" | custom-call | flops 1000 | bytes 1000 | tf_op jit(solution)/shard_map/pallas_call | solution.py:134
  22.9 4.9 %shard_map.67 = f32[2,8,128,128]{3,2,1,0:T(8,128)S(1)} custom-call(f32[8,16,640]{2,1,0:T(8,128)S(1)} %get-tuple-element.19.roots, bf16[8,128,640]{2,1,0:T(8,128)(2,1)S(1)} %copy-done.1, bf16[16,128,640]{2,1,0:T(8,128)(2,1)S(1)} %get-tuple-element.15.refs_8_.refs_1_, bf16[16,128,640]{2,1,0:T(8,128)(2,1)} %collective-permute-done.6.refs_2_.refs_3_, ...), custom_call_target="tpu_custom_call" | custom-call | flops 1000 | bytes 1000 | tf_op jit(solution)/shard_map/pallas_call | solution.py:176
  27.8 1.2 %constant_dynamic-slice_fusion.4 = (f32[2,8,2,1,32,128]{5,4,3,2,1,0:T(8,128)}, f32[2,8,2,1,32,128]{5,4,3,2,1,0:T(8,128)S(1)}, f32[2,8,2,1,32,128]{5,4,3,2,1,0:T(8,128)S(1)}, f32[2,8,2,1,32,128]{5,4,3,2,1,0:T(8,128)}) fusion(f32[2,8,2,2,32,128]{5,4,3,2,1,0:T(8,128)S(1)} %bitcast.66, s32[]{:T(128)S(6)} %select_n.55, s32[]{:T(128)S(6)} %select_n.56, ...), kind=kLoop, calls=%fused_computation.37 | loop fusion | bytes 4194312 | tf_op jit(solution)/shard_map/jit(dynamic_index_in_dim)/dynamic_slice | solution.py:191
  31.2 1.3 %collective-permute-start.4 = (f16[2,8,2,32,128]{4,3,1,0,2:T(8,128)(2,1)}, f16[2,8,2,32,128]{4,3,1,0,2:T(8,128)(2,1)}, u32[]{:S(2)}, u32[]{:S(2)}) collective-permute-start(f16[2,8,2,32,128]{4,3,1,0,2:T(8,128)(2,1)} %fusion.4), channel_id=1, source_target_pairs={{0,1},{1,0},{2,3},{3,2},{4,5},{5,4},{6,7},{7,6},{8,9},{9,8},{10,11... | collective-permute-start | bytes 786440 | tf_op jit(solution)/shard_map/ppermute | solution.py:194
  32.5 1.3 %collective-permute-start.9 = (bf16[8,128,640]{2,1,0:T(8,128)(2,1)}, bf16[8,128,640]{2,1,0:T(8,128)(2,1)}, u32[]{:S(2)}, u32[]{:S(2)}) collective-permute-start(bf16[8,128,640]{2,1,0:T(8,128)(2,1)} %get-tuple-element.20), channel_id=1, source_target_pairs={{0,12},{8,4},{1,13},{9,5},{2,14},{10,6},{3,15},{11,7},{16,28},{24,... | collective-permute-start | bytes 3932168 | tf_op jit(solution)/shard_map/ppermute | solution.py:232
  33.9 4.1 %collective-permute-done.4 = f16[2,8,2,32,128]{4,3,1,0,2:T(8,128)(2,1)} collective-permute-done((f16[2,8,2,32,128]{4,3,1,0,2:T(8,128)(2,1)}, f16[2,8,2,32,128]{4,3,1,0,2:T(8,128)(2,1)}, u32[]{:S(2)}, u32[]{:S(2)}) %collective-permute-start.4) | collective-permute-done | bytes 262176 | tf_op jit(solution)/shard_map/ppermute | solution.py:194
  38.7 2.4 %collective-permute-done.10.refs_3_.refs_1_ = bf16[6,128,640]{2,1,0:T(8,128)(2,1)} collective-permute-done((bf16[6,128,640]{2,1,0:T(8,128)(2,1)}, bf16[6,128,640]{2,1,0:T(8,128)(2,1)}, u32[]{:S(2)}, u32[]{:S(2)}) %collective-permute-start.10) | collective-permute-done | bytes 983072 | tf_op jit(solution)/shard_map/ppermute | solution.py:231
  41.1 1.3 %copy-done.2 = bf16[8,128,640]{2,1,0:T(8,128)(2,1)S(1)} copy-done((bf16[8,128,640]{2,1,0:T(8,128)(2,1)S(1)}, bf16[8,128,640]{2,1,0:T(8,128)(2,1)}, u32[]{:S(2)}) %copy-start.2) | copy-done | bytes 1310744
  42.4 2.4 %shard_map.68.refs_2_.refs_4_ = f32[2,8,128,128]{3,2,1,0:T(8,128)S(1)} custom-call(f32[8,16,640]{2,1,0:T(8,128)S(1)} %get-tuple-element.19.roots, bf16[8,128,640]{2,1,0:T(8,128)(2,1)S(1)} %copy-done.2, bf16[16,128,640]{2,1,0:T(8,128)(2,1)S(1)} %get-tuple-element.15.refs_8_.refs_1_, bf16[2,128,640]{2,1,0:T(8,128)(2,1)S(1)} %collective-permute-done.3.refs_4_.refs_2_.refs_0_, ...), custom_call_target="tpu_custom_call" | custom-call | flops 1000 | bytes 1000 | tf_op jit(solution)/shard_map/pallas_call | solution.py:176
  44.8 1.0 %copy-done.4 = f32[2,8,128,128]{3,2,1,0:T(8,128)} copy-done((f32[2,8,128,128]{3,2,1,0:T(8,128)}, f32[2,8,128,128]{3,2,1,0:T(8,128)S(1)}, u32[]{:S(2)}) %copy-start.4) | copy-done | bytes 1048600
  45.8 1.2 %copy-done.5 = f32[2,8,128,128]{3,2,1,0:T(8,128)S(1)} copy-done((f32[2,8,128,128]{3,2,1,0:T(8,128)S(1)}, f32[2,8,128,128]{3,2,1,0:T(8,128)}, u32[]{:S(2)}) %copy-start.5) | copy-done | bytes 1048600
  47.0 1.4 %collective-permute-start.13 = (bf16[6,128,640]{2,1,0:T(8,128)(2,1)}, bf16[6,128,640]{2,1,0:T(8,128)(2,1)S(1)}, u32[]{:S(2)}, u32[]{:S(2)}) collective-permute-start(bf16[6,128,640]{2,1,0:T(8,128)(2,1)} %get-tuple-element.22), channel_id=1, source_target_pairs={{0,4},{8,12},{1,5},{9,13},{2,6},{10,14},{3,7},{11,15},{16,20},{24,... | collective-permute-start | bytes 2949128 | tf_op jit(solution)/shard_map/ppermute | solution.py:245
  48.5 1.1 %bitcast_add_fusion.3 = f32[2,8,2,32,128]{4,3,1,0,2:T(8,128)S(1)} fusion(f32[2,8,2,1,32,128]{5,4,3,2,1,0:T(8,128)S(1)} %copy-done.12, f16[2,8,2,32,128]{4,3,1,0,2:T(8,128)(2,1)} %collective-permute-done.4), kind=kLoop, calls=%fused_computation.12 | loop fusion | flops 393216 | bytes 1310720 | tf_op jit(solution)/shard_map/add | solution.py:195
  49.7 2.3 %collective-permute-start.5 = (f16[2,8,1,32,128]{4,3,1,0,2:T(8,128)(2,1)S(1)}, f16[2,8,1,32,128]{4,3,1,0,2:T(8,128)(2,1)S(1)}, u32[]{:S(2)}, u32[]{:S(2)}) collective-permute-start(f16[2,8,1,32,128]{4,3,1,0,2:T(8,128)(2,1)S(1)} %multiply_convert_fusion.2), channel_id=1, source_target_pairs={{0,2},{1,3},{2,0},{3,1},{4,6},{5,7},{6,4},{7,5},{8,10},{9,11},{10,... | collective-permute-start | bytes 393224 | tf_op jit(solution)/shard_map/ppermute | solution.py:194
  52.1 1.4 %collective-permute-start.11 = (f16[2,8,2,32,128]{4,3,2,1,0:T(8,128)(2,1)S(1)}, f16[2,8,2,32,128]{4,3,2,1,0:T(8,128)(2,1)S(1)}, u32[]{:S(2)}, u32[]{:S(2)}) collective-permute-start(f16[2,8,2,32,128]{4,3,2,1,0:T(8,128)(2,1)S(1)} %copy.24), channel_id=1, source_target_pairs={{0,1},{1,0},{2,3},{3,2},{4,5},{5,4},{6,7},{7,6},{8,9},{9,8},{10,11... | collective-permute-start | bytes 786440 | tf_op jit(solution)/shard_map/ppermute | solution.py:194
  54.3 1.7 %collective-permute-done.5 = f16[2,8,1,32,128]{4,3,1,0,2:T(8,128)(2,1)S(1)} collective-permute-done((f16[2,8,1,32,128]{4,3,1,0,2:T(8,128)(2,1)S(1)}, f16[2,8,1,32,128]{4,3,1,0,2:T(8,128)(2,1)S(1)}, u32[]{:S(2)}, u32[]{:S(2)}) %collective-permute-start.5) | collective-permute-done | bytes 131104 | tf_op jit(solution)/shard_map/ppermute | solution.py:194
  56.0 1.3 %collective-permute-start.12 = (bf16[2,128,640]{2,1,0:T(8,128)(2,1)S(1)}, bf16[2,128,640]{2,1,0:T(8,128)(2,1)S(1)}, u32[]{:S(2)}, u32[]{:S(2)}) collective-permute-start(bf16[2,128,640]{2,1,0:T(8,128)(2,1)S(1)} %get-tuple-element.21), channel_id=1, source_target_pairs={{0,4},{8,12},{1,5},{9,13},{2,6},{10,14},{3,7},{11,15},{16,20},{24,... | collective-permute-start | bytes 983048 | tf_op jit(solution)/shard_map/ppermute | solution.py:245
  57.3 3.1 %collective-permute-done.11 = f16[2,8,2,32,128]{4,3,2,1,0:T(8,128)(2,1)S(1)} collective-permute-done((f16[2,8,2,32,128]{4,3,2,1,0:T(8,128)(2,1)S(1)}, f16[2,8,2,32,128]{4,3,2,1,0:T(8,128)(2,1)S(1)}, u32[]{:S(2)}, u32[]{:S(2)}) %collective-permute-start.11) | collective-permute-done | bytes 262176 | tf_op jit(solution)/shard_map/ppermute | solution.py:194
  60.4 2.5 %shard_map.69 = f32[2,8,128,128]{3,2,1,0:T(8,128)S(1)} custom-call(f32[8,16,640]{2,1,0:T(8,128)S(1)} %get-tuple-element.19.roots, bf16[8,128,640]{2,1,0:T(8,128)(2,1)S(1)} %copy-done.3, bf16[16,128,640]{2,1,0:T(8,128)(2,1)S(1)} %get-tuple-element.15.refs_8_.refs_1_, bf16[8,128,640]{2,1,0:T(8,128)(2,1)} %collective-permute-done.9.refs_2_, ...), custom_call_target="tpu_custom_call" | custom-call | flops 1000 | bytes 1000 | tf_op jit(solution)/shard_map/pallas_call | solution.py:176
  62.9 1.2 %shard_map.71 = f32[2,8,128,128]{3,2,1,0:T(8,128)S(1)} custom-call(f32[8,16,640]{2,1,0:T(8,128)S(1)} %get-tuple-element.19.roots, bf16[8,128,640]{2,1,0:T(8,128)(2,1)S(1)} %copy-done.3, bf16[16,128,640]{2,1,0:T(8,128)(2,1)S(1)} %get-tuple-element.15.refs_8_.refs_1_, bf16[2,128,640]{2,1,0:T(8,128)(2,1)S(1)} %collective-permute-done.12.refs_2_, ...), custom_call_target="tpu_custom_call" | custom-call | flops 1000 | bytes 1000 | tf_op jit(solution)/shard_map/pallas_call | solution.py:176
  64.4 2.0 %collective-permute-start.14 = (f16[2,8,2,32,128]{4,3,1,0,2:T(8,128)(2,1)S(1)}, f16[2,8,2,32,128]{4,3,1,0,2:T(8,128)(2,1)S(1)}, u32[]{:S(2)}, u32[]{:S(2)}) collective-permute-start(f16[2,8,2,32,128]{4,3,1,0,2:T(8,128)(2,1)S(1)} %fusion.7), channel_id=1, source_target_pairs={{4,5},{5,4},{6,7},{7,6},{12,13},{13,12},{14,15},{15,14},{20,21},{2... | collective-permute-start | bytes 786440 | tf_op jit(solution)/shard_map/ppermute | solution.py:194
  66.6 2.8 %collective-permute-start.16 = (f16[2,8,1,32,128]{4,3,2,1,0:T(8,128)(2,1)S(1)}, f16[2,8,1,32,128]{4,3,2,1,0:T(8,128)(2,1)S(1)}, u32[]{:S(2)}, u32[]{:S(2)}) collective-permute-start(f16[2,8,1,32,128]{4,3,2,1,0:T(8,128)(2,1)S(1)} %fusion.10), channel_id=1, source_target_pairs={{0,2},{1,3},{2,0},{3,1},{4,6},{5,7},{6,4},{7,5},{8,10},{9,11},{10,... | collective-permute-start | bytes 393224 | tf_op jit(solution)/shard_map/ppermute | solution.py:194
  69.4 4.8 %collective-permute-done.14 = f16[2,8,2,32,128]{4,3,1,0,2:T(8,128)(2,1)S(1)} collective-permute-done((f16[2,8,2,32,128]{4,3,1,0,2:T(8,128)(2,1)S(1)}, f16[2,8,2,32,128]{4,3,1,0,2:T(8,128)(2,1)S(1)}, u32[]{:S(2)}, u32[]{:S(2)}) %collective-permute-start.14) | collective-permute-done | bytes 262176 | tf_op jit(solution)/shard_map/ppermute | solution.py:194
  74.3 1.9 %collective-permute-start.15 = (f16[2,8,1,32,128]{4,3,1,0,2:T(8,128)(2,1)S(1)}, f16[2,8,1,32,128]{4,3,1,0,2:T(8,128)(2,1)S(1)}, u32[]{:S(2)}, u32[]{:S(2)}) collective-permute-start(f16[2,8,1,32,128]{4,3,1,0,2:T(8,128)(2,1)S(1)} %multiply_convert_fusion), channel_id=1, source_target_pairs={{4,6},{5,7},{6,4},{7,5},{12,14},{13,15},{14,12},{15,13},{20,22},{2... | collective-permute-start | bytes 393224 | tf_op jit(solution)/shard_map/ppermute | solution.py:194
  76.3 5.0 %collective-permute-done.15 = f16[2,8,1,32,128]{4,3,1,0,2:T(8,128)(2,1)S(1)} collective-permute-done((f16[2,8,1,32,128]{4,3,1,0,2:T(8,128)(2,1)S(1)}, f16[2,8,1,32,128]{4,3,1,0,2:T(8,128)(2,1)S(1)}, u32[]{:S(2)}, u32[]{:S(2)}) %collective-permute-start.15) | collective-permute-done | bytes 131104 | tf_op jit(solution)/shard_map/ppermute | solution.py:194
  (64 shorter events, 6.8 us)
Async XLA Ops:
  0.0 11.2 %copy-start.13 = (s32[1,1,8,3,1]{2,4,3,1,0:T(1,128)S(1)}, s32[1,1,8,3,1]{2,4,3,1,0:T(1,128)}, u32[]{:S(2)}) copy-start(s32[1,1,8,3,1]{2,4,3,1,0:T(1,128)} %param.7) | copy-start | bytes 292
  0.0 2.1 %copy-start.7 = (bf16[1,1,8,3,1,128,640]{6,5,4,3,2,1,0:T(8,128)(2,1)S(1)}, bf16[1,1,8,3,1,128,640]{6,5,4,3,2,1,0:T(8,128)(2,1)}, u32[]{:S(2)}) copy-start(bf16[1,1,8,3,1,128,640]{6,5,4,3,2,1,0:T(8,128)(2,1)} %param.6) | copy-start | bytes 11796484
  2.1 17.1 %copy-start.8 = (f32[10240]{0:T(1024)S(1)}, f32[10240]{0:T(1024)}, u32[]{:S(2)}) copy-start(f32[10240]{0:T(1024)} %param.10) | copy-start | bytes 122884
  2.1 17.1 %copy-start.9 = (f32[8]{0:T(128)S(1)}, f32[8]{0:T(128)}, u32[]{:S(2)}) copy-start(f32[8]{0:T(128)} %refs_4_.1) | copy-start | bytes 100
  2.1 17.1 %copy-start.10 = (f32[2]{0:T(128)S(1)}, f32[2]{0:T(128)}, u32[]{:S(2)}) copy-start(f32[2]{0:T(128)} %refs_5_.1) | copy-start | bytes 28
  4.0 1.1 %copy-start = (bf16[8,128,640]{2,1,0:T(8,128)(2,1)}, bf16[8,128,640]{2,1,0:T(8,128)(2,1)S(1)}, u32[]{:S(2)}) copy-start(bf16[8,128,640]{2,1,0:T(8,128)(2,1)S(1)} %get-tuple-element.14.refs_7_.refs_0_) | copy-start | bytes 3932164
  5.1 17.8 %collective-permute-start.6 = (bf16[16,128,640]{2,1,0:T(8,128)(2,1)S(1)}, bf16[16,128,640]{2,1,0:T(8,128)(2,1)}, u32[]{:S(2)}, u32[]{:S(2)}) collective-permute-start(bf16[16,128,640]{2,1,0:T(8,128)(2,1)S(1)} %get-tuple-element.15.refs_8_.refs_1_), channel_id=1, source_target_pairs={{4,0},{12,8},{5,1},{13,9},{6,2},{14,10},{7,3},{15,11},{20,16},{28,... | collective-permute-start | bytes 7864328 | tf_op jit(solution)/shard_map/ppermute | solution.py:233
  8.6 8.9 %collective-permute-start.3 = (bf16[2,128,640]{2,1,0:T(8,128)(2,1)S(1)}, bf16[2,128,640]{2,1,0:T(8,128)(2,1)S(1)}, u32[]{:S(2)}, u32[]{:S(2)}) collective-permute-start(bf16[2,128,640]{2,1,0:T(8,128)(2,1)S(1)} %get-tuple-element.17), channel_id=1, source_target_pairs={{0,8},{4,12},{8,0},{12,4},{1,9},{5,13},{9,1},{13,5},{2,10},{6,14},... | collective-permute-start | bytes 983048 | tf_op jit(solution)/shard_map/ppermute | solution.py:229
  12.1 5.1 %collective-permute-start = (s32[25]{0:T(128)S(1)}, s32[25]{0:T(128)S(1)}, u32[]{:S(2)}, u32[]{:S(2)}) collective-permute-start(s32[25]{0:T(128)S(1)} %pad_add_fusion.refs_0_), channel_id=1, source_target_pairs={{0,4},{4,8},{8,12},{12,0},{1,5},{5,9},{9,13},{13,1},{2,6},{6,10},{... | collective-permute-start | bytes 308 | tf_op jit(solution)/shard_map/ppermute | solution.py:220
  12.1 5.3 %collective-permute-start.1 = (s32[25]{0:T(128)S(1)}, s32[25]{0:T(128)S(1)}, u32[]{:S(2)}, u32[]{:S(2)}) collective-permute-start(s32[25]{0:T(128)S(1)} %pad_add_fusion.refs_0_), channel_id=1, source_target_pairs={{0,8},{4,12},{8,0},{12,4},{1,9},{5,13},{9,1},{13,5},{2,10},{6,14},... | collective-permute-start | bytes 308 | tf_op jit(solution)/shard_map/ppermute | solution.py:220
  12.2 5.2 %collective-permute-start.2 = (s32[25]{0:T(128)S(1)}, s32[25]{0:T(128)S(1)}, u32[]{:S(2)}, u32[]{:S(2)}) collective-permute-start(s32[25]{0:T(128)S(1)} %pad_add_fusion.refs_0_), channel_id=1, source_target_pairs={{0,12},{4,0},{8,4},{12,8},{1,13},{5,1},{9,5},{13,9},{2,14},{6,2},{... | collective-permute-start | bytes 308 | tf_op jit(solution)/shard_map/ppermute | solution.py:220
  12.9 6.3 %copy-start.1 = (bf16[8,128,640]{2,1,0:T(8,128)(2,1)S(1)}, bf16[8,128,640]{2,1,0:T(8,128)(2,1)}, u32[]{:S(2)}) copy-start(bf16[8,128,640]{2,1,0:T(8,128)(2,1)} %copy-done) | copy-start | bytes 3932164
  17.4 23.7 %collective-permute-start.10 = (bf16[6,128,640]{2,1,0:T(8,128)(2,1)}, bf16[6,128,640]{2,1,0:T(8,128)(2,1)}, u32[]{:S(2)}, u32[]{:S(2)}) collective-permute-start(bf16[6,128,640]{2,1,0:T(8,128)(2,1)} %shard_map.65.refs_9_), channel_id=1, source_target_pairs={{0,8},{4,12},{8,0},{12,4},{1,9},{5,13},{9,1},{13,5},{2,10},{6,14},... | collective-permute-start | bytes 2949128 | tf_op jit(solution)/shard_map/ppermute | solution.py:231
  29.8 4.1 %collective-permute-start.7 = (f16[2,8,2,32,128]{4,3,1,0,2:T(8,128)(2,1)}, f16[2,8,2,32,128]{4,3,1,0,2:T(8,128)(2,1)S(1)}, u32[]{:S(2)}, u32[]{:S(2)}) collective-permute-start(f16[2,8,2,32,128]{4,3,1,0,2:T(8,128)(2,1)} %fusion.5), channel_id=1, source_target_pairs={{0,1},{1,0},{2,3},{3,2},{8,9},{9,8},{10,11},{11,10},{16,17},{17,16... | collective-permute-start | bytes 786440 | tf_op jit(solution)/shard_map/ppermute | solution.py:194
  31.2 6.8 %collective-permute-start.4 = (f16[2,8,2,32,128]{4,3,1,0,2:T(8,128)(2,1)}, f16[2,8,2,32,128]{4,3,1,0,2:T(8,128)(2,1)}, u32[]{:S(2)}, u32[]{:S(2)}) collective-permute-start(f16[2,8,2,32,128]{4,3,1,0,2:T(8,128)(2,1)} %fusion.4), channel_id=1, source_target_pairs={{0,1},{1,0},{2,3},{3,2},{4,5},{5,4},{6,7},{7,6},{8,9},{9,8},{10,11... | collective-permute-start | bytes 786440 | tf_op jit(solution)/shard_map/ppermute | solution.py:194
  32.5 27.9 %collective-permute-start.9 = (bf16[8,128,640]{2,1,0:T(8,128)(2,1)}, bf16[8,128,640]{2,1,0:T(8,128)(2,1)}, u32[]{:S(2)}, u32[]{:S(2)}) collective-permute-start(bf16[8,128,640]{2,1,0:T(8,128)(2,1)} %get-tuple-element.20), channel_id=1, source_target_pairs={{0,12},{8,4},{1,13},{9,5},{2,14},{10,6},{3,15},{11,7},{16,28},{24,... | collective-permute-start | bytes 3932168 | tf_op jit(solution)/shard_map/ppermute | solution.py:232
  41.1 1.3 %copy-start.2 = (bf16[8,128,640]{2,1,0:T(8,128)(2,1)S(1)}, bf16[8,128,640]{2,1,0:T(8,128)(2,1)}, u32[]{:S(2)}) copy-start(bf16[8,128,640]{2,1,0:T(8,128)(2,1)} %copy-done) | copy-start | bytes 3932164
  44.8 1.0 %copy-start.4 = (f32[2,8,128,128]{3,2,1,0:T(8,128)}, f32[2,8,128,128]{3,2,1,0:T(8,128)S(1)}, u32[]{:S(2)}) copy-start(f32[2,8,128,128]{3,2,1,0:T(8,128)S(1)} %shard_map.68.refs_2_.refs_4_) | copy-start | bytes 3145732
  45.8 1.2 %copy-start.5 = (f32[2,8,128,128]{3,2,1,0:T(8,128)S(1)}, f32[2,8,128,128]{3,2,1,0:T(8,128)}, u32[]{:S(2)}) copy-start(f32[2,8,128,128]{3,2,1,0:T(8,128)} %copy-done.4) | copy-start | bytes 3145732
  47.0 1.4 %copy-start.12 = (f32[2,8,2,1,32,128]{5,4,3,2,1,0:T(8,128)S(1)}, f32[2,8,2,1,32,128]{5,4,3,2,1,0:T(8,128)}, u32[]{:S(2)}) copy-start(f32[2,8,2,1,32,128]{5,4,3,2,1,0:T(8,128)} %get-tuple-element.30) | copy-start | bytes 1572868
  47.0 4.9 %copy-start.6 = (f32[2,8,128,128]{3,2,1,0:T(8,128)S(1)}, f32[2,8,128,128]{3,2,1,0:T(8,128)}, u32[]{:S(2)}) copy-start(f32[2,8,128,128]{3,2,1,0:T(8,128)} %copy-done.4) | copy-start | bytes 3145732
  47.0 6.4 %copy-start.11 = (f32[2,8,2,1,32,128]{5,4,3,2,1,0:T(8,128)S(1)}, f32[2,8,2,1,32,128]{5,4,3,2,1,0:T(8,128)}, u32[]{:S(2)}) copy-start(f32[2,8,2,1,32,128]{5,4,3,2,1,0:T(8,128)} %get-tuple-element.25) | copy-start | bytes 1572868
  47.0 15.9 %collective-permute-start.13 = (bf16[6,128,640]{2,1,0:T(8,128)(2,1)}, bf16[6,128,640]{2,1,0:T(8,128)(2,1)S(1)}, u32[]{:S(2)}, u32[]{:S(2)}) collective-permute-start(bf16[6,128,640]{2,1,0:T(8,128)(2,1)} %get-tuple-element.22), channel_id=1, source_target_pairs={{0,4},{8,12},{1,5},{9,13},{2,6},{10,14},{3,7},{11,15},{16,20},{24,... | collective-permute-start | bytes 2949128 | tf_op jit(solution)/shard_map/ppermute | solution.py:245
  48.5 12.0 %copy-start.3 = (bf16[8,128,640]{2,1,0:T(8,128)(2,1)S(1)}, bf16[8,128,640]{2,1,0:T(8,128)(2,1)}, u32[]{:S(2)}) copy-start(bf16[8,128,640]{2,1,0:T(8,128)(2,1)} %copy-done) | copy-start | bytes 3932164
  49.7 6.3 %collective-permute-start.5 = (f16[2,8,1,32,128]{4,3,1,0,2:T(8,128)(2,1)S(1)}, f16[2,8,1,32,128]{4,3,1,0,2:T(8,128)(2,1)S(1)}, u32[]{:S(2)}, u32[]{:S(2)}) collective-permute-start(f16[2,8,1,32,128]{4,3,1,0,2:T(8,128)(2,1)S(1)} %multiply_convert_fusion.2), channel_id=1, source_target_pairs={{0,2},{1,3},{2,0},{3,1},{4,6},{5,7},{6,4},{7,5},{8,10},{9,11},{10,... | collective-permute-start | bytes 393224 | tf_op jit(solution)/shard_map/ppermute | solution.py:194
  52.1 8.3 %collective-permute-start.11 = (f16[2,8,2,32,128]{4,3,2,1,0:T(8,128)(2,1)S(1)}, f16[2,8,2,32,128]{4,3,2,1,0:T(8,128)(2,1)S(1)}, u32[]{:S(2)}, u32[]{:S(2)}) collective-permute-start(f16[2,8,2,32,128]{4,3,2,1,0:T(8,128)(2,1)S(1)} %copy.24), channel_id=1, source_target_pairs={{0,1},{1,0},{2,3},{3,2},{4,5},{5,4},{6,7},{7,6},{8,9},{9,8},{10,11... | collective-permute-start | bytes 786440 | tf_op jit(solution)/shard_map/ppermute | solution.py:194
  53.6 22.7 %collective-permute-start.8 = (f16[2,8,1,32,128]{4,3,1,0,2:T(8,128)(2,1)S(1)}, f16[2,8,1,32,128]{4,3,1,0,2:T(8,128)(2,1)S(1)}, u32[]{:S(2)}, u32[]{:S(2)}) collective-permute-start(f16[2,8,1,32,128]{4,3,1,0,2:T(8,128)(2,1)S(1)} %multiply_convert_fusion.1), channel_id=1, source_target_pairs={{0,2},{1,3},{2,0},{3,1},{8,10},{9,11},{10,8},{11,9},{16,18},{17,19... | collective-permute-start | bytes 393224 | tf_op jit(solution)/shard_map/ppermute | solution.py:194
  56.0 7.0 %collective-permute-start.12 = (bf16[2,128,640]{2,1,0:T(8,128)(2,1)S(1)}, bf16[2,128,640]{2,1,0:T(8,128)(2,1)S(1)}, u32[]{:S(2)}, u32[]{:S(2)}) collective-permute-start(bf16[2,128,640]{2,1,0:T(8,128)(2,1)S(1)} %get-tuple-element.21), channel_id=1, source_target_pairs={{0,4},{8,12},{1,5},{9,13},{2,6},{10,14},{3,7},{11,15},{16,20},{24,... | collective-permute-start | bytes 983048 | tf_op jit(solution)/shard_map/ppermute | solution.py:245
  64.4 9.8 %collective-permute-start.14 = (f16[2,8,2,32,128]{4,3,1,0,2:T(8,128)(2,1)S(1)}, f16[2,8,2,32,128]{4,3,1,0,2:T(8,128)(2,1)S(1)}, u32[]{:S(2)}, u32[]{:S(2)}) collective-permute-start(f16[2,8,2,32,128]{4,3,1,0,2:T(8,128)(2,1)S(1)} %fusion.7), channel_id=1, source_target_pairs={{4,5},{5,4},{6,7},{7,6},{12,13},{13,12},{14,15},{15,14},{20,21},{2... | collective-permute-start | bytes 786440 | tf_op jit(solution)/shard_map/ppermute | solution.py:194
  66.6 9.7 %collective-permute-start.16 = (f16[2,8,1,32,128]{4,3,2,1,0:T(8,128)(2,1)S(1)}, f16[2,8,1,32,128]{4,3,2,1,0:T(8,128)(2,1)S(1)}, u32[]{:S(2)}, u32[]{:S(2)}) collective-permute-start(f16[2,8,1,32,128]{4,3,2,1,0:T(8,128)(2,1)S(1)} %fusion.10), channel_id=1, source_target_pairs={{0,2},{1,3},{2,0},{3,1},{4,6},{5,7},{6,4},{7,5},{8,10},{9,11},{10,... | collective-permute-start | bytes 393224 | tf_op jit(solution)/shard_map/ppermute | solution.py:194
  74.3 7.0 %collective-permute-start.15 = (f16[2,8,1,32,128]{4,3,1,0,2:T(8,128)(2,1)S(1)}, f16[2,8,1,32,128]{4,3,1,0,2:T(8,128)(2,1)S(1)}, u32[]{:S(2)}, u32[]{:S(2)}) collective-permute-start(f16[2,8,1,32,128]{4,3,1,0,2:T(8,128)(2,1)S(1)} %multiply_convert_fusion), channel_id=1, source_target_pairs={{4,6},{5,7},{6,4},{7,5},{12,14},{13,15},{14,12},{15,13},{20,22},{2... | collective-permute-start | bytes 393224 | tf_op jit(solution)/shard_map/ppermute | solution.py:194

commit v8 on v7

--- a/solution.py
+++ b/solution.py
@@ -8,7 +8,7 @@
 from jax.sharding import PartitionSpec as P
 
 LIMIT = 16 << 20
-SPLIT = (2, 6)
+SPLIT = (1, 7)
 COST = pl.CostEstimate(flops=1000, bytes_accessed=1000, transcendentals=0)
 PARAMS = pltpu.CompilerParams(vmem_limit_bytes=LIMIT)
 ANY = pl.BlockSpec(memory_space=pl.ANY)
@@ -83,7 +83,7 @@
     n_aux, n_pair, blocks_dev, band, freq_count = dims
     records = refs[:n_aux]
     occ, freq, table = refs[n_aux : n_aux + 3]
-    own = refs[n_aux + 3 : n_aux + 5]
+    own, far = refs[n_aux + 3 : n_aux + 5], refs[n_aux + 5]
     out, roots = refs[-2:]
     pair_rows = own[0].shape[-1]
     virt_blocks = table.shape[1] // pair_rows
@@ -95,7 +95,7 @@
             live = jnp.where(lax.rem(aux_pos - region + n_aux, n_aux) == k, records[k][blocks_dev * band], live)
         return live
 
-    masked = {}
+    masked, plain, one = {}, {}, {}
     for m in range(blocks_dev):
         block = m * n_aux + aux_pos
         for slot in range(band):
@@ -112,12 +112,16 @@
                 root = jnp.sqrt(2.0 * gap / (gap * gap + omega * omega))
                 roots[m, pl.ds(root_row(band, freq_count, None, slot, w), 1), :] = root
                 masked[m, slot, w] = root * alive.astype(jnp.float32)
+                plain[m, slot, w] = root
                 for delta in range(1, band - slot):
                     there = m + ((aux_pos + delta) >= n_aux).astype(jnp.int32)
                     row = jnp.minimum(there, blocks_dev - 1) * band + slot + delta
                     both = alive & (there < blocks_dev) & (records[(n_aux - delta) % n_aux][row] > 0)
                     spot = root_row(band, freq_count, delta, slot, w)
-                    roots[m, pl.ds(spot, 1), :] = root * both.astype(jnp.float32)
+                    kept = root * both.astype(jnp.float32)
+                    roots[m, pl.ds(spot, 1), :] = kept
+                    if delta == 1:
+                        one[m, slot, w] = kept
     for m in range(blocks_dev):
         for w in range(freq_count):
             total = None
@@ -125,23 +129,30 @@
                 a = (own_tile(own, slot, m, blocks_dev).astype(jnp.float32) * masked[m, slot, w]).astype(jnp.bfloat16)
                 term = dot(a, a)
                 total = term if total is None else total + term
-            out[w, m] = total
-
-
-def first_rows(dims, records, occ, freq, table, own, after):
+            out[w, m, :, : total.shape[1]] = total
+            total = None
+            for slot in range(band - 1):
+                a = (own_tile(own, slot, m, blocks_dev).astype(jnp.float32) * one[m, slot, w]).astype(jnp.bfloat16)
+                b = (far[slot * blocks_dev + m].astype(jnp.float32) * plain[m, slot, w]).astype(jnp.bfloat16)
+                term = dot(a, b)
+                total = term if total is None else total + term
+            out[w, m, :, total.shape[1] :] = total
+
+
+def first_rows(dims, records, occ, freq, table, own, far, after):
     n_aux, n_pair, blocks_dev, band, freq_count = dims
     aux_rows, pair_rows = own[0].shape[-2:]
     return pl.pallas_call(
         functools.partial(first_kernel, dims),
         out_shape=[
-            jax.ShapeDtypeStruct((freq_count, blocks_dev, aux_rows, aux_rows), jnp.float32),
+            jax.ShapeDtypeStruct((freq_count, blocks_dev, aux_rows, 2 * aux_rows), jnp.float32),
             jax.ShapeDtypeStruct((blocks_dev, root_rows(band, freq_count), pair_rows), jnp.float32),
         ],
-        in_specs=[SMEM] * (n_aux + 2) + [VMEM] * 3 + [ANY] * len(after),
+        in_specs=[SMEM] * (n_aux + 2) + [VMEM] * 4 + [ANY] * len(after),
         out_specs=[VMEM, VMEM],
         compiler_params=PARAMS,
         cost_estimate=COST,
-    )(*records, occ, freq, table, *own, *after)
+    )(*records, occ, freq, table, *own, far, *after)
 
 
 def band_kernel(dims, delta, slots, rights, add, roots, *refs):
@@ -186,9 +197,14 @@
 def halve(keep, pair_col, step, n_pair, rings, scale):
     freq_count, count, shares, height, width = keep.shape
     keep = keep.reshape(freq_count, count, shares // 2, 2, height, width)
-    bit = (pair_col // step) & 1
-    part = lax.dynamic_index_in_dim(keep, 1 - bit, 3, keepdims=False)
-    mine = lax.dynamic_index_in_dim(keep, bit, 3, keepdims=False)
+    bit = lax.shift_right_logical(pair_col, jnp.uint32(step.bit_length() - 1)) & jnp.uint32(1)
+
+    def pick(which):
+        zero = jnp.uint32(0)
+        sizes = (freq_count, count, shares // 2, 1, height, width)
+        return lax.dynamic_slice(keep, [zero, zero, zero, which, zero, zero], sizes)[:, :, :, 0]
+
+    part, mine = pick(bit ^ jnp.uint32(1)), pick(bit)
     sent = (part * scale).astype(jnp.float16)
     pairs = [(ring * n_pair + s, ring * n_pair + (s ^ step)) for ring in rings for s in range(n_pair)]
     got = lax.ppermute(sent, ("aux", "pair"), pairs)
@@ -209,7 +225,7 @@
 def on_device(three_centre, locality, live_blocks, occ_energy, virt_energy, frequencies):
     n_aux = lax.axis_size("aux")
     n_pair = lax.axis_size("pair")
-    pair_col = lax.axis_index("pair").astype(jnp.uint32).astype(jnp.int32)
+    pair_col = lax.axis_index("pair").astype(jnp.uint32)
     tiles = three_centre[0, 0, :, :, 0]
     blocks_dev, band, aux_rows, pair_rows = tiles.shape
     freq_count = frequencies.shape[0]
@@ -232,22 +248,21 @@
     b1 = lax.ppermute(to_one, "aux", [(s, (s - 1) % n_aux) for s in evens])
     to_even = lax.ppermute(rest, "aux", [(s, s - 1) for s in odds])
     table = virt_energy.reshape(1, -1)
-    rows0, roots = first_rows(dims, records, occ_energy, frequencies, table, own, [far_two])
+    rows0, roots = first_rows(dims, records, occ_energy, frequencies, table, own, to_even, [far_two])
 
     def rows_of(delta, slots, far, after, add=None):
         return band_rows(dims, delta, slots, roots, own, far, after, add)
 
     z0 = totals(rows0, pair_col, n_pair, whole, scale)
-    rows_even = rows_of(1, [0, 1], [[to_even], [to_even]], [rows0])
-    z_even = totals(rows_even, pair_col, n_pair, evens, scale)
-    rows2 = rows_of(2, [0], [c2], [z0[0], z_even[0]])
+    rows2 = rows_of(2, [0], [c2], [z0[0]])
     z2 = totals(rows2, pair_col, n_pair, whole, scale)
     to_odd = [lax.ppermute(c, "aux", [(s, s + 1) for s in evens]) for c in tie(c2, [rows2])]
     part = rows_of(1, [1], [to_odd], [rows2])
     rows_odd = rows_of(1, [0], [[b1]], [z2[0]])
     z_odd = totals(rows_odd + part, pair_col, n_pair, odds, scale)
-    even = lax.axis_index("aux") % 2 == 0
-    out = jnp.concatenate([z0[1], jnp.where(even, z_even[1], z_odd[1]), z2[1]], axis=-1)
+    even = lax.axis_index("aux").astype(jnp.uint32) & jnp.uint32(1) == 0
+    one = jnp.where(even, z0[1][..., aux_rows:], z_odd[1])
+    out = jnp.concatenate([z0[1][..., :aux_rows], one, z2[1]], axis=-1)
     return out[:, :, None]
 
 

time: 82.9 us -> 80.9 us (0.976)
  local copies, waits for them, and re-layouts: 8.3 us -> 5.77 us
  waiting for transfers between devices: 25.6 us -> 26.9 us
  other arithmetic: 5.25 us -> 4.33 us
    pallas_call x4 -> x3, Pallas kernels: 11 us -> 7.41 us  [band_rows(): pl.pallas_call(functools.partial(band_kernel, dims, delta, slots, rights,...]
    pallas_call x1, Pallas kernels: 3.66 us -> 6.7 us  [first_rows(): pl.pallas_call(functools.partial(first_kernel, dims), out_shape=[jax.Shap...]
    unnamed x29 -> x25, local copies, waits for them, and re-layouts: 6.88 us -> 4.38 us
    ppermute x1, waiting for transfers between devices: 0.01 us -> 2.38 us  [on_device(): b1 = lax.ppermute(to_one, 'aux', [(s, (s - 1) % n_aux) for s in evens])]
    ppermute x3, waiting for transfers between devices: 4.5 us -> 2.57 us  [on_device(): lax.ppermute(record, 'aux', [(s, (s + k) % n_aux) for s in range(n_aux)])]
    ppermute x8 -> x6, starting transfers between devices: 13 us -> 14.2 us  [halve(): got = lax.ppermute(sent, ('aux', 'pair'), pairs)]
    ppermute x1, waiting for transfers between devices: 2.39 us -> 3.45 us  [on_device(): c2.append(lax.ppermute(far_two, 'aux', down2))]
    convert_element_type x8 -> x6, other arithmetic: 1.83 us -> 1.45 us  [halve(): sent = (part * scale).astype(jnp.float16)]
  transfers between devices with their start and end apart: 17 -> 15, of which waited for: 8 -> 9; matrix products, arithmetic and copies ran while one was open for 7% -> 6% of each run, Pallas kernels for 18% -> 18%
where the time goes in v8:
time: 80.9 us; the launch traced here: 80.4 us
  waiting for transfers between devices  26.9 us (33%)
  starting transfers between devices  26.3 us (33%)
  Pallas kernels  16.1 us (20%)
  local copies, waits for them, and re-layouts  5.77 us (7%)
  other arithmetic  4.33 us (5%)
  between operations  0.95 us (1%)
    ppermute x6, waiting for transfers between devices, halve(): got = lax.ppermute(sent, ('aux', 'pair'), pairs)  18.5 us
    ppermute x6, starting transfers between devices, halve(): got = lax.ppermute(sent, ('aux', 'pair'), pairs)  14.2 us
    pallas_call x3, Pallas kernels, band_rows(): pl.pallas_call(functools.partial(band_kernel, dims, delta, slots, rights,...  7.41 us
    pallas_call x1, Pallas kernels, first_rows(): pl.pallas_call(functools.partial(first_kernel, dims), out_shape=[jax.Shap...  6.7 us
    unnamed x25, local copies, waits for them, and re-layouts  4.38 us
    ppermute x1, starting transfers between devices, on_device(): to_even = lax.ppermute(rest, 'aux', [(s, s - 1) for s in odds])  3.57 us
    ppermute x1, waiting for transfers between devices, on_device(): c2.append(lax.ppermute(far_two, 'aux', down2))  3.45 us
    ppermute x2, starting transfers between devices, on_device(): lax.ppermute(c, 'aux', [(s, s + 1) for s in evens])  2.7 us
  transfers between devices with their start and end apart: 15, of which 9 were waited for; matrix products, arithmetic and copies ran while one was open for 6% of the time, Pallas kernels for 18%

profile of v8, /device:TPU:1, one launch (start us, length us, event | category | flops | bytes accessed | tf_op | source)
XLA Modules:
  0.0 80.4 jit_solution(7408986459512150525)
XLA Ops:
  0.0 2.1 %copy-done.5 = bf16[1,1,8,3,1,128,640]{6,5,4,3,2,1,0:T(8,128)(2,1)S(1)} copy-done((bf16[1,1,8,3,1,128,640]{6,5,4,3,2,1,0:T(8,128)(2,1)S(1)}, bf16[1,1,8,3,1,128,640]{6,5,4,3,2,1,0:T(8,128)(2,1)}, u32[]{:S(2)}) %copy-start.5) | copy-done | bytes 3932184
  2.1 1.9 %shard_map.64 = (bf16[8,128,640]{2,1,0:T(8,128)(2,1)S(1)}, bf16[16,128,640]{2,1,0:T(8,128)(2,1)S(1)}, bf16[1,128,640]{2,1,0:T(8,128)(2,1)S(1)}, bf16[7,128,640]{2,1,0:T(8,128)(2,1)}, bf16[8,128,640]{2,1,0:T(8,128)(2,1)}) custom-call(bf16[8,3,128,640]{3,2,1,0:T(8,128)(2,1)S(1)} %bitcast.55), custom_call_target="tpu_custom_call" | custom-call | flops 1000 | bytes 1000 | tf_op jit(solution)/shard_map/pallas_call | solution.py:46
  4.1 1.1 %copy-done = bf16[8,128,640]{2,1,0:T(8,128)(2,1)} copy-done((bf16[8,128,640]{2,1,0:T(8,128)(2,1)}, bf16[8,128,640]{2,1,0:T(8,128)(2,1)S(1)}, u32[]{:S(2)}) %copy-start) | copy-done | bytes 1310744
  5.1 3.6 %collective-permute-start.3 = (bf16[16,128,640]{2,1,0:T(8,128)(2,1)S(1)}, bf16[16,128,640]{2,1,0:T(8,128)(2,1)}, u32[]{:S(2)}, u32[]{:S(2)}) collective-permute-start(bf16[16,128,640]{2,1,0:T(8,128)(2,1)S(1)} %get-tuple-element.15.refs_8_.refs_1_), channel_id=1, source_target_pairs={{4,0},{12,8},{5,1},{13,9},{6,2},{14,10},{7,3},{15,11},{20,16},{28,... | collective-permute-start | bytes 7864328 | tf_op jit(solution)/shard_map/ppermute | solution.py:249
  8.7 2.7 %collective-permute-start.4 = (bf16[1,128,640]{2,1,0:T(8,128)(2,1)S(1)}, bf16[1,128,640]{2,1,0:T(8,128)(2,1)S(1)}, u32[]{:S(2)}, u32[]{:S(2)}) collective-permute-start(bf16[1,128,640]{2,1,0:T(8,128)(2,1)S(1)} %get-tuple-element.17), channel_id=1, source_target_pairs={{0,8},{4,12},{8,0},{12,4},{1,9},{5,13},{9,1},{13,5},{2,10},{6,14},... | collective-permute-start | bytes 491528 | tf_op jit(solution)/shard_map/ppermute | solution.py:245
  13.1 0.8 collective-permute-done.refs_1_
  13.9 0.9 %collective-permute-done.1.refs_2_ = s32[25]{0:T(128)S(1)} collective-permute-done((s32[25]{0:T(128)S(1)}, s32[25]{0:T(128)S(1)}, u32[]{:S(2)}, u32[]{:S(2)}) %collective-permute-start.1) | collective-permute-done | bytes 132 | tf_op jit(solution)/shard_map/ppermute | solution.py:236
  14.7 0.9 %collective-permute-done.2.refs_3_ = s32[25]{0:T(128)S(1)} collective-permute-done((s32[25]{0:T(128)S(1)}, s32[25]{0:T(128)S(1)}, u32[]{:S(2)}, u32[]{:S(2)}) %collective-permute-start.2) | collective-permute-done | bytes 132 | tf_op jit(solution)/shard_map/ppermute | solution.py:236
  15.6 1.1 %collective-permute-start.8 = (bf16[7,128,640]{2,1,0:T(8,128)(2,1)}, bf16[7,128,640]{2,1,0:T(8,128)(2,1)}, u32[]{:S(2)}, u32[]{:S(2)}) collective-permute-start(bf16[7,128,640]{2,1,0:T(8,128)(2,1)} %shard_map.65.refs_10_), channel_id=1, source_target_pairs={{0,8},{4,12},{8,0},{12,4},{1,9},{5,13},{9,1},{13,5},{2,10},{6,14},... | collective-permute-start | bytes 3440648 | tf_op jit(solution)/shard_map/ppermute | solution.py:247
  16.8 6.7 %shard_map.66 = (f32[2,8,128,256]{3,2,1,0:T(8,128)S(1)}, f32[8,16,640]{2,1,0:T(8,128)S(1)}) custom-call(s32[25]{0:T(128)S(1)} %pad_add_fusion.refs_0_, s32[25]{0:T(128)S(1)} %collective-permute-done.refs_1_, s32[25]{0:T(128)S(1)} %collective-permute-done.1.refs_2_, s32[25]{0:T(128)S(1)} %collective-permute-done.2.refs_3_, f32[8]{0:T(128)S(1)} %copy-done.7, ...), custom_call_target="tpu_custom_call" | custom-call | flops 1000 | bytes 1000 | tf_op jit(solution)/shard_map/pallas_call | solution.py:145
  23.5 1.2 %constant_dynamic-slice_fusion.4 = (f32[2,8,2,1,32,256]{5,4,3,2,1,0:T(8,128)}, f32[2,8,2,1,32,256]{5,4,3,2,1,0:T(8,128)S(1)}) fusion(f32[2,8,2,2,32,256]{5,4,3,2,1,0:T(8,128)S(1)} %bitcast.56, u32[]{:T(128)S(6)} %and.15, u32[]{:T(128)S(6)} %xor.4), kind=kLoop, calls=%fused_computation.30 | loop fusion | bytes 4194312 | tf_op jit(solution)/shard_map/dynamic_slice | solution.py:205
  24.8 1.4 %collective-permute-start.5 = (f16[2,8,2,32,256]{4,3,1,0,2:T(8,128)(2,1)S(1)}, f16[2,8,2,32,256]{4,3,1,0,2:T(8,128)(2,1)S(1)}, u32[]{:S(2)}, u32[]{:S(2)}) collective-permute-start(f16[2,8,2,32,256]{4,3,1,0,2:T(8,128)(2,1)S(1)} %fusion.1), channel_id=1, source_target_pairs={{0,1},{1,0},{2,3},{3,2},{4,5},{5,4},{6,7},{7,6},{8,9},{9,8},{10,11... | collective-permute-start | bytes 1572872 | tf_op jit(solution)/shard_map/ppermute | solution.py:210
  26.2 1.3 %collective-permute-start.7 = (bf16[8,128,640]{2,1,0:T(8,128)(2,1)}, bf16[8,128,640]{2,1,0:T(8,128)(2,1)}, u32[]{:S(2)}, u32[]{:S(2)}) collective-permute-start(bf16[8,128,640]{2,1,0:T(8,128)(2,1)} %get-tuple-element.20), channel_id=1, source_target_pairs={{0,12},{8,4},{1,13},{9,5},{2,14},{10,6},{3,15},{11,7},{16,28},{24,... | collective-permute-start | bytes 3932168 | tf_op jit(solution)/shard_map/ppermute | solution.py:248
  27.5 11.1 %collective-permute-done.5 = f16[2,8,2,32,256]{4,3,1,0,2:T(8,128)(2,1)S(1)} collective-permute-done((f16[2,8,2,32,256]{4,3,1,0,2:T(8,128)(2,1)S(1)}, f16[2,8,2,32,256]{4,3,1,0,2:T(8,128)(2,1)S(1)}, u32[]{:S(2)}, u32[]{:S(2)}) %collective-permute-start.5) | collective-permute-done | bytes 524320 | tf_op jit(solution)/shard_map/ppermute | solution.py:210
  38.6 3.4 %collective-permute-done.8.refs_3_.refs_1_ = bf16[7,128,640]{2,1,0:T(8,128)(2,1)} collective-permute-done((bf16[7,128,640]{2,1,0:T(8,128)(2,1)}, bf16[7,128,640]{2,1,0:T(8,128)(2,1)}, u32[]{:S(2)}, u32[]{:S(2)}) %collective-permute-start.8) | collective-permute-done | bytes 1146912 | tf_op jit(solution)/shard_map/ppermute | solution.py:247
  42.0 2.5 %shard_map.67.refs_2_.refs_4_ = f32[2,8,128,128]{3,2,1,0:T(8,128)S(1)} custom-call(f32[8,16,640]{2,1,0:T(8,128)S(1)} %get-tuple-element.19.roots, bf16[8,128,640]{2,1,0:T(8,128)(2,1)S(1)} %copy-done.1, bf16[16,128,640]{2,1,0:T(8,128)(2,1)S(1)} %get-tuple-element.15.refs_8_.refs_1_, bf16[1,128,640]{2,1,0:T(8,128)(2,1)S(1)} %collective-permute-done.4.refs_4_.refs_2_.refs_0_, ...), custom_call_target="tpu_custom_call" | custom-call | flops 1000 | bytes 1000 | tf_op jit(solution)/shard_map/pallas_call | solution.py:187
  44.5 1.1 %copy-done.3 = f32[2,8,128,128]{3,2,1,0:T(8,128)} copy-done((f32[2,8,128,128]{3,2,1,0:T(8,128)}, f32[2,8,128,128]{3,2,1,0:T(8,128)S(1)}, u32[]{:S(2)}) %copy-start.3) | copy-done | bytes 1048600
  45.6 1.3 %collective-permute-start.11 = (bf16[7,128,640]{2,1,0:T(8,128)(2,1)}, bf16[7,128,640]{2,1,0:T(8,128)(2,1)}, u32[]{:S(2)}, u32[]{:S(2)}) collective-permute-start(bf16[7,128,640]{2,1,0:T(8,128)(2,1)} %get-tuple-element.22), channel_id=1, source_target_pairs={{0,4},{8,12},{1,5},{9,13},{2,6},{10,14},{3,7},{11,15},{16,20},{24,... | collective-permute-start | bytes 3440648 | tf_op jit(solution)/shard_map/ppermute | solution.py:259
  46.9 1.4 %collective-permute-start.10 = (bf16[1,128,640]{2,1,0:T(8,128)(2,1)S(1)}, bf16[1,128,640]{2,1,0:T(8,128)(2,1)S(1)}, u32[]{:S(2)}, u32[]{:S(2)}) collective-permute-start(bf16[1,128,640]{2,1,0:T(8,128)(2,1)S(1)} %get-tuple-element.21), channel_id=1, source_target_pairs={{0,4},{8,12},{1,5},{9,13},{2,6},{10,14},{3,7},{11,15},{16,20},{24,... | collective-permute-start | bytes 491528 | tf_op jit(solution)/shard_map/ppermute | solution.py:259
  48.3 1.1 %fusion.4 = f16[2,8,2,32,128]{4,3,1,0,2:T(8,128)(2,1)S(1)} fusion(f32[2,8,2,2,32,128]{5,4,3,2,1,0:T(8,128)} %bitcast.53, u32[]{:T(128)S(6)} %xor.4), kind=kLoop, calls=%fused_computation.13 | loop fusion | flops 262144 | bytes 786436 | tf_op jit(solution)/shard_map/convert_element_type | solution.py:208
  49.5 1.4 %collective-permute-start.9 = (f16[2,8,2,32,128]{4,3,2,1,0:T(8,128)(2,1)S(1)}, f16[2,8,2,32,128]{4,3,2,1,0:T(8,128)(2,1)S(1)}, u32[]{:S(2)}, u32[]{:S(2)}) collective-permute-start(f16[2,8,2,32,128]{4,3,2,1,0:T(8,128)(2,1)S(1)} %copy.22), channel_id=1, source_target_pairs={{0,1},{1,0},{2,3},{3,2},{4,5},{5,4},{6,7},{7,6},{8,9},{9,8},{10,11... | collective-permute-start | bytes 786440 | tf_op jit(solution)/shard_map/ppermute | solution.py:210
  50.9 1.3 %bitcast_add_fusion = f32[2,8,2,32,256]{4,3,1,0,2:T(8,128)S(1)} fusion(f32[2,8,2,1,32,256]{5,4,3,2,1,0:T(8,128)S(1)} %copy-done.9, f16[2,8,2,32,256]{4,3,1,0,2:T(8,128)(2,1)} %copy-done.10), kind=kLoop, calls=%fused_computation.2 | loop fusion | flops 786432 | bytes 2621440 | tf_op jit(solution)/shard_map/add | solution.py:211
  52.3 2.4 %collective-permute-start.6 = (f16[2,8,1,32,256]{4,3,1,0,2:T(8,128)(2,1)S(1)}, f16[2,8,1,32,256]{4,3,1,0,2:T(8,128)(2,1)S(1)}, u32[]{:S(2)}, u32[]{:S(2)}) collective-permute-start(f16[2,8,1,32,256]{4,3,1,0,2:T(8,128)(2,1)S(1)} %multiply_convert_fusion), channel_id=1, source_target_pairs={{0,2},{1,3},{2,0},{3,1},{4,6},{5,7},{6,4},{7,5},{8,10},{9,11},{10,... | collective-permute-start | bytes 786440 | tf_op jit(solution)/shard_map/ppermute | solution.py:210
  54.8 2.4 %collective-permute-done.7.refs_2_ = bf16[8,128,640]{2,1,0:T(8,128)(2,1)} collective-permute-done((bf16[8,128,640]{2,1,0:T(8,128)(2,1)}, bf16[8,128,640]{2,1,0:T(8,128)(2,1)}, u32[]{:S(2)}, u32[]{:S(2)}) %collective-permute-start.7) | collective-permute-done | bytes 1310752 | tf_op jit(solution)/shard_map/ppermute | solution.py:248
  57.2 2.5 %shard_map.68 = f32[2,8,128,128]{3,2,1,0:T(8,128)S(1)} custom-call(f32[8,16,640]{2,1,0:T(8,128)S(1)} %get-tuple-element.19.roots, bf16[8,128,640]{2,1,0:T(8,128)(2,1)S(1)} %copy-done.2, bf16[16,128,640]{2,1,0:T(8,128)(2,1)S(1)} %get-tuple-element.15.refs_8_.refs_1_, bf16[8,128,640]{2,1,0:T(8,128)(2,1)} %collective-permute-done.7.refs_2_, ...), custom_call_target="tpu_custom_call" | custom-call | flops 1000 | bytes 1000 | tf_op jit(solution)/shard_map/pallas_call | solution.py:187
  59.8 2.4 %shard_map.70 = f32[2,8,128,128]{3,2,1,0:T(8,128)S(1)} custom-call(f32[8,16,640]{2,1,0:T(8,128)S(1)} %get-tuple-element.19.roots, bf16[8,128,640]{2,1,0:T(8,128)(2,1)S(1)} %copy-done.2, bf16[16,128,640]{2,1,0:T(8,128)(2,1)S(1)} %get-tuple-element.15.refs_8_.refs_1_, bf16[1,128,640]{2,1,0:T(8,128)(2,1)S(1)} %collective-permute-done.10.refs_2_, ...), custom_call_target="tpu_custom_call" | custom-call | flops 1000 | bytes 1000 | tf_op jit(solution)/shard_map/pallas_call | solution.py:187
  62.6 3.2 %collective-permute-start.12 = (f16[2,8,2,32,128]{4,3,1,0,2:T(8,128)(2,1)S(1)}, f16[2,8,2,32,128]{4,3,1,0,2:T(8,128)(2,1)S(1)}, u32[]{:S(2)}, u32[]{:S(2)}) collective-permute-start(f16[2,8,2,32,128]{4,3,1,0,2:T(8,128)(2,1)S(1)} %fusion.5), channel_id=1, source_target_pairs={{4,5},{5,4},{6,7},{7,6},{12,13},{13,12},{14,15},{15,14},{20,21},{2... | collective-permute-start | bytes 786440 | tf_op jit(solution)/shard_map/ppermute | solution.py:210
  65.8 2.4 %collective-permute-start.14 = (f16[2,8,1,32,128]{4,3,2,1,0:T(8,128)(2,1)S(1)}, f16[2,8,1,32,128]{4,3,2,1,0:T(8,128)(2,1)S(1)}, u32[]{:S(2)}, u32[]{:S(2)}) collective-permute-start(f16[2,8,1,32,128]{4,3,2,1,0:T(8,128)(2,1)S(1)} %fusion.8), channel_id=1, source_target_pairs={{0,2},{1,3},{2,0},{3,1},{4,6},{5,7},{6,4},{7,5},{8,10},{9,11},{10,... | collective-permute-start | bytes 393224 | tf_op jit(solution)/shard_map/ppermute | solution.py:210
  68.3 2.9 %collective-permute-done.12 = f16[2,8,2,32,128]{4,3,1,0,2:T(8,128)(2,1)S(1)} collective-permute-done((f16[2,8,2,32,128]{4,3,1,0,2:T(8,128)(2,1)S(1)}, f16[2,8,2,32,128]{4,3,1,0,2:T(8,128)(2,1)S(1)}, u32[]{:S(2)}, u32[]{:S(2)}) %collective-permute-start.12) | collective-permute-done | bytes 262176 | tf_op jit(solution)/shard_map/ppermute | solution.py:210
  71.3 3.5 %collective-permute-start.13 = (f16[2,8,1,32,128]{4,3,1,0,2:T(8,128)(2,1)S(1)}, f16[2,8,1,32,128]{4,3,1,0,2:T(8,128)(2,1)S(1)}, u32[]{:S(2)}, u32[]{:S(2)}) collective-permute-start(f16[2,8,1,32,128]{4,3,1,0,2:T(8,128)(2,1)S(1)} %multiply_convert_fusion.1), channel_id=1, source_target_pairs={{4,6},{5,7},{6,4},{7,5},{12,14},{13,15},{14,12},{15,13},{20,22},{2... | collective-permute-start | bytes 393224 | tf_op jit(solution)/shard_map/ppermute | solution.py:210
  74.9 4.4 %collective-permute-done.13 = f16[2,8,1,32,128]{4,3,1,0,2:T(8,128)(2,1)S(1)} collective-permute-done((f16[2,8,1,32,128]{4,3,1,0,2:T(8,128)(2,1)S(1)}, f16[2,8,1,32,128]{4,3,1,0,2:T(8,128)(2,1)S(1)}, u32[]{:S(2)}, u32[]{:S(2)}) %collective-permute-start.13) | collective-permute-done | bytes 131104 | tf_op jit(solution)/shard_map/ppermute | solution.py:210
  79.4 0.9 %maximum_bitcast_fusion = f32[2,8,1,32,384]{4,3,2,1,0:T(8,128)} fusion(f32[2,8,32,128]{3,2,1,0:T(8,128)S(1)} %fusion.7, f32[2,8,32,128]{3,2,1,0:T(8,128)S(1)} %get-tuple-element.28, f32[2,8,32,128]{3,2,1,0:T(8,128)S(1)} %get-tuple-element.27), kind=kLoop, calls=%fused_computation.3 | loop fusion | flops 393216 | bytes 1572864 | tf_op jit(solution)/shard_map/broadcast_in_dim | solution.py:266
  (51 shorter events, 2.2 us)
Async XLA Ops:
  0.0 2.1 %copy-start.5 = (bf16[1,1,8,3,1,128,640]{6,5,4,3,2,1,0:T(8,128)(2,1)S(1)}, bf16[1,1,8,3,1,128,640]{6,5,4,3,2,1,0:T(8,128)(2,1)}, u32[]{:S(2)}) copy-start(bf16[1,1,8,3,1,128,640]{6,5,4,3,2,1,0:T(8,128)(2,1)} %param.6) | copy-start | bytes 11796484
  2.1 9.3 %copy-start.11 = (s32[1,1,8,3,1]{2,4,3,1,0:T(1,128)S(1)}, s32[1,1,8,3,1]{2,4,3,1,0:T(1,128)}, u32[]{:S(2)}) copy-start(s32[1,1,8,3,1]{2,4,3,1,0:T(1,128)} %param.7) | copy-start | bytes 292
  4.1 1.1 %copy-start = (bf16[8,128,640]{2,1,0:T(8,128)(2,1)}, bf16[8,128,640]{2,1,0:T(8,128)(2,1)S(1)}, u32[]{:S(2)}) copy-start(bf16[8,128,640]{2,1,0:T(8,128)(2,1)S(1)} %get-tuple-element.14.refs_7_.refs_0_) | copy-start | bytes 3932164
  5.1 11.6 %copy-start.6 = (f32[10240]{0:T(1024)S(1)}, f32[10240]{0:T(1024)}, u32[]{:S(2)}) copy-start(f32[10240]{0:T(1024)} %param.10) | copy-start | bytes 122884
  5.1 11.6 %copy-start.7 = (f32[8]{0:T(128)S(1)}, f32[8]{0:T(128)}, u32[]{:S(2)}) copy-start(f32[8]{0:T(128)} %refs_4_.1) | copy-start | bytes 100
  5.1 11.7 %copy-start.8 = (f32[2]{0:T(128)S(1)}, f32[2]{0:T(128)}, u32[]{:S(2)}) copy-start(f32[2]{0:T(128)} %refs_5_.1) | copy-start | bytes 28
  5.1 11.6 %collective-permute-start.3 = (bf16[16,128,640]{2,1,0:T(8,128)(2,1)S(1)}, bf16[16,128,640]{2,1,0:T(8,128)(2,1)}, u32[]{:S(2)}, u32[]{:S(2)}) collective-permute-start(bf16[16,128,640]{2,1,0:T(8,128)(2,1)S(1)} %get-tuple-element.15.refs_8_.refs_1_), channel_id=1, source_target_pairs={{4,0},{12,8},{5,1},{13,9},{6,2},{14,10},{7,3},{15,11},{20,16},{28,... | collective-permute-start | bytes 7864328 | tf_op jit(solution)/shard_map/ppermute | solution.py:249
  8.7 6.9 %collective-permute-start.4 = (bf16[1,128,640]{2,1,0:T(8,128)(2,1)S(1)}, bf16[1,128,640]{2,1,0:T(8,128)(2,1)S(1)}, u32[]{:S(2)}, u32[]{:S(2)}) collective-permute-start(bf16[1,128,640]{2,1,0:T(8,128)(2,1)S(1)} %get-tuple-element.17), channel_id=1, source_target_pairs={{0,8},{4,12},{8,0},{12,4},{1,9},{5,13},{9,1},{13,5},{2,10},{6,14},... | collective-permute-start | bytes 491528 | tf_op jit(solution)/shard_map/ppermute | solution.py:245
  12.3 1.6 %collective-permute-start = (s32[25]{0:T(128)S(1)}, s32[25]{0:T(128)S(1)}, u32[]{:S(2)}, u32[]{:S(2)}) collective-permute-start(s32[25]{0:T(128)S(1)} %pad_add_fusion.refs_0_), channel_id=1, source_target_pairs={{0,4},{4,8},{8,12},{12,0},{1,5},{5,9},{9,13},{13,1},{2,6},{6,10},{... | collective-permute-start | bytes 308 | tf_op jit(solution)/shard_map/ppermute | solution.py:236
  12.3 2.5 %collective-permute-start.1 = (s32[25]{0:T(128)S(1)}, s32[25]{0:T(128)S(1)}, u32[]{:S(2)}, u32[]{:S(2)}) collective-permute-start(s32[25]{0:T(128)S(1)} %pad_add_fusion.refs_0_), channel_id=1, source_target_pairs={{0,8},{4,12},{8,0},{12,4},{1,9},{5,13},{9,1},{13,5},{2,10},{6,14},... | collective-permute-start | bytes 308 | tf_op jit(solution)/shard_map/ppermute | solution.py:236
  12.4 3.3 %collective-permute-start.2 = (s32[25]{0:T(128)S(1)}, s32[25]{0:T(128)S(1)}, u32[]{:S(2)}, u32[]{:S(2)}) collective-permute-start(s32[25]{0:T(128)S(1)} %pad_add_fusion.refs_0_), channel_id=1, source_target_pairs={{0,12},{4,0},{8,4},{12,8},{1,13},{5,1},{9,5},{13,9},{2,14},{6,2},{... | collective-permute-start | bytes 308 | tf_op jit(solution)/shard_map/ppermute | solution.py:236
  13.1 3.7 %copy-start.1 = (bf16[8,128,640]{2,1,0:T(8,128)(2,1)S(1)}, bf16[8,128,640]{2,1,0:T(8,128)(2,1)}, u32[]{:S(2)}) copy-start(bf16[8,128,640]{2,1,0:T(8,128)(2,1)} %copy-done) | copy-start | bytes 3932164
  15.6 26.4 %collective-permute-start.8 = (bf16[7,128,640]{2,1,0:T(8,128)(2,1)}, bf16[7,128,640]{2,1,0:T(8,128)(2,1)}, u32[]{:S(2)}, u32[]{:S(2)}) collective-permute-start(bf16[7,128,640]{2,1,0:T(8,128)(2,1)} %shard_map.65.refs_10_), channel_id=1, source_target_pairs={{0,8},{4,12},{8,0},{12,4},{1,9},{5,13},{9,1},{13,5},{2,10},{6,14},... | collective-permute-start | bytes 3440648 | tf_op jit(solution)/shard_map/ppermute | solution.py:247
  24.8 13.7 %collective-permute-start.5 = (f16[2,8,2,32,256]{4,3,1,0,2:T(8,128)(2,1)S(1)}, f16[2,8,2,32,256]{4,3,1,0,2:T(8,128)(2,1)S(1)}, u32[]{:S(2)}, u32[]{:S(2)}) collective-permute-start(f16[2,8,2,32,256]{4,3,1,0,2:T(8,128)(2,1)S(1)} %fusion.1), channel_id=1, source_target_pairs={{0,1},{1,0},{2,3},{3,2},{4,5},{5,4},{6,7},{7,6},{8,9},{9,8},{10,11... | collective-permute-start | bytes 1572872 | tf_op jit(solution)/shard_map/ppermute | solution.py:210
  26.2 31.0 %collective-permute-start.7 = (bf16[8,128,640]{2,1,0:T(8,128)(2,1)}, bf16[8,128,640]{2,1,0:T(8,128)(2,1)}, u32[]{:S(2)}, u32[]{:S(2)}) collective-permute-start(bf16[8,128,640]{2,1,0:T(8,128)(2,1)} %get-tuple-element.20), channel_id=1, source_target_pairs={{0,12},{8,4},{1,13},{9,5},{2,14},{10,6},{3,15},{11,7},{16,28},{24,... | collective-permute-start | bytes 3932168 | tf_op jit(solution)/shard_map/ppermute | solution.py:248
  38.6 3.5 %copy-start.10 = (f16[2,8,2,32,256]{4,3,1,0,2:T(8,128)(2,1)}, f16[2,8,2,32,256]{4,3,1,0,2:T(8,128)(2,1)S(1)}, u32[]{:S(2)}) copy-start(f16[2,8,2,32,256]{4,3,1,0,2:T(8,128)(2,1)S(1)} %collective-permute-done.5) | copy-start | bytes 1572868
  44.5 1.1 %copy-start.3 = (f32[2,8,128,128]{3,2,1,0:T(8,128)}, f32[2,8,128,128]{3,2,1,0:T(8,128)S(1)}, u32[]{:S(2)}) copy-start(f32[2,8,128,128]{3,2,1,0:T(8,128)S(1)} %shard_map.67.refs_2_.refs_4_) | copy-start | bytes 3145732
  45.6 14.2 %collective-permute-start.11 = (bf16[7,128,640]{2,1,0:T(8,128)(2,1)}, bf16[7,128,640]{2,1,0:T(8,128)(2,1)}, u32[]{:S(2)}, u32[]{:S(2)}) collective-permute-start(bf16[7,128,640]{2,1,0:T(8,128)(2,1)} %get-tuple-element.22), channel_id=1, source_target_pairs={{0,4},{8,12},{1,5},{9,13},{2,6},{10,14},{3,7},{11,15},{16,20},{24,... | collective-permute-start | bytes 3440648 | tf_op jit(solution)/shard_map/ppermute | solution.py:259
  46.9 4.0 %copy-start.9 = (f32[2,8,2,1,32,256]{5,4,3,2,1,0:T(8,128)S(1)}, f32[2,8,2,1,32,256]{5,4,3,2,1,0:T(8,128)}, u32[]{:S(2)}) copy-start(f32[2,8,2,1,32,256]{5,4,3,2,1,0:T(8,128)} %get-tuple-element.23) | copy-start | bytes 3145732
  46.9 12.9 %collective-permute-start.10 = (bf16[1,128,640]{2,1,0:T(8,128)(2,1)S(1)}, bf16[1,128,640]{2,1,0:T(8,128)(2,1)S(1)}, u32[]{:S(2)}, u32[]{:S(2)}) collective-permute-start(bf16[1,128,640]{2,1,0:T(8,128)(2,1)S(1)} %get-tuple-element.21), channel_id=1, source_target_pairs={{0,4},{8,12},{1,5},{9,13},{2,6},{10,14},{3,7},{11,15},{16,20},{24,... | collective-permute-start | bytes 491528 | tf_op jit(solution)/shard_map/ppermute | solution.py:259
  49.5 5.3 %collective-permute-start.9 = (f16[2,8,2,32,128]{4,3,2,1,0:T(8,128)(2,1)S(1)}, f16[2,8,2,32,128]{4,3,2,1,0:T(8,128)(2,1)S(1)}, u32[]{:S(2)}, u32[]{:S(2)}) collective-permute-start(f16[2,8,2,32,128]{4,3,2,1,0:T(8,128)(2,1)S(1)} %copy.22), channel_id=1, source_target_pairs={{0,1},{1,0},{2,3},{3,2},{4,5},{5,4},{6,7},{7,6},{8,9},{9,8},{10,11... | collective-permute-start | bytes 786440 | tf_op jit(solution)/shard_map/ppermute | solution.py:210
  50.9 6.3 %copy-start.2 = (bf16[8,128,640]{2,1,0:T(8,128)(2,1)S(1)}, bf16[8,128,640]{2,1,0:T(8,128)(2,1)}, u32[]{:S(2)}) copy-start(bf16[8,128,640]{2,1,0:T(8,128)(2,1)} %copy-done) | copy-start | bytes 3932164
  52.3 15.9 %collective-permute-start.6 = (f16[2,8,1,32,256]{4,3,1,0,2:T(8,128)(2,1)S(1)}, f16[2,8,1,32,256]{4,3,1,0,2:T(8,128)(2,1)S(1)}, u32[]{:S(2)}, u32[]{:S(2)}) collective-permute-start(f16[2,8,1,32,256]{4,3,1,0,2:T(8,128)(2,1)S(1)} %multiply_convert_fusion), channel_id=1, source_target_pairs={{0,2},{1,3},{2,0},{3,1},{4,6},{5,7},{6,4},{7,5},{8,10},{9,11},{10,... | collective-permute-start | bytes 786440 | tf_op jit(solution)/shard_map/ppermute | solution.py:210
  54.8 4.9 %copy-start.4 = (f32[2,8,128,128]{3,2,1,0:T(8,128)S(1)}, f32[2,8,128,128]{3,2,1,0:T(8,128)}, u32[]{:S(2)}) copy-start(f32[2,8,128,128]{3,2,1,0:T(8,128)} %copy-done.3) | copy-start | bytes 3145732
  62.6 8.6 %collective-permute-start.12 = (f16[2,8,2,32,128]{4,3,1,0,2:T(8,128)(2,1)S(1)}, f16[2,8,2,32,128]{4,3,1,0,2:T(8,128)(2,1)S(1)}, u32[]{:S(2)}, u32[]{:S(2)}) collective-permute-start(f16[2,8,2,32,128]{4,3,1,0,2:T(8,128)(2,1)S(1)} %fusion.5), channel_id=1, source_target_pairs={{4,5},{5,4},{6,7},{7,6},{12,13},{13,12},{14,15},{15,14},{20,21},{2... | collective-permute-start | bytes 786440 | tf_op jit(solution)/shard_map/ppermute | solution.py:210
  65.8 9.0 %collective-permute-start.14 = (f16[2,8,1,32,128]{4,3,2,1,0:T(8,128)(2,1)S(1)}, f16[2,8,1,32,128]{4,3,2,1,0:T(8,128)(2,1)S(1)}, u32[]{:S(2)}, u32[]{:S(2)}) collective-permute-start(f16[2,8,1,32,128]{4,3,2,1,0:T(8,128)(2,1)S(1)} %fusion.8), channel_id=1, source_target_pairs={{0,2},{1,3},{2,0},{3,1},{4,6},{5,7},{6,4},{7,5},{8,10},{9,11},{10,... | collective-permute-start | bytes 393224 | tf_op jit(solution)/shard_map/ppermute | solution.py:210
  71.3 8.0 %collective-permute-start.13 = (f16[2,8,1,32,128]{4,3,1,0,2:T(8,128)(2,1)S(1)}, f16[2,8,1,32,128]{4,3,1,0,2:T(8,128)(2,1)S(1)}, u32[]{:S(2)}, u32[]{:S(2)}) collective-permute-start(f16[2,8,1,32,128]{4,3,1,0,2:T(8,128)(2,1)S(1)} %multiply_convert_fusion.1), channel_id=1, source_target_pairs={{4,6},{5,7},{6,4},{7,5},{12,14},{13,15},{14,12},{15,13},{20,22},{2... | collective-permute-start | bytes 393224 | tf_op jit(solution)/shard_map/ppermute | solution.py:210

commit v9 on v8

--- a/solution.py
+++ b/solution.py
@@ -8,7 +8,7 @@
 from jax.sharding import PartitionSpec as P
 
 LIMIT = 16 << 20
-SPLIT = (1, 7)
+SPLIT = (4, 4)
 COST = pl.CostEstimate(flops=1000, bytes_accessed=1000, transcendentals=0)
 PARAMS = pltpu.CompilerParams(vmem_limit_bytes=LIMIT)
 ANY = pl.BlockSpec(memory_space=pl.ANY)
@@ -84,7 +84,7 @@
     records = refs[:n_aux]
     occ, freq, table = refs[n_aux : n_aux + 3]
     own, far = refs[n_aux + 3 : n_aux + 5], refs[n_aux + 5]
-    out, roots = refs[-2:]
+    out, out_one, roots = refs[-3:]
     pair_rows = own[0].shape[-1]
     virt_blocks = table.shape[1] // pair_rows
     aux_pos, pair_col = lax.axis_index("aux"), lax.axis_index("pair")
@@ -129,14 +129,14 @@
                 a = (own_tile(own, slot, m, blocks_dev).astype(jnp.float32) * masked[m, slot, w]).astype(jnp.bfloat16)
                 term = dot(a, a)
                 total = term if total is None else total + term
-            out[w, m, :, : total.shape[1]] = total
+            out[w, m] = total
             total = None
             for slot in range(band - 1):
                 a = (own_tile(own, slot, m, blocks_dev).astype(jnp.float32) * one[m, slot, w]).astype(jnp.bfloat16)
                 b = (far[slot * blocks_dev + m].astype(jnp.float32) * plain[m, slot, w]).astype(jnp.bfloat16)
                 term = dot(a, b)
                 total = term if total is None else total + term
-            out[w, m, :, total.shape[1] :] = total
+            out_one[w, m] = total
 
 
 def first_rows(dims, records, occ, freq, table, own, far, after):
@@ -145,11 +145,12 @@
     return pl.pallas_call(
         functools.partial(first_kernel, dims),
         out_shape=[
-            jax.ShapeDtypeStruct((freq_count, blocks_dev, aux_rows, 2 * aux_rows), jnp.float32),
+            jax.ShapeDtypeStruct((freq_count, blocks_dev, aux_rows, aux_rows), jnp.float32),
+            jax.ShapeDtypeStruct((freq_count, blocks_dev, aux_rows, aux_rows), jnp.float32),
             jax.ShapeDtypeStruct((blocks_dev, root_rows(band, freq_count), pair_rows), jnp.float32),
         ],
         in_specs=[SMEM] * (n_aux + 2) + [VMEM] * 4 + [ANY] * len(after),
-        out_specs=[VMEM, VMEM],
+        out_specs=[VMEM, VMEM, VMEM],
         compiler_params=PARAMS,
         cost_estimate=COST,
     )(*records, occ, freq, table, *own, far, *after)
@@ -219,7 +220,7 @@
         keep, got = halve(keep, pair_col, step, n_pair, rings, scale)
         stages.append(got[0, 0, 0].astype(jnp.float32))
         step *= 2
-    return stages[0], keep[:, :, 0]
+    return stages, keep[:, :, 0]
 
 
 def on_device(three_centre, locality, live_blocks, occ_energy, virt_energy, frequencies):
@@ -242,27 +243,25 @@
     first_slot, rest, near_two, far_two, to_one = pack(tiles, plan)
     own = (first_slot, rest)
     down2 = [(s, (s - 2) % n_aux) for s in whole]
-    c2 = [lax.ppermute(near_two, "aux", down2)]
-    (far_two,) = tie([far_two], records[1:] + c2)
-    c2.append(lax.ppermute(far_two, "aux", down2))
-    b1 = lax.ppermute(to_one, "aux", [(s, (s - 1) % n_aux) for s in evens])
+    c2 = [lax.ppermute(p, "aux", down2) for p in tie([near_two, far_two], records[1:])]
     to_even = lax.ppermute(rest, "aux", [(s, s - 1) for s in odds])
     table = virt_energy.reshape(1, -1)
-    rows0, roots = first_rows(dims, records, occ_energy, frequencies, table, own, to_even, [far_two])
+    rows0, rows_even, roots = first_rows(dims, records, occ_energy, frequencies, table, own, to_even, [])
 
     def rows_of(delta, slots, far, after, add=None):
         return band_rows(dims, delta, slots, roots, own, far, after, add)
 
-    z0 = totals(rows0, pair_col, n_pair, whole, scale)
-    rows2 = rows_of(2, [0], [c2], [z0[0]])
-    z2 = totals(rows2, pair_col, n_pair, whole, scale)
+    b1 = lax.ppermute(tie([to_one], [roots])[0], "aux", [(s, (s - 1) % n_aux) for s in evens])
+    bits0, z0 = totals(rows0, pair_col, n_pair, whole, scale)
+    bits_even, z_even = totals(rows_even, pair_col, n_pair, evens, scale)
+    rows2 = rows_of(2, [0], [c2], [bits0[-1], bits_even[-1]])
+    bits2, z2 = totals(rows2, pair_col, n_pair, whole, scale)
     to_odd = [lax.ppermute(c, "aux", [(s, s + 1) for s in evens]) for c in tie(c2, [rows2])]
     part = rows_of(1, [1], [to_odd], [rows2])
-    rows_odd = rows_of(1, [0], [[b1]], [z2[0]])
-    z_odd = totals(rows_odd + part, pair_col, n_pair, odds, scale)
+    rows_odd = rows_of(1, [0], [[b1]], [bits2[0]], part)
+    _, z_odd = totals(rows_odd, pair_col, n_pair, odds, scale)
     even = lax.axis_index("aux").astype(jnp.uint32) & jnp.uint32(1) == 0
-    one = jnp.where(even, z0[1][..., aux_rows:], z_odd[1])
-    out = jnp.concatenate([z0[1][..., :aux_rows], one, z2[1]], axis=-1)
+    out = jnp.concatenate([z0, jnp.where(even, z_even, z_odd), z2], axis=-1)
     return out[:, :, None]
 
 

time: 80.9 us -> 84 us (1.038)
  starting transfers between devices: 26.3 us -> 28.8 us
  local copies, waits for them, and re-layouts: 5.77 us -> 8.26 us
  waiting for transfers between devices: 26.9 us -> 24.7 us
    ppermute x6 -> x8, waiting for transfers between devices: 18.5 us -> 14.2 us  [halve(): got = lax.ppermute(sent, ('aux', 'pair'), pairs)]
    unnamed x25 -> x31, local copies, waits for them, and re-layouts: 4.38 us -> 7.13 us
    ppermute x3, starting transfers between devices: 0.78 us -> 3.45 us  [on_device(): lax.ppermute(record, 'aux', [(s, (s + k) % n_aux) for s in range(n_aux)])]
    ppermute x3, waiting for transfers between devices: 5.83 us -> 8.26 us  [the longest x2 8.26 us: on_device(): lax.ppermute(p, 'aux', down2)]
    ppermute x3, starting transfers between devices: 5.07 us -> 2.75 us  [the longest x2 1.47 us: on_device(): lax.ppermute(p, 'aux', down2)]
    ppermute x6 -> x8, starting transfers between devices: 14.2 us -> 16.5 us  [halve(): got = lax.ppermute(sent, ('aux', 'pair'), pairs)]
    convert_element_type x6 -> x8, other arithmetic: 1.45 us -> 0.41 us  [halve(): sent = (part * scale).astype(jnp.float16)]
    squeeze x2, other arithmetic: 0.11 us -> 1.1 us  [totals(): return (stages, keep[:, :, 0])]
  transfers between devices with their start and end apart: 15 -> 17, of which waited for: 9 -> 8; matrix products, arithmetic and copies ran while one was open for 6% -> 6% of each run, Pallas kernels for 18% -> 14%
where the time goes in v9:
time: 84 us; the launch traced here: 83.3 us
  starting transfers between devices  28.8 us (34%)
  waiting for transfers between devices  24.7 us (29%)
  Pallas kernels  15.9 us (19%)
  local copies, waits for them, and re-layouts  8.26 us (10%)
  other arithmetic  4.6 us (5%)
  between operations  1.02 us (1%)
    ppermute x8, starting transfers between devices, halve(): got = lax.ppermute(sent, ('aux', 'pair'), pairs)  16.5 us
    ppermute x8, waiting for transfers between devices, halve(): got = lax.ppermute(sent, ('aux', 'pair'), pairs)  14.2 us
    ppermute x2, waiting for transfers between devices, on_device(): lax.ppermute(p, 'aux', down2)  8.26 us
    pallas_call x3, Pallas kernels, band_rows(): pl.pallas_call(functools.partial(band_kernel, dims, delta, slots, rights,...  7.47 us
    unnamed x31, local copies, waits for them, and re-layouts  7.13 us
    pallas_call x1, Pallas kernels, first_rows(): pl.pallas_call(functools.partial(first_kernel, dims), out_shape=[jax.Shap...  6.63 us
    ppermute x1, starting transfers between devices, on_device(): to_even = lax.ppermute(rest, 'aux', [(s, s - 1) for s in odds])  3.58 us
    ppermute x3, starting transfers between devices, on_device(): lax.ppermute(record, 'aux', [(s, (s + k) % n_aux) for s in range(n_aux)])  3.45 us
  transfers between devices with their start and end apart: 17, of which 8 were waited for; matrix products, arithmetic and copies ran while one was open for 6% of the time, Pallas kernels for 14%

profile of v9, /device:TPU:1, one launch (start us, length us, event | category | flops | bytes accessed | tf_op | source)
XLA Modules:
  0.0 83.3 jit_solution(11966890195069415103)
XLA Ops:
  0.0 2.1 %copy-done.6 = bf16[1,1,8,3,1,128,640]{6,5,4,3,2,1,0:T(8,128)(2,1)S(1)} copy-done((bf16[1,1,8,3,1,128,640]{6,5,4,3,2,1,0:T(8,128)(2,1)S(1)}, bf16[1,1,8,3,1,128,640]{6,5,4,3,2,1,0:T(8,128)(2,1)}, u32[]{:S(2)}) %copy-start.6) | copy-done | bytes 3932184
  2.1 1.8 %shard_map.64 = (bf16[8,128,640]{2,1,0:T(8,128)(2,1)S(1)}, bf16[16,128,640]{2,1,0:T(8,128)(2,1)S(1)}, bf16[4,128,640]{2,1,0:T(8,128)(2,1)}, bf16[4,128,640]{2,1,0:T(8,128)(2,1)}, bf16[8,128,640]{2,1,0:T(8,128)(2,1)}) custom-call(bf16[8,3,128,640]{3,2,1,0:T(8,128)(2,1)S(1)} %bitcast.66), custom_call_target="tpu_custom_call" | custom-call | flops 1000 | bytes 1000 | tf_op jit(solution)/shard_map/pallas_call | solution.py:46
  3.9 1.1 %copy-done = bf16[8,128,640]{2,1,0:T(8,128)(2,1)} copy-done((bf16[8,128,640]{2,1,0:T(8,128)(2,1)}, bf16[8,128,640]{2,1,0:T(8,128)(2,1)S(1)}, u32[]{:S(2)}) %copy-start) | copy-done | bytes 1310744
  5.0 3.6 %collective-permute-start.3 = (bf16[16,128,640]{2,1,0:T(8,128)(2,1)S(1)}, bf16[16,128,640]{2,1,0:T(8,128)(2,1)}, u32[]{:S(2)}, u32[]{:S(2)}) collective-permute-start(bf16[16,128,640]{2,1,0:T(8,128)(2,1)S(1)} %get-tuple-element.18.refs_8_.refs_1_), channel_id=1, source_target_pairs={{4,0},{12,8},{5,1},{13,9},{6,2},{14,10},{7,3},{15,11},{20,16},{28,... | collective-permute-start | bytes 7864328 | tf_op jit(solution)/shard_map/ppermute | solution.py:247
  9.9 2.3 %collective-permute-start.1 = (s32[25]{0:T(128)S(1)}, s32[25]{0:T(128)S(1)}, u32[]{:S(2)}, u32[]{:S(2)}) collective-permute-start(s32[25]{0:T(128)S(1)} %pad_add_fusion.refs_0_), channel_id=1, source_target_pairs={{0,8},{4,12},{8,0},{12,4},{1,9},{5,13},{9,1},{13,5},{2,10},{6,14},... | collective-permute-start | bytes 308 | tf_op jit(solution)/shard_map/ppermute | solution.py:237
  12.2 0.7 collective-permute-start.2
  13.1 2.0 %collective-permute-done.2.refs_3_.refs_4_ = s32[25]{0:T(128)S(1)} collective-permute-done((s32[25]{0:T(128)S(1)}, s32[25]{0:T(128)S(1)}, u32[]{:S(2)}, u32[]{:S(2)}) %collective-permute-start.2) | collective-permute-done | bytes 132 | tf_op jit(solution)/shard_map/ppermute | solution.py:237
  15.5 1.1 %collective-permute-start.9 = (bf16[4,128,640]{2,1,0:T(8,128)(2,1)}, bf16[4,128,640]{2,1,0:T(8,128)(2,1)}, u32[]{:S(2)}, u32[]{:S(2)}) collective-permute-start(bf16[4,128,640]{2,1,0:T(8,128)(2,1)} %get-tuple-element.25), channel_id=1, source_target_pairs={{0,8},{4,12},{8,0},{12,4},{1,9},{5,13},{9,1},{13,5},{2,10},{6,14},... | collective-permute-start | bytes 1966088 | tf_op jit(solution)/shard_map/ppermute | solution.py:246
  16.7 6.6 %shard_map.65 = (f32[2,8,128,128]{3,2,1,0:T(8,128)S(1)}, f32[2,8,128,128]{3,2,1,0:T(8,128)S(1)}, f32[8,16,640]{2,1,0:T(8,128)S(1)}) custom-call(s32[25]{0:T(128)S(1)} %pad_add_fusion.refs_0_, s32[25]{0:T(128)S(1)} %collective-permute-done.refs_1_.refs_2_, s32[25]{0:T(128)S(1)} %collective-permute-done.1.refs_2_.refs_3_, ...), custom_call_target="tpu_custom_call" | custom-call | flops 1000 | bytes 1000 | tf_op jit(solution)/shard_map/pallas_call | solution.py:145
  24.3 1.4 %collective-permute-start.4 = (f16[2,8,2,32,128]{4,3,1,0,2:T(8,128)(2,1)S(1)}, f16[2,8,2,32,128]{4,3,1,0,2:T(8,128)(2,1)S(1)}, u32[]{:S(2)}, u32[]{:S(2)}) collective-permute-start(f16[2,8,2,32,128]{4,3,1,0,2:T(8,128)(2,1)S(1)} %fusion.4), channel_id=1, source_target_pairs={{0,1},{1,0},{2,3},{3,2},{4,5},{5,4},{6,7},{7,6},{8,9},{9,8},{10,11... | collective-permute-start | bytes 786440 | tf_op jit(solution)/shard_map/ppermute | solution.py:211
  25.7 1.3 %collective-permute-start.8 = (bf16[8,128,640]{2,1,0:T(8,128)(2,1)}, bf16[8,128,640]{2,1,0:T(8,128)(2,1)}, u32[]{:S(2)}, u32[]{:S(2)}) collective-permute-start(bf16[8,128,640]{2,1,0:T(8,128)(2,1)} %shard_map.66), channel_id=1, source_target_pairs={{0,12},{8,4},{1,13},{9,5},{2,14},{10,6},{3,15},{11,7},{16,28},{24,... | collective-permute-start | bytes 3932168 | tf_op jit(solution)/shard_map/ppermute | solution.py:254
  27.8 3.6 %collective-permute-done.4 = f16[2,8,2,32,128]{4,3,1,0,2:T(8,128)(2,1)S(1)} collective-permute-done((f16[2,8,2,32,128]{4,3,1,0,2:T(8,128)(2,1)S(1)}, f16[2,8,2,32,128]{4,3,1,0,2:T(8,128)(2,1)S(1)}, u32[]{:S(2)}, u32[]{:S(2)}) %collective-permute-start.4) | collective-permute-done | bytes 262176 | tf_op jit(solution)/shard_map/ppermute | solution.py:211
  31.6 2.0 %collective-permute-start.5 = (f16[2,8,1,32,128]{4,3,1,0,2:T(8,128)(2,1)S(1)}, f16[2,8,1,32,128]{4,3,1,0,2:T(8,128)(2,1)S(1)}, u32[]{:S(2)}, u32[]{:S(2)}) collective-permute-start(f16[2,8,1,32,128]{4,3,1,0,2:T(8,128)(2,1)S(1)} %multiply_convert_fusion.2), channel_id=1, source_target_pairs={{0,2},{1,3},{2,0},{3,1},{4,6},{5,7},{6,4},{7,5},{8,10},{9,11},{10,... | collective-permute-start | bytes 393224 | tf_op jit(solution)/shard_map/ppermute | solution.py:211
  34.2 2.9 %collective-permute-done.5 = f16[2,8,1,32,128]{4,3,1,0,2:T(8,128)(2,1)S(1)} collective-permute-done((f16[2,8,1,32,128]{4,3,1,0,2:T(8,128)(2,1)S(1)}, f16[2,8,1,32,128]{4,3,1,0,2:T(8,128)(2,1)S(1)}, u32[]{:S(2)}, u32[]{:S(2)}) %collective-permute-start.5) | collective-permute-done | bytes 131104 | tf_op jit(solution)/shard_map/ppermute | solution.py:211
  37.7 8.3 %collective-permute-done.9.refs_2_.refs_0_ = bf16[4,128,640]{2,1,0:T(8,128)(2,1)} collective-permute-done((bf16[4,128,640]{2,1,0:T(8,128)(2,1)}, bf16[4,128,640]{2,1,0:T(8,128)(2,1)}, u32[]{:S(2)}, u32[]{:S(2)}) %collective-permute-start.9) | collective-permute-done | bytes 655392 | tf_op jit(solution)/shard_map/ppermute | solution.py:246
  46.0 2.5 %shard_map.68.refs_2_.refs_4_ = f32[2,8,128,128]{3,2,1,0:T(8,128)S(1)} custom-call(f32[8,16,640]{2,1,0:T(8,128)S(1)} %get-tuple-element.21.refs_1_.roots, bf16[8,128,640]{2,1,0:T(8,128)(2,1)S(1)} %copy-done.1, bf16[16,128,640]{2,1,0:T(8,128)(2,1)S(1)} %get-tuple-element.18.refs_8_.refs_1_, bf16[4,128,640]{2,1,0:T(8,128)(2,1)} %collective-permute-done.9.refs_2_.refs_0_, ...), custom_call_target="tpu_custom_call" | custom-call | flops 1000 | bytes 1000 | tf_op jit(solution)/shard_map/pallas_call | solution.py:188
  48.5 1.3 %collective-permute-start.11 = (bf16[4,128,640]{2,1,0:T(8,128)(2,1)}, bf16[4,128,640]{2,1,0:T(8,128)(2,1)}, u32[]{:S(2)}, u32[]{:S(2)}) collective-permute-start(bf16[4,128,640]{2,1,0:T(8,128)(2,1)} %get-tuple-element.27), channel_id=1, source_target_pairs={{0,4},{8,12},{1,5},{9,13},{2,6},{10,14},{3,7},{11,15},{16,20},{24,... | collective-permute-start | bytes 1966088 | tf_op jit(solution)/shard_map/ppermute | solution.py:259
  49.8 1.3 %collective-permute-start.12 = (bf16[4,128,640]{2,1,0:T(8,128)(2,1)}, bf16[4,128,640]{2,1,0:T(8,128)(2,1)}, u32[]{:S(2)}, u32[]{:S(2)}) collective-permute-start(bf16[4,128,640]{2,1,0:T(8,128)(2,1)} %get-tuple-element.28), channel_id=1, source_target_pairs={{0,4},{8,12},{1,5},{9,13},{2,6},{10,14},{3,7},{11,15},{16,20},{24,... | collective-permute-start | bytes 1966088 | tf_op jit(solution)/shard_map/ppermute | solution.py:259
  51.2 0.8 copy.24
  52.0 1.3 %collective-permute-start.13 = (f16[2,8,2,32,128]{4,3,2,1,0:T(8,128)(2,1)}, f16[2,8,2,32,128]{4,3,2,1,0:T(8,128)(2,1)}, u32[]{:S(2)}, u32[]{:S(2)}) collective-permute-start(f16[2,8,2,32,128]{4,3,2,1,0:T(8,128)(2,1)} %copy.24), channel_id=1, source_target_pairs={{0,1},{1,0},{2,3},{3,2},{4,5},{5,4},{6,7},{7,6},{8,9},{9,8},{10,11... | collective-permute-start | bytes 786440 | tf_op jit(solution)/shard_map/ppermute | solution.py:211
  53.3 1.1 %add_bitcast_fusion = f32[2,8,32,128]{3,2,1,0:T(8,128)S(1)} fusion(f16[2,8,1,32,128]{4,3,1,0,2:T(8,128)(2,1)} %copy-done.13, f32[2,8,2,32,128]{4,3,1,0,2:T(8,128)} %copy-done.10, u32[]{:T(128)S(6)} %and.18), kind=kLoop, calls=%fused_computation.25 | loop fusion | flops 196608 | bytes 655364 | tf_op jit(solution)/shard_map/squeeze | solution.py:223
  54.3 3.2 %collective-permute-done.13 = f16[2,8,2,32,128]{4,3,2,1,0:T(8,128)(2,1)} collective-permute-done((f16[2,8,2,32,128]{4,3,2,1,0:T(8,128)(2,1)}, f16[2,8,2,32,128]{4,3,2,1,0:T(8,128)(2,1)}, u32[]{:S(2)}, u32[]{:S(2)}) %collective-permute-start.13) | collective-permute-done | bytes 262176 | tf_op jit(solution)/shard_map/ppermute | solution.py:211
  58.2 1.3 %copy-done.2 = bf16[8,128,640]{2,1,0:T(8,128)(2,1)S(1)} copy-done((bf16[8,128,640]{2,1,0:T(8,128)(2,1)S(1)}, bf16[8,128,640]{2,1,0:T(8,128)(2,1)}, u32[]{:S(2)}) %copy-start.2) | copy-done | bytes 1310744
  59.5 1.2 %copy-done.4 = f32[2,8,128,128]{3,2,1,0:T(8,128)S(1)} copy-done((f32[2,8,128,128]{3,2,1,0:T(8,128)S(1)}, f32[2,8,128,128]{3,2,1,0:T(8,128)}, u32[]{:S(2)}) %copy-start.4) | copy-done | bytes 1048600
  60.7 2.5 %shard_map.70.refs_3_ = f32[2,8,128,128]{3,2,1,0:T(8,128)S(1)} custom-call(f32[8,16,640]{2,1,0:T(8,128)S(1)} %get-tuple-element.21.refs_1_.roots, bf16[8,128,640]{2,1,0:T(8,128)(2,1)S(1)} %copy-done.2, bf16[16,128,640]{2,1,0:T(8,128)(2,1)S(1)} %get-tuple-element.18.refs_8_.refs_1_, bf16[4,128,640]{2,1,0:T(8,128)(2,1)} %collective-permute-done.11.refs_2_, ...), custom_call_target="tpu_custom_call" | custom-call | flops 1000 | bytes 1000 | tf_op jit(solution)/shard_map/pallas_call | solution.py:188
  63.2 2.5 %shard_map.71 = f32[2,8,128,128]{3,2,1,0:T(8,128)S(1)} custom-call(f32[8,16,640]{2,1,0:T(8,128)S(1)} %get-tuple-element.21.refs_1_.roots, bf16[8,128,640]{2,1,0:T(8,128)(2,1)S(1)} %copy-done.2, bf16[16,128,640]{2,1,0:T(8,128)(2,1)S(1)} %get-tuple-element.18.refs_8_.refs_1_, bf16[8,128,640]{2,1,0:T(8,128)(2,1)} %collective-permute-done.8.refs_2_, ...), custom_call_target="tpu_custom_call" | custom-call | flops 1000 | bytes 1000 | tf_op jit(solution)/shard_map/pallas_call | solution.py:188
  66.0 3.4 %collective-permute-start.14 = (f16[2,8,2,32,128]{4,3,1,0,2:T(8,128)(2,1)S(1)}, f16[2,8,2,32,128]{4,3,1,0,2:T(8,128)(2,1)S(1)}, u32[]{:S(2)}, u32[]{:S(2)}) collective-permute-start(f16[2,8,2,32,128]{4,3,1,0,2:T(8,128)(2,1)S(1)} %fusion.7), channel_id=1, source_target_pairs={{4,5},{5,4},{6,7},{7,6},{12,13},{13,12},{14,15},{15,14},{20,21},{2... | collective-permute-start | bytes 786440 | tf_op jit(solution)/shard_map/ppermute | solution.py:211
  69.3 1.1 %bitcast_add_fusion = f32[2,8,2,32,128]{4,3,2,1,0:T(8,128)S(1)} fusion(f16[2,8,2,32,128]{4,3,2,1,0:T(8,128)(2,1)} %collective-permute-done.13, f32[2,8,2,2,32,128]{5,4,3,2,1,0:T(8,128)S(1)} %bitcast.64, u32[]{:T(128)S(6)} %and.8), kind=kLoop, calls=%fused_computation.9 | loop fusion | flops 393216 | bytes 1310724 | tf_op jit(solution)/shard_map/add | solution.py:212
  70.5 2.4 %collective-permute-start.16 = (f16[2,8,1,32,128]{4,3,2,1,0:T(8,128)(2,1)S(1)}, f16[2,8,1,32,128]{4,3,2,1,0:T(8,128)(2,1)S(1)}, u32[]{:S(2)}, u32[]{:S(2)}) collective-permute-start(f16[2,8,1,32,128]{4,3,2,1,0:T(8,128)(2,1)S(1)} %fusion.10), channel_id=1, source_target_pairs={{0,2},{1,3},{2,0},{3,1},{4,6},{5,7},{6,4},{7,5},{8,10},{9,11},{10,... | collective-permute-start | bytes 393224 | tf_op jit(solution)/shard_map/ppermute | solution.py:211
  73.3 4.7 %collective-permute-start.15 = (f16[2,8,1,32,128]{4,3,1,0,2:T(8,128)(2,1)S(1)}, f16[2,8,1,32,128]{4,3,1,0,2:T(8,128)(2,1)S(1)}, u32[]{:S(2)}, u32[]{:S(2)}) collective-permute-start(f16[2,8,1,32,128]{4,3,1,0,2:T(8,128)(2,1)S(1)} %multiply_convert_fusion), channel_id=1, source_target_pairs={{4,6},{5,7},{6,4},{7,5},{12,14},{13,15},{14,12},{15,13},{20,22},{2... | collective-permute-start | bytes 393224 | tf_op jit(solution)/shard_map/ppermute | solution.py:211
  78.1 4.2 %collective-permute-done.15 = f16[2,8,1,32,128]{4,3,1,0,2:T(8,128)(2,1)S(1)} collective-permute-done((f16[2,8,1,32,128]{4,3,1,0,2:T(8,128)(2,1)S(1)}, f16[2,8,1,32,128]{4,3,1,0,2:T(8,128)(2,1)S(1)}, u32[]{:S(2)}, u32[]{:S(2)}) %collective-permute-start.15) | collective-permute-done | bytes 131104 | tf_op jit(solution)/shard_map/ppermute | solution.py:211
  82.4 0.9 %maximum_bitcast_fusion = f32[2,8,1,32,384]{4,3,2,1,0:T(8,128)} fusion(f32[2,8,32,128]{3,2,1,0:T(8,128)S(1)} %fusion.9, f32[2,8,32,128]{3,2,1,0:T(8,128)S(1)} %select_bitcast_fusion, f32[2,8,32,128]{3,2,1,0:T(8,128)S(1)} %add_bitcast_fusion), kind=kLoop, calls=%fused_computation | loop fusion | flops 393216 | bytes 1572864 | tf_op jit(solution)/shard_map/broadcast_in_dim | solution.py:265
  (66 shorter events, 6.1 us)
Async XLA Ops:
  0.0 2.1 %copy-start.6 = (bf16[1,1,8,3,1,128,640]{6,5,4,3,2,1,0:T(8,128)(2,1)S(1)}, bf16[1,1,8,3,1,128,640]{6,5,4,3,2,1,0:T(8,128)(2,1)}, u32[]{:S(2)}) copy-start(bf16[1,1,8,3,1,128,640]{6,5,4,3,2,1,0:T(8,128)(2,1)} %param.6) | copy-start | bytes 11796484
  2.1 6.5 %copy-start.14 = (s32[1,1,8,3,1]{2,4,3,1,0:T(1,128)S(1)}, s32[1,1,8,3,1]{2,4,3,1,0:T(1,128)}, u32[]{:S(2)}) copy-start(s32[1,1,8,3,1]{2,4,3,1,0:T(1,128)} %param.7) | copy-start | bytes 292
  3.9 1.1 %copy-start = (bf16[8,128,640]{2,1,0:T(8,128)(2,1)}, bf16[8,128,640]{2,1,0:T(8,128)(2,1)S(1)}, u32[]{:S(2)}) copy-start(bf16[8,128,640]{2,1,0:T(8,128)(2,1)S(1)} %get-tuple-element.17.refs_7_.refs_0_) | copy-start | bytes 3932164
  5.0 11.7 %copy-start.7 = (f32[10240]{0:T(1024)S(1)}, f32[10240]{0:T(1024)}, u32[]{:S(2)}) copy-start(f32[10240]{0:T(1024)} %param.10) | copy-start | bytes 122884
  5.0 11.7 %copy-start.8 = (f32[8]{0:T(128)S(1)}, f32[8]{0:T(128)}, u32[]{:S(2)}) copy-start(f32[8]{0:T(128)} %refs_4_.1) | copy-start | bytes 100
  5.0 11.7 %copy-start.9 = (f32[2]{0:T(128)S(1)}, f32[2]{0:T(128)}, u32[]{:S(2)}) copy-start(f32[2]{0:T(128)} %refs_5_.1) | copy-start | bytes 28
  5.0 11.6 %collective-permute-start.3 = (bf16[16,128,640]{2,1,0:T(8,128)(2,1)S(1)}, bf16[16,128,640]{2,1,0:T(8,128)(2,1)}, u32[]{:S(2)}, u32[]{:S(2)}) collective-permute-start(bf16[16,128,640]{2,1,0:T(8,128)(2,1)S(1)} %get-tuple-element.18.refs_8_.refs_1_), channel_id=1, source_target_pairs={{4,0},{12,8},{5,1},{13,9},{6,2},{14,10},{7,3},{15,11},{20,16},{28,... | collective-permute-start | bytes 7864328 | tf_op jit(solution)/shard_map/ppermute | solution.py:247
  9.5 3.5 %collective-permute-start = (s32[25]{0:T(128)S(1)}, s32[25]{0:T(128)S(1)}, u32[]{:S(2)}, u32[]{:S(2)}) collective-permute-start(s32[25]{0:T(128)S(1)} %pad_add_fusion.refs_0_), channel_id=1, source_target_pairs={{0,4},{4,8},{8,12},{12,0},{1,5},{5,9},{9,13},{13,1},{2,6},{6,10},{... | collective-permute-start | bytes 308 | tf_op jit(solution)/shard_map/ppermute | solution.py:237
  9.9 3.2 %collective-permute-start.1 = (s32[25]{0:T(128)S(1)}, s32[25]{0:T(128)S(1)}, u32[]{:S(2)}, u32[]{:S(2)}) collective-permute-start(s32[25]{0:T(128)S(1)} %pad_add_fusion.refs_0_), channel_id=1, source_target_pairs={{0,8},{4,12},{8,0},{12,4},{1,9},{5,13},{9,1},{13,5},{2,10},{6,14},... | collective-permute-start | bytes 308 | tf_op jit(solution)/shard_map/ppermute | solution.py:237
  12.2 3.0 %collective-permute-start.2 = (s32[25]{0:T(128)S(1)}, s32[25]{0:T(128)S(1)}, u32[]{:S(2)}, u32[]{:S(2)}) collective-permute-start(s32[25]{0:T(128)S(1)} %pad_add_fusion.refs_0_), channel_id=1, source_target_pairs={{0,12},{4,0},{8,4},{12,8},{1,13},{5,1},{9,5},{13,9},{2,14},{6,2},{... | collective-permute-start | bytes 308 | tf_op jit(solution)/shard_map/ppermute | solution.py:237
  12.9 3.7 %copy-start.1 = (bf16[8,128,640]{2,1,0:T(8,128)(2,1)S(1)}, bf16[8,128,640]{2,1,0:T(8,128)(2,1)}, u32[]{:S(2)}) copy-start(bf16[8,128,640]{2,1,0:T(8,128)(2,1)} %copy-done) | copy-start | bytes 3932164
  15.2 21.9 %collective-permute-start.10 = (bf16[4,128,640]{2,1,0:T(8,128)(2,1)}, bf16[4,128,640]{2,1,0:T(8,128)(2,1)}, u32[]{:S(2)}, u32[]{:S(2)}) collective-permute-start(bf16[4,128,640]{2,1,0:T(8,128)(2,1)} %get-tuple-element.26), channel_id=1, source_target_pairs={{0,8},{4,12},{8,0},{12,4},{1,9},{5,13},{9,1},{13,5},{2,10},{6,14},... | collective-permute-start | bytes 1966088 | tf_op jit(solution)/shard_map/ppermute | solution.py:246
  15.5 30.5 %collective-permute-start.9 = (bf16[4,128,640]{2,1,0:T(8,128)(2,1)}, bf16[4,128,640]{2,1,0:T(8,128)(2,1)}, u32[]{:S(2)}, u32[]{:S(2)}) collective-permute-start(bf16[4,128,640]{2,1,0:T(8,128)(2,1)} %get-tuple-element.25), channel_id=1, source_target_pairs={{0,8},{4,12},{8,0},{12,4},{1,9},{5,13},{9,1},{13,5},{2,10},{6,14},... | collective-permute-start | bytes 1966088 | tf_op jit(solution)/shard_map/ppermute | solution.py:246
  23.5 3.5 %collective-permute-start.6 = (f16[2,8,2,32,128]{4,3,1,0,2:T(8,128)(2,1)S(1)}, f16[2,8,2,32,128]{4,3,1,0,2:T(8,128)(2,1)S(1)}, u32[]{:S(2)}, u32[]{:S(2)}) collective-permute-start(f16[2,8,2,32,128]{4,3,1,0,2:T(8,128)(2,1)S(1)} %fusion.5), channel_id=1, source_target_pairs={{0,1},{1,0},{2,3},{3,2},{8,9},{9,8},{10,11},{11,10},{16,17},{17,16... | collective-permute-start | bytes 786440 | tf_op jit(solution)/shard_map/ppermute | solution.py:211
  24.3 7.1 %collective-permute-start.4 = (f16[2,8,2,32,128]{4,3,1,0,2:T(8,128)(2,1)S(1)}, f16[2,8,2,32,128]{4,3,1,0,2:T(8,128)(2,1)S(1)}, u32[]{:S(2)}, u32[]{:S(2)}) collective-permute-start(f16[2,8,2,32,128]{4,3,1,0,2:T(8,128)(2,1)S(1)} %fusion.4), channel_id=1, source_target_pairs={{0,1},{1,0},{2,3},{3,2},{4,5},{5,4},{6,7},{7,6},{8,9},{9,8},{10,11... | collective-permute-start | bytes 786440 | tf_op jit(solution)/shard_map/ppermute | solution.py:211
  25.7 37.5 %collective-permute-start.8 = (bf16[8,128,640]{2,1,0:T(8,128)(2,1)}, bf16[8,128,640]{2,1,0:T(8,128)(2,1)}, u32[]{:S(2)}, u32[]{:S(2)}) collective-permute-start(bf16[8,128,640]{2,1,0:T(8,128)(2,1)} %shard_map.66), channel_id=1, source_target_pairs={{0,12},{8,4},{1,13},{9,5},{2,14},{10,6},{3,15},{11,7},{16,28},{24,... | collective-permute-start | bytes 3932168 | tf_op jit(solution)/shard_map/ppermute | solution.py:254
  27.2 6.4 %collective-permute-start.7 = (f16[2,8,1,32,128]{4,3,1,0,2:T(8,128)(2,1)S(1)}, f16[2,8,1,32,128]{4,3,1,0,2:T(8,128)(2,1)S(1)}, u32[]{:S(2)}, u32[]{:S(2)}) collective-permute-start(f16[2,8,1,32,128]{4,3,1,0,2:T(8,128)(2,1)S(1)} %multiply_convert_fusion.1), channel_id=1, source_target_pairs={{0,2},{1,3},{2,0},{3,1},{8,10},{9,11},{10,8},{11,9},{16,18},{17,19... | collective-permute-start | bytes 393224 | tf_op jit(solution)/shard_map/ppermute | solution.py:211
  31.5 5.6 %copy-start.10 = (f32[2,8,2,32,128]{4,3,1,0,2:T(8,128)}, f32[2,8,2,32,128]{4,3,1,0,2:T(8,128)S(1)}, u32[]{:S(2)}) copy-start(f32[2,8,2,32,128]{4,3,1,0,2:T(8,128)S(1)} %bitcast_add_fusion.3) | copy-start | bytes 1572868
  31.6 5.5 %collective-permute-start.5 = (f16[2,8,1,32,128]{4,3,1,0,2:T(8,128)(2,1)S(1)}, f16[2,8,1,32,128]{4,3,1,0,2:T(8,128)(2,1)S(1)}, u32[]{:S(2)}, u32[]{:S(2)}) collective-permute-start(f16[2,8,1,32,128]{4,3,1,0,2:T(8,128)(2,1)S(1)} %multiply_convert_fusion.2), channel_id=1, source_target_pairs={{0,2},{1,3},{2,0},{3,1},{4,6},{5,7},{6,4},{7,5},{8,10},{9,11},{10,... | collective-permute-start | bytes 393224 | tf_op jit(solution)/shard_map/ppermute | solution.py:211
  33.5 0.7 copy-start.11
  37.1 0.7 copy-start.13
  48.5 2.7 %copy-start.3 = (f32[2,8,128,128]{3,2,1,0:T(8,128)}, f32[2,8,128,128]{3,2,1,0:T(8,128)S(1)}, u32[]{:S(2)}) copy-start(f32[2,8,128,128]{3,2,1,0:T(8,128)S(1)} %shard_map.68.refs_2_.refs_4_) | copy-start | bytes 3145732
  48.5 9.7 %collective-permute-start.11 = (bf16[4,128,640]{2,1,0:T(8,128)(2,1)}, bf16[4,128,640]{2,1,0:T(8,128)(2,1)}, u32[]{:S(2)}, u32[]{:S(2)}) collective-permute-start(bf16[4,128,640]{2,1,0:T(8,128)(2,1)} %get-tuple-element.27), channel_id=1, source_target_pairs={{0,4},{8,12},{1,5},{9,13},{2,6},{10,14},{3,7},{11,15},{16,20},{24,... | collective-permute-start | bytes 1966088 | tf_op jit(solution)/shard_map/ppermute | solution.py:259
  49.8 8.4 %collective-permute-start.12 = (bf16[4,128,640]{2,1,0:T(8,128)(2,1)}, bf16[4,128,640]{2,1,0:T(8,128)(2,1)}, u32[]{:S(2)}, u32[]{:S(2)}) collective-permute-start(bf16[4,128,640]{2,1,0:T(8,128)(2,1)} %get-tuple-element.28), channel_id=1, source_target_pairs={{0,4},{8,12},{1,5},{9,13},{2,6},{10,14},{3,7},{11,15},{16,20},{24,... | collective-permute-start | bytes 1966088 | tf_op jit(solution)/shard_map/ppermute | solution.py:259
  52.0 5.5 %collective-permute-start.13 = (f16[2,8,2,32,128]{4,3,2,1,0:T(8,128)(2,1)}, f16[2,8,2,32,128]{4,3,2,1,0:T(8,128)(2,1)}, u32[]{:S(2)}, u32[]{:S(2)}) collective-permute-start(f16[2,8,2,32,128]{4,3,2,1,0:T(8,128)(2,1)} %copy.24), channel_id=1, source_target_pairs={{0,1},{1,0},{2,3},{3,2},{4,5},{5,4},{6,7},{7,6},{8,9},{9,8},{10,11... | collective-permute-start | bytes 786440 | tf_op jit(solution)/shard_map/ppermute | solution.py:211
  58.2 1.3 %copy-start.2 = (bf16[8,128,640]{2,1,0:T(8,128)(2,1)S(1)}, bf16[8,128,640]{2,1,0:T(8,128)(2,1)}, u32[]{:S(2)}) copy-start(bf16[8,128,640]{2,1,0:T(8,128)(2,1)} %copy-done) | copy-start | bytes 3932164
  59.5 1.2 %copy-start.4 = (f32[2,8,128,128]{3,2,1,0:T(8,128)S(1)}, f32[2,8,128,128]{3,2,1,0:T(8,128)}, u32[]{:S(2)}) copy-start(f32[2,8,128,128]{3,2,1,0:T(8,128)} %copy-done.3) | copy-start | bytes 3145732
  65.8 3.6 %copy-start.5 = (f32[2,8,128,128]{3,2,1,0:T(8,128)S(1)}, f32[2,8,128,128]{3,2,1,0:T(8,128)}, u32[]{:S(2)}) copy-start(f32[2,8,128,128]{3,2,1,0:T(8,128)} %copy-done.3) | copy-start | bytes 3145732
  66.0 7.2 %collective-permute-start.14 = (f16[2,8,2,32,128]{4,3,1,0,2:T(8,128)(2,1)S(1)}, f16[2,8,2,32,128]{4,3,1,0,2:T(8,128)(2,1)S(1)}, u32[]{:S(2)}, u32[]{:S(2)}) collective-permute-start(f16[2,8,2,32,128]{4,3,1,0,2:T(8,128)(2,1)S(1)} %fusion.7), channel_id=1, source_target_pairs={{4,5},{5,4},{6,7},{7,6},{12,13},{13,12},{14,15},{15,14},{20,21},{2... | collective-permute-start | bytes 786440 | tf_op jit(solution)/shard_map/ppermute | solution.py:211
  70.4 11.9 %copy-start.12 = (f16[2,8,1,32,128]{4,3,1,0,2:T(8,128)(2,1)S(1)}, f16[2,8,1,32,128]{4,3,1,0,2:T(8,128)(2,1)}, u32[]{:S(2)}) copy-start(f16[2,8,1,32,128]{4,3,1,0,2:T(8,128)(2,1)} %copy-done.11) | copy-start | bytes 393220
  70.5 7.6 %collective-permute-start.16 = (f16[2,8,1,32,128]{4,3,2,1,0:T(8,128)(2,1)S(1)}, f16[2,8,1,32,128]{4,3,2,1,0:T(8,128)(2,1)S(1)}, u32[]{:S(2)}, u32[]{:S(2)}) collective-permute-start(f16[2,8,1,32,128]{4,3,2,1,0:T(8,128)(2,1)S(1)} %fusion.10), channel_id=1, source_target_pairs={{0,2},{1,3},{2,0},{3,1},{4,6},{5,7},{6,4},{7,5},{8,10},{9,11},{10,... | collective-permute-start | bytes 393224 | tf_op jit(solution)/shard_map/ppermute | solution.py:211
  73.3 8.9 %collective-permute-start.15 = (f16[2,8,1,32,128]{4,3,1,0,2:T(8,128)(2,1)S(1)}, f16[2,8,1,32,128]{4,3,1,0,2:T(8,128)(2,1)S(1)}, u32[]{:S(2)}, u32[]{:S(2)}) collective-permute-start(f16[2,8,1,32,128]{4,3,1,0,2:T(8,128)(2,1)S(1)} %multiply_convert_fusion), channel_id=1, source_target_pairs={{4,6},{5,7},{6,4},{7,5},{12,14},{13,15},{14,12},{15,13},{20,22},{2... | collective-permute-start | bytes 393224 | tf_op jit(solution)/shard_map/ppermute | solution.py:211

commit v10 on v9

--- a/solution.py
+++ b/solution.py
@@ -8,7 +8,7 @@
 from jax.sharding import PartitionSpec as P
 
 LIMIT = 16 << 20
-SPLIT = (4, 4)
+SPLIT = (1, 7)
 COST = pl.CostEstimate(flops=1000, bytes_accessed=1000, transcendentals=0)
 PARAMS = pltpu.CompilerParams(vmem_limit_bytes=LIMIT)
 ANY = pl.BlockSpec(memory_space=pl.ANY)
@@ -71,8 +71,7 @@
 
 
 def root_rows(band, freq_count):
-    rows = freq_count * (band + sum(band - d for d in range(1, band)))
-    return -(-rows // 8) * 8
+    return -(-(root_row(band, freq_count, band, 0, 0) + freq_count) // 8) * 8
 
 
 def own_tile(own, slot, m, blocks_dev):
@@ -122,6 +121,13 @@
                     roots[m, pl.ds(spot, 1), :] = kept
                     if delta == 1:
                         one[m, slot, w] = kept
+                if slot == 0:
+                    there = m + ((aux_pos + 2) >= n_aux).astype(jnp.int32)
+                    row = jnp.minimum(there, blocks_dev - 1) * band + 2
+                    both = (centre >= 0) & (number < of_region(region)) & (there < blocks_dev)
+                    both = both & (records[n_aux - 1][m * band + 1] > 0) & (records[n_aux - 2][row] > 0)
+                    spot = root_row(band, freq_count, band, 0, w)
+                    roots[m, pl.ds(spot, 1), :] = root * both.astype(jnp.float32)
     for m in range(blocks_dev):
         for w in range(freq_count):
             total = None
@@ -193,6 +199,37 @@
         compiler_params=PARAMS,
         cost_estimate=COST,
     )(roots, *arrays, *after)
+
+
+def second_kernel(dims, pieces, roots, own, lower, *refs):
+    n_aux, n_pair, blocks_dev, band, freq_count = dims
+    out, out_next = refs[-2:]
+    for m in range(blocks_dev):
+        n, row = pieces[m]
+        left = own[m].astype(jnp.float32)
+        right = refs[n][row].astype(jnp.float32)
+        other = lower[m].astype(jnp.float32)
+        for w in range(freq_count):
+            kept = roots[m, pl.ds(root_row(band, freq_count, 2, 0, w), 1), :]
+            root = roots[m, pl.ds(root_row(band, freq_count, None, 0, w), 1), :]
+            next_kept = roots[m, pl.ds(root_row(band, freq_count, band, 0, w), 1), :]
+            scaled = (right * root).astype(jnp.bfloat16)
+            out[w, m] = dot((left * kept).astype(jnp.bfloat16), scaled)
+            out_next[w, m] = dot((other * next_kept).astype(jnp.bfloat16), scaled)
+
+
+def second_rows(dims, roots, own, lower, c2, after):
+    n_aux, n_pair, blocks_dev, band, freq_count = dims
+    aux_rows = own[0].shape[-2]
+    pieces = [(n, row) for n, array in enumerate(c2) for row in range(array.shape[0])]
+    return pl.pallas_call(
+        functools.partial(second_kernel, dims, pieces),
+        out_shape=[jax.ShapeDtypeStruct((freq_count, blocks_dev, aux_rows, aux_rows), jnp.float32)] * 2,
+        in_specs=[VMEM] * (3 + len(c2)) + [ANY] * len(after),
+        out_specs=[VMEM] * 2,
+        compiler_params=PARAMS,
+        cost_estimate=COST,
+    )(roots, own[0], lower, *c2, *after)
 
 
 def halve(keep, pair_col, step, n_pair, rings, scale):
@@ -243,22 +280,20 @@
     first_slot, rest, near_two, far_two, to_one = pack(tiles, plan)
     own = (first_slot, rest)
     down2 = [(s, (s - 2) % n_aux) for s in whole]
-    c2 = [lax.ppermute(p, "aux", down2) for p in tie([near_two, far_two], records[1:])]
+    c2 = [lax.ppermute(near_two, "aux", down2)]
+    (far_two,) = tie([far_two], records[1:] + c2)
+    c2.append(lax.ppermute(far_two, "aux", down2))
     to_even = lax.ppermute(rest, "aux", [(s, s - 1) for s in odds])
     table = virt_energy.reshape(1, -1)
-    rows0, rows_even, roots = first_rows(dims, records, occ_energy, frequencies, table, own, to_even, [])
-
-    def rows_of(delta, slots, far, after, add=None):
-        return band_rows(dims, delta, slots, roots, own, far, after, add)
-
+    rows0, rows_even, roots = first_rows(dims, records, occ_energy, frequencies, table, own, to_even, [far_two])
     b1 = lax.ppermute(tie([to_one], [roots])[0], "aux", [(s, (s - 1) % n_aux) for s in evens])
     bits0, z0 = totals(rows0, pair_col, n_pair, whole, scale)
     bits_even, z_even = totals(rows_even, pair_col, n_pair, evens, scale)
-    rows2 = rows_of(2, [0], [c2], [bits0[-1], bits_even[-1]])
+    rows2, rows_next = second_rows(dims, roots, own, to_even, c2, [bits0[-1], bits_even[-1]])
     bits2, z2 = totals(rows2, pair_col, n_pair, whole, scale)
-    to_odd = [lax.ppermute(c, "aux", [(s, s + 1) for s in evens]) for c in tie(c2, [rows2])]
-    part = rows_of(1, [1], [to_odd], [rows2])
-    rows_odd = rows_of(1, [0], [[b1]], [bits2[0]], part)
+    term = lax.ppermute((rows_next * scale).astype(jnp.float16), "aux", [(s, s + 1) for s in evens])
+    rows_odd = band_rows(dims, 1, [0], roots, own, [[b1]], [bits2[0]])
+    rows_odd = rows_odd + term.astype(jnp.float32) * (1.0 / scale)
     _, z_odd = totals(rows_odd, pair_col, n_pair, odds, scale)
     even = lax.axis_index("aux").astype(jnp.uint32) & jnp.uint32(1) == 0
     out = jnp.concatenate([z0, jnp.where(even, z_even, z_odd), z2], axis=-1)

time: 84 us -> 78.9 us (0.939)
  local copies, waits for them, and re-layouts: 8.26 us -> 4.03 us
  other arithmetic: 4.6 us -> 6.76 us
  waiting for transfers between devices: 24.7 us -> 22.6 us
  starting transfers between devices: 28.8 us -> 27.1 us
  Pallas kernels: 15.9 us -> 17 us
    ppermute x4 -> x3, waiting for transfers between devices: 8.26 us -> 3.39 us  [the longest x1 3.38 us: on_device(): c2.append(lax.ppermute(far_two, 'aux', down2))]
    unnamed x31 -> x19, local copies, waits for them, and re-layouts: 7.13 us -> 2.86 us
    pallas_call x3 -> x1, Pallas kernels: 7.47 us -> 3.29 us  [band_rows(): pl.pallas_call(functools.partial(band_kernel, dims, delta, slots, rights,...]
    pallas_call x0 -> x1, Pallas kernels: none -> 3.82 us  [second_rows(): pl.pallas_call(functools.partial(second_kernel, dims, pieces), out_shape=...]
    ppermute x3, starting transfers between devices: 3.45 us -> 0.78 us  [on_device(): lax.ppermute(record, 'aux', [(s, (s + k) % n_aux) for s in range(n_aux)])]
    ppermute x1, waiting for transfers between devices: 0.01 us -> 1.83 us  [on_device(): lax.ppermute(tie([to_one], [roots])[0], 'aux', [(s, (s - 1) % n_aux) for...]
    add x0 -> x1, other arithmetic: none -> 1.19 us  [on_device(): rows_odd = rows_odd + term.astype(jnp.float32) * (1.0 / scale)]
    ppermute x4 -> x3, starting transfers between devices: 4.05 us -> 5.07 us  [the longest x1 2.66 us: on_device(): c2 = [lax.ppermute(near_two, 'aux', down2)]]
  transfers between devices with their start and end apart: 17 -> 16, of which waited for: 8 -> 10; matrix products, arithmetic and copies ran while one was open for 6% -> 7% of each run, Pallas kernels for 14% -> 19%
where the time goes in v10:
time: 78.9 us; the launch traced here: 78.4 us
  starting transfers between devices  27.1 us (34%)
  waiting for transfers between devices  22.6 us (29%)
  Pallas kernels  17 us (22%)
  other arithmetic  6.76 us (9%)
  local copies, waits for them, and re-layouts  4.03 us (5%)
  between operations  0.96 us (1%)
    ppermute x8, starting transfers between devices, halve(): got = lax.ppermute(sent, ('aux', 'pair'), pairs)  16.4 us
    ppermute x8, waiting for transfers between devices, halve(): got = lax.ppermute(sent, ('aux', 'pair'), pairs)  14.8 us
    pallas_call x1, Pallas kernels, first_rows(): pl.pallas_call(functools.partial(first_kernel, dims), out_shape=[jax.Shap...  7.43 us
    pallas_call x1, Pallas kernels, second_rows(): pl.pallas_call(functools.partial(second_kernel, dims, pieces), out_shape=...  3.82 us
    ppermute x1, starting transfers between devices, on_device(): to_even = lax.ppermute(rest, 'aux', [(s, s - 1) for s in odds])  3.63 us
    ppermute x1, waiting for transfers between devices, on_device(): c2.append(lax.ppermute(far_two, 'aux', down2))  3.38 us
    pallas_call x1, Pallas kernels, band_rows(): pl.pallas_call(functools.partial(band_kernel, dims, delta, slots, rights,...  3.29 us
    unnamed x19, local copies, waits for them, and re-layouts  2.86 us
  transfers between devices with their start and end apart: 16, of which 10 were waited for; matrix products, arithmetic and copies ran while one was open for 7% of the time, Pallas kernels for 19%

profile of v10, /device:TPU:1, one launch (start us, length us, event | category | flops | bytes accessed | tf_op | source)
XLA Modules:
  0.0 78.4 jit_solution(7557330860086773424)
XLA Ops:
  0.0 2.1 %copy-done = bf16[1,1,8,3,1,128,640]{6,5,4,3,2,1,0:T(8,128)(2,1)S(1)} copy-done((bf16[1,1,8,3,1,128,640]{6,5,4,3,2,1,0:T(8,128)(2,1)S(1)}, bf16[1,1,8,3,1,128,640]{6,5,4,3,2,1,0:T(8,128)(2,1)}, u32[]{:S(2)}) %copy-start) | copy-done | bytes 3932184
  2.1 2.4 %shard_map.64 = (bf16[8,128,640]{2,1,0:T(8,128)(2,1)S(1)}, bf16[16,128,640]{2,1,0:T(8,128)(2,1)}, bf16[1,128,640]{2,1,0:T(8,128)(2,1)S(1)}, bf16[7,128,640]{2,1,0:T(8,128)(2,1)S(1)}, bf16[8,128,640]{2,1,0:T(8,128)(2,1)}) custom-call(bf16[8,3,128,640]{3,2,1,0:T(8,128)(2,1)S(1)} %bitcast.63), custom_call_target="tpu_custom_call" | custom-call | flops 1000 | bytes 1000 | tf_op jit(solution)/shard_map/pallas_call | solution.py:46
  4.6 3.6 %collective-permute-start.3 = (bf16[16,128,640]{2,1,0:T(8,128)(2,1)}, bf16[16,128,640]{2,1,0:T(8,128)(2,1)}, u32[]{:S(2)}, u32[]{:S(2)}) collective-permute-start(bf16[16,128,640]{2,1,0:T(8,128)(2,1)} %get-tuple-element.16.refs_8_.refs_1_), channel_id=1, source_target_pairs={{4,0},{12,8},{5,1},{13,9},{6,2},{14,10},{7,3},{15,11},{20,16},{28,... | collective-permute-start | bytes 7864328 | tf_op jit(solution)/shard_map/ppermute | solution.py:286
  8.2 2.7 %collective-permute-start.4 = (bf16[1,128,640]{2,1,0:T(8,128)(2,1)S(1)}, bf16[1,128,640]{2,1,0:T(8,128)(2,1)S(1)}, u32[]{:S(2)}, u32[]{:S(2)}) collective-permute-start(bf16[1,128,640]{2,1,0:T(8,128)(2,1)S(1)} %get-tuple-element.18), channel_id=1, source_target_pairs={{0,8},{4,12},{8,0},{12,4},{1,9},{5,13},{9,1},{13,5},{2,10},{6,14},... | collective-permute-start | bytes 491528 | tf_op jit(solution)/shard_map/ppermute | solution.py:283
  11.8 0.7 collective-permute-start.2
  12.5 0.7 collective-permute-done.refs_1_
  13.3 0.9 %collective-permute-done.1.refs_2_ = s32[25]{0:T(128)S(1)} collective-permute-done((s32[25]{0:T(128)S(1)}, s32[25]{0:T(128)S(1)}, u32[]{:S(2)}, u32[]{:S(2)}) %collective-permute-start.1) | collective-permute-done | bytes 132 | tf_op jit(solution)/shard_map/ppermute | solution.py:274
  14.2 0.9 %collective-permute-done.2.refs_3_ = s32[25]{0:T(128)S(1)} collective-permute-done((s32[25]{0:T(128)S(1)}, s32[25]{0:T(128)S(1)}, u32[]{:S(2)}, u32[]{:S(2)}) %collective-permute-start.2) | collective-permute-done | bytes 132 | tf_op jit(solution)/shard_map/ppermute | solution.py:274
  15.1 1.1 %collective-permute-start.10 = (bf16[7,128,640]{2,1,0:T(8,128)(2,1)S(1)}, bf16[7,128,640]{2,1,0:T(8,128)(2,1)S(1)}, u32[]{:S(2)}, u32[]{:S(2)}) collective-permute-start(bf16[7,128,640]{2,1,0:T(8,128)(2,1)S(1)} %shard_map.65.refs_10_), channel_id=1, source_target_pairs={{0,8},{4,12},{8,0},{12,4},{1,9},{5,13},{9,1},{13,5},{2,10},{6,14},... | collective-permute-start | bytes 3440648 | tf_op jit(solution)/shard_map/ppermute | solution.py:285
  16.3 7.4 %shard_map.66 = (f32[2,8,128,128]{3,2,1,0:T(8,128)S(1)}, f32[2,8,128,128]{3,2,1,0:T(8,128)S(1)}, f32[8,16,640]{2,1,0:T(8,128)S(1)}) custom-call(s32[25]{0:T(128)S(1)} %pad_add_fusion.refs_0_, s32[25]{0:T(128)S(1)} %collective-permute-done.refs_1_, s32[25]{0:T(128)S(1)} %collective-permute-done.1.refs_2_, s32[25]{0:T(128)S(1)} %collective-permute-done.2.refs_3_, ...), custom_call_target="tpu_custom_call" | custom-call | flops 1000 | bytes 1000 | tf_op jit(solution)/shard_map/pallas_call | solution.py:151
  24.7 1.4 %collective-permute-start.5 = (f16[2,8,2,32,128]{4,3,1,0,2:T(8,128)(2,1)S(1)}, f16[2,8,2,32,128]{4,3,1,0,2:T(8,128)(2,1)S(1)}, u32[]{:S(2)}, u32[]{:S(2)}) collective-permute-start(f16[2,8,2,32,128]{4,3,1,0,2:T(8,128)(2,1)S(1)} %fusion.4), channel_id=1, source_target_pairs={{0,1},{1,0},{2,3},{3,2},{4,5},{5,4},{6,7},{7,6},{8,9},{9,8},{10,11... | collective-permute-start | bytes 786440 | tf_op jit(solution)/shard_map/ppermute | solution.py:248
  26.1 1.3 %collective-permute-start.9 = (bf16[8,128,640]{2,1,0:T(8,128)(2,1)}, bf16[8,128,640]{2,1,0:T(8,128)(2,1)}, u32[]{:S(2)}, u32[]{:S(2)}) collective-permute-start(bf16[8,128,640]{2,1,0:T(8,128)(2,1)} %shard_map.67), channel_id=1, source_target_pairs={{0,12},{8,4},{1,13},{9,5},{2,14},{10,6},{3,15},{11,7},{16,28},{24,... | collective-permute-start | bytes 3932168 | tf_op jit(solution)/shard_map/ppermute | solution.py:289
  28.2 3.5 %collective-permute-done.5 = f16[2,8,2,32,128]{4,3,1,0,2:T(8,128)(2,1)S(1)} collective-permute-done((f16[2,8,2,32,128]{4,3,1,0,2:T(8,128)(2,1)S(1)}, f16[2,8,2,32,128]{4,3,1,0,2:T(8,128)(2,1)S(1)}, u32[]{:S(2)}, u32[]{:S(2)}) %collective-permute-start.5) | collective-permute-done | bytes 262176 | tf_op jit(solution)/shard_map/ppermute | solution.py:248
  31.9 2.2 %collective-permute-start.6 = (f16[2,8,1,32,128]{4,3,1,0,2:T(8,128)(2,1)S(1)}, f16[2,8,1,32,128]{4,3,1,0,2:T(8,128)(2,1)S(1)}, u32[]{:S(2)}, u32[]{:S(2)}) collective-permute-start(f16[2,8,1,32,128]{4,3,1,0,2:T(8,128)(2,1)S(1)} %multiply_convert_fusion.3), channel_id=1, source_target_pairs={{0,2},{1,3},{2,0},{3,1},{4,6},{5,7},{6,4},{7,5},{8,10},{9,11},{10,... | collective-permute-start | bytes 393224 | tf_op jit(solution)/shard_map/ppermute | solution.py:248
  34.0 3.2 %collective-permute-done.6 = f16[2,8,1,32,128]{4,3,1,0,2:T(8,128)(2,1)S(1)} collective-permute-done((f16[2,8,1,32,128]{4,3,1,0,2:T(8,128)(2,1)S(1)}, f16[2,8,1,32,128]{4,3,1,0,2:T(8,128)(2,1)S(1)}, u32[]{:S(2)}, u32[]{:S(2)}) %collective-permute-start.6) | collective-permute-done | bytes 131104 | tf_op jit(solution)/shard_map/ppermute | solution.py:248
  37.9 3.4 %collective-permute-done.10.refs_1_ = bf16[7,128,640]{2,1,0:T(8,128)(2,1)S(1)} collective-permute-done((bf16[7,128,640]{2,1,0:T(8,128)(2,1)S(1)}, bf16[7,128,640]{2,1,0:T(8,128)(2,1)S(1)}, u32[]{:S(2)}, u32[]{:S(2)}) %collective-permute-start.10) | collective-permute-done | bytes 1146912 | tf_op jit(solution)/shard_map/ppermute | solution.py:285
  41.2 3.8 %shard_map.68 = (f32[2,8,128,128]{3,2,1,0:T(8,128)S(1)}, f32[2,8,128,128]{3,2,1,0:T(8,128)S(1)}) custom-call(f32[8,16,640]{2,1,0:T(8,128)S(1)} %get-tuple-element.21.refs_1_.roots, bf16[8,128,640]{2,1,0:T(8,128)(2,1)S(1)} %get-tuple-element.15.refs_7_.own.refs_0_, bf16[16,128,640]{2,1,0:T(8,128)(2,1)} %collective-permute-done.3.refs_9_.lower, ...), custom_call_target="tpu_custom_call" | custom-call | flops 1000 | bytes 1000 | tf_op jit(solution)/shard_map/pallas_call | solution.py:225
  45.1 1.0 %multiply_convert_fusion = f16[2,8,128,128]{3,2,1,0:T(8,128)(2,1)} fusion(f32[2,8,128,128]{3,2,1,0:T(8,128)S(1)} %get-tuple-element.24), kind=kLoop, calls=%fused_computation.1 | loop fusion | flops 524288 | bytes 1572864 | tf_op jit(solution)/shard_map/convert_element_type | solution.py:294
  46.0 1.3 %collective-permute-start.12 = (f16[2,8,128,128]{3,2,1,0:T(8,128)(2,1)}, f16[2,8,128,128]{3,2,1,0:T(8,128)(2,1)}, u32[]{:S(2)}, u32[]{:S(2)}) collective-permute-start(f16[2,8,128,128]{3,2,1,0:T(8,128)(2,1)} %multiply_convert_fusion), channel_id=1, source_target_pairs={{0,4},{8,12},{1,5},{9,13},{2,6},{10,14},{3,7},{11,15},{16,20},{24,... | collective-permute-start | bytes 1572872 | tf_op jit(solution)/shard_map/ppermute | solution.py:294
  47.4 0.8 %copy.21 = f16[2,8,2,32,128]{4,3,2,1,0:T(8,128)(2,1)} copy(f16[2,8,2,32,128]{4,3,1,0,2:T(8,128)(2,1)S(1)} %fusion.6) | data formatting | bytes 524288 | tf_op jit(solution)/shard_map/convert_element_type | solution.py:246
  48.2 1.2 %collective-permute-start.11 = (f16[2,8,2,32,128]{4,3,2,1,0:T(8,128)(2,1)}, f16[2,8,2,32,128]{4,3,2,1,0:T(8,128)(2,1)}, u32[]{:S(2)}, u32[]{:S(2)}) collective-permute-start(f16[2,8,2,32,128]{4,3,2,1,0:T(8,128)(2,1)} %copy.21), channel_id=1, source_target_pairs={{0,1},{1,0},{2,3},{3,2},{4,5},{5,4},{6,7},{7,6},{8,9},{9,8},{10,11... | collective-permute-start | bytes 786440 | tf_op jit(solution)/shard_map/ppermute | solution.py:248
  49.4 1.1 %add_bitcast_fusion = f32[2,8,32,128]{3,2,1,0:T(8,128)S(1)} fusion(f16[2,8,1,32,128]{4,3,1,0,2:T(8,128)(2,1)} %copy-done.7, f32[2,8,2,32,128]{4,3,1,0,2:T(8,128)} %copy-done.4, u32[]{:T(128)S(6)} %and.18), kind=kLoop, calls=%fused_computation.27 | loop fusion | flops 196608 | bytes 655364 | tf_op jit(solution)/shard_map/squeeze | solution.py:260
  50.5 3.2 %collective-permute-done.11 = f16[2,8,2,32,128]{4,3,2,1,0:T(8,128)(2,1)} collective-permute-done((f16[2,8,2,32,128]{4,3,2,1,0:T(8,128)(2,1)}, f16[2,8,2,32,128]{4,3,2,1,0:T(8,128)(2,1)}, u32[]{:S(2)}, u32[]{:S(2)}) %collective-permute-start.11) | collective-permute-done | bytes 262176 | tf_op jit(solution)/shard_map/ppermute | solution.py:248
  54.4 1.8 %collective-permute-done.9.refs_2_ = bf16[8,128,640]{2,1,0:T(8,128)(2,1)} collective-permute-done((bf16[8,128,640]{2,1,0:T(8,128)(2,1)}, bf16[8,128,640]{2,1,0:T(8,128)(2,1)}, u32[]{:S(2)}, u32[]{:S(2)}) %collective-permute-start.9) | collective-permute-done | bytes 1310752 | tf_op jit(solution)/shard_map/ppermute | solution.py:289
  56.3 3.3 %shard_map.69 = f32[2,8,128,128]{3,2,1,0:T(8,128)S(1)} custom-call(f32[8,16,640]{2,1,0:T(8,128)S(1)} %get-tuple-element.21.refs_1_.roots, bf16[8,128,640]{2,1,0:T(8,128)(2,1)S(1)} %get-tuple-element.15.refs_7_.own.refs_0_, bf16[16,128,640]{2,1,0:T(8,128)(2,1)} %get-tuple-element.16.refs_8_.refs_1_, bf16[8,128,640]{2,1,0:T(8,128)(2,1)} %collective-permute-done.9.refs_2_, ...), custom_call_target="tpu_custom_call" | custom-call | flops 1000 | bytes 1000 | tf_op jit(solution)/shard_map/pallas_call | solution.py:194
  59.6 1.2 %multiply_add_fusion = f32[2,8,128,128]{3,2,1,0:T(8,128)S(1)} fusion(f32[2,8,128,128]{3,2,1,0:T(8,128)S(1)} %shard_map.69, f16[2,8,128,128]{3,2,1,0:T(8,128)(2,1)} %collective-permute-done.12), kind=kLoop, calls=%fused_computation | loop fusion | flops 786432 | bytes 2621440 | tf_op jit(solution)/shard_map/add | solution.py:296
  60.9 3.2 %collective-permute-start.13 = (f16[2,8,2,32,128]{4,3,1,0,2:T(8,128)(2,1)S(1)}, f16[2,8,2,32,128]{4,3,1,0,2:T(8,128)(2,1)S(1)}, u32[]{:S(2)}, u32[]{:S(2)}) collective-permute-start(f16[2,8,2,32,128]{4,3,1,0,2:T(8,128)(2,1)S(1)} %fusion.7), channel_id=1, source_target_pairs={{4,5},{5,4},{6,7},{7,6},{12,13},{13,12},{14,15},{15,14},{20,21},{2... | collective-permute-start | bytes 786440 | tf_op jit(solution)/shard_map/ppermute | solution.py:248
  64.1 1.0 %bitcast_add_fusion = f32[2,8,2,32,128]{4,3,2,1,0:T(8,128)S(1)} fusion(f16[2,8,2,32,128]{4,3,2,1,0:T(8,128)(2,1)} %collective-permute-done.11, f32[2,8,2,2,32,128]{5,4,3,2,1,0:T(8,128)S(1)} %bitcast.65, u32[]{:T(128)S(6)} %and.8), kind=kLoop, calls=%fused_computation.11 | loop fusion | flops 393216 | bytes 1310724 | tf_op jit(solution)/shard_map/add | solution.py:249
  65.3 2.4 %collective-permute-start.15 = (f16[2,8,1,32,128]{4,3,2,1,0:T(8,128)(2,1)S(1)}, f16[2,8,1,32,128]{4,3,2,1,0:T(8,128)(2,1)S(1)}, u32[]{:S(2)}, u32[]{:S(2)}) collective-permute-start(f16[2,8,1,32,128]{4,3,2,1,0:T(8,128)(2,1)S(1)} %fusion.10), channel_id=1, source_target_pairs={{0,2},{1,3},{2,0},{3,1},{4,6},{5,7},{6,4},{7,5},{8,10},{9,11},{10,... | collective-permute-start | bytes 393224 | tf_op jit(solution)/shard_map/ppermute | solution.py:248
  68.2 4.7 %collective-permute-start.14 = (f16[2,8,1,32,128]{4,3,1,0,2:T(8,128)(2,1)S(1)}, f16[2,8,1,32,128]{4,3,1,0,2:T(8,128)(2,1)S(1)}, u32[]{:S(2)}, u32[]{:S(2)}) collective-permute-start(f16[2,8,1,32,128]{4,3,1,0,2:T(8,128)(2,1)S(1)} %multiply_convert_fusion.1), channel_id=1, source_target_pairs={{4,6},{5,7},{6,4},{7,5},{12,14},{13,15},{14,12},{15,13},{20,22},{2... | collective-permute-start | bytes 393224 | tf_op jit(solution)/shard_map/ppermute | solution.py:248
  72.9 4.4 %collective-permute-done.14 = f16[2,8,1,32,128]{4,3,1,0,2:T(8,128)(2,1)S(1)} collective-permute-done((f16[2,8,1,32,128]{4,3,1,0,2:T(8,128)(2,1)S(1)}, f16[2,8,1,32,128]{4,3,1,0,2:T(8,128)(2,1)S(1)}, u32[]{:S(2)}, u32[]{:S(2)}) %collective-permute-start.14) | collective-permute-done | bytes 131104 | tf_op jit(solution)/shard_map/ppermute | solution.py:248
  77.5 0.9 %maximum_bitcast_fusion = f32[2,8,1,32,384]{4,3,2,1,0:T(8,128)} fusion(f32[2,8,32,128]{3,2,1,0:T(8,128)S(1)} %fusion.9, f32[2,8,32,128]{3,2,1,0:T(8,128)S(1)} %select_bitcast_fusion, f32[2,8,32,128]{3,2,1,0:T(8,128)S(1)} %add_bitcast_fusion), kind=kLoop, calls=%fused_computation.2 | loop fusion | flops 393216 | bytes 1572864 | tf_op jit(solution)/shard_map/broadcast_in_dim | solution.py:300
  (52 shorter events, 4.5 us)
Async XLA Ops:
  0.0 2.1 %copy-start = (bf16[1,1,8,3,1,128,640]{6,5,4,3,2,1,0:T(8,128)(2,1)S(1)}, bf16[1,1,8,3,1,128,640]{6,5,4,3,2,1,0:T(8,128)(2,1)}, u32[]{:S(2)}) copy-start(bf16[1,1,8,3,1,128,640]{6,5,4,3,2,1,0:T(8,128)(2,1)} %param.6) | copy-start | bytes 11796484
  2.1 8.7 %copy-start.8 = (s32[1,1,8,3,1]{2,4,3,1,0:T(1,128)S(1)}, s32[1,1,8,3,1]{2,4,3,1,0:T(1,128)}, u32[]{:S(2)}) copy-start(s32[1,1,8,3,1]{2,4,3,1,0:T(1,128)} %param.7) | copy-start | bytes 292
  4.6 11.7 %copy-start.1 = (f32[10240]{0:T(1024)S(1)}, f32[10240]{0:T(1024)}, u32[]{:S(2)}) copy-start(f32[10240]{0:T(1024)} %param.10) | copy-start | bytes 122884
  4.6 11.7 %copy-start.2 = (f32[8]{0:T(128)S(1)}, f32[8]{0:T(128)}, u32[]{:S(2)}) copy-start(f32[8]{0:T(128)} %refs_4_.1) | copy-start | bytes 100
  4.6 11.7 %copy-start.3 = (f32[2]{0:T(128)S(1)}, f32[2]{0:T(128)}, u32[]{:S(2)}) copy-start(f32[2]{0:T(128)} %refs_5_.1) | copy-start | bytes 28
  4.6 11.7 %collective-permute-start.3 = (bf16[16,128,640]{2,1,0:T(8,128)(2,1)}, bf16[16,128,640]{2,1,0:T(8,128)(2,1)}, u32[]{:S(2)}, u32[]{:S(2)}) collective-permute-start(bf16[16,128,640]{2,1,0:T(8,128)(2,1)} %get-tuple-element.16.refs_8_.refs_1_), channel_id=1, source_target_pairs={{4,0},{12,8},{5,1},{13,9},{6,2},{14,10},{7,3},{15,11},{20,16},{28,... | collective-permute-start | bytes 7864328 | tf_op jit(solution)/shard_map/ppermute | solution.py:286
  8.2 6.9 %collective-permute-start.4 = (bf16[1,128,640]{2,1,0:T(8,128)(2,1)S(1)}, bf16[1,128,640]{2,1,0:T(8,128)(2,1)S(1)}, u32[]{:S(2)}, u32[]{:S(2)}) collective-permute-start(bf16[1,128,640]{2,1,0:T(8,128)(2,1)S(1)} %get-tuple-element.18), channel_id=1, source_target_pairs={{0,8},{4,12},{8,0},{12,4},{1,9},{5,13},{9,1},{13,5},{2,10},{6,14},... | collective-permute-start | bytes 491528 | tf_op jit(solution)/shard_map/ppermute | solution.py:283
  11.8 1.5 %collective-permute-start = (s32[25]{0:T(128)S(1)}, s32[25]{0:T(128)S(1)}, u32[]{:S(2)}, u32[]{:S(2)}) collective-permute-start(s32[25]{0:T(128)S(1)} %pad_add_fusion.refs_0_), channel_id=1, source_target_pairs={{0,4},{4,8},{8,12},{12,0},{1,5},{5,9},{9,13},{13,1},{2,6},{6,10},{... | collective-permute-start | bytes 308 | tf_op jit(solution)/shard_map/ppermute | solution.py:274
  11.8 2.5 %collective-permute-start.1 = (s32[25]{0:T(128)S(1)}, s32[25]{0:T(128)S(1)}, u32[]{:S(2)}, u32[]{:S(2)}) collective-permute-start(s32[25]{0:T(128)S(1)} %pad_add_fusion.refs_0_), channel_id=1, source_target_pairs={{0,8},{4,12},{8,0},{12,4},{1,9},{5,13},{9,1},{13,5},{2,10},{6,14},... | collective-permute-start | bytes 308 | tf_op jit(solution)/shard_map/ppermute | solution.py:274
  11.8 3.3 %collective-permute-start.2 = (s32[25]{0:T(128)S(1)}, s32[25]{0:T(128)S(1)}, u32[]{:S(2)}, u32[]{:S(2)}) collective-permute-start(s32[25]{0:T(128)S(1)} %pad_add_fusion.refs_0_), channel_id=1, source_target_pairs={{0,12},{4,0},{8,4},{12,8},{1,13},{5,1},{9,5},{13,9},{2,14},{6,2},{... | collective-permute-start | bytes 308 | tf_op jit(solution)/shard_map/ppermute | solution.py:274
  15.1 26.1 %collective-permute-start.10 = (bf16[7,128,640]{2,1,0:T(8,128)(2,1)S(1)}, bf16[7,128,640]{2,1,0:T(8,128)(2,1)S(1)}, u32[]{:S(2)}, u32[]{:S(2)}) collective-permute-start(bf16[7,128,640]{2,1,0:T(8,128)(2,1)S(1)} %shard_map.65.refs_10_), channel_id=1, source_target_pairs={{0,8},{4,12},{8,0},{12,4},{1,9},{5,13},{9,1},{13,5},{2,10},{6,14},... | collective-permute-start | bytes 3440648 | tf_op jit(solution)/shard_map/ppermute | solution.py:285
  23.9 3.5 %collective-permute-start.7 = (f16[2,8,2,32,128]{4,3,1,0,2:T(8,128)(2,1)S(1)}, f16[2,8,2,32,128]{4,3,1,0,2:T(8,128)(2,1)S(1)}, u32[]{:S(2)}, u32[]{:S(2)}) collective-permute-start(f16[2,8,2,32,128]{4,3,1,0,2:T(8,128)(2,1)S(1)} %fusion.5), channel_id=1, source_target_pairs={{0,1},{1,0},{2,3},{3,2},{8,9},{9,8},{10,11},{11,10},{16,17},{17,16... | collective-permute-start | bytes 786440 | tf_op jit(solution)/shard_map/ppermute | solution.py:248
  24.7 7.0 %collective-permute-start.5 = (f16[2,8,2,32,128]{4,3,1,0,2:T(8,128)(2,1)S(1)}, f16[2,8,2,32,128]{4,3,1,0,2:T(8,128)(2,1)S(1)}, u32[]{:S(2)}, u32[]{:S(2)}) collective-permute-start(f16[2,8,2,32,128]{4,3,1,0,2:T(8,128)(2,1)S(1)} %fusion.4), channel_id=1, source_target_pairs={{0,1},{1,0},{2,3},{3,2},{4,5},{5,4},{6,7},{7,6},{8,9},{9,8},{10,11... | collective-permute-start | bytes 786440 | tf_op jit(solution)/shard_map/ppermute | solution.py:248
  26.1 30.1 %collective-permute-start.9 = (bf16[8,128,640]{2,1,0:T(8,128)(2,1)}, bf16[8,128,640]{2,1,0:T(8,128)(2,1)}, u32[]{:S(2)}, u32[]{:S(2)}) collective-permute-start(bf16[8,128,640]{2,1,0:T(8,128)(2,1)} %shard_map.67), channel_id=1, source_target_pairs={{0,12},{8,4},{1,13},{9,5},{2,14},{10,6},{3,15},{11,7},{16,28},{24,... | collective-permute-start | bytes 3932168 | tf_op jit(solution)/shard_map/ppermute | solution.py:289
  27.6 6.5 %collective-permute-start.8 = (f16[2,8,1,32,128]{4,3,1,0,2:T(8,128)(2,1)S(1)}, f16[2,8,1,32,128]{4,3,1,0,2:T(8,128)(2,1)S(1)}, u32[]{:S(2)}, u32[]{:S(2)}) collective-permute-start(f16[2,8,1,32,128]{4,3,1,0,2:T(8,128)(2,1)S(1)} %multiply_convert_fusion.2), channel_id=1, source_target_pairs={{0,2},{1,3},{2,0},{3,1},{8,10},{9,11},{10,8},{11,9},{16,18},{17,19... | collective-permute-start | bytes 393224 | tf_op jit(solution)/shard_map/ppermute | solution.py:248
  31.8 5.4 %copy-start.4 = (f32[2,8,2,32,128]{4,3,1,0,2:T(8,128)}, f32[2,8,2,32,128]{4,3,1,0,2:T(8,128)S(1)}, u32[]{:S(2)}) copy-start(f32[2,8,2,32,128]{4,3,1,0,2:T(8,128)S(1)} %bitcast_add_fusion.3) | copy-start | bytes 1572868
  31.9 5.3 %collective-permute-start.6 = (f16[2,8,1,32,128]{4,3,1,0,2:T(8,128)(2,1)S(1)}, f16[2,8,1,32,128]{4,3,1,0,2:T(8,128)(2,1)S(1)}, u32[]{:S(2)}, u32[]{:S(2)}) collective-permute-start(f16[2,8,1,32,128]{4,3,1,0,2:T(8,128)(2,1)S(1)} %multiply_convert_fusion.3), channel_id=1, source_target_pairs={{0,2},{1,3},{2,0},{3,1},{4,6},{5,7},{6,4},{7,5},{8,10},{9,11},{10,... | collective-permute-start | bytes 393224 | tf_op jit(solution)/shard_map/ppermute | solution.py:248
  34.0 3.2 %copy-start.5 = (f16[2,8,1,32,128]{4,3,1,0,2:T(8,128)(2,1)}, f16[2,8,1,32,128]{4,3,1,0,2:T(8,128)(2,1)S(1)}, u32[]{:S(2)}) copy-start(f16[2,8,1,32,128]{4,3,1,0,2:T(8,128)(2,1)S(1)} %collective-permute-done.8) | copy-start | bytes 393220
  37.2 0.7 copy-start.7
  46.0 13.5 %collective-permute-start.12 = (f16[2,8,128,128]{3,2,1,0:T(8,128)(2,1)}, f16[2,8,128,128]{3,2,1,0:T(8,128)(2,1)}, u32[]{:S(2)}, u32[]{:S(2)}) collective-permute-start(f16[2,8,128,128]{3,2,1,0:T(8,128)(2,1)} %multiply_convert_fusion), channel_id=1, source_target_pairs={{0,4},{8,12},{1,5},{9,13},{2,6},{10,14},{3,7},{11,15},{16,20},{24,... | collective-permute-start | bytes 1572872 | tf_op jit(solution)/shard_map/ppermute | solution.py:294
  48.2 5.5 %collective-permute-start.11 = (f16[2,8,2,32,128]{4,3,2,1,0:T(8,128)(2,1)}, f16[2,8,2,32,128]{4,3,2,1,0:T(8,128)(2,1)}, u32[]{:S(2)}, u32[]{:S(2)}) collective-permute-start(f16[2,8,2,32,128]{4,3,2,1,0:T(8,128)(2,1)} %copy.21), channel_id=1, source_target_pairs={{0,1},{1,0},{2,3},{3,2},{4,5},{5,4},{6,7},{7,6},{8,9},{9,8},{10,11... | collective-permute-start | bytes 786440 | tf_op jit(solution)/shard_map/ppermute | solution.py:248
  60.9 7.1 %collective-permute-start.13 = (f16[2,8,2,32,128]{4,3,1,0,2:T(8,128)(2,1)S(1)}, f16[2,8,2,32,128]{4,3,1,0,2:T(8,128)(2,1)S(1)}, u32[]{:S(2)}, u32[]{:S(2)}) collective-permute-start(f16[2,8,2,32,128]{4,3,1,0,2:T(8,128)(2,1)S(1)} %fusion.7), channel_id=1, source_target_pairs={{4,5},{5,4},{6,7},{7,6},{12,13},{13,12},{14,15},{15,14},{20,21},{2... | collective-permute-start | bytes 786440 | tf_op jit(solution)/shard_map/ppermute | solution.py:248
  65.2 12.2 %copy-start.6 = (f16[2,8,1,32,128]{4,3,1,0,2:T(8,128)(2,1)S(1)}, f16[2,8,1,32,128]{4,3,1,0,2:T(8,128)(2,1)}, u32[]{:S(2)}) copy-start(f16[2,8,1,32,128]{4,3,1,0,2:T(8,128)(2,1)} %copy-done.5) | copy-start | bytes 393220
  65.3 7.6 %collective-permute-start.15 = (f16[2,8,1,32,128]{4,3,2,1,0:T(8,128)(2,1)S(1)}, f16[2,8,1,32,128]{4,3,2,1,0:T(8,128)(2,1)S(1)}, u32[]{:S(2)}, u32[]{:S(2)}) collective-permute-start(f16[2,8,1,32,128]{4,3,2,1,0:T(8,128)(2,1)S(1)} %fusion.10), channel_id=1, source_target_pairs={{0,2},{1,3},{2,0},{3,1},{4,6},{5,7},{6,4},{7,5},{8,10},{9,11},{10,... | collective-permute-start | bytes 393224 | tf_op jit(solution)/shard_map/ppermute | solution.py:248
  68.2 9.2 %collective-permute-start.14 = (f16[2,8,1,32,128]{4,3,1,0,2:T(8,128)(2,1)S(1)}, f16[2,8,1,32,128]{4,3,1,0,2:T(8,128)(2,1)S(1)}, u32[]{:S(2)}, u32[]{:S(2)}) collective-permute-start(f16[2,8,1,32,128]{4,3,1,0,2:T(8,128)(2,1)S(1)} %multiply_convert_fusion.1), channel_id=1, source_target_pairs={{4,6},{5,7},{6,4},{7,5},{12,14},{13,15},{14,12},{15,13},{20,22},{2... | collective-permute-start | bytes 393224 | tf_op jit(solution)/shard_map/ppermute | solution.py:248

commit v11 on v10

--- a/solution.py
+++ b/solution.py
@@ -289,10 +289,11 @@
     b1 = lax.ppermute(tie([to_one], [roots])[0], "aux", [(s, (s - 1) % n_aux) for s in evens])
     bits0, z0 = totals(rows0, pair_col, n_pair, whole, scale)
     bits_even, z_even = totals(rows_even, pair_col, n_pair, evens, scale)
-    rows2, rows_next = second_rows(dims, roots, own, to_even, c2, [bits0[-1], bits_even[-1]])
+    rows2, rows_next = second_rows(dims, roots, own, to_even, c2, [bits_even[-1], bits0[-1]])
     bits2, z2 = totals(rows2, pair_col, n_pair, whole, scale)
     term = lax.ppermute((rows_next * scale).astype(jnp.float16), "aux", [(s, s + 1) for s in evens])
-    rows_odd = band_rows(dims, 1, [0], roots, own, [[b1]], [bits2[0]])
+    rows_odd = band_rows(dims, 1, [0], roots, own, [[b1]], [rows2, z0])
+    (rows_odd,) = tie([rows_odd], [bits2[0]])
     rows_odd = rows_odd + term.astype(jnp.float32) * (1.0 / scale)
     _, z_odd = totals(rows_odd, pair_col, n_pair, odds, scale)
     even = lax.axis_index("aux").astype(jnp.uint32) & jnp.uint32(1) == 0

time: 78.9 us -> 81.7 us (1.035)
  waiting for transfers between devices: 22.6 us -> 26.3 us
  other arithmetic: 6.76 us -> 5.68 us
  local copies, waits for them, and re-layouts: 4.03 us -> 5.03 us
  starting transfers between devices: 27.1 us -> 26.2 us
    ppermute x8, waiting for transfers between devices: 14.8 us -> 20.9 us  [halve(): got = lax.ppermute(sent, ('aux', 'pair'), pairs)]
    ppermute x1, waiting for transfers between devices: 3.38 us -> 0.02 us  [on_device(): c2.append(lax.ppermute(far_two, 'aux', down2))]
    unnamed x19 -> x35, local copies, waits for them, and re-layouts: 2.86 us -> 4.62 us
    ppermute x8, starting transfers between devices: 16.4 us -> 15.3 us  [halve(): got = lax.ppermute(sent, ('aux', 'pair'), pairs)]
    ppermute x1, waiting for transfers between devices: 1.83 us -> 2.84 us  [on_device(): lax.ppermute(tie([to_one], [roots])[0], 'aux', [(s, (s - 1) % n_aux) for...]
    add x4, other arithmetic: 1.3 us -> 0.34 us  [halve(): return (mine + got.astype(jnp.float32) * (1.0 / scale), got)]
  transfers between devices with their start and end apart: 16 -> 16, of which waited for: 10 -> 9; matrix products, arithmetic and copies ran while one was open for 7% -> 5% of each run, Pallas kernels for 19% -> 18%
where the time goes in v11:
time: 81.7 us; the launch traced here: 81.2 us
  waiting for transfers between devices  26.3 us (32%)
  starting transfers between devices  26.2 us (32%)
  Pallas kernels  16.9 us (21%)
  other arithmetic  5.68 us (7%)
  local copies, waits for them, and re-layouts  5.03 us (6%)
  between operations  1.04 us (1%)
    ppermute x8, waiting for transfers between devices, halve(): got = lax.ppermute(sent, ('aux', 'pair'), pairs)  20.9 us
    ppermute x8, starting transfers between devices, halve(): got = lax.ppermute(sent, ('aux', 'pair'), pairs)  15.3 us
    pallas_call x1, Pallas kernels, first_rows(): pl.pallas_call(functools.partial(first_kernel, dims), out_shape=[jax.Shap...  7.43 us
    unnamed x35, local copies, waits for them, and re-layouts  4.62 us
    pallas_call x1, Pallas kernels, second_rows(): pl.pallas_call(functools.partial(second_kernel, dims, pieces), out_shape=...  3.83 us
    ppermute x1, starting transfers between devices, on_device(): to_even = lax.ppermute(rest, 'aux', [(s, s - 1) for s in odds])  3.63 us
    pallas_call x1, Pallas kernels, band_rows(): pl.pallas_call(functools.partial(band_kernel, dims, delta, slots, rights,...  3.29 us
    ppermute x1, waiting for transfers between devices, on_device(): lax.ppermute(tie([to_one], [roots])[0], 'aux', [(s, (s - 1) % n_aux) for...  2.84 us
  transfers between devices with their start and end apart: 16, of which 9 were waited for; matrix products, arithmetic and copies ran while one was open for 5% of the time, Pallas kernels for 18%

profile of v11, /device:TPU:1, one launch (start us, length us, event | category | flops | bytes accessed | tf_op | source)
XLA Modules:
  0.0 81.2 jit_solution(9106428086582558923)
XLA Ops:
  0.0 2.1 %copy-done = bf16[1,1,8,3,1,128,640]{6,5,4,3,2,1,0:T(8,128)(2,1)S(1)} copy-done((bf16[1,1,8,3,1,128,640]{6,5,4,3,2,1,0:T(8,128)(2,1)S(1)}, bf16[1,1,8,3,1,128,640]{6,5,4,3,2,1,0:T(8,128)(2,1)}, u32[]{:S(2)}) %copy-start) | copy-done | bytes 3932184
  2.1 2.4 %shard_map.64 = (bf16[8,128,640]{2,1,0:T(8,128)(2,1)S(1)}, bf16[16,128,640]{2,1,0:T(8,128)(2,1)}, bf16[1,128,640]{2,1,0:T(8,128)(2,1)S(1)}, bf16[7,128,640]{2,1,0:T(8,128)(2,1)S(1)}, bf16[8,128,640]{2,1,0:T(8,128)(2,1)}) custom-call(bf16[8,3,128,640]{3,2,1,0:T(8,128)(2,1)S(1)} %bitcast.65), custom_call_target="tpu_custom_call" | custom-call | flops 1000 | bytes 1000 | tf_op jit(solution)/shard_map/pallas_call | solution.py:46
  4.5 3.6 %collective-permute-start.3 = (bf16[16,128,640]{2,1,0:T(8,128)(2,1)}, bf16[16,128,640]{2,1,0:T(8,128)(2,1)}, u32[]{:S(2)}, u32[]{:S(2)}) collective-permute-start(bf16[16,128,640]{2,1,0:T(8,128)(2,1)} %get-tuple-element.16.refs_8_.refs_1_), channel_id=1, source_target_pairs={{4,0},{12,8},{5,1},{13,9},{6,2},{14,10},{7,3},{15,11},{20,16},{28,... | collective-permute-start | bytes 7864328 | tf_op jit(solution)/shard_map/ppermute | solution.py:286
  8.2 2.7 %collective-permute-start.4 = (bf16[1,128,640]{2,1,0:T(8,128)(2,1)S(1)}, bf16[1,128,640]{2,1,0:T(8,128)(2,1)S(1)}, u32[]{:S(2)}, u32[]{:S(2)}) collective-permute-start(bf16[1,128,640]{2,1,0:T(8,128)(2,1)S(1)} %get-tuple-element.18), channel_id=1, source_target_pairs={{0,8},{4,12},{8,0},{12,4},{1,9},{5,13},{9,1},{13,5},{2,10},{6,14},... | collective-permute-start | bytes 491528 | tf_op jit(solution)/shard_map/ppermute | solution.py:283
  11.8 0.7 collective-permute-start.2
  12.5 0.7 collective-permute-done.refs_1_
  13.2 0.9 %collective-permute-done.1.refs_2_ = s32[25]{0:T(128)S(1)} collective-permute-done((s32[25]{0:T(128)S(1)}, s32[25]{0:T(128)S(1)}, u32[]{:S(2)}, u32[]{:S(2)}) %collective-permute-start.1) | collective-permute-done | bytes 132 | tf_op jit(solution)/shard_map/ppermute | solution.py:274
  14.2 0.9 %collective-permute-done.2.refs_3_ = s32[25]{0:T(128)S(1)} collective-permute-done((s32[25]{0:T(128)S(1)}, s32[25]{0:T(128)S(1)}, u32[]{:S(2)}, u32[]{:S(2)}) %collective-permute-start.2) | collective-permute-done | bytes 132 | tf_op jit(solution)/shard_map/ppermute | solution.py:274
  15.1 1.1 %collective-permute-start.10 = (bf16[7,128,640]{2,1,0:T(8,128)(2,1)S(1)}, bf16[7,128,640]{2,1,0:T(8,128)(2,1)S(1)}, u32[]{:S(2)}, u32[]{:S(2)}) collective-permute-start(bf16[7,128,640]{2,1,0:T(8,128)(2,1)S(1)} %shard_map.65.refs_10_), channel_id=1, source_target_pairs={{0,8},{4,12},{8,0},{12,4},{1,9},{5,13},{9,1},{13,5},{2,10},{6,14},... | collective-permute-start | bytes 3440648 | tf_op jit(solution)/shard_map/ppermute | solution.py:285
  16.2 7.4 %shard_map.66 = (f32[2,8,128,128]{3,2,1,0:T(8,128)S(1)}, f32[2,8,128,128]{3,2,1,0:T(8,128)S(1)}, f32[8,16,640]{2,1,0:T(8,128)S(1)}) custom-call(s32[25]{0:T(128)S(1)} %pad_add_fusion.refs_0_, s32[25]{0:T(128)S(1)} %collective-permute-done.refs_1_, s32[25]{0:T(128)S(1)} %collective-permute-done.1.refs_2_, s32[25]{0:T(128)S(1)} %collective-permute-done.2.refs_3_, ...), custom_call_target="tpu_custom_call" | custom-call | flops 1000 | bytes 1000 | tf_op jit(solution)/shard_map/pallas_call | solution.py:151
  23.9 1.4 %collective-permute-start.5 = (f16[2,8,2,32,128]{4,3,1,0,2:T(8,128)(2,1)S(1)}, f16[2,8,2,32,128]{4,3,1,0,2:T(8,128)(2,1)S(1)}, u32[]{:S(2)}, u32[]{:S(2)}) collective-permute-start(f16[2,8,2,32,128]{4,3,1,0,2:T(8,128)(2,1)S(1)} %fusion.4), channel_id=1, source_target_pairs={{0,1},{1,0},{2,3},{3,2},{4,5},{5,4},{6,7},{7,6},{8,9},{9,8},{10,11... | collective-permute-start | bytes 786440 | tf_op jit(solution)/shard_map/ppermute | solution.py:248
  26.1 1.3 %collective-permute-start.9 = (bf16[8,128,640]{2,1,0:T(8,128)(2,1)}, bf16[8,128,640]{2,1,0:T(8,128)(2,1)}, u32[]{:S(2)}, u32[]{:S(2)}) collective-permute-start(bf16[8,128,640]{2,1,0:T(8,128)(2,1)} %shard_map.67), channel_id=1, source_target_pairs={{0,12},{8,4},{1,13},{9,5},{2,14},{10,6},{3,15},{11,7},{16,28},{24,... | collective-permute-start | bytes 3932168 | tf_op jit(solution)/shard_map/ppermute | solution.py:289
  27.4 4.6 %collective-permute-done.5 = f16[2,8,2,32,128]{4,3,1,0,2:T(8,128)(2,1)S(1)} collective-permute-done((f16[2,8,2,32,128]{4,3,1,0,2:T(8,128)(2,1)S(1)}, f16[2,8,2,32,128]{4,3,1,0,2:T(8,128)(2,1)S(1)}, u32[]{:S(2)}, u32[]{:S(2)}) %collective-permute-start.5) | collective-permute-done | bytes 262176 | tf_op jit(solution)/shard_map/ppermute | solution.py:248
  32.1 2.1 %collective-permute-start.6 = (f16[2,8,1,32,128]{4,3,1,0,2:T(8,128)(2,1)S(1)}, f16[2,8,1,32,128]{4,3,1,0,2:T(8,128)(2,1)}, u32[]{:S(2)}, u32[]{:S(2)}) collective-permute-start(f16[2,8,1,32,128]{4,3,1,0,2:T(8,128)(2,1)S(1)} %multiply_convert_fusion.3), channel_id=1, source_target_pairs={{0,2},{1,3},{2,0},{3,1},{4,6},{5,7},{6,4},{7,5},{8,10},{9,11},{10,... | collective-permute-start | bytes 393224 | tf_op jit(solution)/shard_map/ppermute | solution.py:248
  35.0 5.4 %collective-permute-done.6 = f16[2,8,1,32,128]{4,3,1,0,2:T(8,128)(2,1)} collective-permute-done((f16[2,8,1,32,128]{4,3,1,0,2:T(8,128)(2,1)S(1)}, f16[2,8,1,32,128]{4,3,1,0,2:T(8,128)(2,1)}, u32[]{:S(2)}, u32[]{:S(2)}) %collective-permute-start.6) | collective-permute-done | bytes 131104 | tf_op jit(solution)/shard_map/ppermute | solution.py:248
  40.5 0.7 fusion.12.refs_3_
  41.2 3.8 %shard_map.68 = (f32[2,8,128,128]{3,2,1,0:T(8,128)S(1)}, f32[2,8,128,128]{3,2,1,0:T(8,128)S(1)}) custom-call(f32[8,16,640]{2,1,0:T(8,128)S(1)} %get-tuple-element.21.refs_1_.roots, bf16[8,128,640]{2,1,0:T(8,128)(2,1)S(1)} %get-tuple-element.15.refs_7_.own.refs_0_, bf16[16,128,640]{2,1,0:T(8,128)(2,1)} %collective-permute-done.3.refs_9_.lower, ...), custom_call_target="tpu_custom_call" | custom-call | flops 1000 | bytes 1000 | tf_op jit(solution)/shard_map/pallas_call | solution.py:225
  45.1 1.0 %multiply_convert_fusion = f16[2,8,128,128]{3,2,1,0:T(8,128)(2,1)} fusion(f32[2,8,128,128]{3,2,1,0:T(8,128)S(1)} %get-tuple-element.24), kind=kLoop, calls=%fused_computation.1 | loop fusion | flops 524288 | bytes 1572864 | tf_op jit(solution)/shard_map/convert_element_type | solution.py:294
  46.0 1.4 %collective-permute-start.12 = (f16[2,8,128,128]{3,2,1,0:T(8,128)(2,1)}, f16[2,8,128,128]{3,2,1,0:T(8,128)(2,1)}, u32[]{:S(2)}, u32[]{:S(2)}) collective-permute-start(f16[2,8,128,128]{3,2,1,0:T(8,128)(2,1)} %multiply_convert_fusion), channel_id=1, source_target_pairs={{0,4},{8,12},{1,5},{9,13},{2,6},{10,14},{3,7},{11,15},{16,20},{24,... | collective-permute-start | bytes 1572872 | tf_op jit(solution)/shard_map/ppermute | solution.py:294
  47.6 1.3 %collective-permute-start.11 = (f16[2,8,2,32,128]{4,3,2,1,0:T(8,128)(2,1)S(1)}, f16[2,8,2,32,128]{4,3,2,1,0:T(8,128)(2,1)S(1)}, u32[]{:S(2)}, u32[]{:S(2)}) collective-permute-start(f16[2,8,2,32,128]{4,3,2,1,0:T(8,128)(2,1)S(1)} %copy.22), channel_id=1, source_target_pairs={{0,1},{1,0},{2,3},{3,2},{4,5},{5,4},{6,7},{7,6},{8,9},{9,8},{10,11... | collective-permute-start | bytes 786440 | tf_op jit(solution)/shard_map/ppermute | solution.py:248
  48.8 0.9 %add_bitcast_fusion.refs_4_ = f32[2,8,32,128]{3,2,1,0:T(8,128)S(1)} fusion(f16[2,8,1,32,128]{4,3,1,0,2:T(8,128)(2,1)} %collective-permute-done.6, f32[2,8,2,32,128]{4,3,1,0,2:T(8,128)S(1)} %copy-done.13, u32[]{:T(128)S(6)} %and.18), kind=kLoop, calls=%fused_computation.27 | loop fusion | flops 196608 | bytes 655364 | tf_op jit(solution)/shard_map/squeeze | solution.py:260
  49.8 3.1 %collective-permute-done.11 = f16[2,8,2,32,128]{4,3,2,1,0:T(8,128)(2,1)S(1)} collective-permute-done((f16[2,8,2,32,128]{4,3,2,1,0:T(8,128)(2,1)S(1)}, f16[2,8,2,32,128]{4,3,2,1,0:T(8,128)(2,1)S(1)}, u32[]{:S(2)}, u32[]{:S(2)}) %collective-permute-start.11) | collective-permute-done | bytes 262176 | tf_op jit(solution)/shard_map/ppermute | solution.py:248
  53.6 2.8 %collective-permute-done.9.refs_2_ = bf16[8,128,640]{2,1,0:T(8,128)(2,1)} collective-permute-done((bf16[8,128,640]{2,1,0:T(8,128)(2,1)}, bf16[8,128,640]{2,1,0:T(8,128)(2,1)}, u32[]{:S(2)}, u32[]{:S(2)}) %collective-permute-start.9) | collective-permute-done | bytes 1310752 | tf_op jit(solution)/shard_map/ppermute | solution.py:289
  56.4 1.0 %copy-done.2 = f32[8,16,640]{2,1,0:T(8,128)S(1)} copy-done((f32[8,16,640]{2,1,0:T(8,128)S(1)}, f32[8,16,640]{2,1,0:T(8,128)}, u32[]{:S(2)}) %copy-start.2) | copy-done | bytes 327704
  57.4 3.3 %shard_map.69.refs_0_ = f32[2,8,128,128]{3,2,1,0:T(8,128)S(1)} custom-call(f32[8,16,640]{2,1,0:T(8,128)S(1)} %copy-done.2, bf16[8,128,640]{2,1,0:T(8,128)(2,1)S(1)} %get-tuple-element.15.refs_7_.own.refs_0_, bf16[16,128,640]{2,1,0:T(8,128)(2,1)} %get-tuple-element.16.refs_8_.refs_1_, bf16[8,128,640]{2,1,0:T(8,128)(2,1)} %collective-permute-done.9.refs_2_, ...), custom_call_target="tpu_custom_call" | custom-call | flops 1000 | bytes 1000 | tf_op jit(solution)/shard_map/pallas_call | solution.py:194
  61.4 1.2 %multiply_add_fusion = f32[2,8,128,128]{3,2,1,0:T(8,128)S(1)} fusion(f32[2,8,128,128]{3,2,1,0:T(8,128)S(1)} %shard_map.70, f16[2,8,128,128]{3,2,1,0:T(8,128)(2,1)} %collective-permute-done.12), kind=kLoop, calls=%fused_computation | loop fusion | flops 786432 | bytes 2621440 | tf_op jit(solution)/shard_map/add | solution.py:297
  62.8 3.2 %collective-permute-start.13 = (f16[2,8,2,32,128]{4,3,1,0,2:T(8,128)(2,1)S(1)}, f16[2,8,2,32,128]{4,3,1,0,2:T(8,128)(2,1)S(1)}, u32[]{:S(2)}, u32[]{:S(2)}) collective-permute-start(f16[2,8,2,32,128]{4,3,1,0,2:T(8,128)(2,1)S(1)} %fusion.7), channel_id=1, source_target_pairs={{4,5},{5,4},{6,7},{7,6},{12,13},{13,12},{14,15},{15,14},{20,21},{2... | collective-permute-start | bytes 786440 | tf_op jit(solution)/shard_map/ppermute | solution.py:248
  66.2 2.4 %collective-permute-start.15 = (f16[2,8,1,32,128]{4,3,2,1,0:T(8,128)(2,1)S(1)}, f16[2,8,1,32,128]{4,3,2,1,0:T(8,128)(2,1)S(1)}, u32[]{:S(2)}, u32[]{:S(2)}) collective-permute-start(f16[2,8,1,32,128]{4,3,2,1,0:T(8,128)(2,1)S(1)} %fusion.10), channel_id=1, source_target_pairs={{0,2},{1,3},{2,0},{3,1},{4,6},{5,7},{6,4},{7,5},{8,10},{9,11},{10,... | collective-permute-start | bytes 393224 | tf_op jit(solution)/shard_map/ppermute | solution.py:248
  68.5 3.3 %collective-permute-done.13 = f16[2,8,2,32,128]{4,3,1,0,2:T(8,128)(2,1)S(1)} collective-permute-done((f16[2,8,2,32,128]{4,3,1,0,2:T(8,128)(2,1)S(1)}, f16[2,8,2,32,128]{4,3,1,0,2:T(8,128)(2,1)S(1)}, u32[]{:S(2)}, u32[]{:S(2)}) %collective-permute-start.13) | collective-permute-done | bytes 262176 | tf_op jit(solution)/shard_map/ppermute | solution.py:248
  72.0 3.6 %collective-permute-start.14 = (f16[2,8,1,32,128]{4,3,1,0,2:T(8,128)(2,1)S(1)}, f16[2,8,1,32,128]{4,3,1,0,2:T(8,128)(2,1)S(1)}, u32[]{:S(2)}, u32[]{:S(2)}) collective-permute-start(f16[2,8,1,32,128]{4,3,1,0,2:T(8,128)(2,1)S(1)} %multiply_convert_fusion.1), channel_id=1, source_target_pairs={{4,6},{5,7},{6,4},{7,5},{12,14},{13,15},{14,12},{15,13},{20,22},{2... | collective-permute-start | bytes 393224 | tf_op jit(solution)/shard_map/ppermute | solution.py:248
  75.7 4.5 %collective-permute-done.14 = f16[2,8,1,32,128]{4,3,1,0,2:T(8,128)(2,1)S(1)} collective-permute-done((f16[2,8,1,32,128]{4,3,1,0,2:T(8,128)(2,1)S(1)}, f16[2,8,1,32,128]{4,3,1,0,2:T(8,128)(2,1)S(1)}, u32[]{:S(2)}, u32[]{:S(2)}) %collective-permute-start.14) | collective-permute-done | bytes 131104 | tf_op jit(solution)/shard_map/ppermute | solution.py:248
  80.3 0.9 %maximum_bitcast_fusion = f32[2,8,1,32,384]{4,3,2,1,0:T(8,128)} fusion(f32[2,8,32,128]{3,2,1,0:T(8,128)S(1)} %fusion.9, f32[2,8,32,128]{3,2,1,0:T(8,128)S(1)} %select_bitcast_fusion, f32[2,8,32,128]{3,2,1,0:T(8,128)S(1)} %copy-done.4), kind=kLoop, calls=%fused_computation.2 | loop fusion | flops 393216 | bytes 1572864 | tf_op jit(solution)/shard_map/broadcast_in_dim | solution.py:301
  (69 shorter events, 4.4 us)
Async XLA Ops:
  0.0 2.1 %copy-start = (bf16[1,1,8,3,1,128,640]{6,5,4,3,2,1,0:T(8,128)(2,1)S(1)}, bf16[1,1,8,3,1,128,640]{6,5,4,3,2,1,0:T(8,128)(2,1)}, u32[]{:S(2)}) copy-start(bf16[1,1,8,3,1,128,640]{6,5,4,3,2,1,0:T(8,128)(2,1)} %param.6) | copy-start | bytes 11796484
  2.1 8.7 %copy-start.16 = (s32[1,1,8,3,1]{2,4,3,1,0:T(1,128)S(1)}, s32[1,1,8,3,1]{2,4,3,1,0:T(1,128)}, u32[]{:S(2)}) copy-start(s32[1,1,8,3,1]{2,4,3,1,0:T(1,128)} %param.7) | copy-start | bytes 292
  4.5 11.7 %copy-start.7 = (f32[10240]{0:T(1024)S(1)}, f32[10240]{0:T(1024)}, u32[]{:S(2)}) copy-start(f32[10240]{0:T(1024)} %param.10) | copy-start | bytes 122884
  4.5 11.7 %copy-start.8 = (f32[8]{0:T(128)S(1)}, f32[8]{0:T(128)}, u32[]{:S(2)}) copy-start(f32[8]{0:T(128)} %refs_4_.1) | copy-start | bytes 100
  4.5 11.7 %copy-start.9 = (f32[2]{0:T(128)S(1)}, f32[2]{0:T(128)}, u32[]{:S(2)}) copy-start(f32[2]{0:T(128)} %refs_5_.1) | copy-start | bytes 28
  4.5 11.7 %collective-permute-start.3 = (bf16[16,128,640]{2,1,0:T(8,128)(2,1)}, bf16[16,128,640]{2,1,0:T(8,128)(2,1)}, u32[]{:S(2)}, u32[]{:S(2)}) collective-permute-start(bf16[16,128,640]{2,1,0:T(8,128)(2,1)} %get-tuple-element.16.refs_8_.refs_1_), channel_id=1, source_target_pairs={{4,0},{12,8},{5,1},{13,9},{6,2},{14,10},{7,3},{15,11},{20,16},{28,... | collective-permute-start | bytes 7864328 | tf_op jit(solution)/shard_map/ppermute | solution.py:286
  8.2 6.9 %collective-permute-start.4 = (bf16[1,128,640]{2,1,0:T(8,128)(2,1)S(1)}, bf16[1,128,640]{2,1,0:T(8,128)(2,1)S(1)}, u32[]{:S(2)}, u32[]{:S(2)}) collective-permute-start(bf16[1,128,640]{2,1,0:T(8,128)(2,1)S(1)} %get-tuple-element.18), channel_id=1, source_target_pairs={{0,8},{4,12},{8,0},{12,4},{1,9},{5,13},{9,1},{13,5},{2,10},{6,14},... | collective-permute-start | bytes 491528 | tf_op jit(solution)/shard_map/ppermute | solution.py:283
  11.7 1.5 %collective-permute-start = (s32[25]{0:T(128)S(1)}, s32[25]{0:T(128)S(1)}, u32[]{:S(2)}, u32[]{:S(2)}) collective-permute-start(s32[25]{0:T(128)S(1)} %pad_add_fusion.refs_0_), channel_id=1, source_target_pairs={{0,4},{4,8},{8,12},{12,0},{1,5},{5,9},{9,13},{13,1},{2,6},{6,10},{... | collective-permute-start | bytes 308 | tf_op jit(solution)/shard_map/ppermute | solution.py:274
  11.7 2.5 %collective-permute-start.1 = (s32[25]{0:T(128)S(1)}, s32[25]{0:T(128)S(1)}, u32[]{:S(2)}, u32[]{:S(2)}) collective-permute-start(s32[25]{0:T(128)S(1)} %pad_add_fusion.refs_0_), channel_id=1, source_target_pairs={{0,8},{4,12},{8,0},{12,4},{1,9},{5,13},{9,1},{13,5},{2,10},{6,14},... | collective-permute-start | bytes 308 | tf_op jit(solution)/shard_map/ppermute | solution.py:274
  11.8 3.3 %collective-permute-start.2 = (s32[25]{0:T(128)S(1)}, s32[25]{0:T(128)S(1)}, u32[]{:S(2)}, u32[]{:S(2)}) collective-permute-start(s32[25]{0:T(128)S(1)} %pad_add_fusion.refs_0_), channel_id=1, source_target_pairs={{0,12},{4,0},{8,4},{12,8},{1,13},{5,1},{9,5},{13,9},{2,14},{6,2},{... | collective-permute-start | bytes 308 | tf_op jit(solution)/shard_map/ppermute | solution.py:274
  15.1 8.6 %copy-start.5 = (bf16[1,128,640]{2,1,0:T(8,128)(2,1)}, bf16[1,128,640]{2,1,0:T(8,128)(2,1)S(1)}, u32[]{:S(2)}) copy-start(bf16[1,128,640]{2,1,0:T(8,128)(2,1)S(1)} %collective-permute-done.4.refs_4_.refs_0_) | copy-start | bytes 491524
  15.1 26.1 %collective-permute-start.10 = (bf16[7,128,640]{2,1,0:T(8,128)(2,1)S(1)}, bf16[7,128,640]{2,1,0:T(8,128)(2,1)S(1)}, u32[]{:S(2)}, u32[]{:S(2)}) collective-permute-start(bf16[7,128,640]{2,1,0:T(8,128)(2,1)S(1)} %shard_map.65.refs_10_), channel_id=1, source_target_pairs={{0,8},{4,12},{8,0},{12,4},{1,9},{5,13},{9,1},{13,5},{2,10},{6,14},... | collective-permute-start | bytes 3440648 | tf_op jit(solution)/shard_map/ppermute | solution.py:285
  23.7 17.5 %copy-start.1 = (f32[8,16,640]{2,1,0:T(8,128)}, f32[8,16,640]{2,1,0:T(8,128)S(1)}, u32[]{:S(2)}) copy-start(f32[8,16,640]{2,1,0:T(8,128)S(1)} %get-tuple-element.21.refs_1_.roots) | copy-start | bytes 983044
  23.9 8.1 %collective-permute-start.5 = (f16[2,8,2,32,128]{4,3,1,0,2:T(8,128)(2,1)S(1)}, f16[2,8,2,32,128]{4,3,1,0,2:T(8,128)(2,1)S(1)}, u32[]{:S(2)}, u32[]{:S(2)}) collective-permute-start(f16[2,8,2,32,128]{4,3,1,0,2:T(8,128)(2,1)S(1)} %fusion.4), channel_id=1, source_target_pairs={{0,1},{1,0},{2,3},{3,2},{4,5},{5,4},{6,7},{7,6},{8,9},{9,8},{10,11... | collective-permute-start | bytes 786440 | tf_op jit(solution)/shard_map/ppermute | solution.py:248
  25.4 8.8 %collective-permute-start.7 = (f16[2,8,2,32,128]{4,3,1,0,2:T(8,128)(2,1)S(1)}, f16[2,8,2,32,128]{4,3,1,0,2:T(8,128)(2,1)S(1)}, u32[]{:S(2)}, u32[]{:S(2)}) collective-permute-start(f16[2,8,2,32,128]{4,3,1,0,2:T(8,128)(2,1)S(1)} %fusion.5), channel_id=1, source_target_pairs={{0,1},{1,0},{2,3},{3,2},{8,9},{9,8},{10,11},{11,10},{16,17},{17,16... | collective-permute-start | bytes 786440 | tf_op jit(solution)/shard_map/ppermute | solution.py:248
  26.1 30.3 %collective-permute-start.9 = (bf16[8,128,640]{2,1,0:T(8,128)(2,1)}, bf16[8,128,640]{2,1,0:T(8,128)(2,1)}, u32[]{:S(2)}, u32[]{:S(2)}) collective-permute-start(bf16[8,128,640]{2,1,0:T(8,128)(2,1)} %shard_map.67), channel_id=1, source_target_pairs={{0,12},{8,4},{1,13},{9,5},{2,14},{10,6},{3,15},{11,7},{16,28},{24,... | collective-permute-start | bytes 3932168 | tf_op jit(solution)/shard_map/ppermute | solution.py:289
  32.0 2.2 %copy-start.12 = (f32[2,8,2,32,128]{4,3,1,0,2:T(8,128)}, f32[2,8,2,32,128]{4,3,1,0,2:T(8,128)S(1)}, u32[]{:S(2)}) copy-start(f32[2,8,2,32,128]{4,3,1,0,2:T(8,128)S(1)} %bitcast_add_fusion.3) | copy-start | bytes 1572868
  32.0 9.2 %copy-start.6 = (bf16[1,128,640]{2,1,0:T(8,128)(2,1)S(1)}, bf16[1,128,640]{2,1,0:T(8,128)(2,1)}, u32[]{:S(2)}) copy-start(bf16[1,128,640]{2,1,0:T(8,128)(2,1)} %copy-done.5) | copy-start | bytes 491524
  32.1 8.4 %collective-permute-start.6 = (f16[2,8,1,32,128]{4,3,1,0,2:T(8,128)(2,1)S(1)}, f16[2,8,1,32,128]{4,3,1,0,2:T(8,128)(2,1)}, u32[]{:S(2)}, u32[]{:S(2)}) collective-permute-start(f16[2,8,1,32,128]{4,3,1,0,2:T(8,128)(2,1)S(1)} %multiply_convert_fusion.3), channel_id=1, source_target_pairs={{0,2},{1,3},{2,0},{3,1},{4,6},{5,7},{6,4},{7,5},{8,10},{9,11},{10,... | collective-permute-start | bytes 393224 | tf_op jit(solution)/shard_map/ppermute | solution.py:248
  34.3 6.9 %copy-start.10 = (f32[2,8,2,32,128]{4,3,1,0,2:T(8,128)}, f32[2,8,2,32,128]{4,3,1,0,2:T(8,128)S(1)}, u32[]{:S(2)}) copy-start(f32[2,8,2,32,128]{4,3,1,0,2:T(8,128)S(1)} %bitcast_add_fusion.2) | copy-start | bytes 1572868
  34.4 6.8 %collective-permute-start.8 = (f16[2,8,1,32,128]{4,3,1,0,2:T(8,128)(2,1)S(1)}, f16[2,8,1,32,128]{4,3,1,0,2:T(8,128)(2,1)S(1)}, u32[]{:S(2)}, u32[]{:S(2)}) collective-permute-start(f16[2,8,1,32,128]{4,3,1,0,2:T(8,128)(2,1)S(1)} %multiply_convert_fusion.2), channel_id=1, source_target_pairs={{0,2},{1,3},{2,0},{3,1},{8,10},{9,11},{10,8},{11,9},{16,18},{17,19... | collective-permute-start | bytes 393224 | tf_op jit(solution)/shard_map/ppermute | solution.py:248
  46.0 2.8 %copy-start.13 = (f32[2,8,2,32,128]{4,3,1,0,2:T(8,128)S(1)}, f32[2,8,2,32,128]{4,3,1,0,2:T(8,128)}, u32[]{:S(2)}) copy-start(f32[2,8,2,32,128]{4,3,1,0,2:T(8,128)} %copy-done.12) | copy-start | bytes 1572868
  46.0 15.4 %collective-permute-start.12 = (f16[2,8,128,128]{3,2,1,0:T(8,128)(2,1)}, f16[2,8,128,128]{3,2,1,0:T(8,128)(2,1)}, u32[]{:S(2)}, u32[]{:S(2)}) collective-permute-start(f16[2,8,128,128]{3,2,1,0:T(8,128)(2,1)} %multiply_convert_fusion), channel_id=1, source_target_pairs={{0,4},{8,12},{1,5},{9,13},{2,6},{10,14},{3,7},{11,15},{16,20},{24,... | collective-permute-start | bytes 1572872 | tf_op jit(solution)/shard_map/ppermute | solution.py:294
  47.6 5.3 %collective-permute-start.11 = (f16[2,8,2,32,128]{4,3,2,1,0:T(8,128)(2,1)S(1)}, f16[2,8,2,32,128]{4,3,2,1,0:T(8,128)(2,1)S(1)}, u32[]{:S(2)}, u32[]{:S(2)}) collective-permute-start(f16[2,8,2,32,128]{4,3,2,1,0:T(8,128)(2,1)S(1)} %copy.22), channel_id=1, source_target_pairs={{0,1},{1,0},{2,3},{3,2},{4,5},{5,4},{6,7},{7,6},{8,9},{9,8},{10,11... | collective-permute-start | bytes 786440 | tf_op jit(solution)/shard_map/ppermute | solution.py:248
  56.4 1.0 %copy-start.2 = (f32[8,16,640]{2,1,0:T(8,128)S(1)}, f32[8,16,640]{2,1,0:T(8,128)}, u32[]{:S(2)}) copy-start(f32[8,16,640]{2,1,0:T(8,128)} %copy-done.1) | copy-start | bytes 983044
  60.7 0.7 copy-start.3
  62.6 3.4 %copy-start.15 = (f16[2,8,2,32,128]{4,3,2,1,0:T(8,128)(2,1)S(1)}, f16[2,8,2,32,128]{4,3,2,1,0:T(8,128)(2,1)}, u32[]{:S(2)}) copy-start(f16[2,8,2,32,128]{4,3,2,1,0:T(8,128)(2,1)} %copy-done.14) | copy-start | bytes 786436
  62.8 9.1 %collective-permute-start.13 = (f16[2,8,2,32,128]{4,3,1,0,2:T(8,128)(2,1)S(1)}, f16[2,8,2,32,128]{4,3,1,0,2:T(8,128)(2,1)S(1)}, u32[]{:S(2)}, u32[]{:S(2)}) collective-permute-start(f16[2,8,2,32,128]{4,3,1,0,2:T(8,128)(2,1)S(1)} %fusion.7), channel_id=1, source_target_pairs={{4,5},{5,4},{6,7},{7,6},{12,13},{13,12},{14,15},{15,14},{20,21},{2... | collective-permute-start | bytes 786440 | tf_op jit(solution)/shard_map/ppermute | solution.py:248
  66.1 14.1 %copy-start.11 = (f32[2,8,2,32,128]{4,3,1,0,2:T(8,128)S(1)}, f32[2,8,2,32,128]{4,3,1,0,2:T(8,128)}, u32[]{:S(2)}) copy-start(f32[2,8,2,32,128]{4,3,1,0,2:T(8,128)} %copy-done.10) | copy-start | bytes 1572868
  66.2 9.5 %collective-permute-start.15 = (f16[2,8,1,32,128]{4,3,2,1,0:T(8,128)(2,1)S(1)}, f16[2,8,1,32,128]{4,3,2,1,0:T(8,128)(2,1)S(1)}, u32[]{:S(2)}, u32[]{:S(2)}) collective-permute-start(f16[2,8,1,32,128]{4,3,2,1,0:T(8,128)(2,1)S(1)} %fusion.10), channel_id=1, source_target_pairs={{0,2},{1,3},{2,0},{3,1},{4,6},{5,7},{6,4},{7,5},{8,10},{9,11},{10,... | collective-permute-start | bytes 393224 | tf_op jit(solution)/shard_map/ppermute | solution.py:248
  72.0 8.3 %copy-start.4 = (f32[2,8,32,128]{3,2,1,0:T(8,128)S(1)}, f32[2,8,32,128]{3,2,1,0:T(8,128)}, u32[]{:S(2)}) copy-start(f32[2,8,32,128]{3,2,1,0:T(8,128)} %copy-done.3) | copy-start | bytes 786436
  72.0 8.1 %collective-permute-start.14 = (f16[2,8,1,32,128]{4,3,1,0,2:T(8,128)(2,1)S(1)}, f16[2,8,1,32,128]{4,3,1,0,2:T(8,128)(2,1)S(1)}, u32[]{:S(2)}, u32[]{:S(2)}) collective-permute-start(f16[2,8,1,32,128]{4,3,1,0,2:T(8,128)(2,1)S(1)} %multiply_convert_fusion.1), channel_id=1, source_target_pairs={{4,6},{5,7},{6,4},{7,5},{12,14},{13,15},{14,12},{15,13},{20,22},{2... | collective-permute-start | bytes 393224 | tf_op jit(solution)/shard_map/ppermute | solution.py:248
  (1 other events, 0.7 us)

commit v12 on v11

--- a/solution.py
+++ b/solution.py
@@ -164,7 +164,8 @@
 
 def band_kernel(dims, delta, slots, rights, add, roots, *refs):
     n_aux, n_pair, blocks_dev, band, freq_count = dims
-    out = refs[-1]
+    out, zeros = refs[-2:]
+    zeros[...] = jnp.zeros_like(zeros)
     for m in range(blocks_dev):
         sums = [refs[add][w, m] if add is not None else None for w in range(freq_count)]
         for s, slot in enumerate(slots):
@@ -193,9 +194,12 @@
     arrays += [] if add is None else [add]
     return pl.pallas_call(
         functools.partial(band_kernel, dims, delta, slots, rights, spot),
-        out_shape=jax.ShapeDtypeStruct((freq_count, blocks_dev, aux_rows, aux_rows), jnp.float32),
+        out_shape=[
+            jax.ShapeDtypeStruct((freq_count, blocks_dev, aux_rows, aux_rows), jnp.float32),
+            jax.ShapeDtypeStruct((aux_rows // n_pair, aux_rows), jnp.float32),
+        ],
         in_specs=[VMEM] * (1 + len(arrays)) + [ANY] * len(after),
-        out_specs=VMEM,
+        out_specs=[VMEM] * 2,
         compiler_params=PARAMS,
         cost_estimate=COST,
     )(roots, *arrays, *after)
@@ -292,9 +296,9 @@
     rows2, rows_next = second_rows(dims, roots, own, to_even, c2, [bits_even[-1], bits0[-1]])
     bits2, z2 = totals(rows2, pair_col, n_pair, whole, scale)
     term = lax.ppermute((rows_next * scale).astype(jnp.float16), "aux", [(s, s + 1) for s in evens])
-    rows_odd = band_rows(dims, 1, [0], roots, own, [[b1]], [rows2, z0])
-    (rows_odd,) = tie([rows_odd], [bits2[0]])
-    rows_odd = rows_odd + term.astype(jnp.float32) * (1.0 / scale)
+    term = term.astype(jnp.float32) * (1.0 / scale)
+    rows_odd, zeros = band_rows(dims, 1, [0], roots, own, [[b1]], [], term)
+    (rows_odd,) = tie([rows_odd], [bits2[-1] + zeros])
     _, z_odd = totals(rows_odd, pair_col, n_pair, odds, scale)
     even = lax.axis_index("aux").astype(jnp.uint32) & jnp.uint32(1) == 0
     out = jnp.concatenate([z0, jnp.where(even, z_even, z_odd), z2], axis=-1)

time: 81.7 us -> 77 us (0.942)
  other arithmetic: 5.68 us -> 2.16 us
  local copies, waits for them, and re-layouts: 5.03 us -> 4.06 us
    add x1, other arithmetic: 1.19 us -> 0.01 us  [on_device(): rows_odd, = tie([rows_odd], [bits2[-1] + zeros])]
    unnamed x35 -> x19, local copies, waits for them, and re-layouts: 4.62 us -> 3.62 us
    squeeze x2, other arithmetic: 0.98 us -> 0.08 us  [totals(): return (stages, keep[:, :, 0])]
    convert_element_type x1, other arithmetic: 0.96 us -> 0.14 us  [on_device(): (rows_next * scale).astype(jnp.float16)]
  transfers between devices with their start and end apart: 16 -> 16, of which waited for: 9 -> 10; matrix products, arithmetic and copies ran while one was open for 5% -> 2% of each run, Pallas kernels for 18% -> 19%
where the time goes in v12:
time: 77 us; the launch traced here: 76.6 us
  waiting for transfers between devices  26.9 us (35%)
  starting transfers between devices  26.2 us (34%)
  Pallas kernels  16.3 us (21%)
  local copies, waits for them, and re-layouts  4.06 us (5%)
  other arithmetic  2.16 us (3%)
  between operations  0.99 us (1%)
    ppermute x8, waiting for transfers between devices, halve(): got = lax.ppermute(sent, ('aux', 'pair'), pairs)  20.2 us
    ppermute x8, starting transfers between devices, halve(): got = lax.ppermute(sent, ('aux', 'pair'), pairs)  15.5 us
    pallas_call x1, Pallas kernels, first_rows(): pl.pallas_call(functools.partial(first_kernel, dims), out_shape=[jax.Shap...  7.45 us
    pallas_call x1, Pallas kernels, second_rows(): pl.pallas_call(functools.partial(second_kernel, dims, pieces), out_shape=...  3.83 us
    ppermute x1, starting transfers between devices, on_device(): to_even = lax.ppermute(rest, 'aux', [(s, s - 1) for s in odds])  3.64 us
    unnamed x19, local copies, waits for them, and re-layouts  3.62 us
    ppermute x1, waiting for transfers between devices, on_device(): lax.ppermute(tie([to_one], [roots])[0], 'aux', [(s, (s - 1) % n_aux) for...  3.35 us
    pallas_call x1, Pallas kernels, band_rows(): pl.pallas_call(functools.partial(band_kernel, dims, delta, slots, rights,...  2.96 us
  transfers between devices with their start and end apart: 16, of which 10 were waited for; matrix products, arithmetic and copies ran while one was open for 2% of the time, Pallas kernels for 19%

profile of v12, /device:TPU:1, one launch (start us, length us, event | category | flops | bytes accessed | tf_op | source)
XLA Modules:
  0.0 76.6 jit_solution(7837104521713947183)
XLA Ops:
  0.0 2.1 %copy-done = bf16[1,1,8,3,1,128,640]{6,5,4,3,2,1,0:T(8,128)(2,1)S(1)} copy-done((bf16[1,1,8,3,1,128,640]{6,5,4,3,2,1,0:T(8,128)(2,1)S(1)}, bf16[1,1,8,3,1,128,640]{6,5,4,3,2,1,0:T(8,128)(2,1)}, u32[]{:S(2)}) %copy-start) | copy-done | bytes 3932184
  2.1 2.0 %shard_map.64 = (bf16[8,128,640]{2,1,0:T(8,128)(2,1)S(1)}, bf16[16,128,640]{2,1,0:T(8,128)(2,1)}, bf16[1,128,640]{2,1,0:T(8,128)(2,1)S(1)}, bf16[7,128,640]{2,1,0:T(8,128)(2,1)S(1)}, bf16[8,128,640]{2,1,0:T(8,128)(2,1)S(1)}) custom-call(bf16[8,3,128,640]{3,2,1,0:T(8,128)(2,1)S(1)} %bitcast.64), custom_call_target="tpu_custom_call" | custom-call | flops 1000 | bytes 1000 | tf_op jit(solution)/shard_map/pallas_call | solution.py:46
  4.1 1.1 %copy-done.1 = bf16[8,128,640]{2,1,0:T(8,128)(2,1)} copy-done((bf16[8,128,640]{2,1,0:T(8,128)(2,1)}, bf16[8,128,640]{2,1,0:T(8,128)(2,1)S(1)}, u32[]{:S(2)}) %copy-start.1) | copy-done | bytes 1310744
  5.2 3.6 %collective-permute-start.3 = (bf16[16,128,640]{2,1,0:T(8,128)(2,1)}, bf16[16,128,640]{2,1,0:T(8,128)(2,1)}, u32[]{:S(2)}, u32[]{:S(2)}) collective-permute-start(bf16[16,128,640]{2,1,0:T(8,128)(2,1)} %get-tuple-element.18.refs_8_.refs_1_), channel_id=1, source_target_pairs={{4,0},{12,8},{5,1},{13,9},{6,2},{14,10},{7,3},{15,11},{20,16},{28,... | collective-permute-start | bytes 7864328 | tf_op jit(solution)/shard_map/ppermute | solution.py:290
  8.8 2.7 %collective-permute-start.4 = (bf16[1,128,640]{2,1,0:T(8,128)(2,1)S(1)}, bf16[1,128,640]{2,1,0:T(8,128)(2,1)S(1)}, u32[]{:S(2)}, u32[]{:S(2)}) collective-permute-start(bf16[1,128,640]{2,1,0:T(8,128)(2,1)S(1)} %get-tuple-element.20), channel_id=1, source_target_pairs={{0,8},{4,12},{8,0},{12,4},{1,9},{5,13},{9,1},{13,5},{2,10},{6,14},... | collective-permute-start | bytes 491528 | tf_op jit(solution)/shard_map/ppermute | solution.py:287
  12.5 0.7 collective-permute-start.2
  13.2 0.7 collective-permute-done.refs_1_
  13.9 0.9 %collective-permute-done.1.refs_2_ = s32[25]{0:T(128)S(1)} collective-permute-done((s32[25]{0:T(128)S(1)}, s32[25]{0:T(128)S(1)}, u32[]{:S(2)}, u32[]{:S(2)}) %collective-permute-start.1) | collective-permute-done | bytes 132 | tf_op jit(solution)/shard_map/ppermute | solution.py:278
  14.8 0.9 %collective-permute-done.2.refs_3_ = s32[25]{0:T(128)S(1)} collective-permute-done((s32[25]{0:T(128)S(1)}, s32[25]{0:T(128)S(1)}, u32[]{:S(2)}, u32[]{:S(2)}) %collective-permute-start.2) | collective-permute-done | bytes 132 | tf_op jit(solution)/shard_map/ppermute | solution.py:278
  15.8 1.1 %collective-permute-start.10 = (bf16[7,128,640]{2,1,0:T(8,128)(2,1)S(1)}, bf16[7,128,640]{2,1,0:T(8,128)(2,1)S(1)}, u32[]{:S(2)}, u32[]{:S(2)}) collective-permute-start(bf16[7,128,640]{2,1,0:T(8,128)(2,1)S(1)} %shard_map.65.refs_10_), channel_id=1, source_target_pairs={{0,8},{4,12},{8,0},{12,4},{1,9},{5,13},{9,1},{13,5},{2,10},{6,14},... | collective-permute-start | bytes 3440648 | tf_op jit(solution)/shard_map/ppermute | solution.py:289
  16.9 7.4 %shard_map.66 = (f32[2,8,128,128]{3,2,1,0:T(8,128)S(1)}, f32[2,8,128,128]{3,2,1,0:T(8,128)S(1)}, f32[8,16,640]{2,1,0:T(8,128)S(1)}) custom-call(s32[25]{0:T(128)S(1)} %pad_add_fusion.refs_0_, s32[25]{0:T(128)S(1)} %collective-permute-done.refs_1_, s32[25]{0:T(128)S(1)} %collective-permute-done.1.refs_2_, s32[25]{0:T(128)S(1)} %collective-permute-done.2.refs_3_, ...), custom_call_target="tpu_custom_call" | custom-call | flops 1000 | bytes 1000 | tf_op jit(solution)/shard_map/pallas_call | solution.py:151
  24.5 1.4 %collective-permute-start.5 = (f16[2,8,2,32,128]{4,3,1,0,2:T(8,128)(2,1)S(1)}, f16[2,8,2,32,128]{4,3,1,0,2:T(8,128)(2,1)S(1)}, u32[]{:S(2)}, u32[]{:S(2)}) collective-permute-start(f16[2,8,2,32,128]{4,3,1,0,2:T(8,128)(2,1)S(1)} %fusion.4), channel_id=1, source_target_pairs={{0,1},{1,0},{2,3},{3,2},{4,5},{5,4},{6,7},{7,6},{8,9},{9,8},{10,11... | collective-permute-start | bytes 786440 | tf_op jit(solution)/shard_map/ppermute | solution.py:252
  26.1 0.8 %collective-permute-start.7 = (f16[2,8,2,32,128]{4,3,1,0,2:T(8,128)(2,1)S(1)}, f16[2,8,2,32,128]{4,3,1,0,2:T(8,128)(2,1)S(1)}, u32[]{:S(2)}, u32[]{:S(2)}) collective-permute-start(f16[2,8,2,32,128]{4,3,1,0,2:T(8,128)(2,1)S(1)} %fusion.5), channel_id=1, source_target_pairs={{0,1},{1,0},{2,3},{3,2},{8,9},{9,8},{10,11},{11,10},{16,17},{17,16... | collective-permute-start | bytes 786440 | tf_op jit(solution)/shard_map/ppermute | solution.py:252
  26.9 0.3 copy-done.2
  27.2 1.3 %collective-permute-start.9 = (bf16[8,128,640]{2,1,0:T(8,128)(2,1)S(1)}, bf16[8,128,640]{2,1,0:T(8,128)(2,1)S(1)}, u32[]{:S(2)}, u32[]{:S(2)}) collective-permute-start(bf16[8,128,640]{2,1,0:T(8,128)(2,1)S(1)} %shard_map.67), channel_id=1, source_target_pairs={{0,12},{8,4},{1,13},{9,5},{2,14},{10,6},{3,15},{11,7},{16,28},{24,... | collective-permute-start | bytes 3932168 | tf_op jit(solution)/shard_map/ppermute | solution.py:293
  28.5 4.2 %collective-permute-done.5 = f16[2,8,2,32,128]{4,3,1,0,2:T(8,128)(2,1)S(1)} collective-permute-done((f16[2,8,2,32,128]{4,3,1,0,2:T(8,128)(2,1)S(1)}, f16[2,8,2,32,128]{4,3,1,0,2:T(8,128)(2,1)S(1)}, u32[]{:S(2)}, u32[]{:S(2)}) %collective-permute-start.5) | collective-permute-done | bytes 262176 | tf_op jit(solution)/shard_map/ppermute | solution.py:252
  32.8 2.2 %collective-permute-start.6 = (f16[2,8,1,32,128]{4,3,1,0,2:T(8,128)(2,1)S(1)}, f16[2,8,1,32,128]{4,3,1,0,2:T(8,128)(2,1)S(1)}, u32[]{:S(2)}, u32[]{:S(2)}) collective-permute-start(f16[2,8,1,32,128]{4,3,1,0,2:T(8,128)(2,1)S(1)} %multiply_convert_fusion.4), channel_id=1, source_target_pairs={{0,2},{1,3},{2,0},{3,1},{4,6},{5,7},{6,4},{7,5},{8,10},{9,11},{10,... | collective-permute-start | bytes 393224 | tf_op jit(solution)/shard_map/ppermute | solution.py:252
  35.2 0.7 collective-permute-start.8
  35.8 5.3 %collective-permute-done.6 = f16[2,8,1,32,128]{4,3,1,0,2:T(8,128)(2,1)S(1)} collective-permute-done((f16[2,8,1,32,128]{4,3,1,0,2:T(8,128)(2,1)S(1)}, f16[2,8,1,32,128]{4,3,1,0,2:T(8,128)(2,1)S(1)}, u32[]{:S(2)}, u32[]{:S(2)}) %collective-permute-start.6) | collective-permute-done | bytes 131104 | tf_op jit(solution)/shard_map/ppermute | solution.py:252
  41.2 0.7 collective-permute-done.10.refs_1_
  41.9 3.8 %shard_map.68 = (f32[2,8,128,128]{3,2,1,0:T(8,128)S(1)}, f32[2,8,128,128]{3,2,1,0:T(8,128)S(1)}) custom-call(f32[8,16,640]{2,1,0:T(8,128)S(1)} %get-tuple-element.23.refs_1_.roots, bf16[8,128,640]{2,1,0:T(8,128)(2,1)S(1)} %get-tuple-element.17.refs_7_.own.refs_0_, bf16[16,128,640]{2,1,0:T(8,128)(2,1)} %collective-permute-done.3.refs_9_.lower, ...), custom_call_target="tpu_custom_call" | custom-call | flops 1000 | bytes 1000 | tf_op jit(solution)/shard_map/pallas_call | solution.py:229
  45.9 1.3 %collective-permute-start.12 = (f16[2,8,2,32,128]{4,3,1,0,2:T(8,128)(2,1)S(1)}, f16[2,8,2,32,128]{4,3,1,0,2:T(8,128)(2,1)S(1)}, u32[]{:S(2)}, u32[]{:S(2)}) collective-permute-start(f16[2,8,2,32,128]{4,3,1,0,2:T(8,128)(2,1)S(1)} %fusion.6), channel_id=1, source_target_pairs={{0,1},{1,0},{2,3},{3,2},{4,5},{5,4},{6,7},{7,6},{8,9},{9,8},{10,11... | collective-permute-start | bytes 786440 | tf_op jit(solution)/shard_map/ppermute | solution.py:252
  47.3 1.3 %collective-permute-start.11 = (f16[2,8,128,128]{3,2,1,0:T(8,128)(2,1)S(1)}, f16[2,8,128,128]{3,2,1,0:T(8,128)(2,1)S(1)}, u32[]{:S(2)}, u32[]{:S(2)}) collective-permute-start(f16[2,8,128,128]{3,2,1,0:T(8,128)(2,1)S(1)} %multiply_convert_fusion), channel_id=1, source_target_pairs={{0,4},{8,12},{1,5},{9,13},{2,6},{10,14},{3,7},{11,15},{16,20},{24,... | collective-permute-start | bytes 1572872 | tf_op jit(solution)/shard_map/ppermute | solution.py:298
  48.6 2.5 %collective-permute-done.12 = f16[2,8,2,32,128]{4,3,1,0,2:T(8,128)(2,1)S(1)} collective-permute-done((f16[2,8,2,32,128]{4,3,1,0,2:T(8,128)(2,1)S(1)}, f16[2,8,2,32,128]{4,3,1,0,2:T(8,128)(2,1)S(1)}, u32[]{:S(2)}, u32[]{:S(2)}) %collective-permute-start.12) | collective-permute-done | bytes 262176 | tf_op jit(solution)/shard_map/ppermute | solution.py:252
  51.3 2.3 %collective-permute-start.13 = (f16[2,8,1,32,128]{4,3,2,1,0:T(8,128)(2,1)S(1)}, f16[2,8,1,32,128]{4,3,2,1,0:T(8,128)(2,1)S(1)}, u32[]{:S(2)}, u32[]{:S(2)}) collective-permute-start(f16[2,8,1,32,128]{4,3,2,1,0:T(8,128)(2,1)S(1)} %fusion.10), channel_id=1, source_target_pairs={{0,2},{1,3},{2,0},{3,1},{4,6},{5,7},{6,4},{7,5},{8,10},{9,11},{10,... | collective-permute-start | bytes 393224 | tf_op jit(solution)/shard_map/ppermute | solution.py:252
  53.7 3.3 %collective-permute-done.9.refs_2_ = bf16[8,128,640]{2,1,0:T(8,128)(2,1)S(1)} collective-permute-done((bf16[8,128,640]{2,1,0:T(8,128)(2,1)S(1)}, bf16[8,128,640]{2,1,0:T(8,128)(2,1)S(1)}, u32[]{:S(2)}, u32[]{:S(2)}) %collective-permute-start.9) | collective-permute-done | bytes 1310752 | tf_op jit(solution)/shard_map/ppermute | solution.py:293
  57.1 3.0 %shard_map.69 = (f32[2,8,128,128]{3,2,1,0:T(8,128)S(1)}, f32[32,128]{1,0:T(8,128)S(1)}) custom-call(f32[8,16,640]{2,1,0:T(8,128)S(1)} %get-tuple-element.23.refs_1_.roots, bf16[8,128,640]{2,1,0:T(8,128)(2,1)S(1)} %get-tuple-element.17.refs_7_.own.refs_0_, bf16[16,128,640]{2,1,0:T(8,128)(2,1)} %get-tuple-element.18.refs_8_.refs_1_, ...), custom_call_target="tpu_custom_call" | custom-call | flops 1000 | bytes 1000 | tf_op jit(solution)/shard_map/pallas_call | solution.py:195
  60.3 2.9 %collective-permute-start.14 = (f16[2,8,2,32,128]{4,3,1,0,2:T(8,128)(2,1)S(1)}, f16[2,8,2,32,128]{4,3,1,0,2:T(8,128)(2,1)S(1)}, u32[]{:S(2)}, u32[]{:S(2)}) collective-permute-start(f16[2,8,2,32,128]{4,3,1,0,2:T(8,128)(2,1)S(1)} %fusion.7), channel_id=1, source_target_pairs={{4,5},{5,4},{6,7},{7,6},{12,13},{13,12},{14,15},{15,14},{20,21},{2... | collective-permute-start | bytes 786440 | tf_op jit(solution)/shard_map/ppermute | solution.py:252
  63.3 4.1 %collective-permute-done.14 = f16[2,8,2,32,128]{4,3,1,0,2:T(8,128)(2,1)S(1)} collective-permute-done((f16[2,8,2,32,128]{4,3,1,0,2:T(8,128)(2,1)S(1)}, f16[2,8,2,32,128]{4,3,1,0,2:T(8,128)(2,1)S(1)}, u32[]{:S(2)}, u32[]{:S(2)}) %collective-permute-start.14) | collective-permute-done | bytes 262176 | tf_op jit(solution)/shard_map/ppermute | solution.py:252
  67.5 3.9 %collective-permute-start.15 = (f16[2,8,1,32,128]{4,3,1,0,2:T(8,128)(2,1)S(1)}, f16[2,8,1,32,128]{4,3,1,0,2:T(8,128)(2,1)S(1)}, u32[]{:S(2)}, u32[]{:S(2)}) collective-permute-start(f16[2,8,1,32,128]{4,3,1,0,2:T(8,128)(2,1)S(1)} %multiply_convert_fusion.1), channel_id=1, source_target_pairs={{4,6},{5,7},{6,4},{7,5},{12,14},{13,15},{14,12},{15,13},{20,22},{2... | collective-permute-start | bytes 393224 | tf_op jit(solution)/shard_map/ppermute | solution.py:252
  71.5 4.0 %collective-permute-done.15 = f16[2,8,1,32,128]{4,3,1,0,2:T(8,128)(2,1)S(1)} collective-permute-done((f16[2,8,1,32,128]{4,3,1,0,2:T(8,128)(2,1)S(1)}, f16[2,8,1,32,128]{4,3,1,0,2:T(8,128)(2,1)S(1)}, u32[]{:S(2)}, u32[]{:S(2)}) %collective-permute-start.15) | collective-permute-done | bytes 131104 | tf_op jit(solution)/shard_map/ppermute | solution.py:252
  75.6 0.9 %maximum_bitcast_fusion = f32[2,8,1,32,384]{4,3,2,1,0:T(8,128)} fusion(f32[2,8,32,128]{3,2,1,0:T(8,128)S(1)} %fusion.9, f32[2,8,32,128]{3,2,1,0:T(8,128)S(1)} %select_bitcast_fusion, f32[2,8,32,128]{3,2,1,0:T(8,128)S(1)} %add_bitcast_fusion), kind=kLoop, calls=%fused_computation.2 | loop fusion | flops 393216 | bytes 1572864 | tf_op jit(solution)/shard_map/broadcast_in_dim | solution.py:305
  (53 shorter events, 1.9 us)
Async XLA Ops:
  0.0 2.1 %copy-start = (bf16[1,1,8,3,1,128,640]{6,5,4,3,2,1,0:T(8,128)(2,1)S(1)}, bf16[1,1,8,3,1,128,640]{6,5,4,3,2,1,0:T(8,128)(2,1)}, u32[]{:S(2)}) copy-start(bf16[1,1,8,3,1,128,640]{6,5,4,3,2,1,0:T(8,128)(2,1)} %param.6) | copy-start | bytes 11796484
  2.1 9.4 %copy-start.8 = (s32[1,1,8,3,1]{2,4,3,1,0:T(1,128)S(1)}, s32[1,1,8,3,1]{2,4,3,1,0:T(1,128)}, u32[]{:S(2)}) copy-start(s32[1,1,8,3,1]{2,4,3,1,0:T(1,128)} %param.7) | copy-start | bytes 292
  4.1 1.1 %copy-start.1 = (bf16[8,128,640]{2,1,0:T(8,128)(2,1)}, bf16[8,128,640]{2,1,0:T(8,128)(2,1)S(1)}, u32[]{:S(2)}) copy-start(bf16[8,128,640]{2,1,0:T(8,128)(2,1)S(1)} %get-tuple-element.24.refs_0_) | copy-start | bytes 3932164
  5.2 11.7 %copy-start.3 = (f32[10240]{0:T(1024)S(1)}, f32[10240]{0:T(1024)}, u32[]{:S(2)}) copy-start(f32[10240]{0:T(1024)} %param.10) | copy-start | bytes 122884
  5.2 11.7 %copy-start.4 = (f32[8]{0:T(128)S(1)}, f32[8]{0:T(128)}, u32[]{:S(2)}) copy-start(f32[8]{0:T(128)} %refs_4_.1) | copy-start | bytes 100
  5.2 11.7 %copy-start.5 = (f32[2]{0:T(128)S(1)}, f32[2]{0:T(128)}, u32[]{:S(2)}) copy-start(f32[2]{0:T(128)} %refs_5_.1) | copy-start | bytes 28
  5.2 11.7 %collective-permute-start.3 = (bf16[16,128,640]{2,1,0:T(8,128)(2,1)}, bf16[16,128,640]{2,1,0:T(8,128)(2,1)}, u32[]{:S(2)}, u32[]{:S(2)}) collective-permute-start(bf16[16,128,640]{2,1,0:T(8,128)(2,1)} %get-tuple-element.18.refs_8_.refs_1_), channel_id=1, source_target_pairs={{4,0},{12,8},{5,1},{13,9},{6,2},{14,10},{7,3},{15,11},{20,16},{28,... | collective-permute-start | bytes 7864328 | tf_op jit(solution)/shard_map/ppermute | solution.py:290
  8.8 6.9 %collective-permute-start.4 = (bf16[1,128,640]{2,1,0:T(8,128)(2,1)S(1)}, bf16[1,128,640]{2,1,0:T(8,128)(2,1)S(1)}, u32[]{:S(2)}, u32[]{:S(2)}) collective-permute-start(bf16[1,128,640]{2,1,0:T(8,128)(2,1)S(1)} %get-tuple-element.20), channel_id=1, source_target_pairs={{0,8},{4,12},{8,0},{12,4},{1,9},{5,13},{9,1},{13,5},{2,10},{6,14},... | collective-permute-start | bytes 491528 | tf_op jit(solution)/shard_map/ppermute | solution.py:287
  12.4 1.5 %collective-permute-start = (s32[25]{0:T(128)S(1)}, s32[25]{0:T(128)S(1)}, u32[]{:S(2)}, u32[]{:S(2)}) collective-permute-start(s32[25]{0:T(128)S(1)} %pad_add_fusion.refs_0_), channel_id=1, source_target_pairs={{0,4},{4,8},{8,12},{12,0},{1,5},{5,9},{9,13},{13,1},{2,6},{6,10},{... | collective-permute-start | bytes 308 | tf_op jit(solution)/shard_map/ppermute | solution.py:278
  12.4 2.5 %collective-permute-start.1 = (s32[25]{0:T(128)S(1)}, s32[25]{0:T(128)S(1)}, u32[]{:S(2)}, u32[]{:S(2)}) collective-permute-start(s32[25]{0:T(128)S(1)} %pad_add_fusion.refs_0_), channel_id=1, source_target_pairs={{0,8},{4,12},{8,0},{12,4},{1,9},{5,13},{9,1},{13,5},{2,10},{6,14},... | collective-permute-start | bytes 308 | tf_op jit(solution)/shard_map/ppermute | solution.py:278
  12.5 3.3 %collective-permute-start.2 = (s32[25]{0:T(128)S(1)}, s32[25]{0:T(128)S(1)}, u32[]{:S(2)}, u32[]{:S(2)}) collective-permute-start(s32[25]{0:T(128)S(1)} %pad_add_fusion.refs_0_), channel_id=1, source_target_pairs={{0,12},{4,0},{8,4},{12,8},{1,13},{5,1},{9,5},{13,9},{2,14},{6,2},{... | collective-permute-start | bytes 308 | tf_op jit(solution)/shard_map/ppermute | solution.py:278
  15.8 26.1 %collective-permute-start.10 = (bf16[7,128,640]{2,1,0:T(8,128)(2,1)S(1)}, bf16[7,128,640]{2,1,0:T(8,128)(2,1)S(1)}, u32[]{:S(2)}, u32[]{:S(2)}) collective-permute-start(bf16[7,128,640]{2,1,0:T(8,128)(2,1)S(1)} %shard_map.65.refs_10_), channel_id=1, source_target_pairs={{0,8},{4,12},{8,0},{12,4},{1,9},{5,13},{9,1},{13,5},{2,10},{6,14},... | collective-permute-start | bytes 3440648 | tf_op jit(solution)/shard_map/ppermute | solution.py:289
  24.5 8.1 %collective-permute-start.5 = (f16[2,8,2,32,128]{4,3,1,0,2:T(8,128)(2,1)S(1)}, f16[2,8,2,32,128]{4,3,1,0,2:T(8,128)(2,1)S(1)}, u32[]{:S(2)}, u32[]{:S(2)}) collective-permute-start(f16[2,8,2,32,128]{4,3,1,0,2:T(8,128)(2,1)S(1)} %fusion.4), channel_id=1, source_target_pairs={{0,1},{1,0},{2,3},{3,2},{4,5},{5,4},{6,7},{7,6},{8,9},{9,8},{10,11... | collective-permute-start | bytes 786440 | tf_op jit(solution)/shard_map/ppermute | solution.py:252
  25.9 1.3 %copy-start.2 = (bf16[8,128,640]{2,1,0:T(8,128)(2,1)S(1)}, bf16[8,128,640]{2,1,0:T(8,128)(2,1)}, u32[]{:S(2)}) copy-start(bf16[8,128,640]{2,1,0:T(8,128)(2,1)} %copy-done.1) | copy-start | bytes 3932164
  26.1 9.0 %collective-permute-start.7 = (f16[2,8,2,32,128]{4,3,1,0,2:T(8,128)(2,1)S(1)}, f16[2,8,2,32,128]{4,3,1,0,2:T(8,128)(2,1)S(1)}, u32[]{:S(2)}, u32[]{:S(2)}) collective-permute-start(f16[2,8,2,32,128]{4,3,1,0,2:T(8,128)(2,1)S(1)} %fusion.5), channel_id=1, source_target_pairs={{0,1},{1,0},{2,3},{3,2},{8,9},{9,8},{10,11},{11,10},{16,17},{17,16... | collective-permute-start | bytes 786440 | tf_op jit(solution)/shard_map/ppermute | solution.py:252
  27.2 29.9 %collective-permute-start.9 = (bf16[8,128,640]{2,1,0:T(8,128)(2,1)S(1)}, bf16[8,128,640]{2,1,0:T(8,128)(2,1)S(1)}, u32[]{:S(2)}, u32[]{:S(2)}) collective-permute-start(bf16[8,128,640]{2,1,0:T(8,128)(2,1)S(1)} %shard_map.67), channel_id=1, source_target_pairs={{0,12},{8,4},{1,13},{9,5},{2,14},{10,6},{3,15},{11,7},{16,28},{24,... | collective-permute-start | bytes 3932168 | tf_op jit(solution)/shard_map/ppermute | solution.py:293
  32.8 12.9 %copy-start.6 = (f32[2,8,2,32,128]{4,3,1,0,2:T(8,128)}, f32[2,8,2,32,128]{4,3,1,0,2:T(8,128)S(1)}, u32[]{:S(2)}) copy-start(f32[2,8,2,32,128]{4,3,1,0,2:T(8,128)S(1)} %bitcast_add_fusion.3) | copy-start | bytes 1572868
  32.8 8.3 %collective-permute-start.6 = (f16[2,8,1,32,128]{4,3,1,0,2:T(8,128)(2,1)S(1)}, f16[2,8,1,32,128]{4,3,1,0,2:T(8,128)(2,1)S(1)}, u32[]{:S(2)}, u32[]{:S(2)}) collective-permute-start(f16[2,8,1,32,128]{4,3,1,0,2:T(8,128)(2,1)S(1)} %multiply_convert_fusion.4), channel_id=1, source_target_pairs={{0,2},{1,3},{2,0},{3,1},{4,6},{5,7},{6,4},{7,5},{8,10},{9,11},{10,... | collective-permute-start | bytes 393224 | tf_op jit(solution)/shard_map/ppermute | solution.py:252
  35.2 6.0 %collective-permute-start.8 = (f16[2,8,1,32,128]{4,3,1,0,2:T(8,128)(2,1)S(1)}, f16[2,8,1,32,128]{4,3,1,0,2:T(8,128)(2,1)S(1)}, u32[]{:S(2)}, u32[]{:S(2)}) collective-permute-start(f16[2,8,1,32,128]{4,3,1,0,2:T(8,128)(2,1)S(1)} %multiply_convert_fusion.3), channel_id=1, source_target_pairs={{0,2},{1,3},{2,0},{3,1},{8,10},{9,11},{10,8},{11,9},{16,18},{17,19... | collective-permute-start | bytes 393224 | tf_op jit(solution)/shard_map/ppermute | solution.py:252
  45.9 5.3 %collective-permute-start.12 = (f16[2,8,2,32,128]{4,3,1,0,2:T(8,128)(2,1)S(1)}, f16[2,8,2,32,128]{4,3,1,0,2:T(8,128)(2,1)S(1)}, u32[]{:S(2)}, u32[]{:S(2)}) collective-permute-start(f16[2,8,2,32,128]{4,3,1,0,2:T(8,128)(2,1)S(1)} %fusion.6), channel_id=1, source_target_pairs={{0,1},{1,0},{2,3},{3,2},{4,5},{5,4},{6,7},{7,6},{8,9},{9,8},{10,11... | collective-permute-start | bytes 786440 | tf_op jit(solution)/shard_map/ppermute | solution.py:252
  47.3 6.3 %collective-permute-start.11 = (f16[2,8,128,128]{3,2,1,0:T(8,128)(2,1)S(1)}, f16[2,8,128,128]{3,2,1,0:T(8,128)(2,1)S(1)}, u32[]{:S(2)}, u32[]{:S(2)}) collective-permute-start(f16[2,8,128,128]{3,2,1,0:T(8,128)(2,1)S(1)} %multiply_convert_fusion), channel_id=1, source_target_pairs={{0,4},{8,12},{1,5},{9,13},{2,6},{10,14},{3,7},{11,15},{16,20},{24,... | collective-permute-start | bytes 1572872 | tf_op jit(solution)/shard_map/ppermute | solution.py:298
  51.3 8.7 %collective-permute-start.13 = (f16[2,8,1,32,128]{4,3,2,1,0:T(8,128)(2,1)S(1)}, f16[2,8,1,32,128]{4,3,2,1,0:T(8,128)(2,1)S(1)}, u32[]{:S(2)}, u32[]{:S(2)}) collective-permute-start(f16[2,8,1,32,128]{4,3,2,1,0:T(8,128)(2,1)S(1)} %fusion.10), channel_id=1, source_target_pairs={{0,2},{1,3},{2,0},{3,1},{4,6},{5,7},{6,4},{7,5},{8,10},{9,11},{10,... | collective-permute-start | bytes 393224 | tf_op jit(solution)/shard_map/ppermute | solution.py:252
  60.1 3.1 %copy-start.7 = (f32[2,8,2,32,128]{4,3,1,0,2:T(8,128)S(1)}, f32[2,8,2,32,128]{4,3,1,0,2:T(8,128)}, u32[]{:S(2)}) copy-start(f32[2,8,2,32,128]{4,3,1,0,2:T(8,128)} %copy-done.6) | copy-start | bytes 1572868
  60.3 7.1 %collective-permute-start.14 = (f16[2,8,2,32,128]{4,3,1,0,2:T(8,128)(2,1)S(1)}, f16[2,8,2,32,128]{4,3,1,0,2:T(8,128)(2,1)S(1)}, u32[]{:S(2)}, u32[]{:S(2)}) collective-permute-start(f16[2,8,2,32,128]{4,3,1,0,2:T(8,128)(2,1)S(1)} %fusion.7), channel_id=1, source_target_pairs={{4,5},{5,4},{6,7},{7,6},{12,13},{13,12},{14,15},{15,14},{20,21},{2... | collective-permute-start | bytes 786440 | tf_op jit(solution)/shard_map/ppermute | solution.py:252
  67.5 8.0 %collective-permute-start.15 = (f16[2,8,1,32,128]{4,3,1,0,2:T(8,128)(2,1)S(1)}, f16[2,8,1,32,128]{4,3,1,0,2:T(8,128)(2,1)S(1)}, u32[]{:S(2)}, u32[]{:S(2)}) collective-permute-start(f16[2,8,1,32,128]{4,3,1,0,2:T(8,128)(2,1)S(1)} %multiply_convert_fusion.1), channel_id=1, source_target_pairs={{4,6},{5,7},{6,4},{7,5},{12,14},{13,15},{14,12},{15,13},{20,22},{2... | collective-permute-start | bytes 393224 | tf_op jit(solution)/shard_map/ppermute | solution.py:252

commit v13 on v12

--- a/solution.py
+++ b/solution.py
@@ -262,6 +262,23 @@
         stages.append(got[0, 0, 0].astype(jnp.float32))
         step *= 2
     return stages, keep[:, :, 0]
+
+
+def total_at_once(rows, pair_col, n_pair, rings, scale):
+    freq_count, count, aux_rows, width = rows.shape
+    height = aux_rows // n_pair
+
+    def share(column):
+        zero = jnp.uint32(0)
+        start = column * jnp.uint32(height)
+        return lax.dynamic_slice(rows, [zero, zero, start, zero], (freq_count, count, height, width))
+
+    far = []
+    for k in reversed(range(1, n_pair)):
+        sent = (share(pair_col ^ jnp.uint32(k)) * scale).astype(jnp.float16)
+        pairs = [(ring * n_pair + s, ring * n_pair + (s ^ k)) for ring in rings for s in range(n_pair)]
+        far.append(lax.ppermute(sent, ("aux", "pair"), pairs).astype(jnp.float32))
+    return share(pair_col) + sum(far) * (1.0 / scale)
 
 
 def on_device(three_centre, locality, live_blocks, occ_energy, virt_energy, frequencies):
@@ -299,7 +316,7 @@
     term = term.astype(jnp.float32) * (1.0 / scale)
     rows_odd, zeros = band_rows(dims, 1, [0], roots, own, [[b1]], [], term)
     (rows_odd,) = tie([rows_odd], [bits2[-1] + zeros])
-    _, z_odd = totals(rows_odd, pair_col, n_pair, odds, scale)
+    z_odd = total_at_once(rows_odd, pair_col, n_pair, odds, scale)
     even = lax.axis_index("aux").astype(jnp.uint32) & jnp.uint32(1) == 0
     out = jnp.concatenate([z0, jnp.where(even, z_even, z_odd), z2], axis=-1)
     return out[:, :, None]

time: 77 us -> 75 us (0.974)
  waiting for transfers between devices: 26.9 us -> 22.7 us
  starting transfers between devices: 26.2 us -> 28.6 us
    ppermute x0 -> x3, starting transfers between devices: none -> 9.27 us  [total_at_once(): far.append(lax.ppermute(sent, ('aux', 'pair'), pairs).astype(jnp.float32))]
    ppermute x8 -> x6, waiting for transfers between devices: 20.2 us -> 12 us  [halve(): got = lax.ppermute(sent, ('aux', 'pair'), pairs)]
    ppermute x8 -> x6, starting transfers between devices: 15.5 us -> 8.58 us  [halve(): got = lax.ppermute(sent, ('aux', 'pair'), pairs)]
    ppermute x0 -> x3, waiting for transfers between devices: none -> 4.02 us  [total_at_once(): far.append(lax.ppermute(sent, ('aux', 'pair'), pairs).astype(jnp.float32))]
    unnamed x19 -> x15, local copies, waits for them, and re-layouts: 3.62 us -> 3.61 us
  transfers between devices with their start and end apart: 16 -> 17, of which waited for: 10 -> 10; matrix products, arithmetic and copies ran while one was open for 2% -> 2% of each run, Pallas kernels for 19% -> 19%
where the time goes in v13:
time: 75 us; the launch traced here: 74.6 us
  starting transfers between devices  28.6 us (38%)
  waiting for transfers between devices  22.7 us (30%)
  Pallas kernels  16.2 us (22%)
  local copies, waits for them, and re-layouts  3.96 us (5%)
  other arithmetic  2.11 us (3%)
  between operations  0.95 us (1%)
    ppermute x6, waiting for transfers between devices, halve(): got = lax.ppermute(sent, ('aux', 'pair'), pairs)  12 us
    ppermute x3, starting transfers between devices, total_at_once(): far.append(lax.ppermute(sent, ('aux', 'pair'), pairs).astype(jnp.float32))  9.27 us
    ppermute x6, starting transfers between devices, halve(): got = lax.ppermute(sent, ('aux', 'pair'), pairs)  8.58 us
    pallas_call x1, Pallas kernels, first_rows(): pl.pallas_call(functools.partial(first_kernel, dims), out_shape=[jax.Shap...  7.43 us
    ppermute x3, waiting for transfers between devices, total_at_once(): far.append(lax.ppermute(sent, ('aux', 'pair'), pairs).astype(jnp.float32))  4.02 us
    pallas_call x1, Pallas kernels, second_rows(): pl.pallas_call(functools.partial(second_kernel, dims, pieces), out_shape=...  3.83 us
    ppermute x1, starting transfers between devices, on_device(): to_even = lax.ppermute(rest, 'aux', [(s, s - 1) for s in odds])  3.62 us
    unnamed x15, local copies, waits for them, and re-layouts  3.61 us
  transfers between devices with their start and end apart: 17, of which 10 were waited for; matrix products, arithmetic and copies ran while one was open for 2% of the time, Pallas kernels for 19%

profile of v13, /device:TPU:1, one launch (start us, length us, event | category | flops | bytes accessed | tf_op | source)
XLA Modules:
  0.0 74.6 jit_solution(9955727299718118059)
XLA Ops:
  0.0 2.1 %copy-done = bf16[1,1,8,3,1,128,640]{6,5,4,3,2,1,0:T(8,128)(2,1)S(1)} copy-done((bf16[1,1,8,3,1,128,640]{6,5,4,3,2,1,0:T(8,128)(2,1)S(1)}, bf16[1,1,8,3,1,128,640]{6,5,4,3,2,1,0:T(8,128)(2,1)}, u32[]{:S(2)}) %copy-start) | copy-done | bytes 3932184
  2.1 2.0 %shard_map.64 = (bf16[8,128,640]{2,1,0:T(8,128)(2,1)S(1)}, bf16[16,128,640]{2,1,0:T(8,128)(2,1)}, bf16[1,128,640]{2,1,0:T(8,128)(2,1)S(1)}, bf16[7,128,640]{2,1,0:T(8,128)(2,1)S(1)}, bf16[8,128,640]{2,1,0:T(8,128)(2,1)S(1)}) custom-call(bf16[8,3,128,640]{3,2,1,0:T(8,128)(2,1)S(1)} %bitcast.58), custom_call_target="tpu_custom_call" | custom-call | flops 1000 | bytes 1000 | tf_op jit(solution)/shard_map/pallas_call | solution.py:46
  4.1 1.1 %copy-done.1 = bf16[8,128,640]{2,1,0:T(8,128)(2,1)} copy-done((bf16[8,128,640]{2,1,0:T(8,128)(2,1)}, bf16[8,128,640]{2,1,0:T(8,128)(2,1)S(1)}, u32[]{:S(2)}) %copy-start.1) | copy-done | bytes 1310744
  5.2 3.6 %collective-permute-start.3 = (bf16[16,128,640]{2,1,0:T(8,128)(2,1)}, bf16[16,128,640]{2,1,0:T(8,128)(2,1)}, u32[]{:S(2)}, u32[]{:S(2)}) collective-permute-start(bf16[16,128,640]{2,1,0:T(8,128)(2,1)} %get-tuple-element.18.refs_8_.refs_1_), channel_id=1, source_target_pairs={{4,0},{12,8},{5,1},{13,9},{6,2},{14,10},{7,3},{15,11},{20,16},{28,... | collective-permute-start | bytes 7864328 | tf_op jit(solution)/shard_map/ppermute | solution.py:307
  8.8 2.7 %collective-permute-start.4 = (bf16[1,128,640]{2,1,0:T(8,128)(2,1)S(1)}, bf16[1,128,640]{2,1,0:T(8,128)(2,1)S(1)}, u32[]{:S(2)}, u32[]{:S(2)}) collective-permute-start(bf16[1,128,640]{2,1,0:T(8,128)(2,1)S(1)} %get-tuple-element.20), channel_id=1, source_target_pairs={{0,8},{4,12},{8,0},{12,4},{1,9},{5,13},{9,1},{13,5},{2,10},{6,14},... | collective-permute-start | bytes 491528 | tf_op jit(solution)/shard_map/ppermute | solution.py:304
  12.5 0.7 collective-permute-start.2
  13.2 0.7 collective-permute-done.refs_1_
  13.9 0.9 %collective-permute-done.1.refs_2_ = s32[25]{0:T(128)S(1)} collective-permute-done((s32[25]{0:T(128)S(1)}, s32[25]{0:T(128)S(1)}, u32[]{:S(2)}, u32[]{:S(2)}) %collective-permute-start.1) | collective-permute-done | bytes 132 | tf_op jit(solution)/shard_map/ppermute | solution.py:295
  14.8 0.9 %collective-permute-done.2.refs_3_ = s32[25]{0:T(128)S(1)} collective-permute-done((s32[25]{0:T(128)S(1)}, s32[25]{0:T(128)S(1)}, u32[]{:S(2)}, u32[]{:S(2)}) %collective-permute-start.2) | collective-permute-done | bytes 132 | tf_op jit(solution)/shard_map/ppermute | solution.py:295
  15.8 1.1 %collective-permute-start.10 = (bf16[7,128,640]{2,1,0:T(8,128)(2,1)S(1)}, bf16[7,128,640]{2,1,0:T(8,128)(2,1)S(1)}, u32[]{:S(2)}, u32[]{:S(2)}) collective-permute-start(bf16[7,128,640]{2,1,0:T(8,128)(2,1)S(1)} %shard_map.65.refs_10_), channel_id=1, source_target_pairs={{0,8},{4,12},{8,0},{12,4},{1,9},{5,13},{9,1},{13,5},{2,10},{6,14},... | collective-permute-start | bytes 3440648 | tf_op jit(solution)/shard_map/ppermute | solution.py:306
  16.9 7.4 %shard_map.66 = (f32[2,8,128,128]{3,2,1,0:T(8,128)S(1)}, f32[2,8,128,128]{3,2,1,0:T(8,128)S(1)}, f32[8,16,640]{2,1,0:T(8,128)S(1)}) custom-call(s32[25]{0:T(128)S(1)} %pad_add_fusion.refs_0_, s32[25]{0:T(128)S(1)} %collective-permute-done.refs_1_, s32[25]{0:T(128)S(1)} %collective-permute-done.1.refs_2_, s32[25]{0:T(128)S(1)} %collective-permute-done.2.refs_3_, ...), custom_call_target="tpu_custom_call" | custom-call | flops 1000 | bytes 1000 | tf_op jit(solution)/shard_map/pallas_call | solution.py:151
  24.5 1.4 %collective-permute-start.5 = (f16[2,8,2,32,128]{4,3,1,0,2:T(8,128)(2,1)S(1)}, f16[2,8,2,32,128]{4,3,1,0,2:T(8,128)(2,1)S(1)}, u32[]{:S(2)}, u32[]{:S(2)}) collective-permute-start(f16[2,8,2,32,128]{4,3,1,0,2:T(8,128)(2,1)S(1)} %fusion.3), channel_id=1, source_target_pairs={{0,1},{1,0},{2,3},{3,2},{4,5},{5,4},{6,7},{7,6},{8,9},{9,8},{10,11... | collective-permute-start | bytes 786440 | tf_op jit(solution)/shard_map/ppermute | solution.py:252
  26.0 0.8 %collective-permute-start.7 = (f16[2,8,2,32,128]{4,3,1,0,2:T(8,128)(2,1)S(1)}, f16[2,8,2,32,128]{4,3,1,0,2:T(8,128)(2,1)S(1)}, u32[]{:S(2)}, u32[]{:S(2)}) collective-permute-start(f16[2,8,2,32,128]{4,3,1,0,2:T(8,128)(2,1)S(1)} %fusion.4), channel_id=1, source_target_pairs={{0,1},{1,0},{2,3},{3,2},{8,9},{9,8},{10,11},{11,10},{16,17},{17,16... | collective-permute-start | bytes 786440 | tf_op jit(solution)/shard_map/ppermute | solution.py:252
  27.2 1.3 %collective-permute-start.9 = (bf16[8,128,640]{2,1,0:T(8,128)(2,1)S(1)}, bf16[8,128,640]{2,1,0:T(8,128)(2,1)S(1)}, u32[]{:S(2)}, u32[]{:S(2)}) collective-permute-start(bf16[8,128,640]{2,1,0:T(8,128)(2,1)S(1)} %shard_map.67), channel_id=1, source_target_pairs={{0,12},{8,4},{1,13},{9,5},{2,14},{10,6},{3,15},{11,7},{16,28},{24,... | collective-permute-start | bytes 3932168 | tf_op jit(solution)/shard_map/ppermute | solution.py:310
  28.5 4.1 %collective-permute-done.5 = f16[2,8,2,32,128]{4,3,1,0,2:T(8,128)(2,1)S(1)} collective-permute-done((f16[2,8,2,32,128]{4,3,1,0,2:T(8,128)(2,1)S(1)}, f16[2,8,2,32,128]{4,3,1,0,2:T(8,128)(2,1)S(1)}, u32[]{:S(2)}, u32[]{:S(2)}) %collective-permute-start.5) | collective-permute-done | bytes 262176 | tf_op jit(solution)/shard_map/ppermute | solution.py:252
  32.7 2.1 %collective-permute-start.6 = (f16[2,8,1,32,128]{4,3,1,0,2:T(8,128)(2,1)S(1)}, f16[2,8,1,32,128]{4,3,1,0,2:T(8,128)(2,1)S(1)}, u32[]{:S(2)}, u32[]{:S(2)}) collective-permute-start(f16[2,8,1,32,128]{4,3,1,0,2:T(8,128)(2,1)S(1)} %multiply_convert_fusion.6), channel_id=1, source_target_pairs={{0,2},{1,3},{2,0},{3,1},{4,6},{5,7},{6,4},{7,5},{8,10},{9,11},{10,... | collective-permute-start | bytes 393224 | tf_op jit(solution)/shard_map/ppermute | solution.py:252
  35.0 0.7 collective-permute-start.8
  35.7 5.4 %collective-permute-done.6 = f16[2,8,1,32,128]{4,3,1,0,2:T(8,128)(2,1)S(1)} collective-permute-done((f16[2,8,1,32,128]{4,3,1,0,2:T(8,128)(2,1)S(1)}, f16[2,8,1,32,128]{4,3,1,0,2:T(8,128)(2,1)S(1)}, u32[]{:S(2)}, u32[]{:S(2)}) %collective-permute-start.6) | collective-permute-done | bytes 131104 | tf_op jit(solution)/shard_map/ppermute | solution.py:252
  41.1 0.8 %collective-permute-done.10.refs_1_ = bf16[7,128,640]{2,1,0:T(8,128)(2,1)S(1)} collective-permute-done((bf16[7,128,640]{2,1,0:T(8,128)(2,1)S(1)}, bf16[7,128,640]{2,1,0:T(8,128)(2,1)S(1)}, u32[]{:S(2)}, u32[]{:S(2)}) %collective-permute-start.10) | collective-permute-done | bytes 1146912 | tf_op jit(solution)/shard_map/ppermute | solution.py:306
  41.9 3.8 %shard_map.68 = (f32[2,8,128,128]{3,2,1,0:T(8,128)S(1)}, f32[2,8,128,128]{3,2,1,0:T(8,128)S(1)}) custom-call(f32[8,16,640]{2,1,0:T(8,128)S(1)} %get-tuple-element.23.refs_1_.roots, bf16[8,128,640]{2,1,0:T(8,128)(2,1)S(1)} %get-tuple-element.17.refs_7_.own.refs_0_, bf16[16,128,640]{2,1,0:T(8,128)(2,1)} %collective-permute-done.3.refs_9_.lower, ...), custom_call_target="tpu_custom_call" | custom-call | flops 1000 | bytes 1000 | tf_op jit(solution)/shard_map/pallas_call | solution.py:229
  45.9 1.3 %collective-permute-start.12 = (f16[2,8,2,32,128]{4,3,1,0,2:T(8,128)(2,1)S(1)}, f16[2,8,2,32,128]{4,3,1,0,2:T(8,128)(2,1)S(1)}, u32[]{:S(2)}, u32[]{:S(2)}) collective-permute-start(f16[2,8,2,32,128]{4,3,1,0,2:T(8,128)(2,1)S(1)} %fusion.5), channel_id=1, source_target_pairs={{0,1},{1,0},{2,3},{3,2},{4,5},{5,4},{6,7},{7,6},{8,9},{9,8},{10,11... | collective-permute-start | bytes 786440 | tf_op jit(solution)/shard_map/ppermute | solution.py:252
  47.3 1.3 %collective-permute-start.11 = (f16[2,8,128,128]{3,2,1,0:T(8,128)(2,1)S(1)}, f16[2,8,128,128]{3,2,1,0:T(8,128)(2,1)S(1)}, u32[]{:S(2)}, u32[]{:S(2)}) collective-permute-start(f16[2,8,128,128]{3,2,1,0:T(8,128)(2,1)S(1)} %multiply_convert_fusion), channel_id=1, source_target_pairs={{0,4},{8,12},{1,5},{9,13},{2,6},{10,14},{3,7},{11,15},{16,20},{24,... | collective-permute-start | bytes 1572872 | tf_op jit(solution)/shard_map/ppermute | solution.py:315
  48.7 2.5 %collective-permute-done.12 = f16[2,8,2,32,128]{4,3,1,0,2:T(8,128)(2,1)S(1)} collective-permute-done((f16[2,8,2,32,128]{4,3,1,0,2:T(8,128)(2,1)S(1)}, f16[2,8,2,32,128]{4,3,1,0,2:T(8,128)(2,1)S(1)}, u32[]{:S(2)}, u32[]{:S(2)}) %collective-permute-start.12) | collective-permute-done | bytes 262176 | tf_op jit(solution)/shard_map/ppermute | solution.py:252
  51.3 2.3 %collective-permute-start.13 = (f16[2,8,1,32,128]{4,3,2,1,0:T(8,128)(2,1)S(1)}, f16[2,8,1,32,128]{4,3,2,1,0:T(8,128)(2,1)S(1)}, u32[]{:S(2)}, u32[]{:S(2)}) collective-permute-start(f16[2,8,1,32,128]{4,3,2,1,0:T(8,128)(2,1)S(1)} %fusion.8), channel_id=1, source_target_pairs={{0,2},{1,3},{2,0},{3,1},{4,6},{5,7},{6,4},{7,5},{8,10},{9,11},{10,... | collective-permute-start | bytes 393224 | tf_op jit(solution)/shard_map/ppermute | solution.py:252
  53.7 3.3 %collective-permute-done.9.refs_2_ = bf16[8,128,640]{2,1,0:T(8,128)(2,1)S(1)} collective-permute-done((bf16[8,128,640]{2,1,0:T(8,128)(2,1)S(1)}, bf16[8,128,640]{2,1,0:T(8,128)(2,1)S(1)}, u32[]{:S(2)}, u32[]{:S(2)}) %collective-permute-start.9) | collective-permute-done | bytes 1310752 | tf_op jit(solution)/shard_map/ppermute | solution.py:310
  57.1 3.0 %shard_map.69 = (f32[2,8,128,128]{3,2,1,0:T(8,128)S(1)}, f32[32,128]{1,0:T(8,128)S(1)}) custom-call(f32[8,16,640]{2,1,0:T(8,128)S(1)} %get-tuple-element.23.refs_1_.roots, bf16[8,128,640]{2,1,0:T(8,128)(2,1)S(1)} %get-tuple-element.17.refs_7_.own.refs_0_, bf16[16,128,640]{2,1,0:T(8,128)(2,1)} %get-tuple-element.18.refs_8_.refs_1_, ...), custom_call_target="tpu_custom_call" | custom-call | flops 1000 | bytes 1000 | tf_op jit(solution)/shard_map/pallas_call | solution.py:195
  60.2 5.0 %collective-permute-start.14 = (f16[2,8,32,128]{3,2,1,0:T(8,128)(2,1)S(1)}, f16[2,8,32,128]{3,2,1,0:T(8,128)(2,1)S(1)}, u32[]{:S(2)}, u32[]{:S(2)}) collective-permute-start(f16[2,8,32,128]{3,2,1,0:T(8,128)(2,1)S(1)} %get-tuple-element.29), channel_id=1, source_target_pairs={{4,7},{5,6},{6,5},{7,4},{12,15},{13,14},{14,13},{15,12},{20,23},{2... | collective-permute-start | bytes 393224 | tf_op jit(solution)/shard_map/ppermute | solution.py:280
  65.1 1.9 %collective-permute-start.15 = (f16[2,8,32,128]{3,2,1,0:T(8,128)(2,1)S(1)}, f16[2,8,32,128]{3,2,1,0:T(8,128)(2,1)S(1)}, u32[]{:S(2)}, u32[]{:S(2)}) collective-permute-start(f16[2,8,32,128]{3,2,1,0:T(8,128)(2,1)S(1)} %get-tuple-element.31), channel_id=1, source_target_pairs={{4,6},{5,7},{6,4},{7,5},{12,14},{13,15},{14,12},{15,13},{20,22},{2... | collective-permute-start | bytes 393224 | tf_op jit(solution)/shard_map/ppermute | solution.py:280
  67.1 2.4 %collective-permute-start.16 = (f16[2,8,32,128]{3,2,1,0:T(8,128)(2,1)S(1)}, f16[2,8,32,128]{3,2,1,0:T(8,128)(2,1)S(1)}, u32[]{:S(2)}, u32[]{:S(2)}) collective-permute-start(f16[2,8,32,128]{3,2,1,0:T(8,128)(2,1)S(1)} %get-tuple-element.30), channel_id=1, source_target_pairs={{4,5},{5,4},{6,7},{7,6},{12,13},{13,12},{14,15},{15,14},{20,21},{2... | collective-permute-start | bytes 393224 | tf_op jit(solution)/shard_map/ppermute | solution.py:280
  69.5 2.7 %collective-permute-done.15 = f16[2,8,32,128]{3,2,1,0:T(8,128)(2,1)S(1)} collective-permute-done((f16[2,8,32,128]{3,2,1,0:T(8,128)(2,1)S(1)}, f16[2,8,32,128]{3,2,1,0:T(8,128)(2,1)S(1)}, u32[]{:S(2)}, u32[]{:S(2)}) %collective-permute-start.15) | collective-permute-done | bytes 131104 | tf_op jit(solution)/shard_map/ppermute | solution.py:280
  72.2 1.3 %collective-permute-done.16 = f16[2,8,32,128]{3,2,1,0:T(8,128)(2,1)S(1)} collective-permute-done((f16[2,8,32,128]{3,2,1,0:T(8,128)(2,1)S(1)}, f16[2,8,32,128]{3,2,1,0:T(8,128)(2,1)S(1)}, u32[]{:S(2)}, u32[]{:S(2)}) %collective-permute-start.16) | collective-permute-done | bytes 131104 | tf_op jit(solution)/shard_map/ppermute | solution.py:280
  73.7 0.9 %maximum_bitcast_fusion = f32[2,8,1,32,384]{4,3,2,1,0:T(8,128)} fusion(f32[2,8,32,128]{3,2,1,0:T(8,128)S(1)} %fusion.7, f32[2,8,32,128]{3,2,1,0:T(8,128)S(1)} %bitcast_select_fusion, f32[2,8,32,128]{3,2,1,0:T(8,128)S(1)} %add_bitcast_fusion), kind=kLoop, calls=%fused_computation.2 | loop fusion | flops 393216 | bytes 1572864 | tf_op jit(solution)/shard_map/broadcast_in_dim | solution.py:322
  (48 shorter events, 2.0 us)
Async XLA Ops:
  0.0 2.1 %copy-start = (bf16[1,1,8,3,1,128,640]{6,5,4,3,2,1,0:T(8,128)(2,1)S(1)}, bf16[1,1,8,3,1,128,640]{6,5,4,3,2,1,0:T(8,128)(2,1)}, u32[]{:S(2)}) copy-start(bf16[1,1,8,3,1,128,640]{6,5,4,3,2,1,0:T(8,128)(2,1)} %param.6) | copy-start | bytes 11796484
  2.1 9.4 %copy-start.6 = (s32[1,1,8,3,1]{2,4,3,1,0:T(1,128)S(1)}, s32[1,1,8,3,1]{2,4,3,1,0:T(1,128)}, u32[]{:S(2)}) copy-start(s32[1,1,8,3,1]{2,4,3,1,0:T(1,128)} %param.7) | copy-start | bytes 292
  4.1 1.1 %copy-start.1 = (bf16[8,128,640]{2,1,0:T(8,128)(2,1)}, bf16[8,128,640]{2,1,0:T(8,128)(2,1)S(1)}, u32[]{:S(2)}) copy-start(bf16[8,128,640]{2,1,0:T(8,128)(2,1)S(1)} %get-tuple-element.24.refs_0_) | copy-start | bytes 3932164
  5.2 11.7 %copy-start.3 = (f32[10240]{0:T(1024)S(1)}, f32[10240]{0:T(1024)}, u32[]{:S(2)}) copy-start(f32[10240]{0:T(1024)} %param.10) | copy-start | bytes 122884
  5.2 11.7 %copy-start.4 = (f32[8]{0:T(128)S(1)}, f32[8]{0:T(128)}, u32[]{:S(2)}) copy-start(f32[8]{0:T(128)} %refs_4_.1) | copy-start | bytes 100
  5.2 11.7 %copy-start.5 = (f32[2]{0:T(128)S(1)}, f32[2]{0:T(128)}, u32[]{:S(2)}) copy-start(f32[2]{0:T(128)} %refs_5_.1) | copy-start | bytes 28
  5.2 11.7 %collective-permute-start.3 = (bf16[16,128,640]{2,1,0:T(8,128)(2,1)}, bf16[16,128,640]{2,1,0:T(8,128)(2,1)}, u32[]{:S(2)}, u32[]{:S(2)}) collective-permute-start(bf16[16,128,640]{2,1,0:T(8,128)(2,1)} %get-tuple-element.18.refs_8_.refs_1_), channel_id=1, source_target_pairs={{4,0},{12,8},{5,1},{13,9},{6,2},{14,10},{7,3},{15,11},{20,16},{28,... | collective-permute-start | bytes 7864328 | tf_op jit(solution)/shard_map/ppermute | solution.py:307
  8.8 6.9 %collective-permute-start.4 = (bf16[1,128,640]{2,1,0:T(8,128)(2,1)S(1)}, bf16[1,128,640]{2,1,0:T(8,128)(2,1)S(1)}, u32[]{:S(2)}, u32[]{:S(2)}) collective-permute-start(bf16[1,128,640]{2,1,0:T(8,128)(2,1)S(1)} %get-tuple-element.20), channel_id=1, source_target_pairs={{0,8},{4,12},{8,0},{12,4},{1,9},{5,13},{9,1},{13,5},{2,10},{6,14},... | collective-permute-start | bytes 491528 | tf_op jit(solution)/shard_map/ppermute | solution.py:304
  12.4 1.5 %collective-permute-start = (s32[25]{0:T(128)S(1)}, s32[25]{0:T(128)S(1)}, u32[]{:S(2)}, u32[]{:S(2)}) collective-permute-start(s32[25]{0:T(128)S(1)} %pad_add_fusion.refs_0_), channel_id=1, source_target_pairs={{0,4},{4,8},{8,12},{12,0},{1,5},{5,9},{9,13},{13,1},{2,6},{6,10},{... | collective-permute-start | bytes 308 | tf_op jit(solution)/shard_map/ppermute | solution.py:295
  12.4 2.5 %collective-permute-start.1 = (s32[25]{0:T(128)S(1)}, s32[25]{0:T(128)S(1)}, u32[]{:S(2)}, u32[]{:S(2)}) collective-permute-start(s32[25]{0:T(128)S(1)} %pad_add_fusion.refs_0_), channel_id=1, source_target_pairs={{0,8},{4,12},{8,0},{12,4},{1,9},{5,13},{9,1},{13,5},{2,10},{6,14},... | collective-permute-start | bytes 308 | tf_op jit(solution)/shard_map/ppermute | solution.py:295
  12.5 3.3 %collective-permute-start.2 = (s32[25]{0:T(128)S(1)}, s32[25]{0:T(128)S(1)}, u32[]{:S(2)}, u32[]{:S(2)}) collective-permute-start(s32[25]{0:T(128)S(1)} %pad_add_fusion.refs_0_), channel_id=1, source_target_pairs={{0,12},{4,0},{8,4},{12,8},{1,13},{5,1},{9,5},{13,9},{2,14},{6,2},{... | collective-permute-start | bytes 308 | tf_op jit(solution)/shard_map/ppermute | solution.py:295
  15.8 26.1 %collective-permute-start.10 = (bf16[7,128,640]{2,1,0:T(8,128)(2,1)S(1)}, bf16[7,128,640]{2,1,0:T(8,128)(2,1)S(1)}, u32[]{:S(2)}, u32[]{:S(2)}) collective-permute-start(bf16[7,128,640]{2,1,0:T(8,128)(2,1)S(1)} %shard_map.65.refs_10_), channel_id=1, source_target_pairs={{0,8},{4,12},{8,0},{12,4},{1,9},{5,13},{9,1},{13,5},{2,10},{6,14},... | collective-permute-start | bytes 3440648 | tf_op jit(solution)/shard_map/ppermute | solution.py:306
  24.5 8.1 %collective-permute-start.5 = (f16[2,8,2,32,128]{4,3,1,0,2:T(8,128)(2,1)S(1)}, f16[2,8,2,32,128]{4,3,1,0,2:T(8,128)(2,1)S(1)}, u32[]{:S(2)}, u32[]{:S(2)}) collective-permute-start(f16[2,8,2,32,128]{4,3,1,0,2:T(8,128)(2,1)S(1)} %fusion.3), channel_id=1, source_target_pairs={{0,1},{1,0},{2,3},{3,2},{4,5},{5,4},{6,7},{7,6},{8,9},{9,8},{10,11... | collective-permute-start | bytes 786440 | tf_op jit(solution)/shard_map/ppermute | solution.py:252
  25.9 1.3 %copy-start.2 = (bf16[8,128,640]{2,1,0:T(8,128)(2,1)S(1)}, bf16[8,128,640]{2,1,0:T(8,128)(2,1)}, u32[]{:S(2)}) copy-start(bf16[8,128,640]{2,1,0:T(8,128)(2,1)} %copy-done.1) | copy-start | bytes 3932164
  26.0 8.8 %collective-permute-start.7 = (f16[2,8,2,32,128]{4,3,1,0,2:T(8,128)(2,1)S(1)}, f16[2,8,2,32,128]{4,3,1,0,2:T(8,128)(2,1)S(1)}, u32[]{:S(2)}, u32[]{:S(2)}) collective-permute-start(f16[2,8,2,32,128]{4,3,1,0,2:T(8,128)(2,1)S(1)} %fusion.4), channel_id=1, source_target_pairs={{0,1},{1,0},{2,3},{3,2},{8,9},{9,8},{10,11},{11,10},{16,17},{17,16... | collective-permute-start | bytes 786440 | tf_op jit(solution)/shard_map/ppermute | solution.py:252
  27.2 29.9 %collective-permute-start.9 = (bf16[8,128,640]{2,1,0:T(8,128)(2,1)S(1)}, bf16[8,128,640]{2,1,0:T(8,128)(2,1)S(1)}, u32[]{:S(2)}, u32[]{:S(2)}) collective-permute-start(bf16[8,128,640]{2,1,0:T(8,128)(2,1)S(1)} %shard_map.67), channel_id=1, source_target_pairs={{0,12},{8,4},{1,13},{9,5},{2,14},{10,6},{3,15},{11,7},{16,28},{24,... | collective-permute-start | bytes 3932168 | tf_op jit(solution)/shard_map/ppermute | solution.py:310
  32.7 8.3 %collective-permute-start.6 = (f16[2,8,1,32,128]{4,3,1,0,2:T(8,128)(2,1)S(1)}, f16[2,8,1,32,128]{4,3,1,0,2:T(8,128)(2,1)S(1)}, u32[]{:S(2)}, u32[]{:S(2)}) collective-permute-start(f16[2,8,1,32,128]{4,3,1,0,2:T(8,128)(2,1)S(1)} %multiply_convert_fusion.6), channel_id=1, source_target_pairs={{0,2},{1,3},{2,0},{3,1},{4,6},{5,7},{6,4},{7,5},{8,10},{9,11},{10,... | collective-permute-start | bytes 393224 | tf_op jit(solution)/shard_map/ppermute | solution.py:252
  35.0 6.0 %collective-permute-start.8 = (f16[2,8,1,32,128]{4,3,1,0,2:T(8,128)(2,1)S(1)}, f16[2,8,1,32,128]{4,3,1,0,2:T(8,128)(2,1)S(1)}, u32[]{:S(2)}, u32[]{:S(2)}) collective-permute-start(f16[2,8,1,32,128]{4,3,1,0,2:T(8,128)(2,1)S(1)} %multiply_convert_fusion.5), channel_id=1, source_target_pairs={{0,2},{1,3},{2,0},{3,1},{8,10},{9,11},{10,8},{11,9},{16,18},{17,19... | collective-permute-start | bytes 393224 | tf_op jit(solution)/shard_map/ppermute | solution.py:252
  45.9 5.3 %collective-permute-start.12 = (f16[2,8,2,32,128]{4,3,1,0,2:T(8,128)(2,1)S(1)}, f16[2,8,2,32,128]{4,3,1,0,2:T(8,128)(2,1)S(1)}, u32[]{:S(2)}, u32[]{:S(2)}) collective-permute-start(f16[2,8,2,32,128]{4,3,1,0,2:T(8,128)(2,1)S(1)} %fusion.5), channel_id=1, source_target_pairs={{0,1},{1,0},{2,3},{3,2},{4,5},{5,4},{6,7},{7,6},{8,9},{9,8},{10,11... | collective-permute-start | bytes 786440 | tf_op jit(solution)/shard_map/ppermute | solution.py:252
  47.3 6.3 %collective-permute-start.11 = (f16[2,8,128,128]{3,2,1,0:T(8,128)(2,1)S(1)}, f16[2,8,128,128]{3,2,1,0:T(8,128)(2,1)S(1)}, u32[]{:S(2)}, u32[]{:S(2)}) collective-permute-start(f16[2,8,128,128]{3,2,1,0:T(8,128)(2,1)S(1)} %multiply_convert_fusion), channel_id=1, source_target_pairs={{0,4},{8,12},{1,5},{9,13},{2,6},{10,14},{3,7},{11,15},{16,20},{24,... | collective-permute-start | bytes 1572872 | tf_op jit(solution)/shard_map/ppermute | solution.py:315
  51.3 8.7 %collective-permute-start.13 = (f16[2,8,1,32,128]{4,3,2,1,0:T(8,128)(2,1)S(1)}, f16[2,8,1,32,128]{4,3,2,1,0:T(8,128)(2,1)S(1)}, u32[]{:S(2)}, u32[]{:S(2)}) collective-permute-start(f16[2,8,1,32,128]{4,3,2,1,0:T(8,128)(2,1)S(1)} %fusion.8), channel_id=1, source_target_pairs={{0,2},{1,3},{2,0},{3,1},{4,6},{5,7},{6,4},{7,5},{8,10},{9,11},{10,... | collective-permute-start | bytes 393224 | tf_op jit(solution)/shard_map/ppermute | solution.py:252
  60.2 9.3 %collective-permute-start.14 = (f16[2,8,32,128]{3,2,1,0:T(8,128)(2,1)S(1)}, f16[2,8,32,128]{3,2,1,0:T(8,128)(2,1)S(1)}, u32[]{:S(2)}, u32[]{:S(2)}) collective-permute-start(f16[2,8,32,128]{3,2,1,0:T(8,128)(2,1)S(1)} %get-tuple-element.29), channel_id=1, source_target_pairs={{4,7},{5,6},{6,5},{7,4},{12,15},{13,14},{14,13},{15,12},{20,23},{2... | collective-permute-start | bytes 393224 | tf_op jit(solution)/shard_map/ppermute | solution.py:280
  65.1 7.1 %collective-permute-start.15 = (f16[2,8,32,128]{3,2,1,0:T(8,128)(2,1)S(1)}, f16[2,8,32,128]{3,2,1,0:T(8,128)(2,1)S(1)}, u32[]{:S(2)}, u32[]{:S(2)}) collective-permute-start(f16[2,8,32,128]{3,2,1,0:T(8,128)(2,1)S(1)} %get-tuple-element.31), channel_id=1, source_target_pairs={{4,6},{5,7},{6,4},{7,5},{12,14},{13,15},{14,12},{15,13},{20,22},{2... | collective-permute-start | bytes 393224 | tf_op jit(solution)/shard_map/ppermute | solution.py:280
  67.1 6.5 %collective-permute-start.16 = (f16[2,8,32,128]{3,2,1,0:T(8,128)(2,1)S(1)}, f16[2,8,32,128]{3,2,1,0:T(8,128)(2,1)S(1)}, u32[]{:S(2)}, u32[]{:S(2)}) collective-permute-start(f16[2,8,32,128]{3,2,1,0:T(8,128)(2,1)S(1)} %get-tuple-element.30), channel_id=1, source_target_pairs={{4,5},{5,4},{6,7},{7,6},{12,13},{13,12},{14,15},{15,14},{20,21},{2... | collective-permute-start | bytes 393224 | tf_op jit(solution)/shard_map/ppermute | solution.py:280

commit v14 on v13

--- a/solution.py
+++ b/solution.py
@@ -162,47 +162,33 @@
     )(*records, occ, freq, table, *own, far, *after)
 
 
-def band_kernel(dims, delta, slots, rights, add, roots, *refs):
-    n_aux, n_pair, blocks_dev, band, freq_count = dims
-    out, zeros = refs[-2:]
+def odd_kernel(dims, roots, own, far, add, out, zeros):
+    n_aux, n_pair, blocks_dev, band, freq_count = dims
     zeros[...] = jnp.zeros_like(zeros)
     for m in range(blocks_dev):
-        sums = [refs[add][w, m] if add is not None else None for w in range(freq_count)]
-        for s, slot in enumerate(slots):
-            n, row = rights[s][m]
-            left = own_tile(refs, slot, m, blocks_dev).astype(jnp.float32)
-            right = refs[n][row].astype(jnp.float32)
-            for w in range(freq_count):
-                kept = roots[m, pl.ds(root_row(band, freq_count, delta, slot, w), 1), :]
-                root = roots[m, pl.ds(root_row(band, freq_count, None, slot, w), 1), :]
-                term = dot((left * kept).astype(jnp.bfloat16), (right * root).astype(jnp.bfloat16))
-                sums[w] = term if sums[w] is None else sums[w] + term
+        left = own[m].astype(jnp.float32)
+        right = far[m].astype(jnp.float32)
         for w in range(freq_count):
-            out[w, m] = sums[w]
-
-
-def band_rows(dims, delta, slots, roots, own, far, after, add=None):
-    n_aux, n_pair, blocks_dev, band, freq_count = dims
-    aux_rows = own[0].shape[-2]
-    arrays = list(own)
-    rights = []
-    for group in far:
-        rows = [(len(arrays) + n, row) for n, array in enumerate(group) for row in range(array.shape[0])]
-        rights.append(rows[-blocks_dev:] if len(rights) > 0 else rows[:blocks_dev])
-        arrays += group
-    spot = None if add is None else len(arrays)
-    arrays += [] if add is None else [add]
-    return pl.pallas_call(
-        functools.partial(band_kernel, dims, delta, slots, rights, spot),
+            kept = roots[m, pl.ds(root_row(band, freq_count, 1, 0, w), 1), :]
+            root = roots[m, pl.ds(root_row(band, freq_count, None, 0, w), 1), :]
+            term = dot((left * kept).astype(jnp.bfloat16), (right * root).astype(jnp.bfloat16))
+            out[w, m] = add[w, m] + term
+
+
+def odd_rows(dims, roots, own, far, add):
+    n_aux, n_pair, blocks_dev, band, freq_count = dims
+    aux_rows = own.shape[-2]
+    return pl.pallas_call(
+        functools.partial(odd_kernel, dims),
         out_shape=[
             jax.ShapeDtypeStruct((freq_count, blocks_dev, aux_rows, aux_rows), jnp.float32),
             jax.ShapeDtypeStruct((aux_rows // n_pair, aux_rows), jnp.float32),
         ],
-        in_specs=[VMEM] * (1 + len(arrays)) + [ANY] * len(after),
+        in_specs=[VMEM] * 4,
         out_specs=[VMEM] * 2,
         compiler_params=PARAMS,
         cost_estimate=COST,
-    )(roots, *arrays, *after)
+    )(roots, own, far, add)
 
 
 def second_kernel(dims, pieces, roots, own, lower, *refs):
@@ -314,7 +300,7 @@
     bits2, z2 = totals(rows2, pair_col, n_pair, whole, scale)
     term = lax.ppermute((rows_next * scale).astype(jnp.float16), "aux", [(s, s + 1) for s in evens])
     term = term.astype(jnp.float32) * (1.0 / scale)
-    rows_odd, zeros = band_rows(dims, 1, [0], roots, own, [[b1]], [], term)
+    rows_odd, zeros = odd_rows(dims, roots, first_slot, b1, term)
     (rows_odd,) = tie([rows_odd], [bits2[-1] + zeros])
     z_odd = total_at_once(rows_odd, pair_col, n_pair, odds, scale)
     even = lax.axis_index("aux").astype(jnp.uint32) & jnp.uint32(1) == 0

time: 75 us -> 73.2 us (0.976)
  Pallas kernels: 16.2 us -> 14.5 us
    pallas_call x1, Pallas kernels: 2.96 us -> 1.21 us  [odd_rows(): pl.pallas_call(functools.partial(odd_kernel, dims), out_shape=[jax.ShapeD...]
  transfers between devices with their start and end apart: 17 -> 17, of which waited for: 10 -> 10; matrix products, arithmetic and copies ran while one was open for 2% -> 2% of each run, Pallas kernels for 19% -> 17%
where the time goes in v14:
time: 73.2 us; the launch traced here: 72.9 us
  starting transfers between devices  28.6 us (39%)
  waiting for transfers between devices  22.7 us (31%)
  Pallas kernels  14.5 us (20%)
  local copies, waits for them, and re-layouts  3.96 us (5%)
  other arithmetic  2.11 us (3%)
  between operations  0.95 us (1%)
    ppermute x6, waiting for transfers between devices, halve(): got = lax.ppermute(sent, ('aux', 'pair'), pairs)  12 us
    ppermute x3, starting transfers between devices, total_at_once(): far.append(lax.ppermute(sent, ('aux', 'pair'), pairs).astype(jnp.float32))  9.27 us
    ppermute x6, starting transfers between devices, halve(): got = lax.ppermute(sent, ('aux', 'pair'), pairs)  8.58 us
    pallas_call x1, Pallas kernels, first_rows(): pl.pallas_call(functools.partial(first_kernel, dims), out_shape=[jax.Shap...  7.43 us
    ppermute x3, waiting for transfers between devices, total_at_once(): far.append(lax.ppermute(sent, ('aux', 'pair'), pairs).astype(jnp.float32))  4.02 us
    pallas_call x1, Pallas kernels, second_rows(): pl.pallas_call(functools.partial(second_kernel, dims, pieces), out_shape=...  3.83 us
    ppermute x1, starting transfers between devices, on_device(): to_even = lax.ppermute(rest, 'aux', [(s, s - 1) for s in odds])  3.62 us
    unnamed x15, local copies, waits for them, and re-layouts  3.61 us
  transfers between devices with their start and end apart: 17, of which 10 were waited for; matrix products, arithmetic and copies ran while one was open for 2% of the time, Pallas kernels for 17%

profile of v14, /device:TPU:1, one launch (start us, length us, event | category | flops | bytes accessed | tf_op | source)
XLA Modules:
  0.0 72.9 jit_solution(4579360315572627683)
XLA Ops:
  0.0 2.1 %copy-done = bf16[1,1,8,3,1,128,640]{6,5,4,3,2,1,0:T(8,128)(2,1)S(1)} copy-done((bf16[1,1,8,3,1,128,640]{6,5,4,3,2,1,0:T(8,128)(2,1)S(1)}, bf16[1,1,8,3,1,128,640]{6,5,4,3,2,1,0:T(8,128)(2,1)}, u32[]{:S(2)}) %copy-start) | copy-done | bytes 3932184
  2.1 2.0 %shard_map.64 = (bf16[8,128,640]{2,1,0:T(8,128)(2,1)S(1)}, bf16[16,128,640]{2,1,0:T(8,128)(2,1)}, bf16[1,128,640]{2,1,0:T(8,128)(2,1)S(1)}, bf16[7,128,640]{2,1,0:T(8,128)(2,1)S(1)}, bf16[8,128,640]{2,1,0:T(8,128)(2,1)S(1)}) custom-call(bf16[8,3,128,640]{3,2,1,0:T(8,128)(2,1)S(1)} %bitcast.58), custom_call_target="tpu_custom_call" | custom-call | flops 1000 | bytes 1000 | tf_op jit(solution)/shard_map/pallas_call | solution.py:46
  4.1 1.1 %copy-done.1 = bf16[8,128,640]{2,1,0:T(8,128)(2,1)} copy-done((bf16[8,128,640]{2,1,0:T(8,128)(2,1)}, bf16[8,128,640]{2,1,0:T(8,128)(2,1)S(1)}, u32[]{:S(2)}) %copy-start.1) | copy-done | bytes 1310744
  5.2 3.6 %collective-permute-start.3 = (bf16[16,128,640]{2,1,0:T(8,128)(2,1)}, bf16[16,128,640]{2,1,0:T(8,128)(2,1)}, u32[]{:S(2)}, u32[]{:S(2)}) collective-permute-start(bf16[16,128,640]{2,1,0:T(8,128)(2,1)} %get-tuple-element.18.refs_8_), channel_id=1, source_target_pairs={{4,0},{12,8},{5,1},{13,9},{6,2},{14,10},{7,3},{15,11},{20,16},{28,... | collective-permute-start | bytes 7864328 | tf_op jit(solution)/shard_map/ppermute | solution.py:293
  8.8 2.7 %collective-permute-start.4 = (bf16[1,128,640]{2,1,0:T(8,128)(2,1)S(1)}, bf16[1,128,640]{2,1,0:T(8,128)(2,1)S(1)}, u32[]{:S(2)}, u32[]{:S(2)}) collective-permute-start(bf16[1,128,640]{2,1,0:T(8,128)(2,1)S(1)} %get-tuple-element.20), channel_id=1, source_target_pairs={{0,8},{4,12},{8,0},{12,4},{1,9},{5,13},{9,1},{13,5},{2,10},{6,14},... | collective-permute-start | bytes 491528 | tf_op jit(solution)/shard_map/ppermute | solution.py:290
  12.5 0.7 collective-permute-start.2
  13.2 0.7 %collective-permute-done.refs_1_ = s32[25]{0:T(128)S(1)} collective-permute-done((s32[25]{0:T(128)S(1)}, s32[25]{0:T(128)S(1)}, u32[]{:S(2)}, u32[]{:S(2)}) %collective-permute-start) | collective-permute-done | bytes 132 | tf_op jit(solution)/shard_map/ppermute | solution.py:281
  13.9 0.9 %collective-permute-done.1.refs_2_ = s32[25]{0:T(128)S(1)} collective-permute-done((s32[25]{0:T(128)S(1)}, s32[25]{0:T(128)S(1)}, u32[]{:S(2)}, u32[]{:S(2)}) %collective-permute-start.1) | collective-permute-done | bytes 132 | tf_op jit(solution)/shard_map/ppermute | solution.py:281
  14.8 0.9 %collective-permute-done.2.refs_3_ = s32[25]{0:T(128)S(1)} collective-permute-done((s32[25]{0:T(128)S(1)}, s32[25]{0:T(128)S(1)}, u32[]{:S(2)}, u32[]{:S(2)}) %collective-permute-start.2) | collective-permute-done | bytes 132 | tf_op jit(solution)/shard_map/ppermute | solution.py:281
  15.8 1.1 %collective-permute-start.10 = (bf16[7,128,640]{2,1,0:T(8,128)(2,1)S(1)}, bf16[7,128,640]{2,1,0:T(8,128)(2,1)S(1)}, u32[]{:S(2)}, u32[]{:S(2)}) collective-permute-start(bf16[7,128,640]{2,1,0:T(8,128)(2,1)S(1)} %shard_map.65.refs_10_), channel_id=1, source_target_pairs={{0,8},{4,12},{8,0},{12,4},{1,9},{5,13},{9,1},{13,5},{2,10},{6,14},... | collective-permute-start | bytes 3440648 | tf_op jit(solution)/shard_map/ppermute | solution.py:292
  16.9 7.4 %shard_map.66 = (f32[2,8,128,128]{3,2,1,0:T(8,128)S(1)}, f32[2,8,128,128]{3,2,1,0:T(8,128)S(1)}, f32[8,16,640]{2,1,0:T(8,128)S(1)}) custom-call(s32[25]{0:T(128)S(1)} %pad_add_fusion.refs_0_, s32[25]{0:T(128)S(1)} %collective-permute-done.refs_1_, s32[25]{0:T(128)S(1)} %collective-permute-done.1.refs_2_, s32[25]{0:T(128)S(1)} %collective-permute-done.2.refs_3_, ...), custom_call_target="tpu_custom_call" | custom-call | flops 1000 | bytes 1000 | tf_op jit(solution)/shard_map/pallas_call | solution.py:151
  24.5 1.4 %collective-permute-start.5 = (f16[2,8,2,32,128]{4,3,1,0,2:T(8,128)(2,1)S(1)}, f16[2,8,2,32,128]{4,3,1,0,2:T(8,128)(2,1)S(1)}, u32[]{:S(2)}, u32[]{:S(2)}) collective-permute-start(f16[2,8,2,32,128]{4,3,1,0,2:T(8,128)(2,1)S(1)} %fusion.3), channel_id=1, source_target_pairs={{0,1},{1,0},{2,3},{3,2},{4,5},{5,4},{6,7},{7,6},{8,9},{9,8},{10,11... | collective-permute-start | bytes 786440 | tf_op jit(solution)/shard_map/ppermute | solution.py:238
  26.0 0.8 %collective-permute-start.7 = (f16[2,8,2,32,128]{4,3,1,0,2:T(8,128)(2,1)S(1)}, f16[2,8,2,32,128]{4,3,1,0,2:T(8,128)(2,1)S(1)}, u32[]{:S(2)}, u32[]{:S(2)}) collective-permute-start(f16[2,8,2,32,128]{4,3,1,0,2:T(8,128)(2,1)S(1)} %fusion.4), channel_id=1, source_target_pairs={{0,1},{1,0},{2,3},{3,2},{8,9},{9,8},{10,11},{11,10},{16,17},{17,16... | collective-permute-start | bytes 786440 | tf_op jit(solution)/shard_map/ppermute | solution.py:238
  27.2 1.3 %collective-permute-start.9 = (bf16[8,128,640]{2,1,0:T(8,128)(2,1)S(1)}, bf16[8,128,640]{2,1,0:T(8,128)(2,1)S(1)}, u32[]{:S(2)}, u32[]{:S(2)}) collective-permute-start(bf16[8,128,640]{2,1,0:T(8,128)(2,1)S(1)} %shard_map.67), channel_id=1, source_target_pairs={{0,12},{8,4},{1,13},{9,5},{2,14},{10,6},{3,15},{11,7},{16,28},{24,... | collective-permute-start | bytes 3932168 | tf_op jit(solution)/shard_map/ppermute | solution.py:296
  28.5 4.1 %collective-permute-done.5 = f16[2,8,2,32,128]{4,3,1,0,2:T(8,128)(2,1)S(1)} collective-permute-done((f16[2,8,2,32,128]{4,3,1,0,2:T(8,128)(2,1)S(1)}, f16[2,8,2,32,128]{4,3,1,0,2:T(8,128)(2,1)S(1)}, u32[]{:S(2)}, u32[]{:S(2)}) %collective-permute-start.5) | collective-permute-done | bytes 262176 | tf_op jit(solution)/shard_map/ppermute | solution.py:238
  32.7 2.1 %collective-permute-start.6 = (f16[2,8,1,32,128]{4,3,1,0,2:T(8,128)(2,1)S(1)}, f16[2,8,1,32,128]{4,3,1,0,2:T(8,128)(2,1)S(1)}, u32[]{:S(2)}, u32[]{:S(2)}) collective-permute-start(f16[2,8,1,32,128]{4,3,1,0,2:T(8,128)(2,1)S(1)} %multiply_convert_fusion.6), channel_id=1, source_target_pairs={{0,2},{1,3},{2,0},{3,1},{4,6},{5,7},{6,4},{7,5},{8,10},{9,11},{10,... | collective-permute-start | bytes 393224 | tf_op jit(solution)/shard_map/ppermute | solution.py:238
  35.0 0.7 collective-permute-start.8
  35.7 5.4 %collective-permute-done.6 = f16[2,8,1,32,128]{4,3,1,0,2:T(8,128)(2,1)S(1)} collective-permute-done((f16[2,8,1,32,128]{4,3,1,0,2:T(8,128)(2,1)S(1)}, f16[2,8,1,32,128]{4,3,1,0,2:T(8,128)(2,1)S(1)}, u32[]{:S(2)}, u32[]{:S(2)}) %collective-permute-start.6) | collective-permute-done | bytes 131104 | tf_op jit(solution)/shard_map/ppermute | solution.py:238
  41.1 0.8 %collective-permute-done.10.refs_1_ = bf16[7,128,640]{2,1,0:T(8,128)(2,1)S(1)} collective-permute-done((bf16[7,128,640]{2,1,0:T(8,128)(2,1)S(1)}, bf16[7,128,640]{2,1,0:T(8,128)(2,1)S(1)}, u32[]{:S(2)}, u32[]{:S(2)}) %collective-permute-start.10) | collective-permute-done | bytes 1146912 | tf_op jit(solution)/shard_map/ppermute | solution.py:292
  41.9 3.8 %shard_map.68 = (f32[2,8,128,128]{3,2,1,0:T(8,128)S(1)}, f32[2,8,128,128]{3,2,1,0:T(8,128)S(1)}) custom-call(f32[8,16,640]{2,1,0:T(8,128)S(1)} %get-tuple-element.23.refs_1_.roots, bf16[8,128,640]{2,1,0:T(8,128)(2,1)S(1)} %get-tuple-element.17.refs_7_.own, bf16[16,128,640]{2,1,0:T(8,128)(2,1)} %collective-permute-done.3.refs_9_.lower, ...), custom_call_target="tpu_custom_call" | custom-call | flops 1000 | bytes 1000 | tf_op jit(solution)/shard_map/pallas_call | solution.py:215
  45.9 1.3 %collective-permute-start.12 = (f16[2,8,2,32,128]{4,3,1,0,2:T(8,128)(2,1)S(1)}, f16[2,8,2,32,128]{4,3,1,0,2:T(8,128)(2,1)S(1)}, u32[]{:S(2)}, u32[]{:S(2)}) collective-permute-start(f16[2,8,2,32,128]{4,3,1,0,2:T(8,128)(2,1)S(1)} %fusion.5), channel_id=1, source_target_pairs={{0,1},{1,0},{2,3},{3,2},{4,5},{5,4},{6,7},{7,6},{8,9},{9,8},{10,11... | collective-permute-start | bytes 786440 | tf_op jit(solution)/shard_map/ppermute | solution.py:238
  47.3 1.3 %collective-permute-start.11 = (f16[2,8,128,128]{3,2,1,0:T(8,128)(2,1)S(1)}, f16[2,8,128,128]{3,2,1,0:T(8,128)(2,1)S(1)}, u32[]{:S(2)}, u32[]{:S(2)}) collective-permute-start(f16[2,8,128,128]{3,2,1,0:T(8,128)(2,1)S(1)} %multiply_convert_fusion), channel_id=1, source_target_pairs={{0,4},{8,12},{1,5},{9,13},{2,6},{10,14},{3,7},{11,15},{16,20},{24,... | collective-permute-start | bytes 1572872 | tf_op jit(solution)/shard_map/ppermute | solution.py:301
  48.7 2.5 %collective-permute-done.12 = f16[2,8,2,32,128]{4,3,1,0,2:T(8,128)(2,1)S(1)} collective-permute-done((f16[2,8,2,32,128]{4,3,1,0,2:T(8,128)(2,1)S(1)}, f16[2,8,2,32,128]{4,3,1,0,2:T(8,128)(2,1)S(1)}, u32[]{:S(2)}, u32[]{:S(2)}) %collective-permute-start.12) | collective-permute-done | bytes 262176 | tf_op jit(solution)/shard_map/ppermute | solution.py:238
  51.3 2.3 %collective-permute-start.13 = (f16[2,8,1,32,128]{4,3,2,1,0:T(8,128)(2,1)S(1)}, f16[2,8,1,32,128]{4,3,2,1,0:T(8,128)(2,1)S(1)}, u32[]{:S(2)}, u32[]{:S(2)}) collective-permute-start(f16[2,8,1,32,128]{4,3,2,1,0:T(8,128)(2,1)S(1)} %fusion.8), channel_id=1, source_target_pairs={{0,2},{1,3},{2,0},{3,1},{4,6},{5,7},{6,4},{7,5},{8,10},{9,11},{10,... | collective-permute-start | bytes 393224 | tf_op jit(solution)/shard_map/ppermute | solution.py:238
  53.7 3.3 %collective-permute-done.9.far = bf16[8,128,640]{2,1,0:T(8,128)(2,1)S(1)} collective-permute-done((bf16[8,128,640]{2,1,0:T(8,128)(2,1)S(1)}, bf16[8,128,640]{2,1,0:T(8,128)(2,1)S(1)}, u32[]{:S(2)}, u32[]{:S(2)}) %collective-permute-start.9) | collective-permute-done | bytes 1310752 | tf_op jit(solution)/shard_map/ppermute | solution.py:296
  57.1 1.2 %shard_map.69 = (f32[2,8,128,128]{3,2,1,0:T(8,128)S(1)}, f32[32,128]{1,0:T(8,128)S(1)}) custom-call(f32[8,16,640]{2,1,0:T(8,128)S(1)} %get-tuple-element.23.refs_1_.roots, bf16[8,128,640]{2,1,0:T(8,128)(2,1)S(1)} %get-tuple-element.17.refs_7_.own, bf16[8,128,640]{2,1,0:T(8,128)(2,1)S(1)} %collective-permute-done.9.far, ...), custom_call_target="tpu_custom_call" | custom-call | flops 1000 | bytes 1000 | tf_op jit(solution)/shard_map/pallas_call | solution.py:181
  58.4 5.0 %collective-permute-start.14 = (f16[2,8,32,128]{3,2,1,0:T(8,128)(2,1)S(1)}, f16[2,8,32,128]{3,2,1,0:T(8,128)(2,1)S(1)}, u32[]{:S(2)}, u32[]{:S(2)}) collective-permute-start(f16[2,8,32,128]{3,2,1,0:T(8,128)(2,1)S(1)} %get-tuple-element.29), channel_id=1, source_target_pairs={{4,7},{5,6},{6,5},{7,4},{12,15},{13,14},{14,13},{15,12},{20,23},{2... | collective-permute-start | bytes 393224 | tf_op jit(solution)/shard_map/ppermute | solution.py:266
  63.4 1.9 %collective-permute-start.15 = (f16[2,8,32,128]{3,2,1,0:T(8,128)(2,1)S(1)}, f16[2,8,32,128]{3,2,1,0:T(8,128)(2,1)S(1)}, u32[]{:S(2)}, u32[]{:S(2)}) collective-permute-start(f16[2,8,32,128]{3,2,1,0:T(8,128)(2,1)S(1)} %get-tuple-element.31), channel_id=1, source_target_pairs={{4,6},{5,7},{6,4},{7,5},{12,14},{13,15},{14,12},{15,13},{20,22},{2... | collective-permute-start | bytes 393224 | tf_op jit(solution)/shard_map/ppermute | solution.py:266
  65.3 2.4 %collective-permute-start.16 = (f16[2,8,32,128]{3,2,1,0:T(8,128)(2,1)S(1)}, f16[2,8,32,128]{3,2,1,0:T(8,128)(2,1)S(1)}, u32[]{:S(2)}, u32[]{:S(2)}) collective-permute-start(f16[2,8,32,128]{3,2,1,0:T(8,128)(2,1)S(1)} %get-tuple-element.30), channel_id=1, source_target_pairs={{4,5},{5,4},{6,7},{7,6},{12,13},{13,12},{14,15},{15,14},{20,21},{2... | collective-permute-start | bytes 393224 | tf_op jit(solution)/shard_map/ppermute | solution.py:266
  67.8 2.7 %collective-permute-done.15 = f16[2,8,32,128]{3,2,1,0:T(8,128)(2,1)S(1)} collective-permute-done((f16[2,8,32,128]{3,2,1,0:T(8,128)(2,1)S(1)}, f16[2,8,32,128]{3,2,1,0:T(8,128)(2,1)S(1)}, u32[]{:S(2)}, u32[]{:S(2)}) %collective-permute-start.15) | collective-permute-done | bytes 131104 | tf_op jit(solution)/shard_map/ppermute | solution.py:266
  70.5 1.3 %collective-permute-done.16 = f16[2,8,32,128]{3,2,1,0:T(8,128)(2,1)S(1)} collective-permute-done((f16[2,8,32,128]{3,2,1,0:T(8,128)(2,1)S(1)}, f16[2,8,32,128]{3,2,1,0:T(8,128)(2,1)S(1)}, u32[]{:S(2)}, u32[]{:S(2)}) %collective-permute-start.16) | collective-permute-done | bytes 131104 | tf_op jit(solution)/shard_map/ppermute | solution.py:266
  71.9 0.9 %maximum_bitcast_fusion = f32[2,8,1,32,384]{4,3,2,1,0:T(8,128)} fusion(f32[2,8,32,128]{3,2,1,0:T(8,128)S(1)} %fusion.7, f32[2,8,32,128]{3,2,1,0:T(8,128)S(1)} %bitcast_select_fusion, f32[2,8,32,128]{3,2,1,0:T(8,128)S(1)} %add_bitcast_fusion), kind=kLoop, calls=%fused_computation.2 | loop fusion | flops 393216 | bytes 1572864 | tf_op jit(solution)/shard_map/broadcast_in_dim | solution.py:308
  (48 shorter events, 2.0 us)
Async XLA Ops:
  0.0 2.1 %copy-start = (bf16[1,1,8,3,1,128,640]{6,5,4,3,2,1,0:T(8,128)(2,1)S(1)}, bf16[1,1,8,3,1,128,640]{6,5,4,3,2,1,0:T(8,128)(2,1)}, u32[]{:S(2)}) copy-start(bf16[1,1,8,3,1,128,640]{6,5,4,3,2,1,0:T(8,128)(2,1)} %param.6) | copy-start | bytes 11796484
  2.1 9.4 %copy-start.6 = (s32[1,1,8,3,1]{2,4,3,1,0:T(1,128)S(1)}, s32[1,1,8,3,1]{2,4,3,1,0:T(1,128)}, u32[]{:S(2)}) copy-start(s32[1,1,8,3,1]{2,4,3,1,0:T(1,128)} %param.7) | copy-start | bytes 292
  4.1 1.1 %copy-start.1 = (bf16[8,128,640]{2,1,0:T(8,128)(2,1)}, bf16[8,128,640]{2,1,0:T(8,128)(2,1)S(1)}, u32[]{:S(2)}) copy-start(bf16[8,128,640]{2,1,0:T(8,128)(2,1)S(1)} %get-tuple-element.24.refs_0_) | copy-start | bytes 3932164
  5.2 11.7 %copy-start.3 = (f32[10240]{0:T(1024)S(1)}, f32[10240]{0:T(1024)}, u32[]{:S(2)}) copy-start(f32[10240]{0:T(1024)} %param.10) | copy-start | bytes 122884
  5.2 11.7 %copy-start.4 = (f32[8]{0:T(128)S(1)}, f32[8]{0:T(128)}, u32[]{:S(2)}) copy-start(f32[8]{0:T(128)} %refs_4_.1) | copy-start | bytes 100
  5.2 11.7 %copy-start.5 = (f32[2]{0:T(128)S(1)}, f32[2]{0:T(128)}, u32[]{:S(2)}) copy-start(f32[2]{0:T(128)} %refs_5_.1) | copy-start | bytes 28
  5.2 11.7 %collective-permute-start.3 = (bf16[16,128,640]{2,1,0:T(8,128)(2,1)}, bf16[16,128,640]{2,1,0:T(8,128)(2,1)}, u32[]{:S(2)}, u32[]{:S(2)}) collective-permute-start(bf16[16,128,640]{2,1,0:T(8,128)(2,1)} %get-tuple-element.18.refs_8_), channel_id=1, source_target_pairs={{4,0},{12,8},{5,1},{13,9},{6,2},{14,10},{7,3},{15,11},{20,16},{28,... | collective-permute-start | bytes 7864328 | tf_op jit(solution)/shard_map/ppermute | solution.py:293
  8.8 6.9 %collective-permute-start.4 = (bf16[1,128,640]{2,1,0:T(8,128)(2,1)S(1)}, bf16[1,128,640]{2,1,0:T(8,128)(2,1)S(1)}, u32[]{:S(2)}, u32[]{:S(2)}) collective-permute-start(bf16[1,128,640]{2,1,0:T(8,128)(2,1)S(1)} %get-tuple-element.20), channel_id=1, source_target_pairs={{0,8},{4,12},{8,0},{12,4},{1,9},{5,13},{9,1},{13,5},{2,10},{6,14},... | collective-permute-start | bytes 491528 | tf_op jit(solution)/shard_map/ppermute | solution.py:290
  12.4 1.5 %collective-permute-start = (s32[25]{0:T(128)S(1)}, s32[25]{0:T(128)S(1)}, u32[]{:S(2)}, u32[]{:S(2)}) collective-permute-start(s32[25]{0:T(128)S(1)} %pad_add_fusion.refs_0_), channel_id=1, source_target_pairs={{0,4},{4,8},{8,12},{12,0},{1,5},{5,9},{9,13},{13,1},{2,6},{6,10},{... | collective-permute-start | bytes 308 | tf_op jit(solution)/shard_map/ppermute | solution.py:281
  12.4 2.5 %collective-permute-start.1 = (s32[25]{0:T(128)S(1)}, s32[25]{0:T(128)S(1)}, u32[]{:S(2)}, u32[]{:S(2)}) collective-permute-start(s32[25]{0:T(128)S(1)} %pad_add_fusion.refs_0_), channel_id=1, source_target_pairs={{0,8},{4,12},{8,0},{12,4},{1,9},{5,13},{9,1},{13,5},{2,10},{6,14},... | collective-permute-start | bytes 308 | tf_op jit(solution)/shard_map/ppermute | solution.py:281
  12.5 3.3 %collective-permute-start.2 = (s32[25]{0:T(128)S(1)}, s32[25]{0:T(128)S(1)}, u32[]{:S(2)}, u32[]{:S(2)}) collective-permute-start(s32[25]{0:T(128)S(1)} %pad_add_fusion.refs_0_), channel_id=1, source_target_pairs={{0,12},{4,0},{8,4},{12,8},{1,13},{5,1},{9,5},{13,9},{2,14},{6,2},{... | collective-permute-start | bytes 308 | tf_op jit(solution)/shard_map/ppermute | solution.py:281
  15.8 26.1 %collective-permute-start.10 = (bf16[7,128,640]{2,1,0:T(8,128)(2,1)S(1)}, bf16[7,128,640]{2,1,0:T(8,128)(2,1)S(1)}, u32[]{:S(2)}, u32[]{:S(2)}) collective-permute-start(bf16[7,128,640]{2,1,0:T(8,128)(2,1)S(1)} %shard_map.65.refs_10_), channel_id=1, source_target_pairs={{0,8},{4,12},{8,0},{12,4},{1,9},{5,13},{9,1},{13,5},{2,10},{6,14},... | collective-permute-start | bytes 3440648 | tf_op jit(solution)/shard_map/ppermute | solution.py:292
  24.5 8.1 %collective-permute-start.5 = (f16[2,8,2,32,128]{4,3,1,0,2:T(8,128)(2,1)S(1)}, f16[2,8,2,32,128]{4,3,1,0,2:T(8,128)(2,1)S(1)}, u32[]{:S(2)}, u32[]{:S(2)}) collective-permute-start(f16[2,8,2,32,128]{4,3,1,0,2:T(8,128)(2,1)S(1)} %fusion.3), channel_id=1, source_target_pairs={{0,1},{1,0},{2,3},{3,2},{4,5},{5,4},{6,7},{7,6},{8,9},{9,8},{10,11... | collective-permute-start | bytes 786440 | tf_op jit(solution)/shard_map/ppermute | solution.py:238
  25.9 1.3 %copy-start.2 = (bf16[8,128,640]{2,1,0:T(8,128)(2,1)S(1)}, bf16[8,128,640]{2,1,0:T(8,128)(2,1)}, u32[]{:S(2)}) copy-start(bf16[8,128,640]{2,1,0:T(8,128)(2,1)} %copy-done.1) | copy-start | bytes 3932164
  26.0 8.8 %collective-permute-start.7 = (f16[2,8,2,32,128]{4,3,1,0,2:T(8,128)(2,1)S(1)}, f16[2,8,2,32,128]{4,3,1,0,2:T(8,128)(2,1)S(1)}, u32[]{:S(2)}, u32[]{:S(2)}) collective-permute-start(f16[2,8,2,32,128]{4,3,1,0,2:T(8,128)(2,1)S(1)} %fusion.4), channel_id=1, source_target_pairs={{0,1},{1,0},{2,3},{3,2},{8,9},{9,8},{10,11},{11,10},{16,17},{17,16... | collective-permute-start | bytes 786440 | tf_op jit(solution)/shard_map/ppermute | solution.py:238
  27.2 29.9 %collective-permute-start.9 = (bf16[8,128,640]{2,1,0:T(8,128)(2,1)S(1)}, bf16[8,128,640]{2,1,0:T(8,128)(2,1)S(1)}, u32[]{:S(2)}, u32[]{:S(2)}) collective-permute-start(bf16[8,128,640]{2,1,0:T(8,128)(2,1)S(1)} %shard_map.67), channel_id=1, source_target_pairs={{0,12},{8,4},{1,13},{9,5},{2,14},{10,6},{3,15},{11,7},{16,28},{24,... | collective-permute-start | bytes 3932168 | tf_op jit(solution)/shard_map/ppermute | solution.py:296
  32.7 8.3 %collective-permute-start.6 = (f16[2,8,1,32,128]{4,3,1,0,2:T(8,128)(2,1)S(1)}, f16[2,8,1,32,128]{4,3,1,0,2:T(8,128)(2,1)S(1)}, u32[]{:S(2)}, u32[]{:S(2)}) collective-permute-start(f16[2,8,1,32,128]{4,3,1,0,2:T(8,128)(2,1)S(1)} %multiply_convert_fusion.6), channel_id=1, source_target_pairs={{0,2},{1,3},{2,0},{3,1},{4,6},{5,7},{6,4},{7,5},{8,10},{9,11},{10,... | collective-permute-start | bytes 393224 | tf_op jit(solution)/shard_map/ppermute | solution.py:238
  35.0 6.0 %collective-permute-start.8 = (f16[2,8,1,32,128]{4,3,1,0,2:T(8,128)(2,1)S(1)}, f16[2,8,1,32,128]{4,3,1,0,2:T(8,128)(2,1)S(1)}, u32[]{:S(2)}, u32[]{:S(2)}) collective-permute-start(f16[2,8,1,32,128]{4,3,1,0,2:T(8,128)(2,1)S(1)} %multiply_convert_fusion.5), channel_id=1, source_target_pairs={{0,2},{1,3},{2,0},{3,1},{8,10},{9,11},{10,8},{11,9},{16,18},{17,19... | collective-permute-start | bytes 393224 | tf_op jit(solution)/shard_map/ppermute | solution.py:238
  45.9 5.3 %collective-permute-start.12 = (f16[2,8,2,32,128]{4,3,1,0,2:T(8,128)(2,1)S(1)}, f16[2,8,2,32,128]{4,3,1,0,2:T(8,128)(2,1)S(1)}, u32[]{:S(2)}, u32[]{:S(2)}) collective-permute-start(f16[2,8,2,32,128]{4,3,1,0,2:T(8,128)(2,1)S(1)} %fusion.5), channel_id=1, source_target_pairs={{0,1},{1,0},{2,3},{3,2},{4,5},{5,4},{6,7},{7,6},{8,9},{9,8},{10,11... | collective-permute-start | bytes 786440 | tf_op jit(solution)/shard_map/ppermute | solution.py:238
  47.3 6.3 %collective-permute-start.11 = (f16[2,8,128,128]{3,2,1,0:T(8,128)(2,1)S(1)}, f16[2,8,128,128]{3,2,1,0:T(8,128)(2,1)S(1)}, u32[]{:S(2)}, u32[]{:S(2)}) collective-permute-start(f16[2,8,128,128]{3,2,1,0:T(8,128)(2,1)S(1)} %multiply_convert_fusion), channel_id=1, source_target_pairs={{0,4},{8,12},{1,5},{9,13},{2,6},{10,14},{3,7},{11,15},{16,20},{24,... | collective-permute-start | bytes 1572872 | tf_op jit(solution)/shard_map/ppermute | solution.py:301
  51.3 7.0 %collective-permute-start.13 = (f16[2,8,1,32,128]{4,3,2,1,0:T(8,128)(2,1)S(1)}, f16[2,8,1,32,128]{4,3,2,1,0:T(8,128)(2,1)S(1)}, u32[]{:S(2)}, u32[]{:S(2)}) collective-permute-start(f16[2,8,1,32,128]{4,3,2,1,0:T(8,128)(2,1)S(1)} %fusion.8), channel_id=1, source_target_pairs={{0,2},{1,3},{2,0},{3,1},{4,6},{5,7},{6,4},{7,5},{8,10},{9,11},{10,... | collective-permute-start | bytes 393224 | tf_op jit(solution)/shard_map/ppermute | solution.py:238
  58.4 9.3 %collective-permute-start.14 = (f16[2,8,32,128]{3,2,1,0:T(8,128)(2,1)S(1)}, f16[2,8,32,128]{3,2,1,0:T(8,128)(2,1)S(1)}, u32[]{:S(2)}, u32[]{:S(2)}) collective-permute-start(f16[2,8,32,128]{3,2,1,0:T(8,128)(2,1)S(1)} %get-tuple-element.29), channel_id=1, source_target_pairs={{4,7},{5,6},{6,5},{7,4},{12,15},{13,14},{14,13},{15,12},{20,23},{2... | collective-permute-start | bytes 393224 | tf_op jit(solution)/shard_map/ppermute | solution.py:266
  63.4 7.1 %collective-permute-start.15 = (f16[2,8,32,128]{3,2,1,0:T(8,128)(2,1)S(1)}, f16[2,8,32,128]{3,2,1,0:T(8,128)(2,1)S(1)}, u32[]{:S(2)}, u32[]{:S(2)}) collective-permute-start(f16[2,8,32,128]{3,2,1,0:T(8,128)(2,1)S(1)} %get-tuple-element.31), channel_id=1, source_target_pairs={{4,6},{5,7},{6,4},{7,5},{12,14},{13,15},{14,12},{15,13},{20,22},{2... | collective-permute-start | bytes 393224 | tf_op jit(solution)/shard_map/ppermute | solution.py:266
  65.3 6.5 %collective-permute-start.16 = (f16[2,8,32,128]{3,2,1,0:T(8,128)(2,1)S(1)}, f16[2,8,32,128]{3,2,1,0:T(8,128)(2,1)S(1)}, u32[]{:S(2)}, u32[]{:S(2)}) collective-permute-start(f16[2,8,32,128]{3,2,1,0:T(8,128)(2,1)S(1)} %get-tuple-element.30), channel_id=1, source_target_pairs={{4,5},{5,4},{6,7},{7,6},{12,13},{13,12},{14,15},{15,14},{20,21},{2... | collective-permute-start | bytes 393224 | tf_op jit(solution)/shard_map/ppermute | solution.py:266

commit v15 on v14

--- a/solution.py
+++ b/solution.py
@@ -83,7 +83,7 @@
     records = refs[:n_aux]
     occ, freq, table = refs[n_aux : n_aux + 3]
     own, far = refs[n_aux + 3 : n_aux + 5], refs[n_aux + 5]
-    out, out_one, roots = refs[-3:]
+    out, out_one, roots, to_one = refs[-4:]
     pair_rows = own[0].shape[-1]
     virt_blocks = table.shape[1] // pair_rows
     aux_pos, pair_col = lax.axis_index("aux"), lax.axis_index("pair")
@@ -93,6 +93,9 @@
         for k in range(1, n_aux):
             live = jnp.where(lax.rem(aux_pos - region + n_aux, n_aux) == k, records[k][blocks_dev * band], live)
         return live
+
+    for m in range(blocks_dev):
+        to_one[m] = own[1][jnp.minimum(m + (aux_pos < 1).astype(jnp.int32), blocks_dev - 1)]
 
     masked, plain, one = {}, {}, {}
     for m in range(blocks_dev):
@@ -154,9 +157,10 @@
             jax.ShapeDtypeStruct((freq_count, blocks_dev, aux_rows, aux_rows), jnp.float32),
             jax.ShapeDtypeStruct((freq_count, blocks_dev, aux_rows, aux_rows), jnp.float32),
             jax.ShapeDtypeStruct((blocks_dev, root_rows(band, freq_count), pair_rows), jnp.float32),
+            jax.ShapeDtypeStruct(own[0].shape, own[0].dtype),
         ],
         in_specs=[SMEM] * (n_aux + 2) + [VMEM] * 4 + [ANY] * len(after),
-        out_specs=[VMEM, VMEM, VMEM],
+        out_specs=[VMEM] * 4,
         compiler_params=PARAMS,
         cost_estimate=COST,
     )(*records, occ, freq, table, *own, far, *after)
@@ -283,8 +287,8 @@
     two = chunks_of(blocks_dev, SPLIT)
     whole = list(range(n_aux))
     evens, odds = whole[::2], whole[1::2]
-    plan = [(2, 2, first, count) for first, count in two] + [(1, 1, 0, blocks_dev)]
-    first_slot, rest, near_two, far_two, to_one = pack(tiles, plan)
+    plan = [(2, 2, first, count) for first, count in two]
+    first_slot, rest, near_two, far_two = pack(tiles, plan)
     own = (first_slot, rest)
     down2 = [(s, (s - 2) % n_aux) for s in whole]
     c2 = [lax.ppermute(near_two, "aux", down2)]
@@ -292,8 +296,8 @@
     c2.append(lax.ppermute(far_two, "aux", down2))
     to_even = lax.ppermute(rest, "aux", [(s, s - 1) for s in odds])
     table = virt_energy.reshape(1, -1)
-    rows0, rows_even, roots = first_rows(dims, records, occ_energy, frequencies, table, own, to_even, [far_two])
-    b1 = lax.ppermute(tie([to_one], [roots])[0], "aux", [(s, (s - 1) % n_aux) for s in evens])
+    rows0, rows_even, roots, to_one = first_rows(dims, records, occ_energy, frequencies, table, own, to_even, [far_two])
+    b1 = lax.ppermute(to_one, "aux", [(s, (s - 1) % n_aux) for s in evens])
     bits0, z0 = totals(rows0, pair_col, n_pair, whole, scale)
     bits_even, z_even = totals(rows_even, pair_col, n_pair, evens, scale)
     rows2, rows_next = second_rows(dims, roots, own, to_even, c2, [bits_even[-1], bits0[-1]])

time: 73.2 us -> 72.1 us (0.985)
  local copies, waits for them, and re-layouts: 3.96 us -> 2.56 us
    unnamed x15 -> x11, local copies, waits for them, and re-layouts: 3.61 us -> 2.21 us
where the time goes in v15:
time: 72.1 us; the launch traced here: 71.7 us
  starting transfers between devices  28.5 us (40%)
  waiting for transfers between devices  23.1 us (32%)
  Pallas kernels  14.5 us (20%)
  local copies, waits for them, and re-layouts  2.56 us (4%)
  other arithmetic  2.11 us (3%)
  between operations  0.94 us (1%)
    ppermute x6, waiting for transfers between devices, halve(): got = lax.ppermute(sent, ('aux', 'pair'), pairs)  12.4 us
    ppermute x3, starting transfers between devices, total_at_once(): far.append(lax.ppermute(sent, ('aux', 'pair'), pairs).astype(jnp.float32))  9.27 us
    ppermute x6, starting transfers between devices, halve(): got = lax.ppermute(sent, ('aux', 'pair'), pairs)  8.43 us
    pallas_call x1, Pallas kernels, first_rows(): pl.pallas_call(functools.partial(first_kernel, dims), out_shape=[jax.Shap...  7.51 us
    ppermute x3, waiting for transfers between devices, total_at_once(): far.append(lax.ppermute(sent, ('aux', 'pair'), pairs).astype(jnp.float32))  4 us
    pallas_call x1, Pallas kernels, second_rows(): pl.pallas_call(functools.partial(second_kernel, dims, pieces), out_shape=...  3.82 us
    ppermute x1, starting transfers between devices, on_device(): to_even = lax.ppermute(rest, 'aux', [(s, s - 1) for s in odds])  3.63 us
    ppermute x1, waiting for transfers between devices, on_device(): b1 = lax.ppermute(to_one, 'aux', [(s, (s - 1) % n_aux) for s in evens])  3.36 us
  transfers between devices with their start and end apart: 17, of which 10 were waited for; matrix products, arithmetic and copies ran while one was open for 2% of the time, Pallas kernels for 17%

profile of v15, /device:TPU:1, one launch (start us, length us, event | category | flops | bytes accessed | tf_op | source)
XLA Modules:
  0.0 71.7 jit_solution(12524363803901454141)
XLA Ops:
  0.0 2.1 %copy-done = bf16[1,1,8,3,1,128,640]{6,5,4,3,2,1,0:T(8,128)(2,1)S(1)} copy-done((bf16[1,1,8,3,1,128,640]{6,5,4,3,2,1,0:T(8,128)(2,1)S(1)}, bf16[1,1,8,3,1,128,640]{6,5,4,3,2,1,0:T(8,128)(2,1)}, u32[]{:S(2)}) %copy-start) | copy-done | bytes 3932184
  2.1 1.9 %shard_map.64 = (bf16[8,128,640]{2,1,0:T(8,128)(2,1)S(1)}, bf16[16,128,640]{2,1,0:T(8,128)(2,1)}, bf16[1,128,640]{2,1,0:T(8,128)(2,1)S(1)}, bf16[7,128,640]{2,1,0:T(8,128)(2,1)S(1)}) custom-call(bf16[8,3,128,640]{3,2,1,0:T(8,128)(2,1)S(1)} %bitcast.58), custom_call_target="tpu_custom_call" | custom-call | flops 1000 | bytes 1000 | tf_op jit(solution)/shard_map/pallas_call | solution.py:46
  4.0 3.6 %collective-permute-start.3 = (bf16[16,128,640]{2,1,0:T(8,128)(2,1)}, bf16[16,128,640]{2,1,0:T(8,128)(2,1)}, u32[]{:S(2)}, u32[]{:S(2)}) collective-permute-start(bf16[16,128,640]{2,1,0:T(8,128)(2,1)} %get-tuple-element.18.refs_8_), channel_id=1, source_target_pairs={{4,0},{12,8},{5,1},{13,9},{6,2},{14,10},{7,3},{15,11},{20,16},{28,... | collective-permute-start | bytes 7864328 | tf_op jit(solution)/shard_map/ppermute | solution.py:297
  7.7 2.7 %collective-permute-start.4 = (bf16[1,128,640]{2,1,0:T(8,128)(2,1)S(1)}, bf16[1,128,640]{2,1,0:T(8,128)(2,1)S(1)}, u32[]{:S(2)}, u32[]{:S(2)}) collective-permute-start(bf16[1,128,640]{2,1,0:T(8,128)(2,1)S(1)} %get-tuple-element.20), channel_id=1, source_target_pairs={{0,8},{4,12},{8,0},{12,4},{1,9},{5,13},{9,1},{13,5},{2,10},{6,14},... | collective-permute-start | bytes 491528 | tf_op jit(solution)/shard_map/ppermute | solution.py:294
  11.3 0.7 collective-permute-start.2
  12.0 0.7 %collective-permute-done.refs_1_ = s32[25]{0:T(128)S(1)} collective-permute-done((s32[25]{0:T(128)S(1)}, s32[25]{0:T(128)S(1)}, u32[]{:S(2)}, u32[]{:S(2)}) %collective-permute-start) | collective-permute-done | bytes 132 | tf_op jit(solution)/shard_map/ppermute | solution.py:285
  12.8 0.9 %collective-permute-done.1.refs_2_ = s32[25]{0:T(128)S(1)} collective-permute-done((s32[25]{0:T(128)S(1)}, s32[25]{0:T(128)S(1)}, u32[]{:S(2)}, u32[]{:S(2)}) %collective-permute-start.1) | collective-permute-done | bytes 132 | tf_op jit(solution)/shard_map/ppermute | solution.py:285
  13.7 0.9 %collective-permute-done.2.refs_3_ = s32[25]{0:T(128)S(1)} collective-permute-done((s32[25]{0:T(128)S(1)}, s32[25]{0:T(128)S(1)}, u32[]{:S(2)}, u32[]{:S(2)}) %collective-permute-start.2) | collective-permute-done | bytes 132 | tf_op jit(solution)/shard_map/ppermute | solution.py:285
  14.6 1.1 %collective-permute-start.10 = (bf16[7,128,640]{2,1,0:T(8,128)(2,1)S(1)}, bf16[7,128,640]{2,1,0:T(8,128)(2,1)S(1)}, u32[]{:S(2)}, u32[]{:S(2)}) collective-permute-start(bf16[7,128,640]{2,1,0:T(8,128)(2,1)S(1)} %shard_map.65.refs_10_), channel_id=1, source_target_pairs={{0,8},{4,12},{8,0},{12,4},{1,9},{5,13},{9,1},{13,5},{2,10},{6,14},... | collective-permute-start | bytes 3440648 | tf_op jit(solution)/shard_map/ppermute | solution.py:296
  15.8 7.5 %shard_map.66 = (f32[2,8,128,128]{3,2,1,0:T(8,128)S(1)}, f32[2,8,128,128]{3,2,1,0:T(8,128)S(1)}, f32[8,16,640]{2,1,0:T(8,128)S(1)}, bf16[8,128,640]{2,1,0:T(8,128)(2,1)S(1)}) custom-call(s32[25]{0:T(128)S(1)} %pad_add_fusion.refs_0_, s32[25]{0:T(128)S(1)} %collective-permute-done.refs_1_, s32[25]{0:T(128)S(1)} %collective-permute-done.1.refs_2_, ...), custom_call_target="tpu_custom_call" | custom-call | flops 1000 | bytes 1000 | tf_op jit(solution)/shard_map/pallas_call | solution.py:154
  23.5 1.4 %collective-permute-start.5 = (f16[2,8,2,32,128]{4,3,1,0,2:T(8,128)(2,1)S(1)}, f16[2,8,2,32,128]{4,3,1,0,2:T(8,128)(2,1)S(1)}, u32[]{:S(2)}, u32[]{:S(2)}) collective-permute-start(f16[2,8,2,32,128]{4,3,1,0,2:T(8,128)(2,1)S(1)} %fusion.3), channel_id=1, source_target_pairs={{0,1},{1,0},{2,3},{3,2},{4,5},{5,4},{6,7},{7,6},{8,9},{9,8},{10,11... | collective-permute-start | bytes 786440 | tf_op jit(solution)/shard_map/ppermute | solution.py:242
  25.0 0.7 collective-permute-start.7
  25.7 1.3 %collective-permute-start.9 = (bf16[8,128,640]{2,1,0:T(8,128)(2,1)S(1)}, bf16[8,128,640]{2,1,0:T(8,128)(2,1)S(1)}, u32[]{:S(2)}, u32[]{:S(2)}) collective-permute-start(bf16[8,128,640]{2,1,0:T(8,128)(2,1)S(1)} %get-tuple-element.24), channel_id=1, source_target_pairs={{0,12},{8,4},{1,13},{9,5},{2,14},{10,6},{3,15},{11,7},{16,28},{24,... | collective-permute-start | bytes 3932168 | tf_op jit(solution)/shard_map/ppermute | solution.py:300
  27.0 4.6 %collective-permute-done.5 = f16[2,8,2,32,128]{4,3,1,0,2:T(8,128)(2,1)S(1)} collective-permute-done((f16[2,8,2,32,128]{4,3,1,0,2:T(8,128)(2,1)S(1)}, f16[2,8,2,32,128]{4,3,1,0,2:T(8,128)(2,1)S(1)}, u32[]{:S(2)}, u32[]{:S(2)}) %collective-permute-start.5) | collective-permute-done | bytes 262176 | tf_op jit(solution)/shard_map/ppermute | solution.py:242
  31.7 2.1 %collective-permute-start.6 = (f16[2,8,1,32,128]{4,3,1,0,2:T(8,128)(2,1)S(1)}, f16[2,8,1,32,128]{4,3,1,0,2:T(8,128)(2,1)S(1)}, u32[]{:S(2)}, u32[]{:S(2)}) collective-permute-start(f16[2,8,1,32,128]{4,3,1,0,2:T(8,128)(2,1)S(1)} %multiply_convert_fusion.6), channel_id=1, source_target_pairs={{0,2},{1,3},{2,0},{3,1},{4,6},{5,7},{6,4},{7,5},{8,10},{9,11},{10,... | collective-permute-start | bytes 393224 | tf_op jit(solution)/shard_map/ppermute | solution.py:242
  33.9 0.7 collective-permute-start.8
  34.6 5.3 %collective-permute-done.6 = f16[2,8,1,32,128]{4,3,1,0,2:T(8,128)(2,1)S(1)} collective-permute-done((f16[2,8,1,32,128]{4,3,1,0,2:T(8,128)(2,1)S(1)}, f16[2,8,1,32,128]{4,3,1,0,2:T(8,128)(2,1)S(1)}, u32[]{:S(2)}, u32[]{:S(2)}) %collective-permute-start.6) | collective-permute-done | bytes 131104 | tf_op jit(solution)/shard_map/ppermute | solution.py:242
  40.0 0.8 %collective-permute-done.10.refs_1_ = bf16[7,128,640]{2,1,0:T(8,128)(2,1)S(1)} collective-permute-done((bf16[7,128,640]{2,1,0:T(8,128)(2,1)S(1)}, bf16[7,128,640]{2,1,0:T(8,128)(2,1)S(1)}, u32[]{:S(2)}, u32[]{:S(2)}) %collective-permute-start.10) | collective-permute-done | bytes 1146912 | tf_op jit(solution)/shard_map/ppermute | solution.py:296
  40.7 3.8 %shard_map.67 = (f32[2,8,128,128]{3,2,1,0:T(8,128)S(1)}, f32[2,8,128,128]{3,2,1,0:T(8,128)S(1)}) custom-call(f32[8,16,640]{2,1,0:T(8,128)S(1)} %get-tuple-element.23.roots, bf16[8,128,640]{2,1,0:T(8,128)(2,1)S(1)} %get-tuple-element.17.refs_7_.own, bf16[16,128,640]{2,1,0:T(8,128)(2,1)} %collective-permute-done.3.refs_9_.lower, ...), custom_call_target="tpu_custom_call" | custom-call | flops 1000 | bytes 1000 | tf_op jit(solution)/shard_map/pallas_call | solution.py:219
  44.7 1.3 %collective-permute-start.12 = (f16[2,8,2,32,128]{4,3,1,0,2:T(8,128)(2,1)S(1)}, f16[2,8,2,32,128]{4,3,1,0,2:T(8,128)(2,1)S(1)}, u32[]{:S(2)}, u32[]{:S(2)}) collective-permute-start(f16[2,8,2,32,128]{4,3,1,0,2:T(8,128)(2,1)S(1)} %fusion.5), channel_id=1, source_target_pairs={{0,1},{1,0},{2,3},{3,2},{4,5},{5,4},{6,7},{7,6},{8,9},{9,8},{10,11... | collective-permute-start | bytes 786440 | tf_op jit(solution)/shard_map/ppermute | solution.py:242
  46.0 0.1 multiply_convert_fusion
  46.2 1.3 %collective-permute-start.11 = (f16[2,8,128,128]{3,2,1,0:T(8,128)(2,1)S(1)}, f16[2,8,128,128]{3,2,1,0:T(8,128)(2,1)S(1)}, u32[]{:S(2)}, u32[]{:S(2)}) collective-permute-start(f16[2,8,128,128]{3,2,1,0:T(8,128)(2,1)S(1)} %multiply_convert_fusion), channel_id=1, source_target_pairs={{0,4},{8,12},{1,5},{9,13},{2,6},{10,14},{3,7},{11,15},{16,20},{24,... | collective-permute-start | bytes 1572872 | tf_op jit(solution)/shard_map/ppermute | solution.py:305
  47.5 2.5 %collective-permute-done.12 = f16[2,8,2,32,128]{4,3,1,0,2:T(8,128)(2,1)S(1)} collective-permute-done((f16[2,8,2,32,128]{4,3,1,0,2:T(8,128)(2,1)S(1)}, f16[2,8,2,32,128]{4,3,1,0,2:T(8,128)(2,1)S(1)}, u32[]{:S(2)}, u32[]{:S(2)}) %collective-permute-start.12) | collective-permute-done | bytes 262176 | tf_op jit(solution)/shard_map/ppermute | solution.py:242
  50.1 2.3 %collective-permute-start.13 = (f16[2,8,1,32,128]{4,3,2,1,0:T(8,128)(2,1)S(1)}, f16[2,8,1,32,128]{4,3,2,1,0:T(8,128)(2,1)S(1)}, u32[]{:S(2)}, u32[]{:S(2)}) collective-permute-start(f16[2,8,1,32,128]{4,3,2,1,0:T(8,128)(2,1)S(1)} %fusion.8), channel_id=1, source_target_pairs={{0,2},{1,3},{2,0},{3,1},{4,6},{5,7},{6,4},{7,5},{8,10},{9,11},{10,... | collective-permute-start | bytes 393224 | tf_op jit(solution)/shard_map/ppermute | solution.py:242
  52.6 3.4 %collective-permute-done.9.far = bf16[8,128,640]{2,1,0:T(8,128)(2,1)S(1)} collective-permute-done((bf16[8,128,640]{2,1,0:T(8,128)(2,1)S(1)}, bf16[8,128,640]{2,1,0:T(8,128)(2,1)S(1)}, u32[]{:S(2)}, u32[]{:S(2)}) %collective-permute-start.9) | collective-permute-done | bytes 1310752 | tf_op jit(solution)/shard_map/ppermute | solution.py:300
  55.9 1.2 %shard_map.68 = (f32[2,8,128,128]{3,2,1,0:T(8,128)S(1)}, f32[32,128]{1,0:T(8,128)S(1)}) custom-call(f32[8,16,640]{2,1,0:T(8,128)S(1)} %get-tuple-element.23.roots, bf16[8,128,640]{2,1,0:T(8,128)(2,1)S(1)} %get-tuple-element.17.refs_7_.own, bf16[8,128,640]{2,1,0:T(8,128)(2,1)S(1)} %collective-permute-done.9.far, f32[2,8,128,128]{3,2,1,0:T(8,128)S(1)} %convert_multiply_fusion.add), custom_call_target="tpu_custom_call" | custom-call | flops 1000 | bytes 1000 | tf_op jit(solution)/shard_map/pallas_call | solution.py:185
  57.3 4.9 %collective-permute-start.14 = (f16[2,8,32,128]{3,2,1,0:T(8,128)(2,1)S(1)}, f16[2,8,32,128]{3,2,1,0:T(8,128)(2,1)S(1)}, u32[]{:S(2)}, u32[]{:S(2)}) collective-permute-start(f16[2,8,32,128]{3,2,1,0:T(8,128)(2,1)S(1)} %get-tuple-element.29), channel_id=1, source_target_pairs={{4,7},{5,6},{6,5},{7,4},{12,15},{13,14},{14,13},{15,12},{20,23},{2... | collective-permute-start | bytes 393224 | tf_op jit(solution)/shard_map/ppermute | solution.py:270
  62.2 1.9 %collective-permute-start.15 = (f16[2,8,32,128]{3,2,1,0:T(8,128)(2,1)S(1)}, f16[2,8,32,128]{3,2,1,0:T(8,128)(2,1)S(1)}, u32[]{:S(2)}, u32[]{:S(2)}) collective-permute-start(f16[2,8,32,128]{3,2,1,0:T(8,128)(2,1)S(1)} %get-tuple-element.31), channel_id=1, source_target_pairs={{4,6},{5,7},{6,4},{7,5},{12,14},{13,15},{14,12},{15,13},{20,22},{2... | collective-permute-start | bytes 393224 | tf_op jit(solution)/shard_map/ppermute | solution.py:270
  64.2 2.4 %collective-permute-start.16 = (f16[2,8,32,128]{3,2,1,0:T(8,128)(2,1)S(1)}, f16[2,8,32,128]{3,2,1,0:T(8,128)(2,1)S(1)}, u32[]{:S(2)}, u32[]{:S(2)}) collective-permute-start(f16[2,8,32,128]{3,2,1,0:T(8,128)(2,1)S(1)} %get-tuple-element.30), channel_id=1, source_target_pairs={{4,5},{5,4},{6,7},{7,6},{12,13},{13,12},{14,15},{15,14},{20,21},{2... | collective-permute-start | bytes 393224 | tf_op jit(solution)/shard_map/ppermute | solution.py:270
  66.7 2.7 %collective-permute-done.15 = f16[2,8,32,128]{3,2,1,0:T(8,128)(2,1)S(1)} collective-permute-done((f16[2,8,32,128]{3,2,1,0:T(8,128)(2,1)S(1)}, f16[2,8,32,128]{3,2,1,0:T(8,128)(2,1)S(1)}, u32[]{:S(2)}, u32[]{:S(2)}) %collective-permute-start.15) | collective-permute-done | bytes 131104 | tf_op jit(solution)/shard_map/ppermute | solution.py:270
  69.3 1.3 %collective-permute-done.16 = f16[2,8,32,128]{3,2,1,0:T(8,128)(2,1)S(1)} collective-permute-done((f16[2,8,32,128]{3,2,1,0:T(8,128)(2,1)S(1)}, f16[2,8,32,128]{3,2,1,0:T(8,128)(2,1)S(1)}, u32[]{:S(2)}, u32[]{:S(2)}) %collective-permute-start.16) | collective-permute-done | bytes 131104 | tf_op jit(solution)/shard_map/ppermute | solution.py:270
  70.8 0.9 %maximum_bitcast_fusion = f32[2,8,1,32,384]{4,3,2,1,0:T(8,128)} fusion(f32[2,8,32,128]{3,2,1,0:T(8,128)S(1)} %fusion.7, f32[2,8,32,128]{3,2,1,0:T(8,128)S(1)} %bitcast_select_fusion, f32[2,8,32,128]{3,2,1,0:T(8,128)S(1)} %add_bitcast_fusion), kind=kLoop, calls=%fused_computation.2 | loop fusion | flops 393216 | bytes 1572864 | tf_op jit(solution)/shard_map/broadcast_in_dim | solution.py:312
  (43 shorter events, 1.6 us)
Async XLA Ops:
  0.0 2.1 %copy-start = (bf16[1,1,8,3,1,128,640]{6,5,4,3,2,1,0:T(8,128)(2,1)S(1)}, bf16[1,1,8,3,1,128,640]{6,5,4,3,2,1,0:T(8,128)(2,1)}, u32[]{:S(2)}) copy-start(bf16[1,1,8,3,1,128,640]{6,5,4,3,2,1,0:T(8,128)(2,1)} %param.6) | copy-start | bytes 11796484
  2.1 8.2 %copy-start.4 = (s32[1,1,8,3,1]{2,4,3,1,0:T(1,128)S(1)}, s32[1,1,8,3,1]{2,4,3,1,0:T(1,128)}, u32[]{:S(2)}) copy-start(s32[1,1,8,3,1]{2,4,3,1,0:T(1,128)} %param.7) | copy-start | bytes 292
  4.0 11.7 %copy-start.1 = (f32[10240]{0:T(1024)S(1)}, f32[10240]{0:T(1024)}, u32[]{:S(2)}) copy-start(f32[10240]{0:T(1024)} %param.10) | copy-start | bytes 122884
  4.0 11.7 %copy-start.2 = (f32[8]{0:T(128)S(1)}, f32[8]{0:T(128)}, u32[]{:S(2)}) copy-start(f32[8]{0:T(128)} %refs_4_.1) | copy-start | bytes 100
  4.0 11.7 %copy-start.3 = (f32[2]{0:T(128)S(1)}, f32[2]{0:T(128)}, u32[]{:S(2)}) copy-start(f32[2]{0:T(128)} %refs_5_.1) | copy-start | bytes 28
  4.0 11.7 %collective-permute-start.3 = (bf16[16,128,640]{2,1,0:T(8,128)(2,1)}, bf16[16,128,640]{2,1,0:T(8,128)(2,1)}, u32[]{:S(2)}, u32[]{:S(2)}) collective-permute-start(bf16[16,128,640]{2,1,0:T(8,128)(2,1)} %get-tuple-element.18.refs_8_), channel_id=1, source_target_pairs={{4,0},{12,8},{5,1},{13,9},{6,2},{14,10},{7,3},{15,11},{20,16},{28,... | collective-permute-start | bytes 7864328 | tf_op jit(solution)/shard_map/ppermute | solution.py:297
  7.7 6.9 %collective-permute-start.4 = (bf16[1,128,640]{2,1,0:T(8,128)(2,1)S(1)}, bf16[1,128,640]{2,1,0:T(8,128)(2,1)S(1)}, u32[]{:S(2)}, u32[]{:S(2)}) collective-permute-start(bf16[1,128,640]{2,1,0:T(8,128)(2,1)S(1)} %get-tuple-element.20), channel_id=1, source_target_pairs={{0,8},{4,12},{8,0},{12,4},{1,9},{5,13},{9,1},{13,5},{2,10},{6,14},... | collective-permute-start | bytes 491528 | tf_op jit(solution)/shard_map/ppermute | solution.py:294
  11.2 1.5 %collective-permute-start = (s32[25]{0:T(128)S(1)}, s32[25]{0:T(128)S(1)}, u32[]{:S(2)}, u32[]{:S(2)}) collective-permute-start(s32[25]{0:T(128)S(1)} %pad_add_fusion.refs_0_), channel_id=1, source_target_pairs={{0,4},{4,8},{8,12},{12,0},{1,5},{5,9},{9,13},{13,1},{2,6},{6,10},{... | collective-permute-start | bytes 308 | tf_op jit(solution)/shard_map/ppermute | solution.py:285
  11.2 2.5 %collective-permute-start.1 = (s32[25]{0:T(128)S(1)}, s32[25]{0:T(128)S(1)}, u32[]{:S(2)}, u32[]{:S(2)}) collective-permute-start(s32[25]{0:T(128)S(1)} %pad_add_fusion.refs_0_), channel_id=1, source_target_pairs={{0,8},{4,12},{8,0},{12,4},{1,9},{5,13},{9,1},{13,5},{2,10},{6,14},... | collective-permute-start | bytes 308 | tf_op jit(solution)/shard_map/ppermute | solution.py:285
  11.3 3.3 %collective-permute-start.2 = (s32[25]{0:T(128)S(1)}, s32[25]{0:T(128)S(1)}, u32[]{:S(2)}, u32[]{:S(2)}) collective-permute-start(s32[25]{0:T(128)S(1)} %pad_add_fusion.refs_0_), channel_id=1, source_target_pairs={{0,12},{4,0},{8,4},{12,8},{1,13},{5,1},{9,5},{13,9},{2,14},{6,2},{... | collective-permute-start | bytes 308 | tf_op jit(solution)/shard_map/ppermute | solution.py:285
  14.6 26.1 %collective-permute-start.10 = (bf16[7,128,640]{2,1,0:T(8,128)(2,1)S(1)}, bf16[7,128,640]{2,1,0:T(8,128)(2,1)S(1)}, u32[]{:S(2)}, u32[]{:S(2)}) collective-permute-start(bf16[7,128,640]{2,1,0:T(8,128)(2,1)S(1)} %shard_map.65.refs_10_), channel_id=1, source_target_pairs={{0,8},{4,12},{8,0},{12,4},{1,9},{5,13},{9,1},{13,5},{2,10},{6,14},... | collective-permute-start | bytes 3440648 | tf_op jit(solution)/shard_map/ppermute | solution.py:296
  23.5 8.1 %collective-permute-start.5 = (f16[2,8,2,32,128]{4,3,1,0,2:T(8,128)(2,1)S(1)}, f16[2,8,2,32,128]{4,3,1,0,2:T(8,128)(2,1)S(1)}, u32[]{:S(2)}, u32[]{:S(2)}) collective-permute-start(f16[2,8,2,32,128]{4,3,1,0,2:T(8,128)(2,1)S(1)} %fusion.3), channel_id=1, source_target_pairs={{0,1},{1,0},{2,3},{3,2},{4,5},{5,4},{6,7},{7,6},{8,9},{9,8},{10,11... | collective-permute-start | bytes 786440 | tf_op jit(solution)/shard_map/ppermute | solution.py:242
  25.0 8.8 %collective-permute-start.7 = (f16[2,8,2,32,128]{4,3,1,0,2:T(8,128)(2,1)S(1)}, f16[2,8,2,32,128]{4,3,1,0,2:T(8,128)(2,1)S(1)}, u32[]{:S(2)}, u32[]{:S(2)}) collective-permute-start(f16[2,8,2,32,128]{4,3,1,0,2:T(8,128)(2,1)S(1)} %fusion.4), channel_id=1, source_target_pairs={{0,1},{1,0},{2,3},{3,2},{8,9},{9,8},{10,11},{11,10},{16,17},{17,16... | collective-permute-start | bytes 786440 | tf_op jit(solution)/shard_map/ppermute | solution.py:242
  25.7 30.3 %collective-permute-start.9 = (bf16[8,128,640]{2,1,0:T(8,128)(2,1)S(1)}, bf16[8,128,640]{2,1,0:T(8,128)(2,1)S(1)}, u32[]{:S(2)}, u32[]{:S(2)}) collective-permute-start(bf16[8,128,640]{2,1,0:T(8,128)(2,1)S(1)} %get-tuple-element.24), channel_id=1, source_target_pairs={{0,12},{8,4},{1,13},{9,5},{2,14},{10,6},{3,15},{11,7},{16,28},{24,... | collective-permute-start | bytes 3932168 | tf_op jit(solution)/shard_map/ppermute | solution.py:300
  31.7 8.3 %collective-permute-start.6 = (f16[2,8,1,32,128]{4,3,1,0,2:T(8,128)(2,1)S(1)}, f16[2,8,1,32,128]{4,3,1,0,2:T(8,128)(2,1)S(1)}, u32[]{:S(2)}, u32[]{:S(2)}) collective-permute-start(f16[2,8,1,32,128]{4,3,1,0,2:T(8,128)(2,1)S(1)} %multiply_convert_fusion.6), channel_id=1, source_target_pairs={{0,2},{1,3},{2,0},{3,1},{4,6},{5,7},{6,4},{7,5},{8,10},{9,11},{10,... | collective-permute-start | bytes 393224 | tf_op jit(solution)/shard_map/ppermute | solution.py:242
  33.9 6.0 %collective-permute-start.8 = (f16[2,8,1,32,128]{4,3,1,0,2:T(8,128)(2,1)S(1)}, f16[2,8,1,32,128]{4,3,1,0,2:T(8,128)(2,1)S(1)}, u32[]{:S(2)}, u32[]{:S(2)}) collective-permute-start(f16[2,8,1,32,128]{4,3,1,0,2:T(8,128)(2,1)S(1)} %multiply_convert_fusion.5), channel_id=1, source_target_pairs={{0,2},{1,3},{2,0},{3,1},{8,10},{9,11},{10,8},{11,9},{16,18},{17,19... | collective-permute-start | bytes 393224 | tf_op jit(solution)/shard_map/ppermute | solution.py:242
  44.7 5.3 %collective-permute-start.12 = (f16[2,8,2,32,128]{4,3,1,0,2:T(8,128)(2,1)S(1)}, f16[2,8,2,32,128]{4,3,1,0,2:T(8,128)(2,1)S(1)}, u32[]{:S(2)}, u32[]{:S(2)}) collective-permute-start(f16[2,8,2,32,128]{4,3,1,0,2:T(8,128)(2,1)S(1)} %fusion.5), channel_id=1, source_target_pairs={{0,1},{1,0},{2,3},{3,2},{4,5},{5,4},{6,7},{7,6},{8,9},{9,8},{10,11... | collective-permute-start | bytes 786440 | tf_op jit(solution)/shard_map/ppermute | solution.py:242
  46.2 6.3 %collective-permute-start.11 = (f16[2,8,128,128]{3,2,1,0:T(8,128)(2,1)S(1)}, f16[2,8,128,128]{3,2,1,0:T(8,128)(2,1)S(1)}, u32[]{:S(2)}, u32[]{:S(2)}) collective-permute-start(f16[2,8,128,128]{3,2,1,0:T(8,128)(2,1)S(1)} %multiply_convert_fusion), channel_id=1, source_target_pairs={{0,4},{8,12},{1,5},{9,13},{2,6},{10,14},{3,7},{11,15},{16,20},{24,... | collective-permute-start | bytes 1572872 | tf_op jit(solution)/shard_map/ppermute | solution.py:305
  50.1 7.0 %collective-permute-start.13 = (f16[2,8,1,32,128]{4,3,2,1,0:T(8,128)(2,1)S(1)}, f16[2,8,1,32,128]{4,3,2,1,0:T(8,128)(2,1)S(1)}, u32[]{:S(2)}, u32[]{:S(2)}) collective-permute-start(f16[2,8,1,32,128]{4,3,2,1,0:T(8,128)(2,1)S(1)} %fusion.8), channel_id=1, source_target_pairs={{0,2},{1,3},{2,0},{3,1},{4,6},{5,7},{6,4},{7,5},{8,10},{9,11},{10,... | collective-permute-start | bytes 393224 | tf_op jit(solution)/shard_map/ppermute | solution.py:242
  57.3 9.3 %collective-permute-start.14 = (f16[2,8,32,128]{3,2,1,0:T(8,128)(2,1)S(1)}, f16[2,8,32,128]{3,2,1,0:T(8,128)(2,1)S(1)}, u32[]{:S(2)}, u32[]{:S(2)}) collective-permute-start(f16[2,8,32,128]{3,2,1,0:T(8,128)(2,1)S(1)} %get-tuple-element.29), channel_id=1, source_target_pairs={{4,7},{5,6},{6,5},{7,4},{12,15},{13,14},{14,13},{15,12},{20,23},{2... | collective-permute-start | bytes 393224 | tf_op jit(solution)/shard_map/ppermute | solution.py:270
  62.2 7.1 %collective-permute-start.15 = (f16[2,8,32,128]{3,2,1,0:T(8,128)(2,1)S(1)}, f16[2,8,32,128]{3,2,1,0:T(8,128)(2,1)S(1)}, u32[]{:S(2)}, u32[]{:S(2)}) collective-permute-start(f16[2,8,32,128]{3,2,1,0:T(8,128)(2,1)S(1)} %get-tuple-element.31), channel_id=1, source_target_pairs={{4,6},{5,7},{6,4},{7,5},{12,14},{13,15},{14,12},{15,13},{20,22},{2... | collective-permute-start | bytes 393224 | tf_op jit(solution)/shard_map/ppermute | solution.py:270
  64.2 6.5 %collective-permute-start.16 = (f16[2,8,32,128]{3,2,1,0:T(8,128)(2,1)S(1)}, f16[2,8,32,128]{3,2,1,0:T(8,128)(2,1)S(1)}, u32[]{:S(2)}, u32[]{:S(2)}) collective-permute-start(f16[2,8,32,128]{3,2,1,0:T(8,128)(2,1)S(1)} %get-tuple-element.30), channel_id=1, source_target_pairs={{4,5},{5,4},{6,7},{7,6},{12,13},{13,12},{14,15},{15,14},{20,21},{2... | collective-permute-start | bytes 393224 | tf_op jit(solution)/shard_map/ppermute | solution.py:270

commit v16 on v15

--- a/solution.py
+++ b/solution.py
@@ -264,7 +264,7 @@
         return lax.dynamic_slice(rows, [zero, zero, start, zero], (freq_count, count, height, width))
 
     far = []
-    for k in reversed(range(1, n_pair)):
+    for k in range(1, n_pair):
         sent = (share(pair_col ^ jnp.uint32(k)) * scale).astype(jnp.float16)
         pairs = [(ring * n_pair + s, ring * n_pair + (s ^ k)) for ring in rings for s in range(n_pair)]
         far.append(lax.ppermute(sent, ("aux", "pair"), pairs).astype(jnp.float32))

time: 72.1 us -> 73.4 us (1.018)
  waiting for transfers between devices: 23.1 us -> 24.4 us
    ppermute x3, waiting for transfers between devices: 4 us -> 5.3 us  [total_at_once(): far.append(lax.ppermute(sent, ('aux', 'pair'), pairs).astype(jnp.float32))]
where the time goes in v16:
time: 73.4 us; the launch traced here: 73 us
  starting transfers between devices  28.5 us (39%)
  waiting for transfers between devices  24.4 us (33%)
  Pallas kernels  14.5 us (20%)
  local copies, waits for them, and re-layouts  2.56 us (3%)
  other arithmetic  2.11 us (3%)
  between operations  0.94 us (1%)
    ppermute x6, waiting for transfers between devices, halve(): got = lax.ppermute(sent, ('aux', 'pair'), pairs)  12.4 us
    ppermute x3, starting transfers between devices, total_at_once(): far.append(lax.ppermute(sent, ('aux', 'pair'), pairs).astype(jnp.float32))  9.27 us
    ppermute x6, starting transfers between devices, halve(): got = lax.ppermute(sent, ('aux', 'pair'), pairs)  8.43 us
    pallas_call x1, Pallas kernels, first_rows(): pl.pallas_call(functools.partial(first_kernel, dims), out_shape=[jax.Shap...  7.51 us
    ppermute x3, waiting for transfers between devices, total_at_once(): far.append(lax.ppermute(sent, ('aux', 'pair'), pairs).astype(jnp.float32))  5.3 us
    pallas_call x1, Pallas kernels, second_rows(): pl.pallas_call(functools.partial(second_kernel, dims, pieces), out_shape=...  3.82 us
    ppermute x1, starting transfers between devices, on_device(): to_even = lax.ppermute(rest, 'aux', [(s, s - 1) for s in odds])  3.63 us
    ppermute x1, waiting for transfers between devices, on_device(): b1 = lax.ppermute(to_one, 'aux', [(s, (s - 1) % n_aux) for s in evens])  3.36 us
  transfers between devices with their start and end apart: 17, of which 10 were waited for; matrix products, arithmetic and copies ran while one was open for 2% of the time, Pallas kernels for 17%

profile of v16, /device:TPU:1, one launch (start us, length us, event | category | flops | bytes accessed | tf_op | source)
XLA Modules:
  0.0 73.0 jit_solution(15899608680494341744)
XLA Ops:
  0.0 2.1 %copy-done = bf16[1,1,8,3,1,128,640]{6,5,4,3,2,1,0:T(8,128)(2,1)S(1)} copy-done((bf16[1,1,8,3,1,128,640]{6,5,4,3,2,1,0:T(8,128)(2,1)S(1)}, bf16[1,1,8,3,1,128,640]{6,5,4,3,2,1,0:T(8,128)(2,1)}, u32[]{:S(2)}) %copy-start) | copy-done | bytes 3932184
  2.1 1.9 %shard_map.64 = (bf16[8,128,640]{2,1,0:T(8,128)(2,1)S(1)}, bf16[16,128,640]{2,1,0:T(8,128)(2,1)}, bf16[1,128,640]{2,1,0:T(8,128)(2,1)S(1)}, bf16[7,128,640]{2,1,0:T(8,128)(2,1)S(1)}) custom-call(bf16[8,3,128,640]{3,2,1,0:T(8,128)(2,1)S(1)} %bitcast.58), custom_call_target="tpu_custom_call" | custom-call | flops 1000 | bytes 1000 | tf_op jit(solution)/shard_map/pallas_call | solution.py:46
  4.0 3.6 %collective-permute-start.3 = (bf16[16,128,640]{2,1,0:T(8,128)(2,1)}, bf16[16,128,640]{2,1,0:T(8,128)(2,1)}, u32[]{:S(2)}, u32[]{:S(2)}) collective-permute-start(bf16[16,128,640]{2,1,0:T(8,128)(2,1)} %get-tuple-element.18.refs_8_), channel_id=1, source_target_pairs={{4,0},{12,8},{5,1},{13,9},{6,2},{14,10},{7,3},{15,11},{20,16},{28,... | collective-permute-start | bytes 7864328 | tf_op jit(solution)/shard_map/ppermute | solution.py:297
  7.7 2.7 %collective-permute-start.4 = (bf16[1,128,640]{2,1,0:T(8,128)(2,1)S(1)}, bf16[1,128,640]{2,1,0:T(8,128)(2,1)S(1)}, u32[]{:S(2)}, u32[]{:S(2)}) collective-permute-start(bf16[1,128,640]{2,1,0:T(8,128)(2,1)S(1)} %get-tuple-element.20), channel_id=1, source_target_pairs={{0,8},{4,12},{8,0},{12,4},{1,9},{5,13},{9,1},{13,5},{2,10},{6,14},... | collective-permute-start | bytes 491528 | tf_op jit(solution)/shard_map/ppermute | solution.py:294
  11.3 0.7 collective-permute-start.2
  12.0 0.7 %collective-permute-done.refs_1_ = s32[25]{0:T(128)S(1)} collective-permute-done((s32[25]{0:T(128)S(1)}, s32[25]{0:T(128)S(1)}, u32[]{:S(2)}, u32[]{:S(2)}) %collective-permute-start) | collective-permute-done | bytes 132 | tf_op jit(solution)/shard_map/ppermute | solution.py:285
  12.8 0.9 %collective-permute-done.1.refs_2_ = s32[25]{0:T(128)S(1)} collective-permute-done((s32[25]{0:T(128)S(1)}, s32[25]{0:T(128)S(1)}, u32[]{:S(2)}, u32[]{:S(2)}) %collective-permute-start.1) | collective-permute-done | bytes 132 | tf_op jit(solution)/shard_map/ppermute | solution.py:285
  13.7 0.9 %collective-permute-done.2.refs_3_ = s32[25]{0:T(128)S(1)} collective-permute-done((s32[25]{0:T(128)S(1)}, s32[25]{0:T(128)S(1)}, u32[]{:S(2)}, u32[]{:S(2)}) %collective-permute-start.2) | collective-permute-done | bytes 132 | tf_op jit(solution)/shard_map/ppermute | solution.py:285
  14.6 1.1 %collective-permute-start.10 = (bf16[7,128,640]{2,1,0:T(8,128)(2,1)S(1)}, bf16[7,128,640]{2,1,0:T(8,128)(2,1)S(1)}, u32[]{:S(2)}, u32[]{:S(2)}) collective-permute-start(bf16[7,128,640]{2,1,0:T(8,128)(2,1)S(1)} %shard_map.65.refs_10_), channel_id=1, source_target_pairs={{0,8},{4,12},{8,0},{12,4},{1,9},{5,13},{9,1},{13,5},{2,10},{6,14},... | collective-permute-start | bytes 3440648 | tf_op jit(solution)/shard_map/ppermute | solution.py:296
  15.8 7.5 %shard_map.66 = (f32[2,8,128,128]{3,2,1,0:T(8,128)S(1)}, f32[2,8,128,128]{3,2,1,0:T(8,128)S(1)}, f32[8,16,640]{2,1,0:T(8,128)S(1)}, bf16[8,128,640]{2,1,0:T(8,128)(2,1)S(1)}) custom-call(s32[25]{0:T(128)S(1)} %pad_add_fusion.refs_0_, s32[25]{0:T(128)S(1)} %collective-permute-done.refs_1_, s32[25]{0:T(128)S(1)} %collective-permute-done.1.refs_2_, ...), custom_call_target="tpu_custom_call" | custom-call | flops 1000 | bytes 1000 | tf_op jit(solution)/shard_map/pallas_call | solution.py:154
  23.5 1.4 %collective-permute-start.5 = (f16[2,8,2,32,128]{4,3,1,0,2:T(8,128)(2,1)S(1)}, f16[2,8,2,32,128]{4,3,1,0,2:T(8,128)(2,1)S(1)}, u32[]{:S(2)}, u32[]{:S(2)}) collective-permute-start(f16[2,8,2,32,128]{4,3,1,0,2:T(8,128)(2,1)S(1)} %fusion.3), channel_id=1, source_target_pairs={{0,1},{1,0},{2,3},{3,2},{4,5},{5,4},{6,7},{7,6},{8,9},{9,8},{10,11... | collective-permute-start | bytes 786440 | tf_op jit(solution)/shard_map/ppermute | solution.py:242
  25.0 0.7 collective-permute-start.7
  25.7 1.3 %collective-permute-start.9 = (bf16[8,128,640]{2,1,0:T(8,128)(2,1)S(1)}, bf16[8,128,640]{2,1,0:T(8,128)(2,1)S(1)}, u32[]{:S(2)}, u32[]{:S(2)}) collective-permute-start(bf16[8,128,640]{2,1,0:T(8,128)(2,1)S(1)} %get-tuple-element.24), channel_id=1, source_target_pairs={{0,12},{8,4},{1,13},{9,5},{2,14},{10,6},{3,15},{11,7},{16,28},{24,... | collective-permute-start | bytes 3932168 | tf_op jit(solution)/shard_map/ppermute | solution.py:300
  27.0 4.6 %collective-permute-done.5 = f16[2,8,2,32,128]{4,3,1,0,2:T(8,128)(2,1)S(1)} collective-permute-done((f16[2,8,2,32,128]{4,3,1,0,2:T(8,128)(2,1)S(1)}, f16[2,8,2,32,128]{4,3,1,0,2:T(8,128)(2,1)S(1)}, u32[]{:S(2)}, u32[]{:S(2)}) %collective-permute-start.5) | collective-permute-done | bytes 262176 | tf_op jit(solution)/shard_map/ppermute | solution.py:242
  31.7 2.1 %collective-permute-start.6 = (f16[2,8,1,32,128]{4,3,1,0,2:T(8,128)(2,1)S(1)}, f16[2,8,1,32,128]{4,3,1,0,2:T(8,128)(2,1)S(1)}, u32[]{:S(2)}, u32[]{:S(2)}) collective-permute-start(f16[2,8,1,32,128]{4,3,1,0,2:T(8,128)(2,1)S(1)} %multiply_convert_fusion.6), channel_id=1, source_target_pairs={{0,2},{1,3},{2,0},{3,1},{4,6},{5,7},{6,4},{7,5},{8,10},{9,11},{10,... | collective-permute-start | bytes 393224 | tf_op jit(solution)/shard_map/ppermute | solution.py:242
  33.9 0.7 collective-permute-start.8
  34.6 5.3 %collective-permute-done.6 = f16[2,8,1,32,128]{4,3,1,0,2:T(8,128)(2,1)S(1)} collective-permute-done((f16[2,8,1,32,128]{4,3,1,0,2:T(8,128)(2,1)S(1)}, f16[2,8,1,32,128]{4,3,1,0,2:T(8,128)(2,1)S(1)}, u32[]{:S(2)}, u32[]{:S(2)}) %collective-permute-start.6) | collective-permute-done | bytes 131104 | tf_op jit(solution)/shard_map/ppermute | solution.py:242
  40.0 0.8 %collective-permute-done.10.refs_1_ = bf16[7,128,640]{2,1,0:T(8,128)(2,1)S(1)} collective-permute-done((bf16[7,128,640]{2,1,0:T(8,128)(2,1)S(1)}, bf16[7,128,640]{2,1,0:T(8,128)(2,1)S(1)}, u32[]{:S(2)}, u32[]{:S(2)}) %collective-permute-start.10) | collective-permute-done | bytes 1146912 | tf_op jit(solution)/shard_map/ppermute | solution.py:296
  40.7 3.8 %shard_map.67 = (f32[2,8,128,128]{3,2,1,0:T(8,128)S(1)}, f32[2,8,128,128]{3,2,1,0:T(8,128)S(1)}) custom-call(f32[8,16,640]{2,1,0:T(8,128)S(1)} %get-tuple-element.23.roots, bf16[8,128,640]{2,1,0:T(8,128)(2,1)S(1)} %get-tuple-element.17.refs_7_.own, bf16[16,128,640]{2,1,0:T(8,128)(2,1)} %collective-permute-done.3.refs_9_.lower, ...), custom_call_target="tpu_custom_call" | custom-call | flops 1000 | bytes 1000 | tf_op jit(solution)/shard_map/pallas_call | solution.py:219
  44.7 1.3 %collective-permute-start.12 = (f16[2,8,2,32,128]{4,3,1,0,2:T(8,128)(2,1)S(1)}, f16[2,8,2,32,128]{4,3,1,0,2:T(8,128)(2,1)S(1)}, u32[]{:S(2)}, u32[]{:S(2)}) collective-permute-start(f16[2,8,2,32,128]{4,3,1,0,2:T(8,128)(2,1)S(1)} %fusion.5), channel_id=1, source_target_pairs={{0,1},{1,0},{2,3},{3,2},{4,5},{5,4},{6,7},{7,6},{8,9},{9,8},{10,11... | collective-permute-start | bytes 786440 | tf_op jit(solution)/shard_map/ppermute | solution.py:242
  46.0 0.1 multiply_convert_fusion
  46.2 1.3 %collective-permute-start.11 = (f16[2,8,128,128]{3,2,1,0:T(8,128)(2,1)S(1)}, f16[2,8,128,128]{3,2,1,0:T(8,128)(2,1)S(1)}, u32[]{:S(2)}, u32[]{:S(2)}) collective-permute-start(f16[2,8,128,128]{3,2,1,0:T(8,128)(2,1)S(1)} %multiply_convert_fusion), channel_id=1, source_target_pairs={{0,4},{8,12},{1,5},{9,13},{2,6},{10,14},{3,7},{11,15},{16,20},{24,... | collective-permute-start | bytes 1572872 | tf_op jit(solution)/shard_map/ppermute | solution.py:305
  47.5 2.5 %collective-permute-done.12 = f16[2,8,2,32,128]{4,3,1,0,2:T(8,128)(2,1)S(1)} collective-permute-done((f16[2,8,2,32,128]{4,3,1,0,2:T(8,128)(2,1)S(1)}, f16[2,8,2,32,128]{4,3,1,0,2:T(8,128)(2,1)S(1)}, u32[]{:S(2)}, u32[]{:S(2)}) %collective-permute-start.12) | collective-permute-done | bytes 262176 | tf_op jit(solution)/shard_map/ppermute | solution.py:242
  50.1 2.3 %collective-permute-start.13 = (f16[2,8,1,32,128]{4,3,2,1,0:T(8,128)(2,1)S(1)}, f16[2,8,1,32,128]{4,3,2,1,0:T(8,128)(2,1)S(1)}, u32[]{:S(2)}, u32[]{:S(2)}) collective-permute-start(f16[2,8,1,32,128]{4,3,2,1,0:T(8,128)(2,1)S(1)} %fusion.8), channel_id=1, source_target_pairs={{0,2},{1,3},{2,0},{3,1},{4,6},{5,7},{6,4},{7,5},{8,10},{9,11},{10,... | collective-permute-start | bytes 393224 | tf_op jit(solution)/shard_map/ppermute | solution.py:242
  52.6 3.4 %collective-permute-done.9.far = bf16[8,128,640]{2,1,0:T(8,128)(2,1)S(1)} collective-permute-done((bf16[8,128,640]{2,1,0:T(8,128)(2,1)S(1)}, bf16[8,128,640]{2,1,0:T(8,128)(2,1)S(1)}, u32[]{:S(2)}, u32[]{:S(2)}) %collective-permute-start.9) | collective-permute-done | bytes 1310752 | tf_op jit(solution)/shard_map/ppermute | solution.py:300
  55.9 1.2 %shard_map.68 = (f32[2,8,128,128]{3,2,1,0:T(8,128)S(1)}, f32[32,128]{1,0:T(8,128)S(1)}) custom-call(f32[8,16,640]{2,1,0:T(8,128)S(1)} %get-tuple-element.23.roots, bf16[8,128,640]{2,1,0:T(8,128)(2,1)S(1)} %get-tuple-element.17.refs_7_.own, bf16[8,128,640]{2,1,0:T(8,128)(2,1)S(1)} %collective-permute-done.9.far, f32[2,8,128,128]{3,2,1,0:T(8,128)S(1)} %convert_multiply_fusion.add), custom_call_target="tpu_custom_call" | custom-call | flops 1000 | bytes 1000 | tf_op jit(solution)/shard_map/pallas_call | solution.py:185
  57.3 2.9 %collective-permute-start.14 = (f16[2,8,32,128]{3,2,1,0:T(8,128)(2,1)S(1)}, f16[2,8,32,128]{3,2,1,0:T(8,128)(2,1)S(1)}, u32[]{:S(2)}, u32[]{:S(2)}) collective-permute-start(f16[2,8,32,128]{3,2,1,0:T(8,128)(2,1)S(1)} %get-tuple-element.29), channel_id=1, source_target_pairs={{4,5},{5,4},{6,7},{7,6},{12,13},{13,12},{14,15},{15,14},{20,21},{2... | collective-permute-start | bytes 393224 | tf_op jit(solution)/shard_map/ppermute | solution.py:270
  60.2 4.2 %collective-permute-start.15 = (f16[2,8,32,128]{3,2,1,0:T(8,128)(2,1)S(1)}, f16[2,8,32,128]{3,2,1,0:T(8,128)(2,1)S(1)}, u32[]{:S(2)}, u32[]{:S(2)}) collective-permute-start(f16[2,8,32,128]{3,2,1,0:T(8,128)(2,1)S(1)} %get-tuple-element.31), channel_id=1, source_target_pairs={{4,6},{5,7},{6,4},{7,5},{12,14},{13,15},{14,12},{15,13},{20,22},{2... | collective-permute-start | bytes 393224 | tf_op jit(solution)/shard_map/ppermute | solution.py:270
  64.4 2.1 %collective-permute-start.16 = (f16[2,8,32,128]{3,2,1,0:T(8,128)(2,1)S(1)}, f16[2,8,32,128]{3,2,1,0:T(8,128)(2,1)S(1)}, u32[]{:S(2)}, u32[]{:S(2)}) collective-permute-start(f16[2,8,32,128]{3,2,1,0:T(8,128)(2,1)S(1)} %get-tuple-element.30), channel_id=1, source_target_pairs={{4,7},{5,6},{6,5},{7,4},{12,15},{13,14},{14,13},{15,12},{20,23},{2... | collective-permute-start | bytes 393224 | tf_op jit(solution)/shard_map/ppermute | solution.py:270
  66.7 1.6 %collective-permute-done.15 = f16[2,8,32,128]{3,2,1,0:T(8,128)(2,1)S(1)} collective-permute-done((f16[2,8,32,128]{3,2,1,0:T(8,128)(2,1)S(1)}, f16[2,8,32,128]{3,2,1,0:T(8,128)(2,1)S(1)}, u32[]{:S(2)}, u32[]{:S(2)}) %collective-permute-start.15) | collective-permute-done | bytes 131104 | tf_op jit(solution)/shard_map/ppermute | solution.py:270
  68.2 3.7 %collective-permute-done.16 = f16[2,8,32,128]{3,2,1,0:T(8,128)(2,1)S(1)} collective-permute-done((f16[2,8,32,128]{3,2,1,0:T(8,128)(2,1)S(1)}, f16[2,8,32,128]{3,2,1,0:T(8,128)(2,1)S(1)}, u32[]{:S(2)}, u32[]{:S(2)}) %collective-permute-start.16) | collective-permute-done | bytes 131104 | tf_op jit(solution)/shard_map/ppermute | solution.py:270
  72.1 0.9 %maximum_bitcast_fusion = f32[2,8,1,32,384]{4,3,2,1,0:T(8,128)} fusion(f32[2,8,32,128]{3,2,1,0:T(8,128)S(1)} %fusion.7, f32[2,8,32,128]{3,2,1,0:T(8,128)S(1)} %bitcast_select_fusion, f32[2,8,32,128]{3,2,1,0:T(8,128)S(1)} %add_bitcast_fusion), kind=kLoop, calls=%fused_computation.2 | loop fusion | flops 393216 | bytes 1572864 | tf_op jit(solution)/shard_map/broadcast_in_dim | solution.py:312
  (43 shorter events, 1.6 us)
Async XLA Ops:
  0.0 2.1 %copy-start = (bf16[1,1,8,3,1,128,640]{6,5,4,3,2,1,0:T(8,128)(2,1)S(1)}, bf16[1,1,8,3,1,128,640]{6,5,4,3,2,1,0:T(8,128)(2,1)}, u32[]{:S(2)}) copy-start(bf16[1,1,8,3,1,128,640]{6,5,4,3,2,1,0:T(8,128)(2,1)} %param.6) | copy-start | bytes 11796484
  2.1 8.2 %copy-start.4 = (s32[1,1,8,3,1]{2,4,3,1,0:T(1,128)S(1)}, s32[1,1,8,3,1]{2,4,3,1,0:T(1,128)}, u32[]{:S(2)}) copy-start(s32[1,1,8,3,1]{2,4,3,1,0:T(1,128)} %param.7) | copy-start | bytes 292
  4.0 11.7 %copy-start.1 = (f32[10240]{0:T(1024)S(1)}, f32[10240]{0:T(1024)}, u32[]{:S(2)}) copy-start(f32[10240]{0:T(1024)} %param.10) | copy-start | bytes 122884
  4.0 11.7 %copy-start.2 = (f32[8]{0:T(128)S(1)}, f32[8]{0:T(128)}, u32[]{:S(2)}) copy-start(f32[8]{0:T(128)} %refs_4_.1) | copy-start | bytes 100
  4.0 11.7 %copy-start.3 = (f32[2]{0:T(128)S(1)}, f32[2]{0:T(128)}, u32[]{:S(2)}) copy-start(f32[2]{0:T(128)} %refs_5_.1) | copy-start | bytes 28
  4.0 11.7 %collective-permute-start.3 = (bf16[16,128,640]{2,1,0:T(8,128)(2,1)}, bf16[16,128,640]{2,1,0:T(8,128)(2,1)}, u32[]{:S(2)}, u32[]{:S(2)}) collective-permute-start(bf16[16,128,640]{2,1,0:T(8,128)(2,1)} %get-tuple-element.18.refs_8_), channel_id=1, source_target_pairs={{4,0},{12,8},{5,1},{13,9},{6,2},{14,10},{7,3},{15,11},{20,16},{28,... | collective-permute-start | bytes 7864328 | tf_op jit(solution)/shard_map/ppermute | solution.py:297
  7.7 6.9 %collective-permute-start.4 = (bf16[1,128,640]{2,1,0:T(8,128)(2,1)S(1)}, bf16[1,128,640]{2,1,0:T(8,128)(2,1)S(1)}, u32[]{:S(2)}, u32[]{:S(2)}) collective-permute-start(bf16[1,128,640]{2,1,0:T(8,128)(2,1)S(1)} %get-tuple-element.20), channel_id=1, source_target_pairs={{0,8},{4,12},{8,0},{12,4},{1,9},{5,13},{9,1},{13,5},{2,10},{6,14},... | collective-permute-start | bytes 491528 | tf_op jit(solution)/shard_map/ppermute | solution.py:294
  11.2 1.5 %collective-permute-start = (s32[25]{0:T(128)S(1)}, s32[25]{0:T(128)S(1)}, u32[]{:S(2)}, u32[]{:S(2)}) collective-permute-start(s32[25]{0:T(128)S(1)} %pad_add_fusion.refs_0_), channel_id=1, source_target_pairs={{0,4},{4,8},{8,12},{12,0},{1,5},{5,9},{9,13},{13,1},{2,6},{6,10},{... | collective-permute-start | bytes 308 | tf_op jit(solution)/shard_map/ppermute | solution.py:285
  11.2 2.5 %collective-permute-start.1 = (s32[25]{0:T(128)S(1)}, s32[25]{0:T(128)S(1)}, u32[]{:S(2)}, u32[]{:S(2)}) collective-permute-start(s32[25]{0:T(128)S(1)} %pad_add_fusion.refs_0_), channel_id=1, source_target_pairs={{0,8},{4,12},{8,0},{12,4},{1,9},{5,13},{9,1},{13,5},{2,10},{6,14},... | collective-permute-start | bytes 308 | tf_op jit(solution)/shard_map/ppermute | solution.py:285
  11.3 3.3 %collective-permute-start.2 = (s32[25]{0:T(128)S(1)}, s32[25]{0:T(128)S(1)}, u32[]{:S(2)}, u32[]{:S(2)}) collective-permute-start(s32[25]{0:T(128)S(1)} %pad_add_fusion.refs_0_), channel_id=1, source_target_pairs={{0,12},{4,0},{8,4},{12,8},{1,13},{5,1},{9,5},{13,9},{2,14},{6,2},{... | collective-permute-start | bytes 308 | tf_op jit(solution)/shard_map/ppermute | solution.py:285
  14.6 26.1 %collective-permute-start.10 = (bf16[7,128,640]{2,1,0:T(8,128)(2,1)S(1)}, bf16[7,128,640]{2,1,0:T(8,128)(2,1)S(1)}, u32[]{:S(2)}, u32[]{:S(2)}) collective-permute-start(bf16[7,128,640]{2,1,0:T(8,128)(2,1)S(1)} %shard_map.65.refs_10_), channel_id=1, source_target_pairs={{0,8},{4,12},{8,0},{12,4},{1,9},{5,13},{9,1},{13,5},{2,10},{6,14},... | collective-permute-start | bytes 3440648 | tf_op jit(solution)/shard_map/ppermute | solution.py:296
  23.5 8.1 %collective-permute-start.5 = (f16[2,8,2,32,128]{4,3,1,0,2:T(8,128)(2,1)S(1)}, f16[2,8,2,32,128]{4,3,1,0,2:T(8,128)(2,1)S(1)}, u32[]{:S(2)}, u32[]{:S(2)}) collective-permute-start(f16[2,8,2,32,128]{4,3,1,0,2:T(8,128)(2,1)S(1)} %fusion.3), channel_id=1, source_target_pairs={{0,1},{1,0},{2,3},{3,2},{4,5},{5,4},{6,7},{7,6},{8,9},{9,8},{10,11... | collective-permute-start | bytes 786440 | tf_op jit(solution)/shard_map/ppermute | solution.py:242
  25.0 8.8 %collective-permute-start.7 = (f16[2,8,2,32,128]{4,3,1,0,2:T(8,128)(2,1)S(1)}, f16[2,8,2,32,128]{4,3,1,0,2:T(8,128)(2,1)S(1)}, u32[]{:S(2)}, u32[]{:S(2)}) collective-permute-start(f16[2,8,2,32,128]{4,3,1,0,2:T(8,128)(2,1)S(1)} %fusion.4), channel_id=1, source_target_pairs={{0,1},{1,0},{2,3},{3,2},{8,9},{9,8},{10,11},{11,10},{16,17},{17,16... | collective-permute-start | bytes 786440 | tf_op jit(solution)/shard_map/ppermute | solution.py:242
  25.7 30.3 %collective-permute-start.9 = (bf16[8,128,640]{2,1,0:T(8,128)(2,1)S(1)}, bf16[8,128,640]{2,1,0:T(8,128)(2,1)S(1)}, u32[]{:S(2)}, u32[]{:S(2)}) collective-permute-start(bf16[8,128,640]{2,1,0:T(8,128)(2,1)S(1)} %get-tuple-element.24), channel_id=1, source_target_pairs={{0,12},{8,4},{1,13},{9,5},{2,14},{10,6},{3,15},{11,7},{16,28},{24,... | collective-permute-start | bytes 3932168 | tf_op jit(solution)/shard_map/ppermute | solution.py:300
  31.7 8.3 %collective-permute-start.6 = (f16[2,8,1,32,128]{4,3,1,0,2:T(8,128)(2,1)S(1)}, f16[2,8,1,32,128]{4,3,1,0,2:T(8,128)(2,1)S(1)}, u32[]{:S(2)}, u32[]{:S(2)}) collective-permute-start(f16[2,8,1,32,128]{4,3,1,0,2:T(8,128)(2,1)S(1)} %multiply_convert_fusion.6), channel_id=1, source_target_pairs={{0,2},{1,3},{2,0},{3,1},{4,6},{5,7},{6,4},{7,5},{8,10},{9,11},{10,... | collective-permute-start | bytes 393224 | tf_op jit(solution)/shard_map/ppermute | solution.py:242
  33.9 6.0 %collective-permute-start.8 = (f16[2,8,1,32,128]{4,3,1,0,2:T(8,128)(2,1)S(1)}, f16[2,8,1,32,128]{4,3,1,0,2:T(8,128)(2,1)S(1)}, u32[]{:S(2)}, u32[]{:S(2)}) collective-permute-start(f16[2,8,1,32,128]{4,3,1,0,2:T(8,128)(2,1)S(1)} %multiply_convert_fusion.5), channel_id=1, source_target_pairs={{0,2},{1,3},{2,0},{3,1},{8,10},{9,11},{10,8},{11,9},{16,18},{17,19... | collective-permute-start | bytes 393224 | tf_op jit(solution)/shard_map/ppermute | solution.py:242
  44.7 5.3 %collective-permute-start.12 = (f16[2,8,2,32,128]{4,3,1,0,2:T(8,128)(2,1)S(1)}, f16[2,8,2,32,128]{4,3,1,0,2:T(8,128)(2,1)S(1)}, u32[]{:S(2)}, u32[]{:S(2)}) collective-permute-start(f16[2,8,2,32,128]{4,3,1,0,2:T(8,128)(2,1)S(1)} %fusion.5), channel_id=1, source_target_pairs={{0,1},{1,0},{2,3},{3,2},{4,5},{5,4},{6,7},{7,6},{8,9},{9,8},{10,11... | collective-permute-start | bytes 786440 | tf_op jit(solution)/shard_map/ppermute | solution.py:242
  46.2 6.3 %collective-permute-start.11 = (f16[2,8,128,128]{3,2,1,0:T(8,128)(2,1)S(1)}, f16[2,8,128,128]{3,2,1,0:T(8,128)(2,1)S(1)}, u32[]{:S(2)}, u32[]{:S(2)}) collective-permute-start(f16[2,8,128,128]{3,2,1,0:T(8,128)(2,1)S(1)} %multiply_convert_fusion), channel_id=1, source_target_pairs={{0,4},{8,12},{1,5},{9,13},{2,6},{10,14},{3,7},{11,15},{16,20},{24,... | collective-permute-start | bytes 1572872 | tf_op jit(solution)/shard_map/ppermute | solution.py:305
  50.1 7.0 %collective-permute-start.13 = (f16[2,8,1,32,128]{4,3,2,1,0:T(8,128)(2,1)S(1)}, f16[2,8,1,32,128]{4,3,2,1,0:T(8,128)(2,1)S(1)}, u32[]{:S(2)}, u32[]{:S(2)}) collective-permute-start(f16[2,8,1,32,128]{4,3,2,1,0:T(8,128)(2,1)S(1)} %fusion.8), channel_id=1, source_target_pairs={{0,2},{1,3},{2,0},{3,1},{4,6},{5,7},{6,4},{7,5},{8,10},{9,11},{10,... | collective-permute-start | bytes 393224 | tf_op jit(solution)/shard_map/ppermute | solution.py:242
  57.3 9.3 %collective-permute-start.14 = (f16[2,8,32,128]{3,2,1,0:T(8,128)(2,1)S(1)}, f16[2,8,32,128]{3,2,1,0:T(8,128)(2,1)S(1)}, u32[]{:S(2)}, u32[]{:S(2)}) collective-permute-start(f16[2,8,32,128]{3,2,1,0:T(8,128)(2,1)S(1)} %get-tuple-element.29), channel_id=1, source_target_pairs={{4,5},{5,4},{6,7},{7,6},{12,13},{13,12},{14,15},{15,14},{20,21},{2... | collective-permute-start | bytes 393224 | tf_op jit(solution)/shard_map/ppermute | solution.py:270
  60.2 8.0 %collective-permute-start.15 = (f16[2,8,32,128]{3,2,1,0:T(8,128)(2,1)S(1)}, f16[2,8,32,128]{3,2,1,0:T(8,128)(2,1)S(1)}, u32[]{:S(2)}, u32[]{:S(2)}) collective-permute-start(f16[2,8,32,128]{3,2,1,0:T(8,128)(2,1)S(1)} %get-tuple-element.31), channel_id=1, source_target_pairs={{4,6},{5,7},{6,4},{7,5},{12,14},{13,15},{14,12},{15,13},{20,22},{2... | collective-permute-start | bytes 393224 | tf_op jit(solution)/shard_map/ppermute | solution.py:270
  64.4 7.5 %collective-permute-start.16 = (f16[2,8,32,128]{3,2,1,0:T(8,128)(2,1)S(1)}, f16[2,8,32,128]{3,2,1,0:T(8,128)(2,1)S(1)}, u32[]{:S(2)}, u32[]{:S(2)}) collective-permute-start(f16[2,8,32,128]{3,2,1,0:T(8,128)(2,1)S(1)} %get-tuple-element.30), channel_id=1, source_target_pairs={{4,7},{5,6},{6,5},{7,4},{12,15},{13,14},{14,13},{15,12},{20,23},{2... | collective-permute-start | bytes 393224 | tf_op jit(solution)/shard_map/ppermute | solution.py:270

commit v17 on v15

--- a/solution.py
+++ b/solution.py
@@ -8,7 +8,7 @@
 from jax.sharding import PartitionSpec as P
 
 LIMIT = 16 << 20
-SPLIT = (1, 7)
+SPLIT = (2, 6)
 COST = pl.CostEstimate(flops=1000, bytes_accessed=1000, transcendentals=0)
 PARAMS = pltpu.CompilerParams(vmem_limit_bytes=LIMIT)
 ANY = pl.BlockSpec(memory_space=pl.ANY)

time: 72.1 us -> 74.1 us (1.028)
  starting transfers between devices: 28.5 us -> 31.1 us
  waiting for transfers between devices: 23.1 us -> 21.7 us
    ppermute x6, waiting for transfers between devices: 12.4 us -> 8.21 us  [halve(): got = lax.ppermute(sent, ('aux', 'pair'), pairs)]
    ppermute x1, waiting for transfers between devices: 3.36 us -> 0.01 us  [on_device(): b1 = lax.ppermute(to_one, 'aux', [(s, (s - 1) % n_aux) for s in evens])]
    ppermute x1, waiting for transfers between devices: 0.01 us -> 2.02 us  [on_device(): lax.ppermute((rows_next * scale).astype(jnp.float16), 'aux', [(s, s + 1)...]
    ppermute x3, waiting for transfers between devices: 2.57 us -> 4.45 us  [on_device(): lax.ppermute(record, 'aux', [(s, (s + k) % n_aux) for s in range(n_aux)])]
    ppermute x6, starting transfers between devices: 8.43 us -> 9.96 us  [halve(): got = lax.ppermute(sent, ('aux', 'pair'), pairs)]
    ppermute x3, waiting for transfers between devices: 4 us -> 5.51 us  [total_at_once(): far.append(lax.ppermute(sent, ('aux', 'pair'), pairs).astype(jnp.float32))]
    ppermute x1, waiting for transfers between devices: 0.77 us -> 1.53 us  [on_device(): c2.append(lax.ppermute(far_two, 'aux', down2))]
  transfers between devices with their start and end apart: 17 -> 17, of which waited for: 10 -> 9; matrix products, arithmetic and copies ran while one was open for 2% -> 2% of each run, Pallas kernels for 17% -> 17%
where the time goes in v17:
time: 74.1 us; the launch traced here: 73 us
  starting transfers between devices  31.1 us (42%)
  waiting for transfers between devices  21.7 us (29%)
  Pallas kernels  14.5 us (20%)
  local copies, waits for them, and re-layouts  2.56 us (3%)
  other arithmetic  2.12 us (3%)
  between operations  0.95 us (1%)
    ppermute x6, starting transfers between devices, halve(): got = lax.ppermute(sent, ('aux', 'pair'), pairs)  9.96 us
    ppermute x3, starting transfers between devices, total_at_once(): far.append(lax.ppermute(sent, ('aux', 'pair'), pairs).astype(jnp.float32))  9.85 us
    ppermute x6, waiting for transfers between devices, halve(): got = lax.ppermute(sent, ('aux', 'pair'), pairs)  8.21 us
    pallas_call x1, Pallas kernels, first_rows(): pl.pallas_call(functools.partial(first_kernel, dims), out_shape=[jax.Shap...  7.5 us
    ppermute x3, waiting for transfers between devices, total_at_once(): far.append(lax.ppermute(sent, ('aux', 'pair'), pairs).astype(jnp.float32))  5.51 us
    ppermute x3, waiting for transfers between devices, on_device(): lax.ppermute(record, 'aux', [(s, (s + k) % n_aux) for s in range(n_aux)])  4.45 us
    pallas_call x1, Pallas kernels, second_rows(): pl.pallas_call(functools.partial(second_kernel, dims, pieces), out_shape=...  3.83 us
    ppermute x1, starting transfers between devices, on_device(): to_even = lax.ppermute(rest, 'aux', [(s, s - 1) for s in odds])  3.5 us
  transfers between devices with their start and end apart: 17, of which 9 were waited for; matrix products, arithmetic and copies ran while one was open for 2% of the time, Pallas kernels for 17%

profile of v17, /device:TPU:1, one launch (start us, length us, event | category | flops | bytes accessed | tf_op | source)
XLA Modules:
  0.0 73.0 jit_solution(1760347479024664294)
XLA Ops:
  0.0 2.1 %copy-done = bf16[1,1,8,3,1,128,640]{6,5,4,3,2,1,0:T(8,128)(2,1)S(1)} copy-done((bf16[1,1,8,3,1,128,640]{6,5,4,3,2,1,0:T(8,128)(2,1)S(1)}, bf16[1,1,8,3,1,128,640]{6,5,4,3,2,1,0:T(8,128)(2,1)}, u32[]{:S(2)}) %copy-start) | copy-done | bytes 3932184
  2.1 1.9 %shard_map.64 = (bf16[8,128,640]{2,1,0:T(8,128)(2,1)S(1)}, bf16[16,128,640]{2,1,0:T(8,128)(2,1)}, bf16[2,128,640]{2,1,0:T(8,128)(2,1)S(1)}, bf16[6,128,640]{2,1,0:T(8,128)(2,1)S(1)}) custom-call(bf16[8,3,128,640]{3,2,1,0:T(8,128)(2,1)S(1)} %bitcast.58), custom_call_target="tpu_custom_call" | custom-call | flops 1000 | bytes 1000 | tf_op jit(solution)/shard_map/pallas_call | solution.py:46
  4.1 3.5 %collective-permute-start.3 = (bf16[16,128,640]{2,1,0:T(8,128)(2,1)}, bf16[16,128,640]{2,1,0:T(8,128)(2,1)}, u32[]{:S(2)}, u32[]{:S(2)}) collective-permute-start(bf16[16,128,640]{2,1,0:T(8,128)(2,1)} %get-tuple-element.18.refs_8_), channel_id=1, source_target_pairs={{4,0},{12,8},{5,1},{13,9},{6,2},{14,10},{7,3},{15,11},{20,16},{28,... | collective-permute-start | bytes 7864328 | tf_op jit(solution)/shard_map/ppermute | solution.py:297
  7.6 2.7 %collective-permute-start.4 = (bf16[2,128,640]{2,1,0:T(8,128)(2,1)S(1)}, bf16[2,128,640]{2,1,0:T(8,128)(2,1)S(1)}, u32[]{:S(2)}, u32[]{:S(2)}) collective-permute-start(bf16[2,128,640]{2,1,0:T(8,128)(2,1)S(1)} %get-tuple-element.20), channel_id=1, source_target_pairs={{0,8},{4,12},{8,0},{12,4},{1,9},{5,13},{9,1},{13,5},{2,10},{6,14},... | collective-permute-start | bytes 983048 | tf_op jit(solution)/shard_map/ppermute | solution.py:294
  11.2 0.7 collective-permute-start.2
  11.9 4.3 %collective-permute-done.refs_1_ = s32[25]{0:T(128)S(1)} collective-permute-done((s32[25]{0:T(128)S(1)}, s32[25]{0:T(128)S(1)}, u32[]{:S(2)}, u32[]{:S(2)}) %collective-permute-start) | collective-permute-done | bytes 132 | tf_op jit(solution)/shard_map/ppermute | solution.py:285
  16.2 0.2 collective-permute-done.1.refs_2_
  16.4 1.8 %collective-permute-start.10 = (bf16[6,128,640]{2,1,0:T(8,128)(2,1)S(1)}, bf16[6,128,640]{2,1,0:T(8,128)(2,1)S(1)}, u32[]{:S(2)}, u32[]{:S(2)}) collective-permute-start(bf16[6,128,640]{2,1,0:T(8,128)(2,1)S(1)} %shard_map.65.refs_10_), channel_id=1, source_target_pairs={{0,8},{4,12},{8,0},{12,4},{1,9},{5,13},{9,1},{13,5},{2,10},{6,14},... | collective-permute-start | bytes 2949128 | tf_op jit(solution)/shard_map/ppermute | solution.py:296
  18.2 7.5 %shard_map.66 = (f32[2,8,128,128]{3,2,1,0:T(8,128)S(1)}, f32[2,8,128,128]{3,2,1,0:T(8,128)S(1)}, f32[8,16,640]{2,1,0:T(8,128)S(1)}, bf16[8,128,640]{2,1,0:T(8,128)(2,1)S(1)}) custom-call(s32[25]{0:T(128)S(1)} %pad_add_fusion.refs_0_, s32[25]{0:T(128)S(1)} %collective-permute-done.refs_1_, s32[25]{0:T(128)S(1)} %collective-permute-done.1.refs_2_, ...), custom_call_target="tpu_custom_call" | custom-call | flops 1000 | bytes 1000 | tf_op jit(solution)/shard_map/pallas_call | solution.py:154
  25.9 1.4 %collective-permute-start.5 = (f16[2,8,2,32,128]{4,3,1,0,2:T(8,128)(2,1)S(1)}, f16[2,8,2,32,128]{4,3,1,0,2:T(8,128)(2,1)S(1)}, u32[]{:S(2)}, u32[]{:S(2)}) collective-permute-start(f16[2,8,2,32,128]{4,3,1,0,2:T(8,128)(2,1)S(1)} %fusion.3), channel_id=1, source_target_pairs={{0,1},{1,0},{2,3},{3,2},{4,5},{5,4},{6,7},{7,6},{8,9},{9,8},{10,11... | collective-permute-start | bytes 786440 | tf_op jit(solution)/shard_map/ppermute | solution.py:242
  27.4 0.7 collective-permute-start.7
  28.1 1.3 %collective-permute-start.9 = (bf16[8,128,640]{2,1,0:T(8,128)(2,1)S(1)}, bf16[8,128,640]{2,1,0:T(8,128)(2,1)S(1)}, u32[]{:S(2)}, u32[]{:S(2)}) collective-permute-start(bf16[8,128,640]{2,1,0:T(8,128)(2,1)S(1)} %get-tuple-element.24), channel_id=1, source_target_pairs={{0,12},{8,4},{1,13},{9,5},{2,14},{10,6},{3,15},{11,7},{16,28},{24,... | collective-permute-start | bytes 3932168 | tf_op jit(solution)/shard_map/ppermute | solution.py:300
  29.4 3.5 %collective-permute-done.5 = f16[2,8,2,32,128]{4,3,1,0,2:T(8,128)(2,1)S(1)} collective-permute-done((f16[2,8,2,32,128]{4,3,1,0,2:T(8,128)(2,1)S(1)}, f16[2,8,2,32,128]{4,3,1,0,2:T(8,128)(2,1)S(1)}, u32[]{:S(2)}, u32[]{:S(2)}) %collective-permute-start.5) | collective-permute-done | bytes 262176 | tf_op jit(solution)/shard_map/ppermute | solution.py:242
  33.0 2.4 %collective-permute-start.6 = (f16[2,8,1,32,128]{4,3,1,0,2:T(8,128)(2,1)S(1)}, f16[2,8,1,32,128]{4,3,1,0,2:T(8,128)(2,1)S(1)}, u32[]{:S(2)}, u32[]{:S(2)}) collective-permute-start(f16[2,8,1,32,128]{4,3,1,0,2:T(8,128)(2,1)S(1)} %multiply_convert_fusion.6), channel_id=1, source_target_pairs={{0,2},{1,3},{2,0},{3,1},{4,6},{5,7},{6,4},{7,5},{8,10},{9,11},{10,... | collective-permute-start | bytes 393224 | tf_op jit(solution)/shard_map/ppermute | solution.py:242
  35.5 0.7 collective-permute-start.8
  36.2 2.0 %collective-permute-done.6 = f16[2,8,1,32,128]{4,3,1,0,2:T(8,128)(2,1)S(1)} collective-permute-done((f16[2,8,1,32,128]{4,3,1,0,2:T(8,128)(2,1)S(1)}, f16[2,8,1,32,128]{4,3,1,0,2:T(8,128)(2,1)S(1)}, u32[]{:S(2)}, u32[]{:S(2)}) %collective-permute-start.6) | collective-permute-done | bytes 131104 | tf_op jit(solution)/shard_map/ppermute | solution.py:242
  38.2 1.5 %collective-permute-done.10.refs_1_ = bf16[6,128,640]{2,1,0:T(8,128)(2,1)S(1)} collective-permute-done((bf16[6,128,640]{2,1,0:T(8,128)(2,1)S(1)}, bf16[6,128,640]{2,1,0:T(8,128)(2,1)S(1)}, u32[]{:S(2)}, u32[]{:S(2)}) %collective-permute-start.10) | collective-permute-done | bytes 983072 | tf_op jit(solution)/shard_map/ppermute | solution.py:296
  39.7 3.8 %shard_map.67 = (f32[2,8,128,128]{3,2,1,0:T(8,128)S(1)}, f32[2,8,128,128]{3,2,1,0:T(8,128)S(1)}) custom-call(f32[8,16,640]{2,1,0:T(8,128)S(1)} %get-tuple-element.23.roots, bf16[8,128,640]{2,1,0:T(8,128)(2,1)S(1)} %get-tuple-element.17.refs_7_.own, bf16[16,128,640]{2,1,0:T(8,128)(2,1)} %collective-permute-done.3.refs_9_.lower, ...), custom_call_target="tpu_custom_call" | custom-call | flops 1000 | bytes 1000 | tf_op jit(solution)/shard_map/pallas_call | solution.py:219
  43.7 2.2 %collective-permute-start.12 = (f16[2,8,2,32,128]{4,3,1,0,2:T(8,128)(2,1)S(1)}, f16[2,8,2,32,128]{4,3,1,0,2:T(8,128)(2,1)S(1)}, u32[]{:S(2)}, u32[]{:S(2)}) collective-permute-start(f16[2,8,2,32,128]{4,3,1,0,2:T(8,128)(2,1)S(1)} %fusion.5), channel_id=1, source_target_pairs={{0,1},{1,0},{2,3},{3,2},{4,5},{5,4},{6,7},{7,6},{8,9},{9,8},{10,11... | collective-permute-start | bytes 786440 | tf_op jit(solution)/shard_map/ppermute | solution.py:242
  45.9 0.1 multiply_convert_fusion
  46.1 1.3 %collective-permute-start.11 = (f16[2,8,128,128]{3,2,1,0:T(8,128)(2,1)S(1)}, f16[2,8,128,128]{3,2,1,0:T(8,128)(2,1)S(1)}, u32[]{:S(2)}, u32[]{:S(2)}) collective-permute-start(f16[2,8,128,128]{3,2,1,0:T(8,128)(2,1)S(1)} %multiply_convert_fusion), channel_id=1, source_target_pairs={{0,4},{8,12},{1,5},{9,13},{2,6},{10,14},{3,7},{11,15},{16,20},{24,... | collective-permute-start | bytes 1572872 | tf_op jit(solution)/shard_map/ppermute | solution.py:305
  47.4 2.8 %collective-permute-done.12 = f16[2,8,2,32,128]{4,3,1,0,2:T(8,128)(2,1)S(1)} collective-permute-done((f16[2,8,2,32,128]{4,3,1,0,2:T(8,128)(2,1)S(1)}, f16[2,8,2,32,128]{4,3,1,0,2:T(8,128)(2,1)S(1)}, u32[]{:S(2)}, u32[]{:S(2)}) %collective-permute-start.12) | collective-permute-done | bytes 262176 | tf_op jit(solution)/shard_map/ppermute | solution.py:242
  50.3 2.7 %collective-permute-start.13 = (f16[2,8,1,32,128]{4,3,2,1,0:T(8,128)(2,1)S(1)}, f16[2,8,1,32,128]{4,3,2,1,0:T(8,128)(2,1)S(1)}, u32[]{:S(2)}, u32[]{:S(2)}) collective-permute-start(f16[2,8,1,32,128]{4,3,2,1,0:T(8,128)(2,1)S(1)} %fusion.8), channel_id=1, source_target_pairs={{0,2},{1,3},{2,0},{3,1},{4,6},{5,7},{6,4},{7,5},{8,10},{9,11},{10,... | collective-permute-start | bytes 393224 | tf_op jit(solution)/shard_map/ppermute | solution.py:242
  53.0 2.0 %collective-permute-done.11 = f16[2,8,128,128]{3,2,1,0:T(8,128)(2,1)S(1)} collective-permute-done((f16[2,8,128,128]{3,2,1,0:T(8,128)(2,1)S(1)}, f16[2,8,128,128]{3,2,1,0:T(8,128)(2,1)S(1)}, u32[]{:S(2)}, u32[]{:S(2)}) %collective-permute-start.11) | collective-permute-done | bytes 524320 | tf_op jit(solution)/shard_map/ppermute | solution.py:305
  55.1 1.2 %shard_map.68 = (f32[2,8,128,128]{3,2,1,0:T(8,128)S(1)}, f32[32,128]{1,0:T(8,128)S(1)}) custom-call(f32[8,16,640]{2,1,0:T(8,128)S(1)} %get-tuple-element.23.roots, bf16[8,128,640]{2,1,0:T(8,128)(2,1)S(1)} %get-tuple-element.17.refs_7_.own, bf16[8,128,640]{2,1,0:T(8,128)(2,1)S(1)} %collective-permute-done.9.far, f32[2,8,128,128]{3,2,1,0:T(8,128)S(1)} %convert_multiply_fusion.add), custom_call_target="tpu_custom_call" | custom-call | flops 1000 | bytes 1000 | tf_op jit(solution)/shard_map/pallas_call | solution.py:185
  56.5 5.7 %collective-permute-start.14 = (f16[2,8,32,128]{3,2,1,0:T(8,128)(2,1)S(1)}, f16[2,8,32,128]{3,2,1,0:T(8,128)(2,1)S(1)}, u32[]{:S(2)}, u32[]{:S(2)}) collective-permute-start(f16[2,8,32,128]{3,2,1,0:T(8,128)(2,1)S(1)} %get-tuple-element.29), channel_id=1, source_target_pairs={{4,7},{5,6},{6,5},{7,4},{12,15},{13,14},{14,13},{15,12},{20,23},{2... | collective-permute-start | bytes 393224 | tf_op jit(solution)/shard_map/ppermute | solution.py:270
  62.2 1.9 %collective-permute-start.15 = (f16[2,8,32,128]{3,2,1,0:T(8,128)(2,1)S(1)}, f16[2,8,32,128]{3,2,1,0:T(8,128)(2,1)S(1)}, u32[]{:S(2)}, u32[]{:S(2)}) collective-permute-start(f16[2,8,32,128]{3,2,1,0:T(8,128)(2,1)S(1)} %get-tuple-element.31), channel_id=1, source_target_pairs={{4,6},{5,7},{6,4},{7,5},{12,14},{13,15},{14,12},{15,13},{20,22},{2... | collective-permute-start | bytes 393224 | tf_op jit(solution)/shard_map/ppermute | solution.py:270
  64.2 2.2 %collective-permute-start.16 = (f16[2,8,32,128]{3,2,1,0:T(8,128)(2,1)S(1)}, f16[2,8,32,128]{3,2,1,0:T(8,128)(2,1)S(1)}, u32[]{:S(2)}, u32[]{:S(2)}) collective-permute-start(f16[2,8,32,128]{3,2,1,0:T(8,128)(2,1)S(1)} %get-tuple-element.30), channel_id=1, source_target_pairs={{4,5},{5,4},{6,7},{7,6},{12,13},{13,12},{14,15},{15,14},{20,21},{2... | collective-permute-start | bytes 393224 | tf_op jit(solution)/shard_map/ppermute | solution.py:270
  66.4 4.3 %collective-permute-done.15 = f16[2,8,32,128]{3,2,1,0:T(8,128)(2,1)S(1)} collective-permute-done((f16[2,8,32,128]{3,2,1,0:T(8,128)(2,1)S(1)}, f16[2,8,32,128]{3,2,1,0:T(8,128)(2,1)S(1)}, u32[]{:S(2)}, u32[]{:S(2)}) %collective-permute-start.15) | collective-permute-done | bytes 131104 | tf_op jit(solution)/shard_map/ppermute | solution.py:270
  70.8 1.2 %collective-permute-done.16 = f16[2,8,32,128]{3,2,1,0:T(8,128)(2,1)S(1)} collective-permute-done((f16[2,8,32,128]{3,2,1,0:T(8,128)(2,1)S(1)}, f16[2,8,32,128]{3,2,1,0:T(8,128)(2,1)S(1)}, u32[]{:S(2)}, u32[]{:S(2)}) %collective-permute-start.16) | collective-permute-done | bytes 131104 | tf_op jit(solution)/shard_map/ppermute | solution.py:270
  71.9 0.1 bitcast_select_fusion
  72.0 0.9 %maximum_bitcast_fusion = f32[2,8,1,32,384]{4,3,2,1,0:T(8,128)} fusion(f32[2,8,32,128]{3,2,1,0:T(8,128)S(1)} %fusion.7, f32[2,8,32,128]{3,2,1,0:T(8,128)S(1)} %bitcast_select_fusion, f32[2,8,32,128]{3,2,1,0:T(8,128)S(1)} %add_bitcast_fusion), kind=kLoop, calls=%fused_computation.2 | loop fusion | flops 393216 | bytes 1572864 | tf_op jit(solution)/shard_map/broadcast_in_dim | solution.py:312
  (43 shorter events, 1.5 us)
Async XLA Ops:
  0.0 10.2 %copy-start.4 = (s32[1,1,8,3,1]{2,4,3,1,0:T(1,128)S(1)}, s32[1,1,8,3,1]{2,4,3,1,0:T(1,128)}, u32[]{:S(2)}) copy-start(s32[1,1,8,3,1]{2,4,3,1,0:T(1,128)} %param.7) | copy-start | bytes 292
  0.0 2.1 %copy-start = (bf16[1,1,8,3,1,128,640]{6,5,4,3,2,1,0:T(8,128)(2,1)S(1)}, bf16[1,1,8,3,1,128,640]{6,5,4,3,2,1,0:T(8,128)(2,1)}, u32[]{:S(2)}) copy-start(bf16[1,1,8,3,1,128,640]{6,5,4,3,2,1,0:T(8,128)(2,1)} %param.6) | copy-start | bytes 11796484
  2.1 16.0 %copy-start.1 = (f32[10240]{0:T(1024)S(1)}, f32[10240]{0:T(1024)}, u32[]{:S(2)}) copy-start(f32[10240]{0:T(1024)} %param.10) | copy-start | bytes 122884
  2.1 16.0 %copy-start.2 = (f32[8]{0:T(128)S(1)}, f32[8]{0:T(128)}, u32[]{:S(2)}) copy-start(f32[8]{0:T(128)} %refs_4_.1) | copy-start | bytes 100
  2.1 16.1 %copy-start.3 = (f32[2]{0:T(128)S(1)}, f32[2]{0:T(128)}, u32[]{:S(2)}) copy-start(f32[2]{0:T(128)} %refs_5_.1) | copy-start | bytes 28
  4.1 14.1 %collective-permute-start.3 = (bf16[16,128,640]{2,1,0:T(8,128)(2,1)}, bf16[16,128,640]{2,1,0:T(8,128)(2,1)}, u32[]{:S(2)}, u32[]{:S(2)}) collective-permute-start(bf16[16,128,640]{2,1,0:T(8,128)(2,1)} %get-tuple-element.18.refs_8_), channel_id=1, source_target_pairs={{4,0},{12,8},{5,1},{13,9},{6,2},{14,10},{7,3},{15,11},{20,16},{28,... | collective-permute-start | bytes 7864328 | tf_op jit(solution)/shard_map/ppermute | solution.py:297
  7.6 8.8 %collective-permute-start.4 = (bf16[2,128,640]{2,1,0:T(8,128)(2,1)S(1)}, bf16[2,128,640]{2,1,0:T(8,128)(2,1)S(1)}, u32[]{:S(2)}, u32[]{:S(2)}) collective-permute-start(bf16[2,128,640]{2,1,0:T(8,128)(2,1)S(1)} %get-tuple-element.20), channel_id=1, source_target_pairs={{0,8},{4,12},{8,0},{12,4},{1,9},{5,13},{9,1},{13,5},{2,10},{6,14},... | collective-permute-start | bytes 983048 | tf_op jit(solution)/shard_map/ppermute | solution.py:294
  11.1 5.1 %collective-permute-start = (s32[25]{0:T(128)S(1)}, s32[25]{0:T(128)S(1)}, u32[]{:S(2)}, u32[]{:S(2)}) collective-permute-start(s32[25]{0:T(128)S(1)} %pad_add_fusion.refs_0_), channel_id=1, source_target_pairs={{0,4},{4,8},{8,12},{12,0},{1,5},{5,9},{9,13},{13,1},{2,6},{6,10},{... | collective-permute-start | bytes 308 | tf_op jit(solution)/shard_map/ppermute | solution.py:285
  11.1 5.2 %collective-permute-start.1 = (s32[25]{0:T(128)S(1)}, s32[25]{0:T(128)S(1)}, u32[]{:S(2)}, u32[]{:S(2)}) collective-permute-start(s32[25]{0:T(128)S(1)} %pad_add_fusion.refs_0_), channel_id=1, source_target_pairs={{0,8},{4,12},{8,0},{12,4},{1,9},{5,13},{9,1},{13,5},{2,10},{6,14},... | collective-permute-start | bytes 308 | tf_op jit(solution)/shard_map/ppermute | solution.py:285
  11.2 5.2 %collective-permute-start.2 = (s32[25]{0:T(128)S(1)}, s32[25]{0:T(128)S(1)}, u32[]{:S(2)}, u32[]{:S(2)}) collective-permute-start(s32[25]{0:T(128)S(1)} %pad_add_fusion.refs_0_), channel_id=1, source_target_pairs={{0,12},{4,0},{8,4},{12,8},{1,13},{5,1},{9,5},{13,9},{2,14},{6,2},{... | collective-permute-start | bytes 308 | tf_op jit(solution)/shard_map/ppermute | solution.py:285
  16.4 23.3 %collective-permute-start.10 = (bf16[6,128,640]{2,1,0:T(8,128)(2,1)S(1)}, bf16[6,128,640]{2,1,0:T(8,128)(2,1)S(1)}, u32[]{:S(2)}, u32[]{:S(2)}) collective-permute-start(bf16[6,128,640]{2,1,0:T(8,128)(2,1)S(1)} %shard_map.65.refs_10_), channel_id=1, source_target_pairs={{0,8},{4,12},{8,0},{12,4},{1,9},{5,13},{9,1},{13,5},{2,10},{6,14},... | collective-permute-start | bytes 2949128 | tf_op jit(solution)/shard_map/ppermute | solution.py:296
  25.9 7.0 %collective-permute-start.5 = (f16[2,8,2,32,128]{4,3,1,0,2:T(8,128)(2,1)S(1)}, f16[2,8,2,32,128]{4,3,1,0,2:T(8,128)(2,1)S(1)}, u32[]{:S(2)}, u32[]{:S(2)}) collective-permute-start(f16[2,8,2,32,128]{4,3,1,0,2:T(8,128)(2,1)S(1)} %fusion.3), channel_id=1, source_target_pairs={{0,1},{1,0},{2,3},{3,2},{4,5},{5,4},{6,7},{7,6},{8,9},{9,8},{10,11... | collective-permute-start | bytes 786440 | tf_op jit(solution)/shard_map/ppermute | solution.py:242
  27.4 8.0 %collective-permute-start.7 = (f16[2,8,2,32,128]{4,3,1,0,2:T(8,128)(2,1)S(1)}, f16[2,8,2,32,128]{4,3,1,0,2:T(8,128)(2,1)S(1)}, u32[]{:S(2)}, u32[]{:S(2)}) collective-permute-start(f16[2,8,2,32,128]{4,3,1,0,2:T(8,128)(2,1)S(1)} %fusion.4), channel_id=1, source_target_pairs={{0,1},{1,0},{2,3},{3,2},{8,9},{9,8},{10,11},{11,10},{16,17},{17,16... | collective-permute-start | bytes 786440 | tf_op jit(solution)/shard_map/ppermute | solution.py:242
  28.1 27.0 %collective-permute-start.9 = (bf16[8,128,640]{2,1,0:T(8,128)(2,1)S(1)}, bf16[8,128,640]{2,1,0:T(8,128)(2,1)S(1)}, u32[]{:S(2)}, u32[]{:S(2)}) collective-permute-start(bf16[8,128,640]{2,1,0:T(8,128)(2,1)S(1)} %get-tuple-element.24), channel_id=1, source_target_pairs={{0,12},{8,4},{1,13},{9,5},{2,14},{10,6},{3,15},{11,7},{16,28},{24,... | collective-permute-start | bytes 3932168 | tf_op jit(solution)/shard_map/ppermute | solution.py:300
  33.0 5.2 %collective-permute-start.6 = (f16[2,8,1,32,128]{4,3,1,0,2:T(8,128)(2,1)S(1)}, f16[2,8,1,32,128]{4,3,1,0,2:T(8,128)(2,1)S(1)}, u32[]{:S(2)}, u32[]{:S(2)}) collective-permute-start(f16[2,8,1,32,128]{4,3,1,0,2:T(8,128)(2,1)S(1)} %multiply_convert_fusion.6), channel_id=1, source_target_pairs={{0,2},{1,3},{2,0},{3,1},{4,6},{5,7},{6,4},{7,5},{8,10},{9,11},{10,... | collective-permute-start | bytes 393224 | tf_op jit(solution)/shard_map/ppermute | solution.py:242
  35.5 2.7 %collective-permute-start.8 = (f16[2,8,1,32,128]{4,3,1,0,2:T(8,128)(2,1)S(1)}, f16[2,8,1,32,128]{4,3,1,0,2:T(8,128)(2,1)S(1)}, u32[]{:S(2)}, u32[]{:S(2)}) collective-permute-start(f16[2,8,1,32,128]{4,3,1,0,2:T(8,128)(2,1)S(1)} %multiply_convert_fusion.5), channel_id=1, source_target_pairs={{0,2},{1,3},{2,0},{3,1},{8,10},{9,11},{10,8},{11,9},{16,18},{17,19... | collective-permute-start | bytes 393224 | tf_op jit(solution)/shard_map/ppermute | solution.py:242
  43.7 6.5 %collective-permute-start.12 = (f16[2,8,2,32,128]{4,3,1,0,2:T(8,128)(2,1)S(1)}, f16[2,8,2,32,128]{4,3,1,0,2:T(8,128)(2,1)S(1)}, u32[]{:S(2)}, u32[]{:S(2)}) collective-permute-start(f16[2,8,2,32,128]{4,3,1,0,2:T(8,128)(2,1)S(1)} %fusion.5), channel_id=1, source_target_pairs={{0,1},{1,0},{2,3},{3,2},{4,5},{5,4},{6,7},{7,6},{8,9},{9,8},{10,11... | collective-permute-start | bytes 786440 | tf_op jit(solution)/shard_map/ppermute | solution.py:242
  46.1 8.9 %collective-permute-start.11 = (f16[2,8,128,128]{3,2,1,0:T(8,128)(2,1)S(1)}, f16[2,8,128,128]{3,2,1,0:T(8,128)(2,1)S(1)}, u32[]{:S(2)}, u32[]{:S(2)}) collective-permute-start(f16[2,8,128,128]{3,2,1,0:T(8,128)(2,1)S(1)} %multiply_convert_fusion), channel_id=1, source_target_pairs={{0,4},{8,12},{1,5},{9,13},{2,6},{10,14},{3,7},{11,15},{16,20},{24,... | collective-permute-start | bytes 1572872 | tf_op jit(solution)/shard_map/ppermute | solution.py:305
  50.3 6.0 %collective-permute-start.13 = (f16[2,8,1,32,128]{4,3,2,1,0:T(8,128)(2,1)S(1)}, f16[2,8,1,32,128]{4,3,2,1,0:T(8,128)(2,1)S(1)}, u32[]{:S(2)}, u32[]{:S(2)}) collective-permute-start(f16[2,8,1,32,128]{4,3,2,1,0:T(8,128)(2,1)S(1)} %fusion.8), channel_id=1, source_target_pairs={{0,2},{1,3},{2,0},{3,1},{4,6},{5,7},{6,4},{7,5},{8,10},{9,11},{10,... | collective-permute-start | bytes 393224 | tf_op jit(solution)/shard_map/ppermute | solution.py:242
  56.5 9.9 %collective-permute-start.14 = (f16[2,8,32,128]{3,2,1,0:T(8,128)(2,1)S(1)}, f16[2,8,32,128]{3,2,1,0:T(8,128)(2,1)S(1)}, u32[]{:S(2)}, u32[]{:S(2)}) collective-permute-start(f16[2,8,32,128]{3,2,1,0:T(8,128)(2,1)S(1)} %get-tuple-element.29), channel_id=1, source_target_pairs={{4,7},{5,6},{6,5},{7,4},{12,15},{13,14},{14,13},{15,12},{20,23},{2... | collective-permute-start | bytes 393224 | tf_op jit(solution)/shard_map/ppermute | solution.py:270
  62.2 8.5 %collective-permute-start.15 = (f16[2,8,32,128]{3,2,1,0:T(8,128)(2,1)S(1)}, f16[2,8,32,128]{3,2,1,0:T(8,128)(2,1)S(1)}, u32[]{:S(2)}, u32[]{:S(2)}) collective-permute-start(f16[2,8,32,128]{3,2,1,0:T(8,128)(2,1)S(1)} %get-tuple-element.31), channel_id=1, source_target_pairs={{4,6},{5,7},{6,4},{7,5},{12,14},{13,15},{14,12},{15,13},{20,22},{2... | collective-permute-start | bytes 393224 | tf_op jit(solution)/shard_map/ppermute | solution.py:270
  64.2 7.8 %collective-permute-start.16 = (f16[2,8,32,128]{3,2,1,0:T(8,128)(2,1)S(1)}, f16[2,8,32,128]{3,2,1,0:T(8,128)(2,1)S(1)}, u32[]{:S(2)}, u32[]{:S(2)}) collective-permute-start(f16[2,8,32,128]{3,2,1,0:T(8,128)(2,1)S(1)} %get-tuple-element.30), channel_id=1, source_target_pairs={{4,5},{5,4},{6,7},{7,6},{12,13},{13,12},{14,15},{15,14},{20,21},{2... | collective-permute-start | bytes 393224 | tf_op jit(solution)/shard_map/ppermute | solution.py:270
